TPU v7x, 32 devices: a whole 2x2x4 slice. The times are simulated.
32 devices in a mesh: row: 4 (over z), col: 8 (over y, x, core).
Axes of the slice: x: 2, y: 2, z: 4, core: 2. Of those that a mesh axis runs over, the one named last changes fastest.
Arguments:
- features: bfloat16 [8192, 512], P('row'), may hold values from -6 to 6
- logits: float32 [8192, 128], P(('row', 'col')), may hold values from -16 to 16
Outputs:
- memberships: float32 [8192, 128], P(('row', 'col'))
- standardized: float32 [8192, 128], P(('row', 'col'))
All inputs are finite; a program needn't handle non-finite values.
Results may differ from a plain program's by a relative error of at most 0.0003.
Values may be sent and summed in bfloat16 or wider, within the bound.
No kernel may reach another device: no remote copies, remote signals or barrier semaphores. Data moves between devices by JAX's collectives and lax.ppermute only.
A program may use at most 64 MiB of HBM per device.

v0:
```python
import math

import jax
import jax.numpy as jnp
from jax import lax
from jax.sharding import PartitionSpec as P

ITERS = 2


def kernel_product(left_rows, right_rows, members):
    count = left_rows.shape[0]
    feature_width = left_rows.shape[1]
    block_rows = math.gcd(count, 512)
    blocks = left_rows.reshape(count // block_rows, block_rows, feature_width)

    def block_product(block):
        inner = jnp.einsum("bf,nf->bn", block, right_rows, preferred_element_type=jnp.float32)
        base = 1.0 + inner / feature_width
        kernel = base * base * base
        return jnp.dot(
            kernel, members, precision=lax.Precision.HIGHEST, preferred_element_type=jnp.float32
        )

    return lax.map(block_product, blocks).reshape(count, members.shape[1])


def on_device(features, logits):
    frames = logits.shape[0]
    column = lax.axis_index("col")
    own_rows = lax.dynamic_slice_in_dim(features, column * frames, frames, 0)
    column_panel = lax.all_gather(own_rows, "row", axis=0, tiled=True)
    raised = jnp.exp(logits)
    members = raised / jnp.sum(raised, axis=1, keepdims=True)
    standardized = members
    for iteration in range(ITERS):
        members_row = lax.all_gather(members, "col", axis=0, tiled=True)
        scores = lax.psum_scatter(
            kernel_product(column_panel, features, members_row),
            "row",
            scatter_dimension=0,
            tiled=True,
        )
        cluster_size, weighted = lax.psum(
            (jnp.sum(members, axis=0), jnp.sum(members * scores, axis=0)), ("row", "col")
        )
        compact = weighted / (cluster_size * cluster_size)
        distance = compact[None, :] - 2.0 * scores / cluster_size[None, :]
        centered = distance - jnp.mean(distance, axis=1, keepdims=True)
        spread = jnp.mean(centered * centered, axis=1, keepdims=True)
        standardized = centered / jnp.sqrt(spread + 1e-06)
        raised = jnp.exp(-2.0 * standardized)
        members = raised / jnp.sum(raised, axis=1, keepdims=True)
    return (members, standardized)


def solution(mesh):
    return jax.shard_map(
        on_device,
        mesh=mesh,
        in_specs=(P("row", None), P(("row", "col"), None)),
        out_specs=(P(("row", "col"), None), P(("row", "col"), None)),
        check_vma=False,
    )
```

profile of v0, /device:TPU:0, one launch (start us, length us, event | category | flops | bytes accessed | tf_op | source)
XLA Modules:
  0.0 256.8 jit_solution(18136561742326605987)
XLA Ops:
  7.2 0.0 all-gather.4.cloned.1.call-start
  7.2 1.7 constant_dynamic-slice_fusion
  8.9 0.0 all-gather.4.cloned.1.call-update
  8.9 0.0 all-gather.6.cloned.1.call-start
  9.0 1.0 exponential_reduce_fusion
  10.0 1.7 exponential_divide_fusion
  11.7 0.0 all-gather.6.cloned.1.call-update
  11.7 0.0 reduce-scatter.3.cloned.1.call-start
  11.8 28.5 %all-gather.4.cloned.1.call-done = bf16[1024,512]{1,0:T(8,128)(2,1)} async-done(((bf16[256,512]{1,0:T(8,128)(2,1)}), bf16[1024,512]{1,0:T(8,128)(2,1)}) %all-gather.4.cloned.1.call-update) | async-done | bytes 1048592 | tf_op jit(solution)/shard_map/all_gather | solution.py:32
  40.2 25.5 %all-gather.6.cloned.1.call-done = f32[2048,128]{1,0:T(8,128)} async-done(((f32[256,128]{1,0:T(8,128)}), f32[2048,128]{1,0:T(8,128)}) %all-gather.6.cloned.1.call-update) | async-done | bytes 1048592 | tf_op jit(solution)/shard_map/all_gather | solution.py:37
  65.7 0.0 copy-start.3
  65.8 13.7 %while.20 = (s32[]{:T(128)}, f32[2,512,128]{2,1,0:T(8,128)S(1)}, bf16[2,512,512]{2,1,0:T(8,128)(2,1)}, bf16[2048,512]{1,0:T(8,128)(2,1)}, f32[2048,128]{1,0:T(8,128)}, /*index=5*/s32[]{:T(128)}) while((s32[]{:T(128)}, f32[2,512,128]{2,1,0:T(8,128)S(1)}, bf16[2,512,512]{2,1,0:T(8,128)(2,1)}, bf16[2048,512]{1,0:T(8,128)(2,1)}, ...), condition=%wide.region_2.3_spmd, body=%wide.region_1.2_spmd.sunk | while | flops 2688548864 | bytes 16515685 | solution.py:25
  65.8 0.0 copy-start.5
  65.8 3.1 %fusion.48 = f32[512,2048]{1,0:T(8,128)S(1)} fusion(bf16[2048,512]{1,0:T(8,128)(2,1)} %get-tuple-element.165, bf16[2,512,512]{2,1,0:T(8,128)(2,1)} %get-tuple-element.164, s32[]{:T(128)} %get-tuple-element.156), kind=kOutput, calls=%fused_computation.8.clone.1 | convolution fusion | flops 1073741824 | bytes 6816256 | tf_op jit(solution)/shard_map/while/body/eval_jaxpr/bf,nf->bn/dot_general | solution.py:18
  68.9 0.0 copy-done.5
  68.9 3.7 %fusion.49 = f32[2,512,128]{2,1,0:T(8,128)S(1)} fusion(f32[2,512,128]{2,1,0:T(8,128)S(1)} %get-tuple-element.157, s32[]{:T(128)} %get-tuple-element.156, f32[2048,128]{1,0:T(8,128)S(1)} %copy-done.5, f32[512,2048]{1,0:T(8,128)S(1)} %fusion.48), kind=kOutput, calls=%fused_computation.7.clone.1 | convolution fusion | flops 1614807040 | bytes 5505028 | tf_op jit(solution)/shard_map/while/body/eval_jaxpr/dot_general | solution.py:21
  72.6 0.0 copy-start.5
  72.6 3.1 %fusion.48 = f32[512,2048]{1,0:T(8,128)S(1)} fusion(bf16[2048,512]{1,0:T(8,128)(2,1)} %get-tuple-element.165, bf16[2,512,512]{2,1,0:T(8,128)(2,1)} %get-tuple-element.164, s32[]{:T(128)} %get-tuple-element.156), kind=kOutput, calls=%fused_computation.8.clone.1 | convolution fusion | flops 1073741824 | bytes 6816256 | tf_op jit(solution)/shard_map/while/body/eval_jaxpr/bf,nf->bn/dot_general | solution.py:18
  75.8 0.0 copy-done.5
  75.8 3.7 %fusion.49 = f32[2,512,128]{2,1,0:T(8,128)S(1)} fusion(f32[2,512,128]{2,1,0:T(8,128)S(1)} %get-tuple-element.157, s32[]{:T(128)} %get-tuple-element.156, f32[2048,128]{1,0:T(8,128)S(1)} %copy-done.5, f32[512,2048]{1,0:T(8,128)S(1)} %fusion.48), kind=kOutput, calls=%fused_computation.7.clone.1 | convolution fusion | flops 1614807040 | bytes 5505028 | tf_op jit(solution)/shard_map/while/body/eval_jaxpr/dot_general | solution.py:21
  79.5 0.0 copy-start.2
  79.5 0.8 copy-done.2
  80.3 0.0 reduce-scatter.3.cloned.1.call-update
  80.3 0.0 all-gather.8.cloned.1.call-start
  80.4 21.7 %reduce-scatter.3.cloned.1.call-done = f32[256,128]{1,0:T(8,128)} async-done(((f32[1024,128]{1,0:T(8,128)}), f32[256,128]{1,0:T(8,128)}) %reduce-scatter.3.cloned.1.call-update) | async-done | bytes 131088 | tf_op jit(solution)/shard_map/reduce_scatter | solution.py:38
  102.1 0.0 copy-done.3
  102.1 1.0 multiply_reduce_fusion.3
  103.1 38.6 %all-reduce.1 = (f32[128]{0:T(128)S(1)}, f32[128]{0:T(128)S(1)}) all-reduce(f32[128]{0:T(128)S(1)} %get-tuple-element.61, f32[128]{0:T(128)S(1)} %get-tuple-element.60), channel_id=1, replica_groups=mesh['row'=4,'col'=8] {'row','col'}, use_global_device_ids=true, to_apply=%region_7.8 | all-reduce | flops 256 | bytes 2048 | tf_op jit(solution)/shard_map/psum | solution.py:44
  141.7 1.0 fusion.30
  142.7 1.1 multiply_reduce_fusion.2
  143.8 1.1 fusion.28
  145.0 1.7 broadcast_divide_fusion
  146.7 0.0 all-gather.8.cloned.1.call-update
  146.7 0.0 reduce-scatter.5.cloned.1.call-start
  146.8 23.4 %all-gather.8.cloned.1.call-done = f32[2048,128]{1,0:T(8,128)} async-done(((f32[256,128]{1,0:T(8,128)}), f32[2048,128]{1,0:T(8,128)}) %all-gather.8.cloned.1.call-update) | async-done | bytes 1048592 | tf_op jit(solution)/shard_map/all_gather | solution.py:37
  170.2 0.0 copy-start
  170.2 13.7 %while.21 = (s32[]{:T(128)}, f32[2,512,128]{2,1,0:T(8,128)S(1)}, bf16[2,512,512]{2,1,0:T(8,128)(2,1)}, bf16[2048,512]{1,0:T(8,128)(2,1)}, f32[2048,128]{1,0:T(8,128)}, /*index=5*/s32[]{:T(128)}) while((s32[]{:T(128)}, f32[2,512,128]{2,1,0:T(8,128)S(1)}, bf16[2,512,512]{2,1,0:T(8,128)(2,1)}, bf16[2048,512]{1,0:T(8,128)(2,1)}, ...), condition=%wide.region_12.13_spmd, body=%wide.region_11.12_spmd.sunk | while | flops 2688548864 | bytes 16515685 | solution.py:25
  170.2 0.0 copy-start.6
  170.2 3.1 %fusion.53 = f32[512,2048]{1,0:T(8,128)S(1)} fusion(bf16[2048,512]{1,0:T(8,128)(2,1)} %get-tuple-element.183, bf16[2,512,512]{2,1,0:T(8,128)(2,1)} %get-tuple-element.182, s32[]{:T(128)} %get-tuple-element.174), kind=kOutput, calls=%fused_computation.22.clone.1 | convolution fusion | flops 1073741824 | bytes 6816256 | tf_op jit(solution)/shard_map/while/body/eval_jaxpr/bf,nf->bn/dot_general | solution.py:18
  173.3 0.0 copy-done.6
  173.4 3.7 %fusion.54 = f32[2,512,128]{2,1,0:T(8,128)S(1)} fusion(f32[2,512,128]{2,1,0:T(8,128)S(1)} %get-tuple-element.175, s32[]{:T(128)} %get-tuple-element.174, f32[2048,128]{1,0:T(8,128)S(1)} %copy-done.6, f32[512,2048]{1,0:T(8,128)S(1)} %fusion.53), kind=kOutput, calls=%fused_computation.21.clone.1 | convolution fusion | flops 1614807040 | bytes 5505028 | tf_op jit(solution)/shard_map/while/body/eval_jaxpr/dot_general | solution.py:21
  177.1 0.0 copy-start.6
  177.1 3.1 %fusion.53 = f32[512,2048]{1,0:T(8,128)S(1)} fusion(bf16[2048,512]{1,0:T(8,128)(2,1)} %get-tuple-element.183, bf16[2,512,512]{2,1,0:T(8,128)(2,1)} %get-tuple-element.182, s32[]{:T(128)} %get-tuple-element.174), kind=kOutput, calls=%fused_computation.22.clone.1 | convolution fusion | flops 1073741824 | bytes 6816256 | tf_op jit(solution)/shard_map/while/body/eval_jaxpr/bf,nf->bn/dot_general | solution.py:18
  180.2 0.0 copy-done.6
  180.2 3.7 %fusion.54 = f32[2,512,128]{2,1,0:T(8,128)S(1)} fusion(f32[2,512,128]{2,1,0:T(8,128)S(1)} %get-tuple-element.175, s32[]{:T(128)} %get-tuple-element.174, f32[2048,128]{1,0:T(8,128)S(1)} %copy-done.6, f32[512,2048]{1,0:T(8,128)S(1)} %fusion.53), kind=kOutput, calls=%fused_computation.21.clone.1 | convolution fusion | flops 1614807040 | bytes 5505028 | tf_op jit(solution)/shard_map/while/body/eval_jaxpr/dot_general | solution.py:21
  183.9 0.0 copy-start.1
  183.9 0.8 copy-done.1
  184.7 0.0 reduce-scatter.5.cloned.1.call-update
  184.7 21.8 %reduce-scatter.5.cloned.1.call-done = f32[256,128]{1,0:T(8,128)} async-done(((f32[1024,128]{1,0:T(8,128)}), f32[256,128]{1,0:T(8,128)}) %reduce-scatter.5.cloned.1.call-update) | async-done | bytes 131088 | tf_op jit(solution)/shard_map/reduce_scatter | solution.py:38
  206.5 0.0 copy-done
  206.5 1.1 multiply_reduce_fusion.1
  207.6 38.6 %all-reduce = (f32[128]{0:T(128)S(1)}, f32[128]{0:T(128)S(1)}) all-reduce(f32[128]{0:T(128)S(1)} %get-tuple-element.59, f32[128]{0:T(128)S(1)} %get-tuple-element.58), channel_id=1, replica_groups=mesh['row'=4,'col'=8] {'row','col'}, use_global_device_ids=true, to_apply=%region_17.18 | all-reduce | flops 256 | bytes 2048 | tf_op jit(solution)/shard_map/psum | solution.py:44
  246.2 1.0 fusion.29
  247.2 1.1 multiply_reduce_fusion
  248.3 1.1 fusion.27
  249.5 0.0 copy-start.4
  249.5 0.8 fusion.26
  250.2 0.0 copy-done.4
  (8 shorter events, 0.1 us)
Async XLA Ops:
  7.2 33.1 %all-gather.4.cloned.1.call-start = ((), (), s32[]{:S(2)}) async-start(), calls=%async_computation.2 | async-start | bytes 1310720 | tf_op jit(solution)/shard_map/all_gather | solution.py:32
  8.9 56.8 %all-gather.6.cloned.1.call-start = ((), (), s32[]{:S(2)}) async-start(), calls=%async_computation.3 | async-start | bytes 1179648 | tf_op jit(solution)/shard_map/all_gather | solution.py:37
  11.7 90.4 %reduce-scatter.3.cloned.1.call-start = ((), (), s32[]{:S(2)}) async-start(), calls=%async_computation.4 | async-start | bytes 655360 | tf_op jit(solution)/shard_map/reduce_scatter | solution.py:38
  65.7 36.4 %copy-start.3 = (f32[256,128]{1,0:T(8,128)S(1)}, f32[256,128]{1,0:T(8,128)}, u32[]{:S(2)}) copy-start(f32[256,128]{1,0:T(8,128)} %param.7) | copy-start | bytes 393220
  65.8 3.1 %copy-start.5 = (f32[2048,128]{1,0:T(8,128)S(1)}, f32[2048,128]{1,0:T(8,128)}, u32[]{:S(2)}) copy-start(f32[2048,128]{1,0:T(8,128)} %get-tuple-element.166) | copy-start | bytes 3145732 | tf_op jit(solution)/shard_map/while
  72.6 3.1 %copy-start.5 = (f32[2048,128]{1,0:T(8,128)S(1)}, f32[2048,128]{1,0:T(8,128)}, u32[]{:S(2)}) copy-start(f32[2048,128]{1,0:T(8,128)} %get-tuple-element.166) | copy-start | bytes 3145732 | tf_op jit(solution)/shard_map/while
  79.5 0.8 copy-start.2
  80.3 89.8 %all-gather.8.cloned.1.call-start = ((), (), s32[]{:S(2)}) async-start(), calls=%async_computation.5 | async-start | bytes 1179648 | tf_op jit(solution)/shard_map/all_gather | solution.py:37
  146.7 59.8 %reduce-scatter.5.cloned.1.call-start = ((), (), s32[]{:S(2)}) async-start(), calls=%async_computation.6 | async-start | bytes 655360 | tf_op jit(solution)/shard_map/reduce_scatter | solution.py:38
  170.2 36.4 %copy-start = (f32[256,128]{1,0:T(8,128)S(1)}, f32[256,128]{1,0:T(8,128)}, u32[]{:S(2)}) copy-start(f32[256,128]{1,0:T(8,128)} %reduce-scatter.3.cloned.1.call-done) | copy-start | bytes 393220
  170.2 3.1 %copy-start.6 = (f32[2048,128]{1,0:T(8,128)S(1)}, f32[2048,128]{1,0:T(8,128)}, u32[]{:S(2)}) copy-start(f32[2048,128]{1,0:T(8,128)} %get-tuple-element.184) | copy-start | bytes 3145732 | tf_op jit(solution)/shard_map/while
  177.1 3.1 %copy-start.6 = (f32[2048,128]{1,0:T(8,128)S(1)}, f32[2048,128]{1,0:T(8,128)}, u32[]{:S(2)}) copy-start(f32[2048,128]{1,0:T(8,128)} %get-tuple-element.184) | copy-start | bytes 3145732 | tf_op jit(solution)/shard_map/while
  183.9 0.8 copy-start.1
  249.5 0.8 copy-start.4
Sparse Core Ops, SparseCore 0:
  9.6 30.6 all-gather.3
  42.7 22.9 all-gather.5
  80.4 21.6 reduce-scatter.2
  146.9 23.2 all-gather.7
  184.8 21.6 reduce-scatter.4
where the time goes:
time: 257 us
  waiting for transfers between devices  121 us (47%)
  blocking collectives  77.1 us (30%)
  matrix products  27.2 us (11%)
  between operations  13.9 us (5%)
  other arithmetic  13.8 us (5%)
  local copies, waits for them, and re-layouts  3.39 us (1%)
    psum x2, blocking collectives, on_device(): lax.psum((jnp.sum(members, axis=0), jnp.sum(members * scores, axis=0)), (...  77.1 us
    all_gather x2, waiting for transfers between devices, on_device(): members_row = lax.all_gather(members, 'col', axis=0, tiled=True)  48.8 us
    reduce_scatter x2, waiting for transfers between devices, on_device(): lax.psum_scatter(kernel_product(column_panel, features, members_row), 'ro...  43.5 us
    all_gather x1, waiting for transfers between devices, on_device(): column_panel = lax.all_gather(own_rows, 'row', axis=0, tiled=True)  28.5 us
    dot_general x4, matrix products, block_product(): jnp.dot(kernel, members, precision=lax.Precision.HIGHEST, preferred_eleme...  14.7 us
    dot_general x4, matrix products, block_product(): jnp.einsum('bf,nf->bn', block, right_rows, preferred_element_type=jnp.flo...  12.5 us
  transfers between devices with their start and end apart: 5, of which 5 were waited for; matrix products, arithmetic and copies ran while one was open for 1% of the time, Pallas kernels for 0%

commit v1 on v0

v1 whole, which is shorter than its diff:
```python
import functools

import jax
import jax.numpy as jnp
from jax import lax
from jax.experimental import pallas as pl
from jax.experimental.pallas import tpu as pltpu
from jax.sharding import PartitionSpec as P

ITERS = 2
STAT_ROWS = 8
VMEM_BYTES = 48 * 1024 * 1024


def split(x):
    high = x.astype(jnp.bfloat16)
    low = (x - high.astype(jnp.float32)).astype(jnp.bfloat16)
    return high, low


def kernel_body(rows_ref, plane_ref, high_ref, low_ref):
    inner = lax.dot_general(
        rows_ref[...],
        plane_ref[...],
        (((1,), (1,)), ((), ())),
        preferred_element_type=jnp.float32,
    )
    t = inner / rows_ref.shape[1]
    high_ref[...], low_ref[...] = split(t * (3.0 + t * (3.0 + t)))


def kernel_block(rows, plane):
    count, width = rows.shape
    total = plane.shape[0]
    step = min(total, 512)
    return pl.pallas_call(
        kernel_body,
        grid=(total // step,),
        in_specs=[
            pl.BlockSpec((count, width), lambda i: (0, 0)),
            pl.BlockSpec((step, width), lambda i: (i, 0)),
        ],
        out_specs=[pl.BlockSpec((count, step), lambda i: (0, i))] * 2,
        out_shape=[jax.ShapeDtypeStruct((count, total), jnp.bfloat16)] * 2,
        compiler_params=pltpu.CompilerParams(vmem_limit_bytes=VMEM_BYTES),
        cost_estimate=pl.CostEstimate(
            flops=2 * count * total * width,
            bytes_accessed=2 * (count + total) * width + 4 * count * total,
            transcendentals=0,
        ),
    )(rows, plane)


def standardize(scores, size, weighted):
    distance = weighted / (size * size) - 2.0 * scores / size
    centered = distance - jnp.mean(distance, axis=1, keepdims=True)
    spread = jnp.mean(centered * centered, axis=1, keepdims=True)
    return centered / jnp.sqrt(spread + 1e-06)


def normalize(raised):
    return raised / jnp.sum(raised, axis=1, keepdims=True)


def product_body(first, n, crosses, has_near, *refs):
    refs = list(refs)
    take = lambda count: [refs.pop(0) for _ in range(count)]
    stats = None if first else take(1)[0]
    (even, odd) = take(2)
    others = take(crosses + has_near)
    blocks = crosses + has_near + 1
    kernels = take(2 * blocks)
    diag_out, = take(1)
    other_outs = take(crosses + has_near)
    t_even, t_odd = take(2)
    plane_hl, = take(1)
    (other_m,) = take(1)
    half = even.shape[0]
    clusters = even.shape[1]

    if first:
        member_of = lambda x: normalize(jnp.exp(x))
    else:
        weighted = stats[0:1, :]
        size = stats[1:2, :]
        member_of = lambda x: normalize(jnp.exp(-2.0 * standardize(x, size, weighted)))

    own = None
    for part, src in enumerate((even, odd)):
        for j in range(half // n):
            m = member_of(src[j * n : (j + 1) * n, :])
            if own is None:
                own = m
            high, low = split(m)
            at = part * half + j * n
            plane_hl[at : at + n, :clusters] = high
            plane_hl[at : at + n, clusters:] = low
    for i, src in enumerate(others):
        other_m[i * n : (i + 1) * n, :] = member_of(src[...])

    def product(high, low):
        both = jnp.dot(high[...], plane_hl[...], preferred_element_type=jnp.float32)
        rest = jnp.dot(low[...], plane_hl[:, :clusters], preferred_element_type=jnp.float32)
        return both[:, :clusters] + (both[:, clusters:] + rest)

    s = product(kernels[0], kernels[1])
    diag_out[...] = s
    total = jnp.sum(own * s, axis=0, keepdims=True)
    for i in range(crosses + has_near):
        s = product(kernels[2 + 2 * i], kernels[3 + 2 * i])
        other_outs[i][...] = s
        scale = 1.0 if has_near and i == 0 else 2.0
        total += scale * jnp.sum(other_m[i * n : (i + 1) * n, :] * s, axis=0, keepdims=True)
    over = (((0,), (0,)), ((), ()))
    for part, dst in enumerate((t_even, t_odd)):
        acc = None
        for i in range(has_near, crosses + has_near):
            high, low = split(other_m[i * n : (i + 1) * n, :])
            both = jnp.concatenate([high, low], axis=1)
            cols = slice(part * half, (part + 1) * half)
            a = lax.dot_general(
                kernels[2 + 2 * i][:, cols], both, over, preferred_element_type=jnp.float32
            )
            b = lax.dot_general(
                kernels[3 + 2 * i][:, cols], high, over, preferred_element_type=jnp.float32
            )
            a = a[:, :clusters] + (a[:, clusters:] + b)
            acc = a if acc is None else acc + a
        dst[:half, :] = jnp.zeros((half, clusters), jnp.float32) if acc is None else acc
    row = lax.broadcasted_iota(jnp.int32, (STAT_ROWS, clusters), 0)
    size = jnp.sum(own, axis=0, keepdims=True)
    stat = jnp.where(row == 0, total, jnp.where(row == 1, size, 0.0))
    t_even[half:, :] = stat
    t_odd[half:, :] = stat


def product_call(first, n, has_near, stats, even, odd, others, kernels):
    half, clusters = even.shape
    crosses = len(others) - has_near
    vmem = pl.BlockSpec(memory_space=pltpu.VMEM)
    args = ([] if first else [stats]) + [even, odd] + others + kernels
    f32 = jnp.float32
    outs = [jax.ShapeDtypeStruct((n, clusters), f32)] * (1 + len(others))
    outs += [jax.ShapeDtypeStruct((half + STAT_ROWS, clusters), f32)] * 2
    return pl.pallas_call(
        functools.partial(product_body, first, n, crosses, has_near),
        in_specs=[vmem] * len(args),
        out_specs=[vmem] * len(outs),
        out_shape=outs,
        scratch_shapes=[
            pltpu.VMEM((2 * half, 2 * clusters), jnp.bfloat16),
            pltpu.VMEM((max(n * len(others), 8), clusters), f32),
        ],
        compiler_params=pltpu.CompilerParams(vmem_limit_bytes=VMEM_BYTES),
        cost_estimate=pl.CostEstimate(
            flops=6 * (1 + len(others) + crosses) * n * 2 * half * clusters,
            bytes_accessed=8 * (1 + len(others)) * n * half,
            transcendentals=2 * half * clusters,
        ),
    )(*args)


def on_device(rows, cols, features, logits):
    n = logits.shape[0]
    column = lax.axis_index("col")
    masks = list(range(2, cols, 2))
    order = [0] + masks
    order = order + [k + 1 for k in order]
    has_near = int(rows % 2 == 0)
    half_rows = rows // 2
    if has_near:
        place = [2 * q if q < half_rows else 2 * (q - half_rows) + 1 for q in range(rows)]
        offsets = range(1, half_rows)
    else:
        place = list(range(rows))
        offsets = range(1, half_rows + 1)

    def by_col(x, mask):
        return lax.ppermute(x, "col", [(i, i ^ mask) for i in range(cols)])

    def near(x):
        return lax.ppermute(x, "row", [(i, i ^ 1) for i in range(rows)])

    def cross(x, d):
        return lax.ppermute(x, "row", [(place[(q + d) % rows], place[q]) for q in range(rows)])

    def cross_back(x, d):
        return lax.ppermute(x, "row", [(place[q], place[(q + d) % rows]) for q in range(rows)])

    def gather(x):
        crossed = [cross(x, d) for d in offsets]
        even = jnp.concatenate([x] + [by_col(x, k) for k in masks])
        nears = [near(x)] if has_near else []
        return even, by_col(even, 1), nears + crossed

    own_rows = lax.dynamic_slice_in_dim(features, column * n, n, 0)
    row_blocks = [cross(own_rows, d) for d in offsets]
    row_blocks = [own_rows] + ([near(own_rows)] if has_near else []) + row_blocks
    even, odd, others = gather(logits)
    plane = jnp.concatenate(
        [lax.dynamic_slice_in_dim(features, (column ^ k) * n, n, 0) for k in order]
    )
    kernels = []
    for block in row_blocks:
        kernels += kernel_block(block, plane)

    half = even.shape[0]
    stats = None
    for iteration in range(ITERS):
        outs = product_call(iteration == 0, n, has_near, stats, even, odd, others, kernels)
        own, back, t_even, t_odd = outs[0], outs[1:-2], outs[-2], outs[-1]
        back = list(back)
        scores = own
        if has_near:
            scores = scores + near(back.pop(0))
        for d, part in zip(offsets, back):
            scores = scores + cross_back(part, d)
        summed = t_even + by_col(t_odd, 1)
        stats = summed[half:]
        scores = scores + summed[:n]
        for j, k in enumerate(masks):
            sent = jnp.concatenate([summed[(j + 1) * n : (j + 2) * n], summed[half:]])
            part = by_col(sent, k)
            scores = scores + part[:n]
            stats = stats + part[n:]
        own_stats = stats
        for k in range(1, rows):
            stats = stats + lax.ppermute(
                own_stats, "row", [(i, (i + k) % rows) for i in range(rows)]
            )
        if iteration < ITERS - 1:
            even, odd, others = gather(scores)
    standardized = standardize(scores, stats[1:2], stats[0:1])
    members = normalize(jnp.exp(-2.0 * standardized))
    return (members, standardized)


def solution(mesh):
    return jax.shard_map(
        functools.partial(on_device, mesh.shape["row"], mesh.shape["col"]),
        mesh=mesh,
        in_specs=(P("row", None), P(("row", "col"), None)),
        out_specs=(P(("row", "col"), None), P(("row", "col"), None)),
        check_vma=False,
    )
```

time: 257 us -> 104 us (0.40)
  waiting for transfers between devices: 121 us -> 34.4 us
  blocking collectives: 77.1 us -> 0 us
  starting transfers between devices: 0.2 us -> 38.1 us
  matrix products: 27.2 us -> 0 us
  Pallas kernels: 0 us -> 17.5 us
  between operations: 13.9 us -> 0.99 us
  other arithmetic: 13.8 us -> 1.66 us
  local copies, waits for them, and re-layouts: 3.39 us -> 10.8 us
    all_gather x3 -> x0, waiting for transfers between devices: 77.3 us -> none  [the longest x2 48.8 us: on_device(): members_row = lax.all_gather(members, 'col', axis=0, tiled=True)]
    psum x2 -> x0, blocking collectives: 77.1 us -> none  [on_device(): lax.psum((jnp.sum(members, axis=0), jnp.sum(members * scores, axis=0)), (...]
    reduce_scatter x2 -> x0, waiting for transfers between devices: 43.5 us -> none  [on_device(): lax.psum_scatter(kernel_product(column_panel, features, members_row), 'ro...]
    ppermute x0 -> x32, starting transfers between devices: none -> 38.1 us  [the longest x16 14.9 us: by_col(): return lax.ppermute(x, 'col', [(i, i ^ mask) for i in range(cols)])]
    ppermute x0 -> x32, waiting for transfers between devices: none -> 34.4 us  [the longest x16 15.3 us: by_col(): return lax.ppermute(x, 'col', [(i, i ^ mask) for i in range(cols)])]
    dot_general x8 -> x0, matrix products: 27.2 us -> none  [the longest x4 14.7 us: block_product(): jnp.dot(kernel, members, precision=lax.Precision.HIGHEST, preferred_eleme...]
    pallas_call x0 -> x5, Pallas kernels: none -> 17.5 us  [the longest x2 9.85 us: product_call(): pl.pallas_call(functools.partial(product_body, first, n, crosses, has_nea...]
    reduce_sum x9 -> x3, other arithmetic: 9.61 us -> 0.57 us  [the longest x1 0.24 us: normalize(): return raised / jnp.sum(raised, axis=1, keepdims=True)]
  transfers between devices with their start and end apart: 5 -> 32, of which waited for: 5 -> 15; matrix products, arithmetic and copies ran while one was open for 1% -> 8% of each run, Pallas kernels for 0% -> 7%
where the time goes in v1:
time: 104 us; the launch traced here: 103 us
  starting transfers between devices  38.1 us (37%)
  waiting for transfers between devices  34.4 us (33%)
  Pallas kernels  17.5 us (17%)
  local copies, waits for them, and re-layouts  10.8 us (10%)
  other arithmetic  1.66 us (2%)
    ppermute x16, waiting for transfers between devices, by_col(): return lax.ppermute(x, 'col', [(i, i ^ mask) for i in range(cols)])  15.3 us
    ppermute x16, starting transfers between devices, by_col(): return lax.ppermute(x, 'col', [(i, i ^ mask) for i in range(cols)])  14.9 us
    pallas_call x2, Pallas kernels, product_call(): pl.pallas_call(functools.partial(product_body, first, n, crosses, has_nea...  9.85 us
    unnamed x18, local copies, waits for them, and re-layouts  9.71 us
    ppermute x5, waiting for transfers between devices, near(): return lax.ppermute(x, 'row', [(i, i ^ 1) for i in range(rows)])  8.11 us
    ppermute x6, starting transfers between devices, on_device(): lax.ppermute(own_stats, 'row', [(i, (i + k) % rows) for i in range(rows)])  7.75 us
    pallas_call x3, Pallas kernels, kernel_block(): pl.pallas_call(kernel_body, grid=(total // step,), in_specs=[pl.BlockSpec...  7.67 us
    ppermute x5, starting transfers between devices, near(): return lax.ppermute(x, 'row', [(i, i ^ 1) for i in range(rows)])  6.95 us
  transfers between devices with their start and end apart: 32, of which 15 were waited for; matrix products, arithmetic and copies ran while one was open for 8% of the time, Pallas kernels for 7%

profile of v1, /device:TPU:0, one launch (start us, length us, event | category | flops | bytes accessed | tf_op | source)
XLA Modules:
  0.0 103.4 jit_solution(7096214609717808724)
XLA Ops:
  0.6 1.0 constant_dynamic-update-slice_fusion.4
  1.6 3.1 %collective-permute-start.6 = (bf16[256,512]{1,0:T(8,128)(2,1)S(1)}, bf16[256,512]{1,0:T(8,128)(2,1)}, u32[]{:S(2)}, u32[]{:S(2)}) collective-permute-start(bf16[256,512]{1,0:T(8,128)(2,1)S(1)} %get-tuple-element.39.rows_ref), channel_id=1, source_target_pairs={{0,8},{8,0},{16,24},{24,16},{1,9},{9,1},{17,25},{25,17},{2,10},{10... | collective-permute-start | bytes 786440 | tf_op jit(solution)/shard_map/ppermute | solution.py:182
  4.7 2.5 %collective-permute-start.7 = (bf16[256,512]{1,0:T(8,128)(2,1)S(1)}, bf16[256,512]{1,0:T(8,128)(2,1)}, u32[]{:S(2)}, u32[]{:S(2)}) collective-permute-start(bf16[256,512]{1,0:T(8,128)(2,1)S(1)} %get-tuple-element.39.rows_ref), channel_id=1, source_target_pairs={{16,0},{8,16},{24,8},{0,24},{17,1},{9,17},{25,9},{1,25},{18,2},{10... | collective-permute-start | bytes 786440 | tf_op jit(solution)/shard_map/ppermute | solution.py:185
  7.2 1.5 %collective-permute-start = (f32[256,128]{1,0:T(8,128)}, f32[256,128]{1,0:T(8,128)S(1)}, u32[]{:S(2)}, u32[]{:S(2)}) collective-permute-start(f32[256,128]{1,0:T(8,128)} %param.3), channel_id=1, source_target_pairs={{0,2},{1,3},{2,0},{3,1},{4,6},{5,7},{6,4},{7,5},{8,10},{9,11},{10,... | collective-permute-start | bytes 393224 | tf_op jit(solution)/shard_map/ppermute | solution.py:179
  8.7 1.5 %collective-permute-start.1 = (f32[256,128]{1,0:T(8,128)}, f32[256,128]{1,0:T(8,128)S(1)}, u32[]{:S(2)}, u32[]{:S(2)}) collective-permute-start(f32[256,128]{1,0:T(8,128)} %param.3), channel_id=1, source_target_pairs={{0,4},{1,5},{2,6},{3,7},{4,0},{5,1},{6,2},{7,3},{8,12},{9,13},{10,... | collective-permute-start | bytes 393224 | tf_op jit(solution)/shard_map/ppermute | solution.py:179
  10.2 0.5 collective-permute-start.2
  10.7 1.0 dynamic-slice_dynamic-update-slice_fusion.6
  11.7 1.0 dynamic-slice_dynamic-update-slice_fusion.5
  12.6 1.0 dynamic-slice_dynamic-update-slice_fusion.4
  13.6 0.9 constant_dynamic-update-slice_fusion.3
  14.6 0.7 collective-permute-start.4
  15.3 1.4 %collective-permute-done.1 = f32[256,128]{1,0:T(8,128)S(1)} collective-permute-done((f32[256,128]{1,0:T(8,128)}, f32[256,128]{1,0:T(8,128)S(1)}, u32[]{:S(2)}, u32[]{:S(2)}) %collective-permute-start.1) | collective-permute-done | bytes 131104 | tf_op jit(solution)/shard_map/ppermute | solution.py:179
  16.7 0.3 collective-permute-start.5
  17.1 1.0 dynamic-slice_dynamic-update-slice_fusion.3
  18.1 1.0 dynamic-slice_dynamic-update-slice_fusion.2
  19.1 1.0 dynamic-slice_dynamic-update-slice_fusion.1
  20.1 1.0 dynamic-slice_dynamic-update-slice_fusion.plane_ref
  21.1 1.9 %shard_map.41 = (bf16[256,2048]{1,0:T(8,128)(2,1)S(1)}, bf16[256,2048]{1,0:T(8,128)(2,1)S(1)}) custom-call(bf16[256,512]{1,0:T(8,128)(2,1)S(1)} %get-tuple-element.39.rows_ref, bf16[2048,512]{1,0:T(8,128)(2,1)S(1)} %dynamic-slice_dynamic-update-slice_fusion.plane_ref), custom_call_target="tpu_custom_call" | custom-call | flops 536870912 | bytes 4456448 | tf_op jit(solution)/shard_map/pallas_call | solution.py:36
  22.9 2.8 %shard_map.42 = (bf16[256,2048]{1,0:T(8,128)(2,1)S(1)}, bf16[256,2048]{1,0:T(8,128)(2,1)S(1)}) custom-call(bf16[256,512]{1,0:T(8,128)(2,1)} %collective-permute-done.6.rows_ref, bf16[2048,512]{1,0:T(8,128)(2,1)S(1)} %dynamic-slice_dynamic-update-slice_fusion.plane_ref), custom_call_target="tpu_custom_call" | custom-call | flops 536870912 | bytes 4456448 | tf_op jit(solution)/shard_map/pallas_call | solution.py:36
  25.8 3.0 %shard_map.43 = (bf16[256,2048]{1,0:T(8,128)(2,1)S(1)}, bf16[256,2048]{1,0:T(8,128)(2,1)S(1)}) custom-call(bf16[256,512]{1,0:T(8,128)(2,1)} %collective-permute-done.7.rows_ref, bf16[2048,512]{1,0:T(8,128)(2,1)S(1)} %dynamic-slice_dynamic-update-slice_fusion.plane_ref), custom_call_target="tpu_custom_call" | custom-call | flops 536870912 | bytes 4456448 | tf_op jit(solution)/shard_map/pallas_call | solution.py:36
  28.8 1.0 copy-done.1
  29.8 1.0 copy-done.2
  30.8 4.4 %shard_map.44 = (f32[256,128]{1,0:T(8,128)S(1)}, f32[256,128]{1,0:T(8,128)S(1)}, f32[256,128]{1,0:T(8,128)S(1)}, f32[1032,128]{1,0:T(8,128)S(1)}, f32[1032,128]{1,0:T(8,128)S(1)}) custom-call(f32[1024,128]{1,0:T(8,128)S(1)} %constant_dynamic-update-slice_fusion.refs_0_, f32[1024,128]{1,0:T(8,128)S(1)} %collective-permute-done.3.refs_1_, ...), custom_call_target="tpu_custom_call" | custom-call | flops 1610612736 | bytes 6291456 | tf_op jit(solution)/shard_map/pallas_call | solution.py:145
  35.2 0.6 collective-permute-start.8
  35.7 1.5 %collective-permute-done.8 = f32[1032,128]{1,0:T(8,128)S(1)} collective-permute-done((f32[1032,128]{1,0:T(8,128)S(1)}, f32[1032,128]{1,0:T(8,128)S(1)}, u32[]{:S(2)}, u32[]{:S(2)}) %collective-permute-start.8) | collective-permute-done | bytes 528416 | tf_op jit(solution)/shard_map/ppermute | solution.py:179
  37.4 1.2 %collective-permute-start.10 = (f32[264,128]{1,0:T(8,128)S(1)}, f32[264,128]{1,0:T(8,128)S(1)}, u32[]{:S(2)}, u32[]{:S(2)}) collective-permute-start(f32[264,128]{1,0:T(8,128)S(1)} %get-tuple-element.49), channel_id=1, source_target_pairs={{0,4},{1,5},{2,6},{3,7},{4,0},{5,1},{6,2},{7,3},{8,12},{9,13},{10,... | collective-permute-start | bytes 405512 | tf_op jit(solution)/shard_map/ppermute | solution.py:179
  38.6 1.5 %collective-permute-start.9 = (f32[264,128]{1,0:T(8,128)S(1)}, f32[264,128]{1,0:T(8,128)S(1)}, u32[]{:S(2)}, u32[]{:S(2)}) collective-permute-start(f32[264,128]{1,0:T(8,128)S(1)} %get-tuple-element.48), channel_id=1, source_target_pairs={{0,2},{1,3},{2,0},{3,1},{4,6},{5,7},{6,4},{7,5},{8,10},{9,11},{10,... | collective-permute-start | bytes 405512 | tf_op jit(solution)/shard_map/ppermute | solution.py:179
  40.1 0.9 collective-permute-start.11
  41.0 0.7 collective-permute-start.15
  41.6 2.6 %collective-permute-start.16 = (f32[256,128]{1,0:T(8,128)S(1)}, f32[256,128]{1,0:T(8,128)S(1)}, u32[]{:S(2)}, u32[]{:S(2)}) collective-permute-start(f32[256,128]{1,0:T(8,128)S(1)} %get-tuple-element.28), channel_id=1, source_target_pairs={{0,16},{16,8},{8,24},{24,0},{1,17},{17,9},{9,25},{25,1},{2,18},{18... | collective-permute-start | bytes 393224 | tf_op jit(solution)/shard_map/ppermute | solution.py:188
  44.2 1.7 %collective-permute-done.15 = f32[256,128]{1,0:T(8,128)S(1)} collective-permute-done((f32[256,128]{1,0:T(8,128)S(1)}, f32[256,128]{1,0:T(8,128)S(1)}, u32[]{:S(2)}, u32[]{:S(2)}) %collective-permute-start.15) | collective-permute-done | bytes 131104 | tf_op jit(solution)/shard_map/ppermute | solution.py:182
  45.9 4.8 %collective-permute-done.16 = f32[256,128]{1,0:T(8,128)S(1)} collective-permute-done((f32[256,128]{1,0:T(8,128)S(1)}, f32[256,128]{1,0:T(8,128)S(1)}, u32[]{:S(2)}, u32[]{:S(2)}) %collective-permute-start.16) | collective-permute-done | bytes 131104 | tf_op jit(solution)/shard_map/ppermute | solution.py:188
  50.7 0.1 slice_add_fusion.4
  50.8 0.4 collective-permute-start.17
  51.3 1.4 %collective-permute-start.18 = (f32[256,128]{1,0:T(8,128)S(1)}, f32[256,128]{1,0:T(8,128)S(1)}, u32[]{:S(2)}, u32[]{:S(2)}) collective-permute-start(f32[256,128]{1,0:T(8,128)S(1)} %slice_add_fusion.4), channel_id=1, source_target_pairs={{0,4},{1,5},{2,6},{3,7},{4,0},{5,1},{6,2},{7,3},{8,12},{9,13},{10,... | collective-permute-start | bytes 393224 | tf_op jit(solution)/shard_map/ppermute | solution.py:179
  52.7 1.7 %collective-permute-start.19 = (f32[256,128]{1,0:T(8,128)S(1)}, f32[256,128]{1,0:T(8,128)S(1)}, u32[]{:S(2)}, u32[]{:S(2)}) collective-permute-start(f32[256,128]{1,0:T(8,128)S(1)} %slice_add_fusion.4), channel_id=1, source_target_pairs={{0,6},{1,7},{2,4},{3,5},{4,2},{5,3},{6,0},{7,1},{8,14},{9,15},{10,... | collective-permute-start | bytes 393224 | tf_op jit(solution)/shard_map/ppermute | solution.py:179
  54.4 1.6 %collective-permute-done.17 = f32[256,128]{1,0:T(8,128)S(1)} collective-permute-done((f32[256,128]{1,0:T(8,128)S(1)}, f32[256,128]{1,0:T(8,128)S(1)}, u32[]{:S(2)}, u32[]{:S(2)}) %collective-permute-start.17) | collective-permute-done | bytes 131104 | tf_op jit(solution)/shard_map/ppermute | solution.py:179
  56.0 0.6 collective-permute-done.18
  56.7 1.9 %collective-permute-done.19 = f32[256,128]{1,0:T(8,128)S(1)} collective-permute-done((f32[256,128]{1,0:T(8,128)S(1)}, f32[256,128]{1,0:T(8,128)S(1)}, u32[]{:S(2)}, u32[]{:S(2)}) %collective-permute-start.19) | collective-permute-done | bytes 131104 | tf_op jit(solution)/shard_map/ppermute | solution.py:179
  58.7 0.7 collective-permute-start.12
  59.4 3.0 %collective-permute-start.13 = (f32[8,128]{1,0:T(8,128)S(1)}, f32[8,128]{1,0:T(8,128)S(1)}, u32[]{:S(2)}, u32[]{:S(2)}) collective-permute-start(f32[8,128]{1,0:T(8,128)S(1)} %slice_add_fusion.11), channel_id=1, source_target_pairs={{0,16},{8,24},{16,0},{24,8},{1,17},{9,25},{17,1},{25,9},{2,18},{10... | collective-permute-start | bytes 12296 | tf_op jit(solution)/shard_map/ppermute | solution.py:228
  62.4 0.1 collective-permute-start.14
  62.5 1.9 %collective-permute-start.21 = (f32[256,128]{1,0:T(8,128)S(1)}, f32[256,128]{1,0:T(8,128)S(1)}, u32[]{:S(2)}, u32[]{:S(2)}) collective-permute-start(f32[256,128]{1,0:T(8,128)S(1)} %slice_add_fusion.4), channel_id=1, source_target_pairs={{0,8},{8,0},{16,24},{24,16},{1,9},{9,1},{17,25},{25,17},{2,10},{10... | collective-permute-start | bytes 393224 | tf_op jit(solution)/shard_map/ppermute | solution.py:182
  64.4 1.6 %collective-permute-start.22 = (f32[256,128]{1,0:T(8,128)S(1)}, f32[256,128]{1,0:T(8,128)S(1)}, u32[]{:S(2)}, u32[]{:S(2)}) collective-permute-start(f32[256,128]{1,0:T(8,128)S(1)} %slice_add_fusion.4), channel_id=1, source_target_pairs={{16,0},{8,16},{24,8},{0,24},{17,1},{9,17},{25,9},{1,25},{18,2},{10... | collective-permute-start | bytes 393224 | tf_op jit(solution)/shard_map/ppermute | solution.py:185
  66.0 2.8 %collective-permute-done.21.refs_3_ = f32[256,128]{1,0:T(8,128)S(1)} collective-permute-done((f32[256,128]{1,0:T(8,128)S(1)}, f32[256,128]{1,0:T(8,128)S(1)}, u32[]{:S(2)}, u32[]{:S(2)}) %collective-permute-start.21) | collective-permute-done | bytes 131104 | tf_op jit(solution)/shard_map/ppermute | solution.py:182
  68.8 4.0 %collective-permute-done.22.refs_4_ = f32[256,128]{1,0:T(8,128)S(1)} collective-permute-done((f32[256,128]{1,0:T(8,128)S(1)}, f32[256,128]{1,0:T(8,128)S(1)}, u32[]{:S(2)}, u32[]{:S(2)}) %collective-permute-start.22) | collective-permute-done | bytes 131104 | tf_op jit(solution)/shard_map/ppermute | solution.py:185
  72.9 5.4 %shard_map.45 = (f32[256,128]{1,0:T(8,128)S(1)}, f32[256,128]{1,0:T(8,128)S(1)}, f32[256,128]{1,0:T(8,128)S(1)}, f32[1032,128]{1,0:T(8,128)S(1)}, f32[1032,128]{1,0:T(8,128)S(1)}) custom-call(f32[8,128]{1,0:T(8,128)S(1)} %add_add_fusion.1.refs_0_, f32[1024,128]{1,0:T(8,128)S(1)} %pad_maximum_fusion.refs_1_, f32[1024,128]{1,0:T(8,128)S(1)} %collective-permute-done.20.refs_2_, ...), custom_call_target="tpu_custom_call" | custom-call | flops 1610612736 | bytes 6291456 | tf_op jit(solution)/shard_map/pallas_call | solution.py:145
  78.4 1.9 %collective-permute-done.23 = f32[1032,128]{1,0:T(8,128)S(1)} collective-permute-done((f32[1032,128]{1,0:T(8,128)S(1)}, f32[1032,128]{1,0:T(8,128)S(1)}, u32[]{:S(2)}, u32[]{:S(2)}) %collective-permute-start.23) | collective-permute-done | bytes 528416 | tf_op jit(solution)/shard_map/ppermute | solution.py:179
  80.4 1.7 %collective-permute-start.24 = (f32[264,128]{1,0:T(8,128)S(1)}, f32[264,128]{1,0:T(8,128)S(1)}, u32[]{:S(2)}, u32[]{:S(2)}) collective-permute-start(f32[264,128]{1,0:T(8,128)S(1)} %get-tuple-element.46), channel_id=1, source_target_pairs={{0,2},{1,3},{2,0},{3,1},{4,6},{5,7},{6,4},{7,5},{8,10},{9,11},{10,... | collective-permute-start | bytes 405512 | tf_op jit(solution)/shard_map/ppermute | solution.py:179
  82.1 1.0 %collective-permute-start.25 = (f32[264,128]{1,0:T(8,128)S(1)}, f32[264,128]{1,0:T(8,128)S(1)}, u32[]{:S(2)}, u32[]{:S(2)}) collective-permute-start(f32[264,128]{1,0:T(8,128)S(1)} %get-tuple-element.47), channel_id=1, source_target_pairs={{0,4},{1,5},{2,6},{3,7},{4,0},{5,1},{6,2},{7,3},{8,12},{9,13},{10,... | collective-permute-start | bytes 405512 | tf_op jit(solution)/shard_map/ppermute | solution.py:179
  83.1 0.9 collective-permute-start.26
  84.0 2.5 %collective-permute-done.24 = f32[264,128]{1,0:T(8,128)S(1)} collective-permute-done((f32[264,128]{1,0:T(8,128)S(1)}, f32[264,128]{1,0:T(8,128)S(1)}, u32[]{:S(2)}, u32[]{:S(2)}) %collective-permute-start.24) | collective-permute-done | bytes 135200 | tf_op jit(solution)/shard_map/ppermute | solution.py:179
  86.5 3.9 %collective-permute-done.25 = f32[264,128]{1,0:T(8,128)S(1)} collective-permute-done((f32[264,128]{1,0:T(8,128)S(1)}, f32[264,128]{1,0:T(8,128)S(1)}, u32[]{:S(2)}, u32[]{:S(2)}) %collective-permute-start.25) | collective-permute-done | bytes 135200 | tf_op jit(solution)/shard_map/ppermute | solution.py:179
  90.4 1.7 %collective-permute-start.28 = (f32[8,128]{1,0:T(8,128)S(1)}, f32[8,128]{1,0:T(8,128)S(1)}, u32[]{:S(2)}, u32[]{:S(2)}) collective-permute-start(f32[8,128]{1,0:T(8,128)S(1)} %slice_add_fusion.8), channel_id=1, source_target_pairs={{0,16},{8,24},{16,0},{24,8},{1,17},{9,25},{17,1},{25,9},{2,18},{10... | collective-permute-start | bytes 12296 | tf_op jit(solution)/shard_map/ppermute | solution.py:228
  92.1 2.1 %collective-permute-start.29 = (f32[8,128]{1,0:T(8,128)S(1)}, f32[8,128]{1,0:T(8,128)S(1)}, u32[]{:S(2)}, u32[]{:S(2)}) collective-permute-start(f32[8,128]{1,0:T(8,128)S(1)} %slice_add_fusion.8), channel_id=1, source_target_pairs={{0,24},{8,0},{16,8},{24,16},{1,25},{9,1},{17,9},{25,17},{2,26},{10... | collective-permute-start | bytes 12296 | tf_op jit(solution)/shard_map/ppermute | solution.py:228
  94.2 0.6 collective-permute-start.30
  94.8 1.5 %collective-permute-start.31 = (f32[256,128]{1,0:T(8,128)S(1)}, f32[256,128]{1,0:T(8,128)S(1)}, u32[]{:S(2)}, u32[]{:S(2)}) collective-permute-start(f32[256,128]{1,0:T(8,128)S(1)} %get-tuple-element.33), channel_id=1, source_target_pairs={{0,16},{16,8},{8,24},{24,0},{1,17},{17,9},{9,25},{25,1},{2,18},{18... | collective-permute-start | bytes 393224 | tf_op jit(solution)/shard_map/ppermute | solution.py:188
  96.3 0.1 collective-permute-done.29
  96.4 3.6 %collective-permute-done.30 = f32[256,128]{1,0:T(8,128)S(1)} collective-permute-done((f32[256,128]{1,0:T(8,128)S(1)}, f32[256,128]{1,0:T(8,128)S(1)}, u32[]{:S(2)}, u32[]{:S(2)}) %collective-permute-start.30) | collective-permute-done | bytes 131104 | tf_op jit(solution)/shard_map/ppermute | solution.py:182
  100.0 2.0 %collective-permute-done.31 = f32[256,128]{1,0:T(8,128)S(1)} collective-permute-done((f32[256,128]{1,0:T(8,128)S(1)}, f32[256,128]{1,0:T(8,128)S(1)}, u32[]{:S(2)}, u32[]{:S(2)}) %collective-permute-start.31) | collective-permute-done | bytes 131104 | tf_op jit(solution)/shard_map/ppermute | solution.py:188
  102.1 0.2 fusion.6
  102.2 0.2 multiply_reduce_fusion
  102.4 0.2 fusion.4
  102.7 0.8 fusion.3
  (48 shorter events, 0.7 us)
Async XLA Ops:
  1.6 21.3 %collective-permute-start.6 = (bf16[256,512]{1,0:T(8,128)(2,1)S(1)}, bf16[256,512]{1,0:T(8,128)(2,1)}, u32[]{:S(2)}, u32[]{:S(2)}) collective-permute-start(bf16[256,512]{1,0:T(8,128)(2,1)S(1)} %get-tuple-element.39.rows_ref), channel_id=1, source_target_pairs={{0,8},{8,0},{16,24},{24,16},{1,9},{9,1},{17,25},{25,17},{2,10},{10... | collective-permute-start | bytes 786440 | tf_op jit(solution)/shard_map/ppermute | solution.py:182
  4.7 21.0 %collective-permute-start.7 = (bf16[256,512]{1,0:T(8,128)(2,1)S(1)}, bf16[256,512]{1,0:T(8,128)(2,1)}, u32[]{:S(2)}, u32[]{:S(2)}) collective-permute-start(bf16[256,512]{1,0:T(8,128)(2,1)S(1)} %get-tuple-element.39.rows_ref), channel_id=1, source_target_pairs={{16,0},{8,16},{24,8},{0,24},{17,1},{9,17},{25,9},{1,25},{18,2},{10... | collective-permute-start | bytes 786440 | tf_op jit(solution)/shard_map/ppermute | solution.py:185
  7.2 7.4 %collective-permute-start = (f32[256,128]{1,0:T(8,128)}, f32[256,128]{1,0:T(8,128)S(1)}, u32[]{:S(2)}, u32[]{:S(2)}) collective-permute-start(f32[256,128]{1,0:T(8,128)} %param.3), channel_id=1, source_target_pairs={{0,2},{1,3},{2,0},{3,1},{4,6},{5,7},{6,4},{7,5},{8,10},{9,11},{10,... | collective-permute-start | bytes 393224 | tf_op jit(solution)/shard_map/ppermute | solution.py:179
  8.7 8.0 %collective-permute-start.1 = (f32[256,128]{1,0:T(8,128)}, f32[256,128]{1,0:T(8,128)S(1)}, u32[]{:S(2)}, u32[]{:S(2)}) collective-permute-start(f32[256,128]{1,0:T(8,128)} %param.3), channel_id=1, source_target_pairs={{0,4},{1,5},{2,6},{3,7},{4,0},{5,1},{6,2},{7,3},{8,12},{9,13},{10,... | collective-permute-start | bytes 393224 | tf_op jit(solution)/shard_map/ppermute | solution.py:179
  10.2 6.8 %collective-permute-start.2 = (f32[256,128]{1,0:T(8,128)}, f32[256,128]{1,0:T(8,128)S(1)}, u32[]{:S(2)}, u32[]{:S(2)}) collective-permute-start(f32[256,128]{1,0:T(8,128)} %param.3), channel_id=1, source_target_pairs={{0,6},{1,7},{2,4},{3,5},{4,2},{5,3},{6,0},{7,1},{8,14},{9,15},{10,... | collective-permute-start | bytes 393224 | tf_op jit(solution)/shard_map/ppermute | solution.py:179
  14.6 16.2 %collective-permute-start.4 = (f32[256,128]{1,0:T(8,128)}, f32[256,128]{1,0:T(8,128)S(1)}, u32[]{:S(2)}, u32[]{:S(2)}) collective-permute-start(f32[256,128]{1,0:T(8,128)} %param.3), channel_id=1, source_target_pairs={{0,8},{8,0},{16,24},{24,16},{1,9},{9,1},{17,25},{25,17},{2,10},{10... | collective-permute-start | bytes 393224 | tf_op jit(solution)/shard_map/ppermute | solution.py:182
  16.7 14.1 %collective-permute-start.5 = (f32[256,128]{1,0:T(8,128)}, f32[256,128]{1,0:T(8,128)}, u32[]{:S(2)}, u32[]{:S(2)}) collective-permute-start(f32[256,128]{1,0:T(8,128)} %param.3), channel_id=1, source_target_pairs={{16,0},{8,16},{24,8},{0,24},{17,1},{9,17},{25,9},{1,25},{18,2},{10... | collective-permute-start | bytes 393224 | tf_op jit(solution)/shard_map/ppermute | solution.py:185
  17.0 13.7 %collective-permute-start.3 = (f32[1024,128]{1,0:T(8,128)S(1)}, f32[1024,128]{1,0:T(8,128)S(1)}, u32[]{:S(2)}, u32[]{:S(2)}) collective-permute-start(f32[1024,128]{1,0:T(8,128)S(1)} %constant_dynamic-update-slice_fusion.refs_0_), channel_id=1, source_target_pairs={{0,1},{1,0},{2,3},{3,2},{4,5},{5,4},{6,7},{7,6},{8,9},{9,8},{10,11... | collective-permute-start | bytes 1572872 | tf_op jit(solution)/shard_map/ppermute | solution.py:179
  25.7 5.0 %copy-start = (bf16[256,2048]{1,0:T(8,128)(2,1)}, bf16[256,2048]{1,0:T(8,128)(2,1)S(1)}, u32[]{:S(2)}) copy-start(bf16[256,2048]{1,0:T(8,128)(2,1)S(1)} %get-tuple-element.21.refs_7_.refs_8_) | copy-start | bytes 3145732
  28.8 1.0 copy-start.1
  29.8 1.0 copy-start.2
  35.2 2.1 %collective-permute-start.8 = (f32[1032,128]{1,0:T(8,128)S(1)}, f32[1032,128]{1,0:T(8,128)S(1)}, u32[]{:S(2)}, u32[]{:S(2)}) collective-permute-start(f32[1032,128]{1,0:T(8,128)S(1)} %get-tuple-element.25), channel_id=1, source_target_pairs={{0,1},{1,0},{2,3},{3,2},{4,5},{5,4},{6,7},{7,6},{8,9},{9,8},{10,11... | collective-permute-start | bytes 1585160 | tf_op jit(solution)/shard_map/ppermute | solution.py:179
  37.4 13.3 %collective-permute-start.10 = (f32[264,128]{1,0:T(8,128)S(1)}, f32[264,128]{1,0:T(8,128)S(1)}, u32[]{:S(2)}, u32[]{:S(2)}) collective-permute-start(f32[264,128]{1,0:T(8,128)S(1)} %get-tuple-element.49), channel_id=1, source_target_pairs={{0,4},{1,5},{2,6},{3,7},{4,0},{5,1},{6,2},{7,3},{8,12},{9,13},{10,... | collective-permute-start | bytes 405512 | tf_op jit(solution)/shard_map/ppermute | solution.py:179
  38.6 12.1 %collective-permute-start.9 = (f32[264,128]{1,0:T(8,128)S(1)}, f32[264,128]{1,0:T(8,128)S(1)}, u32[]{:S(2)}, u32[]{:S(2)}) collective-permute-start(f32[264,128]{1,0:T(8,128)S(1)} %get-tuple-element.48), channel_id=1, source_target_pairs={{0,2},{1,3},{2,0},{3,1},{4,6},{5,7},{6,4},{7,5},{8,10},{9,11},{10,... | collective-permute-start | bytes 405512 | tf_op jit(solution)/shard_map/ppermute | solution.py:179
  40.1 10.6 %collective-permute-start.11 = (f32[264,128]{1,0:T(8,128)S(1)}, f32[264,128]{1,0:T(8,128)S(1)}, u32[]{:S(2)}, u32[]{:S(2)}) collective-permute-start(f32[264,128]{1,0:T(8,128)S(1)} %concatenate.36), channel_id=1, source_target_pairs={{0,6},{1,7},{2,4},{3,5},{4,2},{5,3},{6,0},{7,1},{8,14},{9,15},{10,... | collective-permute-start | bytes 405512 | tf_op jit(solution)/shard_map/ppermute | solution.py:179
  41.0 5.0 %collective-permute-start.15 = (f32[256,128]{1,0:T(8,128)S(1)}, f32[256,128]{1,0:T(8,128)S(1)}, u32[]{:S(2)}, u32[]{:S(2)}) collective-permute-start(f32[256,128]{1,0:T(8,128)S(1)} %get-tuple-element.27), channel_id=1, source_target_pairs={{0,8},{8,0},{16,24},{24,16},{1,9},{9,1},{17,25},{25,17},{2,10},{10... | collective-permute-start | bytes 393224 | tf_op jit(solution)/shard_map/ppermute | solution.py:182
  41.6 9.1 %collective-permute-start.16 = (f32[256,128]{1,0:T(8,128)S(1)}, f32[256,128]{1,0:T(8,128)S(1)}, u32[]{:S(2)}, u32[]{:S(2)}) collective-permute-start(f32[256,128]{1,0:T(8,128)S(1)} %get-tuple-element.28), channel_id=1, source_target_pairs={{0,16},{16,8},{8,24},{24,0},{1,17},{17,9},{9,25},{25,1},{2,18},{18... | collective-permute-start | bytes 393224 | tf_op jit(solution)/shard_map/ppermute | solution.py:188
  50.8 5.2 %collective-permute-start.17 = (f32[256,128]{1,0:T(8,128)S(1)}, f32[256,128]{1,0:T(8,128)S(1)}, u32[]{:S(2)}, u32[]{:S(2)}) collective-permute-start(f32[256,128]{1,0:T(8,128)S(1)} %slice_add_fusion.4), channel_id=1, source_target_pairs={{0,2},{1,3},{2,0},{3,1},{4,6},{5,7},{6,4},{7,5},{8,10},{9,11},{10,... | collective-permute-start | bytes 393224 | tf_op jit(solution)/shard_map/ppermute | solution.py:179
  51.3 5.4 %collective-permute-start.18 = (f32[256,128]{1,0:T(8,128)S(1)}, f32[256,128]{1,0:T(8,128)S(1)}, u32[]{:S(2)}, u32[]{:S(2)}) collective-permute-start(f32[256,128]{1,0:T(8,128)S(1)} %slice_add_fusion.4), channel_id=1, source_target_pairs={{0,4},{1,5},{2,6},{3,7},{4,0},{5,1},{6,2},{7,3},{8,12},{9,13},{10,... | collective-permute-start | bytes 393224 | tf_op jit(solution)/shard_map/ppermute | solution.py:179
  52.7 5.9 %collective-permute-start.19 = (f32[256,128]{1,0:T(8,128)S(1)}, f32[256,128]{1,0:T(8,128)S(1)}, u32[]{:S(2)}, u32[]{:S(2)}) collective-permute-start(f32[256,128]{1,0:T(8,128)S(1)} %slice_add_fusion.4), channel_id=1, source_target_pairs={{0,6},{1,7},{2,4},{3,5},{4,2},{5,3},{6,0},{7,1},{8,14},{9,15},{10,... | collective-permute-start | bytes 393224 | tf_op jit(solution)/shard_map/ppermute | solution.py:179
  58.6 14.3 %collective-permute-start.20 = (f32[1024,128]{1,0:T(8,128)S(1)}, f32[1024,128]{1,0:T(8,128)S(1)}, u32[]{:S(2)}, u32[]{:S(2)}) collective-permute-start(f32[1024,128]{1,0:T(8,128)S(1)} %pad_maximum_fusion.refs_1_), channel_id=1, source_target_pairs={{0,1},{1,0},{2,3},{3,2},{4,5},{5,4},{6,7},{7,6},{8,9},{9,8},{10,11... | collective-permute-start | bytes 1572872 | tf_op jit(solution)/shard_map/ppermute | solution.py:179
  58.7 5.8 %collective-permute-start.12 = (f32[8,128]{1,0:T(8,128)S(1)}, f32[8,128]{1,0:T(8,128)S(1)}, u32[]{:S(2)}, u32[]{:S(2)}) collective-permute-start(f32[8,128]{1,0:T(8,128)S(1)} %slice_add_fusion.11), channel_id=1, source_target_pairs={{0,8},{8,16},{16,24},{24,0},{1,9},{9,17},{17,25},{25,1},{2,10},{10... | collective-permute-start | bytes 12296 | tf_op jit(solution)/shard_map/ppermute | solution.py:228
  59.4 6.7 %collective-permute-start.13 = (f32[8,128]{1,0:T(8,128)S(1)}, f32[8,128]{1,0:T(8,128)S(1)}, u32[]{:S(2)}, u32[]{:S(2)}) collective-permute-start(f32[8,128]{1,0:T(8,128)S(1)} %slice_add_fusion.11), channel_id=1, source_target_pairs={{0,16},{8,24},{16,0},{24,8},{1,17},{9,25},{17,1},{25,9},{2,18},{10... | collective-permute-start | bytes 12296 | tf_op jit(solution)/shard_map/ppermute | solution.py:228
  62.4 3.6 %collective-permute-start.14 = (f32[8,128]{1,0:T(8,128)S(1)}, f32[8,128]{1,0:T(8,128)S(1)}, u32[]{:S(2)}, u32[]{:S(2)}) collective-permute-start(f32[8,128]{1,0:T(8,128)S(1)} %slice_add_fusion.11), channel_id=1, source_target_pairs={{0,24},{8,0},{16,8},{24,16},{1,25},{9,1},{17,9},{25,17},{2,26},{10... | collective-permute-start | bytes 12296 | tf_op jit(solution)/shard_map/ppermute | solution.py:228
  62.5 6.3 %collective-permute-start.21 = (f32[256,128]{1,0:T(8,128)S(1)}, f32[256,128]{1,0:T(8,128)S(1)}, u32[]{:S(2)}, u32[]{:S(2)}) collective-permute-start(f32[256,128]{1,0:T(8,128)S(1)} %slice_add_fusion.4), channel_id=1, source_target_pairs={{0,8},{8,0},{16,24},{24,16},{1,9},{9,1},{17,25},{25,17},{2,10},{10... | collective-permute-start | bytes 393224 | tf_op jit(solution)/shard_map/ppermute | solution.py:182
  64.4 8.4 %collective-permute-start.22 = (f32[256,128]{1,0:T(8,128)S(1)}, f32[256,128]{1,0:T(8,128)S(1)}, u32[]{:S(2)}, u32[]{:S(2)}) collective-permute-start(f32[256,128]{1,0:T(8,128)S(1)} %slice_add_fusion.4), channel_id=1, source_target_pairs={{16,0},{8,16},{24,8},{0,24},{17,1},{9,17},{25,9},{1,25},{18,2},{10... | collective-permute-start | bytes 393224 | tf_op jit(solution)/shard_map/ppermute | solution.py:185
  78.3 2.0 %collective-permute-start.23 = (f32[1032,128]{1,0:T(8,128)S(1)}, f32[1032,128]{1,0:T(8,128)S(1)}, u32[]{:S(2)}, u32[]{:S(2)}) collective-permute-start(f32[1032,128]{1,0:T(8,128)S(1)} %get-tuple-element.30), channel_id=1, source_target_pairs={{0,1},{1,0},{2,3},{3,2},{4,5},{5,4},{6,7},{7,6},{8,9},{9,8},{10,11... | collective-permute-start | bytes 1585160 | tf_op jit(solution)/shard_map/ppermute | solution.py:179
  80.4 6.0 %collective-permute-start.24 = (f32[264,128]{1,0:T(8,128)S(1)}, f32[264,128]{1,0:T(8,128)S(1)}, u32[]{:S(2)}, u32[]{:S(2)}) collective-permute-start(f32[264,128]{1,0:T(8,128)S(1)} %get-tuple-element.46), channel_id=1, source_target_pairs={{0,2},{1,3},{2,0},{3,1},{4,6},{5,7},{6,4},{7,5},{8,10},{9,11},{10,... | collective-permute-start | bytes 405512 | tf_op jit(solution)/shard_map/ppermute | solution.py:179
  82.1 8.2 %collective-permute-start.25 = (f32[264,128]{1,0:T(8,128)S(1)}, f32[264,128]{1,0:T(8,128)S(1)}, u32[]{:S(2)}, u32[]{:S(2)}) collective-permute-start(f32[264,128]{1,0:T(8,128)S(1)} %get-tuple-element.47), channel_id=1, source_target_pairs={{0,4},{1,5},{2,6},{3,7},{4,0},{5,1},{6,2},{7,3},{8,12},{9,13},{10,... | collective-permute-start | bytes 405512 | tf_op jit(solution)/shard_map/ppermute | solution.py:179
  83.1 7.2 %collective-permute-start.26 = (f32[264,128]{1,0:T(8,128)S(1)}, f32[264,128]{1,0:T(8,128)S(1)}, u32[]{:S(2)}, u32[]{:S(2)}) collective-permute-start(f32[264,128]{1,0:T(8,128)S(1)} %concatenate.37), channel_id=1, source_target_pairs={{0,6},{1,7},{2,4},{3,5},{4,2},{5,3},{6,0},{7,1},{8,14},{9,15},{10,... | collective-permute-start | bytes 405512 | tf_op jit(solution)/shard_map/ppermute | solution.py:179
  90.3 5.9 %collective-permute-start.27 = (f32[8,128]{1,0:T(8,128)S(1)}, f32[8,128]{1,0:T(8,128)S(1)}, u32[]{:S(2)}, u32[]{:S(2)}) collective-permute-start(f32[8,128]{1,0:T(8,128)S(1)} %slice_add_fusion.8), channel_id=1, source_target_pairs={{0,8},{8,16},{16,24},{24,0},{1,9},{9,17},{17,25},{25,1},{2,10},{10... | collective-permute-start | bytes 12296 | tf_op jit(solution)/shard_map/ppermute | solution.py:228
  90.4 5.8 %collective-permute-start.28 = (f32[8,128]{1,0:T(8,128)S(1)}, f32[8,128]{1,0:T(8,128)S(1)}, u32[]{:S(2)}, u32[]{:S(2)}) collective-permute-start(f32[8,128]{1,0:T(8,128)S(1)} %slice_add_fusion.8), channel_id=1, source_target_pairs={{0,16},{8,24},{16,0},{24,8},{1,17},{9,25},{17,1},{25,9},{2,18},{10... | collective-permute-start | bytes 12296 | tf_op jit(solution)/shard_map/ppermute | solution.py:228
  92.1 4.2 %collective-permute-start.29 = (f32[8,128]{1,0:T(8,128)S(1)}, f32[8,128]{1,0:T(8,128)S(1)}, u32[]{:S(2)}, u32[]{:S(2)}) collective-permute-start(f32[8,128]{1,0:T(8,128)S(1)} %slice_add_fusion.8), channel_id=1, source_target_pairs={{0,24},{8,0},{16,8},{24,16},{1,25},{9,1},{17,9},{25,17},{2,26},{10... | collective-permute-start | bytes 12296 | tf_op jit(solution)/shard_map/ppermute | solution.py:228
  94.2 5.8 %collective-permute-start.30 = (f32[256,128]{1,0:T(8,128)S(1)}, f32[256,128]{1,0:T(8,128)S(1)}, u32[]{:S(2)}, u32[]{:S(2)}) collective-permute-start(f32[256,128]{1,0:T(8,128)S(1)} %get-tuple-element.32), channel_id=1, source_target_pairs={{0,8},{8,0},{16,24},{24,16},{1,9},{9,1},{17,25},{25,17},{2,10},{10... | collective-permute-start | bytes 393224 | tf_op jit(solution)/shard_map/ppermute | solution.py:182
  94.8 7.3 %collective-permute-start.31 = (f32[256,128]{1,0:T(8,128)S(1)}, f32[256,128]{1,0:T(8,128)S(1)}, u32[]{:S(2)}, u32[]{:S(2)}) collective-permute-start(f32[256,128]{1,0:T(8,128)S(1)} %get-tuple-element.33), channel_id=1, source_target_pairs={{0,16},{16,8},{8,24},{24,0},{1,17},{17,9},{9,25},{25,1},{2,18},{18... | collective-permute-start | bytes 393224 | tf_op jit(solution)/shard_map/ppermute | solution.py:188
  102.7 0.8 copy-start.3

commit v2 on v0

v2 whole, which is shorter than its diff:
```python
import functools

import jax
import jax.numpy as jnp
from jax import lax
from jax.experimental import pallas as pl
from jax.experimental.pallas import tpu as pltpu
from jax.sharding import PartitionSpec as P

ITERS = 2
STAT_ROWS = 8
BACK_ROWS = 16
VMEM_BYTES = 24 * 1024 * 1024


def split(x):
    high = x.astype(jnp.bfloat16)
    low = (x - high.astype(jnp.float32)).astype(jnp.bfloat16)
    return high, low


def kernel_body(order, own, column_ref, *refs):
    plane_ref, high_ref, low_ref = refs[-3:]
    n, total = high_ref.shape[0], plane_ref.shape[0]
    column = column_ref[0]

    def frames(k):
        start = pl.multiple_of(lax.bitwise_xor(column, k) * n, n)
        return plane_ref[pl.ds(start, n), :]

    rows = frames(0) if own else refs[0][...]
    for j, k in enumerate(order):
        inner = lax.dot_general(
            rows, frames(k), (((1,), (1,)), ((), ())), preferred_element_type=jnp.float32
        )
        t = inner / plane_ref.shape[1]
        high, low = split(t * (3.0 + t * (3.0 + t)))
        high_ref[:, j * n : (j + 1) * n] = high
        low_ref[:, j * n : (j + 1) * n] = low


def kernel_block(order, column, rows, plane, n):
    total, width = plane.shape
    vmem = pl.BlockSpec(memory_space=pltpu.VMEM)
    own = rows is None
    args = ([] if own else [rows]) + [plane]
    return pl.pallas_call(
        functools.partial(kernel_body, order, own),
        in_specs=[pl.BlockSpec(memory_space=pltpu.SMEM)] + [vmem] * len(args),
        out_specs=[vmem] * 2,
        out_shape=[jax.ShapeDtypeStruct((n, total), jnp.bfloat16)] * 2,
        compiler_params=pltpu.CompilerParams(vmem_limit_bytes=VMEM_BYTES),
        cost_estimate=pl.CostEstimate(
            flops=2 * n * total * width,
            bytes_accessed=2 * (n + total) * width + 4 * n * total,
            transcendentals=0,
        ),
    )(column, *args)


def standardize(scores, size, weighted):
    distance = weighted / (size * size) - 2.0 * scores / size
    centered = distance - jnp.mean(distance, axis=1, keepdims=True)
    spread = jnp.mean(centered * centered, axis=1, keepdims=True)
    return centered / jnp.sqrt(spread + 1e-06)


def normalize(raised):
    return raised / jnp.sum(raised, axis=1, keepdims=True)


VMEM = pl.BlockSpec(memory_space=pltpu.VMEM)
ANY = pl.BlockSpec(memory_space=pl.ANY)
F32 = jnp.float32


def call(body, args, outs, unused=(), scratch=(), flops=0):
    bytes_accessed = sum(x.size * x.dtype.itemsize for x in list(args) + list(outs))
    return pl.pallas_call(
        body,
        in_specs=[VMEM] * len(args) + [ANY] * len(unused),
        out_specs=[VMEM] * len(outs),
        out_shape=list(outs),
        scratch_shapes=list(scratch),
        compiler_params=pltpu.CompilerParams(vmem_limit_bytes=VMEM_BYTES),
        cost_estimate=pl.CostEstimate(
            flops=flops, bytes_accessed=bytes_accessed, transcendentals=0
        ),
    )(*args, *unused)


def shaped(rows, columns, dtype=F32):
    return jax.ShapeDtypeStruct((rows, columns), dtype)


def members_body(first, n, smalls, parts, others, unused, *refs):
    refs = list(refs)
    stats, refs = refs[:smalls], refs[smalls:]
    evens, refs = refs[:parts], refs[parts:]
    rest, refs = refs[:others], refs[others + unused :]
    even_hl, member = refs
    clusters = member.shape[1]
    if first:
        member_of = lambda x: normalize(jnp.exp(x))
    else:
        stat = stats[0][...]
        for ref in stats[1:]:
            stat += ref[...]
        for ref in rest:
            stat += ref[n:, :]
        weighted = stat[0:1, :]
        size = stat[1:2, :]
        member_of = lambda x: normalize(jnp.exp(-2.0 * standardize(x, size, weighted)))
    for j, src in enumerate(evens):
        m = member_of(src[...])
        high, low = split(m)
        even_hl[j * n : (j + 1) * n, :clusters] = high
        even_hl[j * n : (j + 1) * n, clusters:] = low
        if j == 0:
            member[:n, :] = m
    for i, src in enumerate(rest):
        member[(i + 1) * n : (i + 2) * n, :] = member_of(src[:n, :])


def members_call(first, n, stats, evens, others, unused):
    clusters = evens[0].shape[1]
    return call(
        functools.partial(
            members_body, first, n, len(stats), len(evens), len(others), len(unused)
        ),
        stats + evens + others,
        [
            shaped(n * len(evens), 2 * clusters, jnp.bfloat16),
            shaped(n * (1 + len(others)), clusters),
        ],
        unused,
    )


def product(high, low, members):
    clusters = members.shape[1] // 2
    both = jnp.dot(high, members, preferred_element_type=F32)
    rest = jnp.dot(low, members[:, :clusters], preferred_element_type=F32)
    return both[:, :clusters] + (both[:, clusters:] + rest)


def even_body(n, half, members, *refs):
    out = refs[-1]
    for i in range(len(refs) // 2):
        out[i * n : (i + 1) * n, :] = product(
            refs[2 * i][:, :half], refs[2 * i + 1][:, :half], members[...]
        )


def even_call(n, members, kernels):
    half, clusters = members.shape[0], members.shape[1] // 2
    rows = n * len(kernels) // 2
    return call(
        functools.partial(even_body, n, half),
        [members] + kernels,
        [shaped(rows, clusters)],
        flops=6 * rows * half * clusters,
    )[0]


def odd_body(n, has_near, members, partial, member, *refs):
    half, clusters = members.shape[0], members.shape[1] // 2
    blocks = partial.shape[0] // n
    kernels, refs = refs[: 2 * blocks], refs[2 * blocks :]
    outs, (t_even, t_odd) = refs[:blocks], refs[blocks:]
    total = None
    for i in range(blocks):
        rows = slice(i * n, (i + 1) * n)
        s = partial[rows, :] + product(
            kernels[2 * i][:, half:], kernels[2 * i + 1][:, half:], members[...]
        )
        outs[i][:n, :] = s
        if i > 0:
            outs[i][n:, :] = jnp.zeros((BACK_ROWS, clusters), F32)
        part = jnp.sum(member[rows, :] * s, axis=0, keepdims=True)
        if i > has_near:
            part = 2.0 * part
        total = part if total is None else total + part
    over = (((0,), (0,)), ((), ()))
    for part, dst in enumerate((t_even, t_odd)):
        columns = slice(part * half, (part + 1) * half)
        acc = jnp.zeros((half, clusters), F32)
        for i in range(has_near + 1, blocks):
            high, low = split(member[i * n : (i + 1) * n, :])
            both = jnp.concatenate([high, low], axis=1)
            a = lax.dot_general(
                kernels[2 * i][:, columns], both, over, preferred_element_type=F32
            )
            b = lax.dot_general(
                kernels[2 * i + 1][:, columns], high, over, preferred_element_type=F32
            )
            acc += a[:, :clusters] + (a[:, clusters:] + b)
        dst[:half, :] = acc
    row = lax.broadcasted_iota(jnp.int32, (STAT_ROWS, clusters), 0)
    size = jnp.sum(member[:n, :], axis=0, keepdims=True)
    stat = jnp.where(row == 0, total, jnp.where(row == 1, size, 0.0))
    t_even[half:, :] = stat
    t_odd[half:, :] = stat


def odd_call(n, has_near, members, partial, member, kernels):
    half, clusters = members.shape[0], members.shape[1] // 2
    blocks = partial.shape[0] // n
    return call(
        functools.partial(odd_body, n, has_near),
        [members, partial, member] + kernels,
        [shaped(n, clusters)]
        + [shaped(n + BACK_ROWS, clusters)] * (blocks - 1)
        + [shaped(half + STAT_ROWS, clusters)] * 2,
        flops=6 * (2 * blocks - has_near) * n * half * clusters,
    )


def fold_body(n, t_even, received, *outs):
    half = t_even.shape[0] - STAT_ROWS
    stat = t_even[half:, :] + received[half:, :]
    for j, out in enumerate(outs):
        rows = slice(j * n, (j + 1) * n)
        out[:n, :] = t_even[rows, :] + received[rows, :]
        out[n:, :] = stat


def sum_body(n, *refs):
    wide, backs, (full, scores, stats) = refs[0], refs[1:-3], refs[-3:]
    total = wide[:n, :]
    stat = wide[n:, :]
    for ref in backs:
        total += ref[:n, :]
        if ref.shape[0] == n + STAT_ROWS:
            stat += ref[n:, :]
    full[:n, :] = total
    full[n:, :] = stat
    scores[...] = total
    stats[...] = stat


def finish_body(scores, *refs):
    stats, (members, standardized) = refs[:-2], refs[-2:]
    stat = stats[0][...]
    for ref in stats[1:]:
        stat += ref[...]
    x = standardize(scores[...], stat[1:2, :], stat[0:1, :])
    standardized[...] = x
    members[...] = normalize(jnp.exp(-2.0 * x))


def on_device(rows, cols, features, logits):
    n = logits.shape[0]
    column = lax.axis_index("col")
    masks = list(range(2, cols, 2))
    order = [0] + masks
    order = order + [k + 1 for k in order]
    has_near = int(rows % 2 == 0)
    half_rows = rows // 2
    if has_near:
        place = [2 * q if q < half_rows else 2 * (q - half_rows) + 1 for q in range(rows)]
        offsets = list(range(1, half_rows))
    else:
        place = list(range(rows))
        offsets = list(range(1, half_rows + 1))

    def by_col(x, mask):
        return lax.ppermute(x, "col", [(i, i ^ mask) for i in range(cols)])

    def near(x):
        return lax.ppermute(x, "row", [(i, i ^ 1) for i in range(rows)])

    def shift(x, d):
        return lax.ppermute(x, "row", [(place[(q + d) % rows], place[q]) for q in range(rows)])

    own_rows = lax.dynamic_slice_in_dim(features, column * n, n, 0)
    row_blocks = [None] + ([near(own_rows)] if has_near else [])
    row_blocks += [shift(own_rows, d) for d in offsets]
    index = jnp.reshape(column, (1,)).astype(jnp.int32)
    kernels = []
    for block in row_blocks:
        kernels += kernel_block(tuple(order), index, block, features, n)

    evens = [logits] + [by_col(logits, k) for k in masks]
    padded = jnp.pad(logits, ((0, BACK_ROWS), (0, 0)))
    others = ([near(logits)] if has_near else []) + [shift(padded, d) for d in offsets]
    stats, after = [], kernels[1::2]
    for iteration in range(ITERS):
        even, member = members_call(iteration == 0, n, stats, evens, others, after)
        odd = by_col(even, 1)
        partial = even_call(n, even, kernels)
        outs = odd_call(n, has_near, odd, partial, member, kernels)
        own, back, t_even, t_odd = outs[0], list(outs[1:-2]), outs[-2], outs[-1]
        clusters = own.shape[1]
        sent = call(
            functools.partial(fold_body, n),
            [t_even, by_col(t_odd, 1)],
            [shaped(n + STAT_ROWS, clusters)] * (1 + len(masks)),
        )
        parts = [by_col(x, k) for k, x in zip(masks, sent[1:])]
        back = [
            near(x) if d == 0 else shift(x, -d)
            for d, x in zip(([0] if has_near else []) + offsets, back)
        ]
        full, scores, stats = call(
            functools.partial(sum_body, n),
            [sent[0], own] + back + parts,
            [shaped(n + STAT_ROWS, clusters), shaped(n, clusters), shaped(STAT_ROWS, clusters)],
        )
        if iteration < ITERS - 1:
            evens = [scores] + [by_col(scores, k) for k in masks]
            others = ([near(full)] if has_near else []) + [shift(full, d) for d in offsets]
            stats = [stats] + [shift(stats, -d) for d in offsets]
            after = []
    stats = [stats] + [shift(stats, d) for d in range(1, rows)]
    return tuple(call(finish_body, [scores] + stats, [shaped(*scores.shape)] * 2))


def solution(mesh):
    return jax.shard_map(
        functools.partial(on_device, mesh.shape["row"], mesh.shape["col"]),
        mesh=mesh,
        in_specs=(P("row", None), P(("row", "col"), None)),
        out_specs=(P(("row", "col"), None), P(("row", "col"), None)),
        check_vma=False,
    )
```

time: 257 us -> 82.2 us (0.32)
  waiting for transfers between devices: 121 us -> 29.6 us
  blocking collectives: 77.1 us -> 0 us
  starting transfers between devices: 0.2 us -> 36.9 us
  matrix products: 27.2 us -> 0 us
  other arithmetic: 13.8 us -> 0 us
  between operations: 13.9 us -> 0.8 us
  Pallas kernels: 0 us -> 11.2 us
    all_gather x3 -> x0, waiting for transfers between devices: 77.3 us -> none  [the longest x2 48.8 us: on_device(): members_row = lax.all_gather(members, 'col', axis=0, tiled=True)]
    psum x2 -> x0, blocking collectives: 77.1 us -> none  [on_device(): lax.psum((jnp.sum(members, axis=0), jnp.sum(members * scores, axis=0)), (...]
    reduce_scatter x2 -> x0, waiting for transfers between devices: 43.5 us -> none  [on_device(): lax.psum_scatter(kernel_product(column_panel, features, members_row), 'ro...]
    ppermute x0 -> x30, starting transfers between devices: none -> 36.9 us  [the longest x9 17.3 us: shift(): lax.ppermute(x, 'row', [(place[(q + d) % rows], place[q]) for q in range(...]
    ppermute x0 -> x30, waiting for transfers between devices: none -> 29.6 us  [the longest x9 17 us: shift(): lax.ppermute(x, 'row', [(place[(q + d) % rows], place[q]) for q in range(...]
    dot_general x8 -> x0, matrix products: 27.2 us -> none  [the longest x4 14.7 us: block_product(): jnp.dot(kernel, members, precision=lax.Precision.HIGHEST, preferred_eleme...]
    pallas_call x0 -> x14, Pallas kernels: none -> 11.2 us  [the longest x11 8.54 us: call(): pl.pallas_call(body, in_specs=[VMEM] * len(args) + [ANY] * len(unused), o...]
    reduce_sum x9 -> x0, other arithmetic: 9.61 us -> none  [the longest x3 3.29 us: on_device(): members = raised / jnp.sum(raised, axis=1, keepdims=True)]
  transfers between devices with their start and end apart: 5 -> 30, of which waited for: 5 -> 18; matrix products, arithmetic and copies ran while one was open for 1% -> 1% of each run, Pallas kernels for 0% -> 6%
where the time goes in v2:
time: 82.2 us; the launch traced here: 82 us
  starting transfers between devices  36.9 us (45%)
  waiting for transfers between devices  29.6 us (36%)
  Pallas kernels  11.2 us (14%)
  local copies, waits for them, and re-layouts  3.52 us (4%)
    ppermute x9, starting transfers between devices, shift(): lax.ppermute(x, 'row', [(place[(q + d) % rows], place[q]) for q in range(...  17.3 us
    ppermute x9, waiting for transfers between devices, shift(): lax.ppermute(x, 'row', [(place[(q + d) % rows], place[q]) for q in range(...  17 us
    ppermute x16, starting transfers between devices, by_col(): return lax.ppermute(x, 'col', [(i, i ^ mask) for i in range(cols)])  15.6 us
    ppermute x16, waiting for transfers between devices, by_col(): return lax.ppermute(x, 'col', [(i, i ^ mask) for i in range(cols)])  10.4 us
    pallas_call x11, Pallas kernels, call(): pl.pallas_call(body, in_specs=[VMEM] * len(args) + [ANY] * len(unused), o...  8.54 us
    ppermute x5, starting transfers between devices, near(): return lax.ppermute(x, 'row', [(i, i ^ 1) for i in range(rows)])  4 us
    pallas_call x3, Pallas kernels, kernel_block(): pl.pallas_call(functools.partial(kernel_body, order, own), in_specs=[pl.B...  2.62 us
    ppermute x5, waiting for transfers between devices, near(): return lax.ppermute(x, 'row', [(i, i ^ 1) for i in range(rows)])  2.28 us
  transfers between devices with their start and end apart: 30, of which 18 were waited for; matrix products, arithmetic and copies ran while one was open for 1% of the time, Pallas kernels for 6%

profile of v2, /device:TPU:0, one launch (start us, length us, event | category | flops | bytes accessed | tf_op | source)
XLA Modules:
  0.0 82.0 jit_solution(9108044229481950212)
XLA Ops:
  0.6 1.0 %constant_dynamic-slice_fusion = bf16[256,512]{1,0:T(8,128)(2,1)S(1)} fusion(bf16[2048,512]{1,0:T(8,128)(2,1)} %refs_1_.3, s32[]{:T(128)S(6)} %select_n.3), kind=kLoop, calls=%fused_computation | loop fusion | bytes 524292 | tf_op jit(solution)/shard_map/dynamic_slice | solution.py:276
  1.6 5.1 %collective-permute-start.6 = (bf16[256,512]{1,0:T(8,128)(2,1)S(1)}, bf16[256,512]{1,0:T(8,128)(2,1)S(1)}, u32[]{:S(2)}, u32[]{:S(2)}) collective-permute-start(bf16[256,512]{1,0:T(8,128)(2,1)S(1)} %constant_dynamic-slice_fusion), channel_id=1, source_target_pairs={{16,0},{8,16},{24,8},{0,24},{17,1},{9,17},{25,9},{1,25},{18,2},{10... | collective-permute-start | bytes 786440 | tf_op jit(solution)/shard_map/ppermute | solution.py:274
  6.7 0.0 collective-permute-start.5
  6.7 2.0 %collective-permute-start.3 = (f32[256,128]{1,0:T(8,128)}, f32[256,128]{1,0:T(8,128)S(1)}, u32[]{:S(2)}, u32[]{:S(2)}) collective-permute-start(f32[256,128]{1,0:T(8,128)} %refs_0_.3), channel_id=1, source_target_pairs={{0,8},{8,0},{16,24},{24,16},{1,9},{9,1},{17,25},{25,17},{2,10},{10... | collective-permute-start | bytes 393224 | tf_op jit(solution)/shard_map/ppermute | solution.py:271
  8.7 2.4 %collective-permute-start.2 = (f32[256,128]{1,0:T(8,128)}, f32[256,128]{1,0:T(8,128)S(1)}, u32[]{:S(2)}, u32[]{:S(2)}) collective-permute-start(f32[256,128]{1,0:T(8,128)} %refs_0_.3), channel_id=1, source_target_pairs={{0,6},{1,7},{2,4},{3,5},{4,2},{5,3},{6,0},{7,1},{8,14},{9,15},{10,... | collective-permute-start | bytes 393224 | tf_op jit(solution)/shard_map/ppermute | solution.py:268
  11.2 0.5 collective-permute-start.1
  11.7 0.9 %pad.4 = f32[272,128]{1,0:T(8,128)S(1)} pad(f32[256,128]{1,0:T(8,128)} %refs_0_.3, f32[]{:T(128)} %constant.2.clone.1), padding=0_16x0_0 | pad | bytes 270340 | tf_op jit(solution)/shard_map/jit(_pad)/pad | solution.py:285
  12.6 5.1 %collective-permute-done.6.refs_0_ = bf16[256,512]{1,0:T(8,128)(2,1)S(1)} collective-permute-done((bf16[256,512]{1,0:T(8,128)(2,1)S(1)}, bf16[256,512]{1,0:T(8,128)(2,1)S(1)}, u32[]{:S(2)}, u32[]{:S(2)}) %collective-permute-start.6) | collective-permute-done | bytes 262176 | tf_op jit(solution)/shard_map/ppermute | solution.py:274
  17.7 1.5 %collective-permute-start = (f32[256,128]{1,0:T(8,128)}, f32[256,128]{1,0:T(8,128)S(1)}, u32[]{:S(2)}, u32[]{:S(2)}) collective-permute-start(f32[256,128]{1,0:T(8,128)} %refs_0_.3), channel_id=1, source_target_pairs={{0,2},{1,3},{2,0},{3,1},{4,6},{5,7},{6,4},{7,5},{8,10},{9,11},{10,... | collective-permute-start | bytes 393224 | tf_op jit(solution)/shard_map/ppermute | solution.py:268
  19.3 1.1 %collective-permute-done.5.refs_0_ = bf16[256,512]{1,0:T(8,128)(2,1)S(1)} collective-permute-done((bf16[256,512]{1,0:T(8,128)(2,1)S(1)}, bf16[256,512]{1,0:T(8,128)(2,1)S(1)}, u32[]{:S(2)}, u32[]{:S(2)}) %collective-permute-start.5) | collective-permute-done | bytes 262176 | tf_op jit(solution)/shard_map/ppermute | solution.py:271
  20.3 1.5 %collective-permute-start.4 = (f32[272,128]{1,0:T(8,128)S(1)}, f32[272,128]{1,0:T(8,128)S(1)}, u32[]{:S(2)}, u32[]{:S(2)}) collective-permute-start(f32[272,128]{1,0:T(8,128)S(1)} %pad.4), channel_id=1, source_target_pairs={{16,0},{8,16},{24,8},{0,24},{17,1},{9,17},{25,9},{1,25},{18,2},{10... | collective-permute-start | bytes 417800 | tf_op jit(solution)/shard_map/ppermute | solution.py:274
  21.9 1.6 %copy-done = bf16[2048,512]{1,0:T(8,128)(2,1)S(1)} copy-done((bf16[2048,512]{1,0:T(8,128)(2,1)S(1)}, bf16[2048,512]{1,0:T(8,128)(2,1)}, u32[]{:S(2)}) %copy-start) | copy-done | bytes 2097176
  23.4 0.9 %shard_map.41 = (bf16[256,2048]{1,0:T(8,128)(2,1)S(1)}, bf16[256,2048]{1,0:T(8,128)(2,1)S(1)}) custom-call(s32[1]{0:T(128)} %bitcast.column_ref, bf16[2048,512]{1,0:T(8,128)(2,1)S(1)} %copy-done), custom_call_target="tpu_custom_call" | custom-call | flops 536870912 | bytes 4456448 | tf_op jit(solution)/shard_map/pallas_call | solution.py:47
  24.3 0.0 copy-start.1
  24.3 0.9 %shard_map.42 = (bf16[256,2048]{1,0:T(8,128)(2,1)S(1)}, bf16[256,2048]{1,0:T(8,128)(2,1)S(1)}) custom-call(s32[1]{0:T(128)} %bitcast.column_ref, bf16[256,512]{1,0:T(8,128)(2,1)S(1)} %collective-permute-done.5.refs_0_, bf16[2048,512]{1,0:T(8,128)(2,1)S(1)} %copy-done), custom_call_target="tpu_custom_call" | custom-call | flops 536870912 | bytes 4456448 | tf_op jit(solution)/shard_map/pallas_call | solution.py:47
  25.2 0.9 %shard_map.43 = (bf16[256,2048]{1,0:T(8,128)(2,1)S(1)}, bf16[256,2048]{1,0:T(8,128)(2,1)S(1)}) custom-call(s32[1]{0:T(128)} %bitcast.column_ref, bf16[256,512]{1,0:T(8,128)(2,1)S(1)} %collective-permute-done.6.refs_0_, bf16[2048,512]{1,0:T(8,128)(2,1)S(1)} %copy-done), custom_call_target="tpu_custom_call" | custom-call | flops 536870912 | bytes 4456448 | tf_op jit(solution)/shard_map/pallas_call | solution.py:47
  26.1 1.6 %collective-permute-done.4.refs_5_ = f32[272,128]{1,0:T(8,128)S(1)} collective-permute-done((f32[272,128]{1,0:T(8,128)S(1)}, f32[272,128]{1,0:T(8,128)S(1)}, u32[]{:S(2)}, u32[]{:S(2)}) %collective-permute-start.4) | collective-permute-done | bytes 139296 | tf_op jit(solution)/shard_map/ppermute | solution.py:274
  27.8 0.3 shard_map.44
  28.1 0.1 collective-permute-start.7
  28.2 1.0 %shard_map.45.partial = f32[768,128]{1,0:T(8,128)S(1)} custom-call(bf16[1024,256]{1,0:T(8,128)(2,1)S(1)} %get-tuple-element.38.members, bf16[256,2048]{1,0:T(8,128)(2,1)S(1)} %get-tuple-element.39.refs_0_, bf16[256,2048]{1,0:T(8,128)(2,1)S(1)} %get-tuple-element.35.refs_6_.refs_1_, bf16[256,2048]{1,0:T(8,128)(2,1)S(1)} %get-tuple-element.40.refs_2_, ...), custom_call_target="tpu_custom_call" | custom-call | flops 603979776 | bytes 7208960 | tf_op jit(solution)/shard_map/pallas_call | solution.py:79
  29.1 0.9 %collective-permute-done.7.members = bf16[1024,256]{1,0:T(8,128)(2,1)S(1)} collective-permute-done((bf16[1024,256]{1,0:T(8,128)(2,1)S(1)}, bf16[1024,256]{1,0:T(8,128)(2,1)S(1)}, u32[]{:S(2)}, u32[]{:S(2)}) %collective-permute-start.7) | collective-permute-done | bytes 524320 | tf_op jit(solution)/shard_map/ppermute | solution.py:268
  30.1 1.6 %shard_map.46 = (f32[256,128]{1,0:T(8,128)S(1)}, f32[272,128]{1,0:T(8,128)S(1)}, f32[272,128]{1,0:T(8,128)S(1)}, f32[1032,128]{1,0:T(8,128)S(1)}, f32[1032,128]{1,0:T(8,128)S(1)}) custom-call(bf16[1024,256]{1,0:T(8,128)(2,1)S(1)} %collective-permute-done.7.members, f32[768,128]{1,0:T(8,128)S(1)} %shard_map.45.partial, ...), custom_call_target="tpu_custom_call" | custom-call | flops 1006632960 | bytes 9068544 | tf_op jit(solution)/shard_map/pallas_call | solution.py:79
  31.6 0.2 collective-permute-start.8
  31.9 1.6 %collective-permute-start.10 = (f32[272,128]{1,0:T(8,128)S(1)}, f32[272,128]{1,0:T(8,128)S(1)}, u32[]{:S(2)}, u32[]{:S(2)}) collective-permute-start(f32[272,128]{1,0:T(8,128)S(1)} %get-tuple-element.48), channel_id=1, source_target_pairs={{24,0},{0,16},{16,8},{8,24},{25,1},{1,17},{17,9},{9,25},{26,2},{2,... | collective-permute-start | bytes 417800 | tf_op jit(solution)/shard_map/ppermute | solution.py:274
  33.5 0.2 collective-permute-done.8.received
  33.6 0.1 shard_map.47
  33.7 1.6 %collective-permute-start.11 = (f32[264,128]{1,0:T(8,128)S(1)}, f32[264,128]{1,0:T(8,128)S(1)}, u32[]{:S(2)}, u32[]{:S(2)}) collective-permute-start(f32[264,128]{1,0:T(8,128)S(1)} %get-tuple-element.49), channel_id=1, source_target_pairs={{0,2},{1,3},{2,0},{3,1},{4,6},{5,7},{6,4},{7,5},{8,10},{9,11},{10,... | collective-permute-start | bytes 405512 | tf_op jit(solution)/shard_map/ppermute | solution.py:268
  35.3 1.5 %collective-permute-start.12 = (f32[264,128]{1,0:T(8,128)S(1)}, f32[264,128]{1,0:T(8,128)S(1)}, u32[]{:S(2)}, u32[]{:S(2)}) collective-permute-start(f32[264,128]{1,0:T(8,128)S(1)} %get-tuple-element.50), channel_id=1, source_target_pairs={{0,4},{1,5},{2,6},{3,7},{4,0},{5,1},{6,2},{7,3},{8,12},{9,13},{10,... | collective-permute-start | bytes 405512 | tf_op jit(solution)/shard_map/ppermute | solution.py:268
  36.8 0.4 collective-permute-start.13
  37.2 1.1 %collective-permute-done.9.refs_2_ = f32[272,128]{1,0:T(8,128)S(1)} collective-permute-done((f32[272,128]{1,0:T(8,128)S(1)}, f32[272,128]{1,0:T(8,128)S(1)}, u32[]{:S(2)}, u32[]{:S(2)}) %collective-permute-start.9) | collective-permute-done | bytes 139296 | tf_op jit(solution)/shard_map/ppermute | solution.py:271
  38.4 2.4 %collective-permute-done.10.refs_3_ = f32[272,128]{1,0:T(8,128)S(1)} collective-permute-done((f32[272,128]{1,0:T(8,128)S(1)}, f32[272,128]{1,0:T(8,128)S(1)}, u32[]{:S(2)}, u32[]{:S(2)}) %collective-permute-start.10) | collective-permute-done | bytes 139296 | tf_op jit(solution)/shard_map/ppermute | solution.py:274
  40.8 2.7 %collective-permute-done.12.refs_5_ = f32[264,128]{1,0:T(8,128)S(1)} collective-permute-done((f32[264,128]{1,0:T(8,128)S(1)}, f32[264,128]{1,0:T(8,128)S(1)}, u32[]{:S(2)}, u32[]{:S(2)}) %collective-permute-start.12) | collective-permute-done | bytes 135200 | tf_op jit(solution)/shard_map/ppermute | solution.py:268
  43.5 0.1 shard_map.48
  43.6 1.4 %collective-permute-start.14 = (f32[8,128]{1,0:T(8,128)S(1)}, f32[8,128]{1,0:T(8,128)S(1)}, u32[]{:S(2)}, u32[]{:S(2)}) collective-permute-start(f32[8,128]{1,0:T(8,128)S(1)} %get-tuple-element.52.refs_0_), channel_id=1, source_target_pairs={{24,0},{0,16},{16,8},{8,24},{25,1},{1,17},{17,9},{9,25},{26,2},{2,... | collective-permute-start | bytes 12296 | tf_op jit(solution)/shard_map/ppermute | solution.py:274
  45.1 2.4 %collective-permute-start.19 = (f32[264,128]{1,0:T(8,128)S(1)}, f32[264,128]{1,0:T(8,128)S(1)}, u32[]{:S(2)}, u32[]{:S(2)}) collective-permute-start(f32[264,128]{1,0:T(8,128)S(1)} %get-tuple-element.54), channel_id=1, source_target_pairs={{16,0},{8,16},{24,8},{0,24},{17,1},{9,17},{25,9},{1,25},{18,2},{10... | collective-permute-start | bytes 405512 | tf_op jit(solution)/shard_map/ppermute | solution.py:274
  47.5 1.5 %collective-permute-start.17 = (f32[256,128]{1,0:T(8,128)S(1)}, f32[256,128]{1,0:T(8,128)S(1)}, u32[]{:S(2)}, u32[]{:S(2)}) collective-permute-start(f32[256,128]{1,0:T(8,128)S(1)} %get-tuple-element.53.refs_2_), channel_id=1, source_target_pairs={{0,6},{1,7},{2,4},{3,5},{4,2},{5,3},{6,0},{7,1},{8,14},{9,15},{10,... | collective-permute-start | bytes 393224 | tf_op jit(solution)/shard_map/ppermute | solution.py:268
  49.0 1.2 %collective-permute-start.16 = (f32[256,128]{1,0:T(8,128)S(1)}, f32[256,128]{1,0:T(8,128)S(1)}, u32[]{:S(2)}, u32[]{:S(2)}) collective-permute-start(f32[256,128]{1,0:T(8,128)S(1)} %get-tuple-element.53.refs_2_), channel_id=1, source_target_pairs={{0,4},{1,5},{2,6},{3,7},{4,0},{5,1},{6,2},{7,3},{8,12},{9,13},{10,... | collective-permute-start | bytes 393224 | tf_op jit(solution)/shard_map/ppermute | solution.py:268
  50.2 0.8 collective-permute-start.15
  51.0 2.8 %collective-permute-done.17.refs_5_ = f32[256,128]{1,0:T(8,128)S(1)} collective-permute-done((f32[256,128]{1,0:T(8,128)S(1)}, f32[256,128]{1,0:T(8,128)S(1)}, u32[]{:S(2)}, u32[]{:S(2)}) %collective-permute-start.17) | collective-permute-done | bytes 131104 | tf_op jit(solution)/shard_map/ppermute | solution.py:268
  53.8 1.2 %collective-permute-done.16.refs_4_ = f32[256,128]{1,0:T(8,128)S(1)} collective-permute-done((f32[256,128]{1,0:T(8,128)S(1)}, f32[256,128]{1,0:T(8,128)S(1)}, u32[]{:S(2)}, u32[]{:S(2)}) %collective-permute-start.16) | collective-permute-done | bytes 131104 | tf_op jit(solution)/shard_map/ppermute | solution.py:268
  55.1 0.2 collective-permute-done.15.refs_3_
  55.2 1.2 %shard_map.49 = (bf16[1024,256]{1,0:T(8,128)(2,1)S(1)}, f32[768,128]{1,0:T(8,128)S(1)}) custom-call(f32[8,128]{1,0:T(8,128)S(1)} %get-tuple-element.52.refs_0_, f32[8,128]{1,0:T(8,128)S(1)} %collective-permute-done.14.refs_1_, f32[256,128]{1,0:T(8,128)S(1)} %get-tuple-element.53.refs_2_, f32[256,128]{1,0:T(8,128)S(1)} %collective-permute-done.15.refs_3_, ...), custom_call_target="tpu_custom_call" | custom-call | bytes 1720320 | tf_op jit(solution)/shard_map/pallas_call | solution.py:79
  56.4 0.1 collective-permute-start.20
  56.5 1.0 %shard_map.50.partial = f32[768,128]{1,0:T(8,128)S(1)} custom-call(bf16[1024,256]{1,0:T(8,128)(2,1)S(1)} %get-tuple-element.55.members, bf16[256,2048]{1,0:T(8,128)(2,1)S(1)} %get-tuple-element.39.refs_0_, bf16[256,2048]{1,0:T(8,128)(2,1)S(1)} %get-tuple-element.35.refs_6_.refs_1_, bf16[256,2048]{1,0:T(8,128)(2,1)S(1)} %get-tuple-element.40.refs_2_, ...), custom_call_target="tpu_custom_call" | custom-call | flops 603979776 | bytes 7208960 | tf_op jit(solution)/shard_map/pallas_call | solution.py:79
  57.5 0.9 %collective-permute-done.20.members = bf16[1024,256]{1,0:T(8,128)(2,1)S(1)} collective-permute-done((bf16[1024,256]{1,0:T(8,128)(2,1)S(1)}, bf16[1024,256]{1,0:T(8,128)(2,1)S(1)}, u32[]{:S(2)}, u32[]{:S(2)}) %collective-permute-start.20) | collective-permute-done | bytes 524320 | tf_op jit(solution)/shard_map/ppermute | solution.py:268
  58.4 1.6 %shard_map.51 = (f32[256,128]{1,0:T(8,128)S(1)}, f32[272,128]{1,0:T(8,128)S(1)}, f32[272,128]{1,0:T(8,128)S(1)}, f32[1032,128]{1,0:T(8,128)S(1)}, f32[1032,128]{1,0:T(8,128)S(1)}) custom-call(bf16[1024,256]{1,0:T(8,128)(2,1)S(1)} %collective-permute-done.20.members, f32[768,128]{1,0:T(8,128)S(1)} %shard_map.50.partial, ...), custom_call_target="tpu_custom_call" | custom-call | flops 1006632960 | bytes 9068544 | tf_op jit(solution)/shard_map/pallas_call | solution.py:79
  60.0 0.2 collective-permute-start.21
  60.2 2.0 %collective-permute-start.22 = (f32[272,128]{1,0:T(8,128)S(1)}, f32[272,128]{1,0:T(8,128)S(1)}, u32[]{:S(2)}, u32[]{:S(2)}) collective-permute-start(f32[272,128]{1,0:T(8,128)S(1)} %get-tuple-element.61), channel_id=1, source_target_pairs={{0,8},{8,0},{16,24},{24,16},{1,9},{9,1},{17,25},{25,17},{2,10},{10... | collective-permute-start | bytes 417800 | tf_op jit(solution)/shard_map/ppermute | solution.py:271
  62.2 0.5 collective-permute-start.23
  62.7 0.1 shard_map.52
  62.7 0.9 %collective-permute-start.24 = (f32[264,128]{1,0:T(8,128)S(1)}, f32[264,128]{1,0:T(8,128)S(1)}, u32[]{:S(2)}, u32[]{:S(2)}) collective-permute-start(f32[264,128]{1,0:T(8,128)S(1)} %get-tuple-element.63), channel_id=1, source_target_pairs={{0,2},{1,3},{2,0},{3,1},{4,6},{5,7},{6,4},{7,5},{8,10},{9,11},{10,... | collective-permute-start | bytes 405512 | tf_op jit(solution)/shard_map/ppermute | solution.py:268
  63.7 1.5 %collective-permute-start.25 = (f32[264,128]{1,0:T(8,128)S(1)}, f32[264,128]{1,0:T(8,128)S(1)}, u32[]{:S(2)}, u32[]{:S(2)}) collective-permute-start(f32[264,128]{1,0:T(8,128)S(1)} %get-tuple-element.64), channel_id=1, source_target_pairs={{0,4},{1,5},{2,6},{3,7},{4,0},{5,1},{6,2},{7,3},{8,12},{9,13},{10,... | collective-permute-start | bytes 405512 | tf_op jit(solution)/shard_map/ppermute | solution.py:268
  65.1 1.2 %collective-permute-start.26 = (f32[264,128]{1,0:T(8,128)S(1)}, f32[264,128]{1,0:T(8,128)S(1)}, u32[]{:S(2)}, u32[]{:S(2)}) collective-permute-start(f32[264,128]{1,0:T(8,128)S(1)} %get-tuple-element.65), channel_id=1, source_target_pairs={{0,6},{1,7},{2,4},{3,5},{4,2},{5,3},{6,0},{7,1},{8,14},{9,15},{10,... | collective-permute-start | bytes 405512 | tf_op jit(solution)/shard_map/ppermute | solution.py:268
  66.3 0.1 collective-permute-done.22.refs_2_
  66.4 3.9 %collective-permute-done.23.refs_3_ = f32[272,128]{1,0:T(8,128)S(1)} collective-permute-done((f32[272,128]{1,0:T(8,128)S(1)}, f32[272,128]{1,0:T(8,128)S(1)}, u32[]{:S(2)}, u32[]{:S(2)}) %collective-permute-start.23) | collective-permute-done | bytes 139296 | tf_op jit(solution)/shard_map/ppermute | solution.py:274
  70.3 1.4 %collective-permute-done.25.refs_5_ = f32[264,128]{1,0:T(8,128)S(1)} collective-permute-done((f32[264,128]{1,0:T(8,128)S(1)}, f32[264,128]{1,0:T(8,128)S(1)}, u32[]{:S(2)}, u32[]{:S(2)}) %collective-permute-start.25) | collective-permute-done | bytes 135200 | tf_op jit(solution)/shard_map/ppermute | solution.py:268
  71.7 0.7 shard_map.53
  72.5 1.4 %collective-permute-start.29 = (f32[8,128]{1,0:T(8,128)S(1)}, f32[8,128]{1,0:T(8,128)S(1)}, u32[]{:S(2)}, u32[]{:S(2)}) collective-permute-start(f32[8,128]{1,0:T(8,128)S(1)} %get-tuple-element.67.refs_0_), channel_id=1, source_target_pairs={{24,0},{0,16},{16,8},{8,24},{25,1},{1,17},{17,9},{9,25},{26,2},{2,... | collective-permute-start | bytes 12296 | tf_op jit(solution)/shard_map/ppermute | solution.py:274
  73.9 2.6 %collective-permute-start.28 = (f32[8,128]{1,0:T(8,128)S(1)}, f32[8,128]{1,0:T(8,128)S(1)}, u32[]{:S(2)}, u32[]{:S(2)}) collective-permute-start(f32[8,128]{1,0:T(8,128)S(1)} %get-tuple-element.67.refs_0_), channel_id=1, source_target_pairs={{8,0},{24,16},{0,8},{16,24},{9,1},{25,17},{1,9},{17,25},{10,2},{26... | collective-permute-start | bytes 12296 | tf_op jit(solution)/shard_map/ppermute | solution.py:274
  76.5 0.6 collective-permute-start.27
  77.2 0.7 collective-permute-done.29.refs_3_
  77.9 0.2 collective-permute-done.28.refs_2_
  78.1 2.9 %collective-permute-done.27.refs_1_ = f32[8,128]{1,0:T(8,128)S(1)} collective-permute-done((f32[8,128]{1,0:T(8,128)S(1)}, f32[8,128]{1,0:T(8,128)S(1)}, u32[]{:S(2)}, u32[]{:S(2)}) %collective-permute-start.27) | collective-permute-done | bytes 4128 | tf_op jit(solution)/shard_map/ppermute | solution.py:274
  81.0 1.0 %shard_map.54 = (f32[256,128]{1,0:T(8,128)}, f32[256,128]{1,0:T(8,128)}) custom-call(f32[256,128]{1,0:T(8,128)S(1)} %get-tuple-element.66.scores, f32[8,128]{1,0:T(8,128)S(1)} %get-tuple-element.67.refs_0_, f32[8,128]{1,0:T(8,128)S(1)} %collective-permute-done.27.refs_1_, f32[8,128]{1,0:T(8,128)S(1)} %collective-permute-done.28.refs_2_, ...), custom_call_target="tpu_custom_call" | custom-call | bytes 409600 | tf_op jit(solution)/shard_map/pallas_call | solution.py:79
  (16 shorter events, 0.0 us)
Async XLA Ops:
  1.6 16.1 %collective-permute-start.6 = (bf16[256,512]{1,0:T(8,128)(2,1)S(1)}, bf16[256,512]{1,0:T(8,128)(2,1)S(1)}, u32[]{:S(2)}, u32[]{:S(2)}) collective-permute-start(bf16[256,512]{1,0:T(8,128)(2,1)S(1)} %constant_dynamic-slice_fusion), channel_id=1, source_target_pairs={{16,0},{8,16},{24,8},{0,24},{17,1},{9,17},{25,9},{1,25},{18,2},{10... | collective-permute-start | bytes 786440 | tf_op jit(solution)/shard_map/ppermute | solution.py:274
  6.7 13.6 %collective-permute-start.5 = (bf16[256,512]{1,0:T(8,128)(2,1)S(1)}, bf16[256,512]{1,0:T(8,128)(2,1)S(1)}, u32[]{:S(2)}, u32[]{:S(2)}) collective-permute-start(bf16[256,512]{1,0:T(8,128)(2,1)S(1)} %constant_dynamic-slice_fusion), channel_id=1, source_target_pairs={{0,8},{8,0},{16,24},{24,16},{1,9},{9,1},{17,25},{25,17},{2,10},{10... | collective-permute-start | bytes 786440 | tf_op jit(solution)/shard_map/ppermute | solution.py:271
  6.7 19.4 %collective-permute-start.3 = (f32[256,128]{1,0:T(8,128)}, f32[256,128]{1,0:T(8,128)S(1)}, u32[]{:S(2)}, u32[]{:S(2)}) collective-permute-start(f32[256,128]{1,0:T(8,128)} %refs_0_.3), channel_id=1, source_target_pairs={{0,8},{8,0},{16,24},{24,16},{1,9},{9,1},{17,25},{25,17},{2,10},{10... | collective-permute-start | bytes 393224 | tf_op jit(solution)/shard_map/ppermute | solution.py:271
  8.7 17.4 %collective-permute-start.2 = (f32[256,128]{1,0:T(8,128)}, f32[256,128]{1,0:T(8,128)S(1)}, u32[]{:S(2)}, u32[]{:S(2)}) collective-permute-start(f32[256,128]{1,0:T(8,128)} %refs_0_.3), channel_id=1, source_target_pairs={{0,6},{1,7},{2,4},{3,5},{4,2},{5,3},{6,0},{7,1},{8,14},{9,15},{10,... | collective-permute-start | bytes 393224 | tf_op jit(solution)/shard_map/ppermute | solution.py:268
  11.2 14.9 %collective-permute-start.1 = (f32[256,128]{1,0:T(8,128)}, f32[256,128]{1,0:T(8,128)S(1)}, u32[]{:S(2)}, u32[]{:S(2)}) collective-permute-start(f32[256,128]{1,0:T(8,128)} %refs_0_.3), channel_id=1, source_target_pairs={{0,4},{1,5},{2,6},{3,7},{4,0},{5,1},{6,2},{7,3},{8,12},{9,13},{10,... | collective-permute-start | bytes 393224 | tf_op jit(solution)/shard_map/ppermute | solution.py:268
  17.7 8.4 %collective-permute-start = (f32[256,128]{1,0:T(8,128)}, f32[256,128]{1,0:T(8,128)S(1)}, u32[]{:S(2)}, u32[]{:S(2)}) collective-permute-start(f32[256,128]{1,0:T(8,128)} %refs_0_.3), channel_id=1, source_target_pairs={{0,2},{1,3},{2,0},{3,1},{4,6},{5,7},{6,4},{7,5},{8,10},{9,11},{10,... | collective-permute-start | bytes 393224 | tf_op jit(solution)/shard_map/ppermute | solution.py:268
  20.3 7.4 %collective-permute-start.4 = (f32[272,128]{1,0:T(8,128)S(1)}, f32[272,128]{1,0:T(8,128)S(1)}, u32[]{:S(2)}, u32[]{:S(2)}) collective-permute-start(f32[272,128]{1,0:T(8,128)S(1)} %pad.4), channel_id=1, source_target_pairs={{16,0},{8,16},{24,8},{0,24},{17,1},{9,17},{25,9},{1,25},{18,2},{10... | collective-permute-start | bytes 417800 | tf_op jit(solution)/shard_map/ppermute | solution.py:274
  21.9 1.6 %copy-start = (bf16[2048,512]{1,0:T(8,128)(2,1)S(1)}, bf16[2048,512]{1,0:T(8,128)(2,1)}, u32[]{:S(2)}) copy-start(bf16[2048,512]{1,0:T(8,128)(2,1)} %refs_1_.3) | copy-start | bytes 6291460
  24.3 3.5 %copy-start.1 = (f32[256,128]{1,0:T(8,128)S(1)}, f32[256,128]{1,0:T(8,128)}, u32[]{:S(2)}) copy-start(f32[256,128]{1,0:T(8,128)} %refs_0_.3) | copy-start | bytes 393220
  28.1 2.0 %collective-permute-start.7 = (bf16[1024,256]{1,0:T(8,128)(2,1)S(1)}, bf16[1024,256]{1,0:T(8,128)(2,1)S(1)}, u32[]{:S(2)}, u32[]{:S(2)}) collective-permute-start(bf16[1024,256]{1,0:T(8,128)(2,1)S(1)} %get-tuple-element.38.members), channel_id=1, source_target_pairs={{0,1},{1,0},{2,3},{3,2},{4,5},{5,4},{6,7},{7,6},{8,9},{9,8},{10,11... | collective-permute-start | bytes 1572872 | tf_op jit(solution)/shard_map/ppermute | solution.py:268
  31.6 2.0 %collective-permute-start.8 = (f32[1032,128]{1,0:T(8,128)S(1)}, f32[1032,128]{1,0:T(8,128)S(1)}, u32[]{:S(2)}, u32[]{:S(2)}) collective-permute-start(f32[1032,128]{1,0:T(8,128)S(1)} %get-tuple-element.44), channel_id=1, source_target_pairs={{0,1},{1,0},{2,3},{3,2},{4,5},{5,4},{6,7},{7,6},{8,9},{9,8},{10,11... | collective-permute-start | bytes 1585160 | tf_op jit(solution)/shard_map/ppermute | solution.py:268
  31.9 6.5 %collective-permute-start.9 = (f32[272,128]{1,0:T(8,128)S(1)}, f32[272,128]{1,0:T(8,128)S(1)}, u32[]{:S(2)}, u32[]{:S(2)}) collective-permute-start(f32[272,128]{1,0:T(8,128)S(1)} %get-tuple-element.47), channel_id=1, source_target_pairs={{0,8},{8,0},{16,24},{24,16},{1,9},{9,1},{17,25},{25,17},{2,10},{10... | collective-permute-start | bytes 417800 | tf_op jit(solution)/shard_map/ppermute | solution.py:271
  31.9 8.9 %collective-permute-start.10 = (f32[272,128]{1,0:T(8,128)S(1)}, f32[272,128]{1,0:T(8,128)S(1)}, u32[]{:S(2)}, u32[]{:S(2)}) collective-permute-start(f32[272,128]{1,0:T(8,128)S(1)} %get-tuple-element.48), channel_id=1, source_target_pairs={{24,0},{0,16},{16,8},{8,24},{25,1},{1,17},{17,9},{9,25},{26,2},{2,... | collective-permute-start | bytes 417800 | tf_op jit(solution)/shard_map/ppermute | solution.py:274
  33.7 7.1 %collective-permute-start.11 = (f32[264,128]{1,0:T(8,128)S(1)}, f32[264,128]{1,0:T(8,128)S(1)}, u32[]{:S(2)}, u32[]{:S(2)}) collective-permute-start(f32[264,128]{1,0:T(8,128)S(1)} %get-tuple-element.49), channel_id=1, source_target_pairs={{0,2},{1,3},{2,0},{3,1},{4,6},{5,7},{6,4},{7,5},{8,10},{9,11},{10,... | collective-permute-start | bytes 405512 | tf_op jit(solution)/shard_map/ppermute | solution.py:268
  35.3 8.2 %collective-permute-start.12 = (f32[264,128]{1,0:T(8,128)S(1)}, f32[264,128]{1,0:T(8,128)S(1)}, u32[]{:S(2)}, u32[]{:S(2)}) collective-permute-start(f32[264,128]{1,0:T(8,128)S(1)} %get-tuple-element.50), channel_id=1, source_target_pairs={{0,4},{1,5},{2,6},{3,7},{4,0},{5,1},{6,2},{7,3},{8,12},{9,13},{10,... | collective-permute-start | bytes 405512 | tf_op jit(solution)/shard_map/ppermute | solution.py:268
  36.8 6.7 %collective-permute-start.13 = (f32[264,128]{1,0:T(8,128)S(1)}, f32[264,128]{1,0:T(8,128)S(1)}, u32[]{:S(2)}, u32[]{:S(2)}) collective-permute-start(f32[264,128]{1,0:T(8,128)S(1)} %get-tuple-element.51), channel_id=1, source_target_pairs={{0,6},{1,7},{2,4},{3,5},{4,2},{5,3},{6,0},{7,1},{8,14},{9,15},{10,... | collective-permute-start | bytes 405512 | tf_op jit(solution)/shard_map/ppermute | solution.py:268
  43.6 6.6 %collective-permute-start.14 = (f32[8,128]{1,0:T(8,128)S(1)}, f32[8,128]{1,0:T(8,128)S(1)}, u32[]{:S(2)}, u32[]{:S(2)}) collective-permute-start(f32[8,128]{1,0:T(8,128)S(1)} %get-tuple-element.52.refs_0_), channel_id=1, source_target_pairs={{24,0},{0,16},{16,8},{8,24},{25,1},{1,17},{17,9},{9,25},{26,2},{2,... | collective-permute-start | bytes 12296 | tf_op jit(solution)/shard_map/ppermute | solution.py:274
  45.1 10.2 %collective-permute-start.19 = (f32[264,128]{1,0:T(8,128)S(1)}, f32[264,128]{1,0:T(8,128)S(1)}, u32[]{:S(2)}, u32[]{:S(2)}) collective-permute-start(f32[264,128]{1,0:T(8,128)S(1)} %get-tuple-element.54), channel_id=1, source_target_pairs={{16,0},{8,16},{24,8},{0,24},{17,1},{9,17},{25,9},{1,25},{18,2},{10... | collective-permute-start | bytes 405512 | tf_op jit(solution)/shard_map/ppermute | solution.py:274
  47.5 7.8 %collective-permute-start.18 = (f32[264,128]{1,0:T(8,128)S(1)}, f32[264,128]{1,0:T(8,128)S(1)}, u32[]{:S(2)}, u32[]{:S(2)}) collective-permute-start(f32[264,128]{1,0:T(8,128)S(1)} %get-tuple-element.54), channel_id=1, source_target_pairs={{0,8},{8,0},{16,24},{24,16},{1,9},{9,1},{17,25},{25,17},{2,10},{10... | collective-permute-start | bytes 405512 | tf_op jit(solution)/shard_map/ppermute | solution.py:271
  47.5 6.3 %collective-permute-start.17 = (f32[256,128]{1,0:T(8,128)S(1)}, f32[256,128]{1,0:T(8,128)S(1)}, u32[]{:S(2)}, u32[]{:S(2)}) collective-permute-start(f32[256,128]{1,0:T(8,128)S(1)} %get-tuple-element.53.refs_2_), channel_id=1, source_target_pairs={{0,6},{1,7},{2,4},{3,5},{4,2},{5,3},{6,0},{7,1},{8,14},{9,15},{10,... | collective-permute-start | bytes 393224 | tf_op jit(solution)/shard_map/ppermute | solution.py:268
  49.0 6.1 %collective-permute-start.16 = (f32[256,128]{1,0:T(8,128)S(1)}, f32[256,128]{1,0:T(8,128)S(1)}, u32[]{:S(2)}, u32[]{:S(2)}) collective-permute-start(f32[256,128]{1,0:T(8,128)S(1)} %get-tuple-element.53.refs_2_), channel_id=1, source_target_pairs={{0,4},{1,5},{2,6},{3,7},{4,0},{5,1},{6,2},{7,3},{8,12},{9,13},{10,... | collective-permute-start | bytes 393224 | tf_op jit(solution)/shard_map/ppermute | solution.py:268
  50.2 5.0 %collective-permute-start.15 = (f32[256,128]{1,0:T(8,128)S(1)}, f32[256,128]{1,0:T(8,128)S(1)}, u32[]{:S(2)}, u32[]{:S(2)}) collective-permute-start(f32[256,128]{1,0:T(8,128)S(1)} %get-tuple-element.53.refs_2_), channel_id=1, source_target_pairs={{0,2},{1,3},{2,0},{3,1},{4,6},{5,7},{6,4},{7,5},{8,10},{9,11},{10,... | collective-permute-start | bytes 393224 | tf_op jit(solution)/shard_map/ppermute | solution.py:268
  56.4 2.0 %collective-permute-start.20 = (bf16[1024,256]{1,0:T(8,128)(2,1)S(1)}, bf16[1024,256]{1,0:T(8,128)(2,1)S(1)}, u32[]{:S(2)}, u32[]{:S(2)}) collective-permute-start(bf16[1024,256]{1,0:T(8,128)(2,1)S(1)} %get-tuple-element.55.members), channel_id=1, source_target_pairs={{0,1},{1,0},{2,3},{3,2},{4,5},{5,4},{6,7},{7,6},{8,9},{9,8},{10,11... | collective-permute-start | bytes 1572872 | tf_op jit(solution)/shard_map/ppermute | solution.py:268
  60.0 2.7 %collective-permute-start.21 = (f32[1032,128]{1,0:T(8,128)S(1)}, f32[1032,128]{1,0:T(8,128)S(1)}, u32[]{:S(2)}, u32[]{:S(2)}) collective-permute-start(f32[1032,128]{1,0:T(8,128)S(1)} %get-tuple-element.58), channel_id=1, source_target_pairs={{0,1},{1,0},{2,3},{3,2},{4,5},{5,4},{6,7},{7,6},{8,9},{9,8},{10,11... | collective-permute-start | bytes 1585160 | tf_op jit(solution)/shard_map/ppermute | solution.py:268
  60.2 6.2 %collective-permute-start.22 = (f32[272,128]{1,0:T(8,128)S(1)}, f32[272,128]{1,0:T(8,128)S(1)}, u32[]{:S(2)}, u32[]{:S(2)}) collective-permute-start(f32[272,128]{1,0:T(8,128)S(1)} %get-tuple-element.61), channel_id=1, source_target_pairs={{0,8},{8,0},{16,24},{24,16},{1,9},{9,1},{17,25},{25,17},{2,10},{10... | collective-permute-start | bytes 417800 | tf_op jit(solution)/shard_map/ppermute | solution.py:271
  62.2 8.1 %collective-permute-start.23 = (f32[272,128]{1,0:T(8,128)S(1)}, f32[272,128]{1,0:T(8,128)S(1)}, u32[]{:S(2)}, u32[]{:S(2)}) collective-permute-start(f32[272,128]{1,0:T(8,128)S(1)} %get-tuple-element.62), channel_id=1, source_target_pairs={{24,0},{0,16},{16,8},{8,24},{25,1},{1,17},{17,9},{9,25},{26,2},{2,... | collective-permute-start | bytes 417800 | tf_op jit(solution)/shard_map/ppermute | solution.py:274
  62.7 7.6 %collective-permute-start.24 = (f32[264,128]{1,0:T(8,128)S(1)}, f32[264,128]{1,0:T(8,128)S(1)}, u32[]{:S(2)}, u32[]{:S(2)}) collective-permute-start(f32[264,128]{1,0:T(8,128)S(1)} %get-tuple-element.63), channel_id=1, source_target_pairs={{0,2},{1,3},{2,0},{3,1},{4,6},{5,7},{6,4},{7,5},{8,10},{9,11},{10,... | collective-permute-start | bytes 405512 | tf_op jit(solution)/shard_map/ppermute | solution.py:268
  63.7 8.1 %collective-permute-start.25 = (f32[264,128]{1,0:T(8,128)S(1)}, f32[264,128]{1,0:T(8,128)S(1)}, u32[]{:S(2)}, u32[]{:S(2)}) collective-permute-start(f32[264,128]{1,0:T(8,128)S(1)} %get-tuple-element.64), channel_id=1, source_target_pairs={{0,4},{1,5},{2,6},{3,7},{4,0},{5,1},{6,2},{7,3},{8,12},{9,13},{10,... | collective-permute-start | bytes 405512 | tf_op jit(solution)/shard_map/ppermute | solution.py:268
  65.1 6.6 %collective-permute-start.26 = (f32[264,128]{1,0:T(8,128)S(1)}, f32[264,128]{1,0:T(8,128)S(1)}, u32[]{:S(2)}, u32[]{:S(2)}) collective-permute-start(f32[264,128]{1,0:T(8,128)S(1)} %get-tuple-element.65), channel_id=1, source_target_pairs={{0,6},{1,7},{2,4},{3,5},{4,2},{5,3},{6,0},{7,1},{8,14},{9,15},{10,... | collective-permute-start | bytes 405512 | tf_op jit(solution)/shard_map/ppermute | solution.py:268
  72.5 5.4 %collective-permute-start.29 = (f32[8,128]{1,0:T(8,128)S(1)}, f32[8,128]{1,0:T(8,128)S(1)}, u32[]{:S(2)}, u32[]{:S(2)}) collective-permute-start(f32[8,128]{1,0:T(8,128)S(1)} %get-tuple-element.67.refs_0_), channel_id=1, source_target_pairs={{24,0},{0,16},{16,8},{8,24},{25,1},{1,17},{17,9},{9,25},{26,2},{2,... | collective-permute-start | bytes 12296 | tf_op jit(solution)/shard_map/ppermute | solution.py:274
  73.9 4.2 %collective-permute-start.28 = (f32[8,128]{1,0:T(8,128)S(1)}, f32[8,128]{1,0:T(8,128)S(1)}, u32[]{:S(2)}, u32[]{:S(2)}) collective-permute-start(f32[8,128]{1,0:T(8,128)S(1)} %get-tuple-element.67.refs_0_), channel_id=1, source_target_pairs={{8,0},{24,16},{0,8},{16,24},{9,1},{25,17},{1,9},{17,25},{10,2},{26... | collective-permute-start | bytes 12296 | tf_op jit(solution)/shard_map/ppermute | solution.py:274
  76.5 4.5 %collective-permute-start.27 = (f32[8,128]{1,0:T(8,128)S(1)}, f32[8,128]{1,0:T(8,128)S(1)}, u32[]{:S(2)}, u32[]{:S(2)}) collective-permute-start(f32[8,128]{1,0:T(8,128)S(1)} %get-tuple-element.67.refs_0_), channel_id=1, source_target_pairs={{16,0},{8,16},{24,8},{0,24},{17,1},{9,17},{25,9},{1,25},{18,2},{10... | collective-permute-start | bytes 12296 | tf_op jit(solution)/shard_map/ppermute | solution.py:274

commit v3 on v0

v3 whole, which is shorter than its diff:
```python
import functools

import jax
import jax.numpy as jnp
from jax import lax
from jax.experimental import pallas as pl
from jax.experimental.pallas import tpu as pltpu
from jax.sharding import PartitionSpec as P

ITERS = 2
STAT_ROWS = 8
BACK_ROWS = 16
VMEM_BYTES = 24 * 1024 * 1024
VMEM = pl.BlockSpec(memory_space=pltpu.VMEM)
SMEM = pl.BlockSpec(memory_space=pltpu.SMEM)
ANY = pl.BlockSpec(memory_space=pl.ANY)
HBM = pl.BlockSpec(memory_space=pltpu.HBM)
BF16 = jnp.bfloat16
F32 = jnp.float32


def shaped(rows, columns, dtype=F32):
    return jax.ShapeDtypeStruct((rows, columns), dtype)


def call(body, args, outs, specs=None, scratch=(), flops=0, hidden=False):
    bytes_accessed = sum(x.size * x.dtype.itemsize for x in list(args) + list(outs))
    if hidden:
        flops = bytes_accessed = 0
    made = pl.pallas_call(
        body,
        in_specs=specs or [VMEM] * len(args),
        out_specs=[VMEM] * len(outs),
        out_shape=list(outs),
        scratch_shapes=list(scratch),
        compiler_params=pltpu.CompilerParams(vmem_limit_bytes=VMEM_BYTES),
        cost_estimate=pl.CostEstimate(
            flops=flops, bytes_accessed=bytes_accessed, transcendentals=0
        ),
    )(*args)
    return list(made)


def split(x):
    high = x.astype(BF16)
    low = (x - high.astype(F32)).astype(BF16)
    return high, low


def whole(pair):
    clusters = pair.shape[1] // 2
    return pair[:, :clusters].astype(F32) + pair[:, clusters:].astype(F32)


def standardize(scores, size, weighted):
    distance = weighted / (size * size) - 2.0 * scores / size
    centered = distance - jnp.mean(distance, axis=1, keepdims=True)
    spread = jnp.mean(centered * centered, axis=1, keepdims=True)
    return centered / jnp.sqrt(spread + 1e-06)


def normalize(raised):
    return raised / jnp.sum(raised, axis=1, keepdims=True)


def store_pair(out, rows, x):
    clusters = x.shape[1]
    high, low = split(x)
    out[rows, :clusters] = high
    out[rows, clusters:] = low


def prepare_body(column_ref, features, logits, message, pair, sem):
    n, clusters = logits.shape
    width = features.shape[1]
    start = pl.multiple_of(column_ref[0] * n, n)
    copy = pltpu.make_async_copy(
        features.at[pl.ds(start, n), :], message.at[:, pl.ds(0, width)], sem
    )
    copy.start()
    high, low = split(normalize(jnp.exp(logits[...])))
    pair[:, :clusters] = high
    pair[:, clusters:] = low
    message[:, width : width + clusters] = high
    message[:, width + clusters :] = low
    copy.wait()


def kernel_body(order, column_ref, rows_ref, plane_ref, *refs):
    high_ref, low_ref = refs[-2:]
    n, width = rows_ref.shape[0], plane_ref.shape[1]
    column = column_ref[0]
    rows = rows_ref[:, :width]
    for j, k in enumerate(order):
        start = pl.multiple_of(lax.bitwise_xor(column, k) * n, n)
        inner = lax.dot_general(
            rows,
            plane_ref[pl.ds(start, n), :],
            (((1,), (1,)), ((), ())),
            preferred_element_type=F32,
        )
        t = inner / width
        high, low = split(t * (3.0 + t * (3.0 + t)))
        high_ref[:, j * n : (j + 1) * n] = high
        low_ref[:, j * n : (j + 1) * n] = low


def kernel_call(order, column, rows, plane, after=()):
    n, total = rows.shape[0], plane.shape[0]
    return call(
        functools.partial(kernel_body, tuple(order)),
        [column, rows, plane, *after],
        [shaped(n, total, BF16)] * 2,
        [SMEM, VMEM, VMEM] + [ANY] * len(after),
        hidden=True,
    )


def scores_body(at, pieces, kernels, partials, *refs):
    members, refs = refs[:pieces], refs[pieces:]
    blocks, refs = refs[:kernels], refs[kernels:]
    before, outs = refs[:partials], refs[partials:]
    n = blocks[0].shape[0]
    clusters = members[0].shape[1] // 2
    for i, out in enumerate(outs):
        both, rest, start = None, None, at
        for piece in members:
            columns = slice(start, start + piece.shape[0])
            start += piece.shape[0]
            a = jnp.dot(blocks[2 * i][:, columns], piece[...], preferred_element_type=F32)
            b = jnp.dot(
                blocks[2 * i + 1][:, columns],
                piece[:, :clusters],
                preferred_element_type=F32,
            )
            both = a if both is None else both + a
            rest = b if rest is None else rest + b
        s = both[:, :clusters] + (both[:, clusters:] + rest)
        if partials:
            s += before[i][:n, :]
        out[:n, :] = s
        if out.shape[0] > n:
            out[n:, :] = jnp.zeros((out.shape[0] - n, clusters), F32)


def scores_call(at, members, kernels, partials, extra, hidden=False):
    n, clusters = kernels[0].shape[0], members[0].shape[1] // 2
    depth = sum(x.shape[0] for x in members)
    return call(
        functools.partial(scores_body, at, len(members), len(kernels), len(partials)),
        members + kernels + partials,
        [shaped(n + e, clusters) for e in extra],
        flops=3 * n * len(kernels) * depth * clusters,
        hidden=hidden,
    )


def members_body(n, smalls, evens, others, *refs):
    stats, refs = refs[:smalls], refs[smalls:]
    own, refs = refs[:evens], refs[evens:]
    rest, refs = refs[:others], refs[others:]
    even, pairs = refs[0], refs[1:]
    stat = stats[0][...]
    for ref in stats[1:]:
        stat += ref[...]
    for ref in rest:
        stat += ref[n:, :]
    weighted, size = stat[0:1, :], stat[1:2, :]

    def member_of(x):
        return normalize(jnp.exp(-2.0 * standardize(x, size, weighted)))

    for j, ref in enumerate(own):
        store_pair(even, slice(j * n, (j + 1) * n), member_of(ref[...]))
    for pair, ref in zip(pairs, rest):
        store_pair(pair, slice(0, n), member_of(ref[:n, :]))


def members_call(n, stats, evens, others):
    clusters = evens[0].shape[1]
    return call(
        functools.partial(members_body, n, len(stats), len(evens), len(others)),
        stats + evens + others,
        [shaped(n * len(evens), 2 * clusters, BF16)]
        + [shaped(n, 2 * clusters, BF16)] * len(others),
    )


def stat_body(has_near, own, *refs):
    out, refs = refs[-1], refs[:-1]
    count = len(refs) // 2
    scores, pairs = refs[: count + 1], refs[count + 1 :]
    n, clusters = scores[0].shape
    member = whole(own[:n, :])
    total = jnp.sum(member * scores[0][...], axis=0, keepdims=True)
    for i in range(count):
        pair = pairs[i]
        other = whole(pair[:, pair.shape[1] - 2 * clusters :])
        part = jnp.sum(other * scores[i + 1][:n, :], axis=0, keepdims=True)
        total += part if i < has_near else 2.0 * part
    size = jnp.sum(member, axis=0, keepdims=True)
    row = lax.broadcasted_iota(jnp.int32, out.shape, 0)
    out[...] = jnp.where(row == 0, total, jnp.where(row == 1, size, 0.0))


def stat_call(has_near, own, scores, pairs):
    clusters = scores[0].shape[1]
    return call(
        functools.partial(stat_body, has_near),
        [own] + scores + pairs,
        [shaped(STAT_ROWS, clusters)],
    )[0]


def other_body(count, *refs):
    pairs, refs = refs[:count], refs[count:]
    kernels, refs = refs[: 2 * count], refs[2 * count :]
    stat, (even, odd) = refs[:-2], refs[-2:]
    half, clusters = even.shape
    over = (((0,), (0,)), ((), ()))
    for part, out in enumerate((odd, even)):
        columns = slice((1 - part) * half, (2 - part) * half)
        acc = jnp.zeros((half, clusters), F32)
        for i, pair in enumerate(pairs):
            both = pair[:, pair.shape[1] - 2 * clusters :]
            a = lax.dot_general(
                kernels[2 * i][:, columns], both, over, preferred_element_type=F32
            )
            b = lax.dot_general(
                kernels[2 * i + 1][:, columns],
                both[:, :clusters],
                over,
                preferred_element_type=F32,
            )
            acc += a[:, :clusters] + (a[:, clusters:] + b)
        out[:half, :] = acc
    if stat:
        odd[half:, :] = stat[0][...]


def other_call(half, clusters, pairs, kernels, stat):
    n = pairs[0].shape[0] if pairs else 0
    return call(
        functools.partial(other_body, len(pairs)),
        pairs + kernels + stat,
        [shaped(half, clusters), shaped(half + STAT_ROWS * len(stat), clusters)],
        flops=12 * n * len(pairs) * half * clusters,
    )


def fold_body(n, count, even, received, *refs):
    stats, outs = refs[:count], refs[count:]
    half = even.shape[0]
    stat = stats[0][...]
    for ref in stats[1:]:
        stat += ref[...]
    if received.shape[0] > half:
        stat += received[half:, :]
    for j, out in enumerate(outs):
        rows = slice(j * n, (j + 1) * n)
        out[:n, :] = even[rows, :] + received[rows, :]
        out[n:, :] = stat


def sum_body(n, last, *refs):
    many = 2 if last else 3
    refs, outs = refs[:-many], refs[-many:]
    total, stat = refs[0][:n, :], refs[0][n:, :]
    for ref in refs[1:]:
        total += ref[:n, :]
        if ref.shape[0] == n + STAT_ROWS:
            stat += ref[n:, :]
    if last:
        members, standardized = outs
        x = standardize(total, stat[1:2, :], stat[0:1, :])
        standardized[...] = x
        members[...] = normalize(jnp.exp(-2.0 * x))
    else:
        full, scores, stats = outs
        full[:n, :] = total
        full[n:, :] = stat
        scores[...] = total
        stats[...] = stat


def on_device(rows, cols, features, logits):
    n, clusters = logits.shape
    width = features.shape[1]
    half = n * cols // 2
    masks = list(range(2, cols, 2))
    order = [0] + masks
    order = order + [k + 1 for k in order]
    has_near = int(rows % 2 == 0)
    half_rows = rows // 2
    if has_near:
        place = [2 * q if q < half_rows else 2 * (q - half_rows) + 1 for q in range(rows)]
        offsets = list(range(1, half_rows))
    else:
        place = list(range(rows))
        offsets = list(range(1, half_rows + 1))
    steps = ([0] if has_near else []) + offsets

    def by_col(x, mask):
        return lax.ppermute(x, "col", [(i, i ^ mask) for i in range(cols)])

    def shift(x, d):
        if d == 0:
            pairs = [(i, i ^ 1) for i in range(rows)]
        else:
            pairs = [(place[(q + d) % rows], place[q]) for q in range(rows)]
        return lax.ppermute(x, "row", pairs)

    column = jnp.reshape(lax.axis_index("col"), (1,)).astype(jnp.int32)
    message, pair = call(
        prepare_body,
        [column, features, logits],
        [shaped(n, width + 2 * clusters, BF16), shaped(n, 2 * clusters, BF16)],
        [SMEM, HBM, VMEM],
        [pltpu.SemaphoreType.DMA],
    )
    others = [shift(message, d) for d in steps]
    members = [pair] + [by_col(pair, k) for k in order[1:]]
    early = 1 + has_near
    extra = [0] + [BACK_ROWS] * len(steps)
    rows_of = [message] + others
    kernels = []
    for x in rows_of[:early]:
        kernels += kernel_call(order, column, x, features)
    scores = scores_call(0, members, kernels, [], extra[:early], True)
    cross = []
    for x in rows_of[early:]:
        cross += kernel_call(order, column, x, features, scores)
    scores += scores_call(0, members, cross, [], extra[early:], True)
    kernels += cross
    own = pair

    for iteration in range(ITERS):
        last = iteration == ITERS - 1
        if iteration > 0:
            even, *others = members_call(n, stats, evens, others)
            odd = by_col(even, 1)
            scores = scores_call(0, [even], kernels, [], extra)
            scores = scores_call(half, [odd], kernels, scores, extra)
            own = even
        stat = stat_call(has_near, own, scores, others)
        t_even, t_odd = other_call(
            half, clusters, others[has_near:], cross, [] if last else [stat]
        )
        if last:
            planes = [shift(stat, d) for d in list(range(1, rows))]
            for x in planes:
                stat = stat + x
            stats = [stat, by_col(stat, 1)]
        else:
            stats = [stat]
        sent = call(
            functools.partial(fold_body, n, len(stats)),
            [t_even, by_col(t_odd, 1)] + stats,
            [shaped(n + STAT_ROWS, clusters)] * (1 + len(masks)),
        )
        parts = [by_col(x, k) for k, x in zip(masks, sent[1:])]
        back = [shift(x, -d) for d, x in zip(steps, scores[1:])]
        outs = [shaped(n, clusters)] * 2
        if not last:
            outs = [shaped(n + STAT_ROWS, clusters), outs[0], shaped(STAT_ROWS, clusters)]
        done = call(
            functools.partial(sum_body, n, last),
            [sent[0], scores[0]] + back + parts,
            outs,
        )
        if not last:
            full, total, stats = done
            evens = [total] + [by_col(total, k) for k in masks]
            others = [shift(full, d) for d in steps]
            stats = [stats] + [shift(stats, -d) for d in offsets]
    return tuple(done)


def solution(mesh):
    return jax.shard_map(
        functools.partial(on_device, mesh.shape["row"], mesh.shape["col"]),
        mesh=mesh,
        in_specs=(P("row", None), P(("row", "col"), None)),
        out_specs=(P(("row", "col"), None), P(("row", "col"), None)),
        check_vma=False,
    )
```

time: 257 us -> 84.5 us (0.33)
  waiting for transfers between devices: 121 us -> 32.1 us
  blocking collectives: 77.1 us -> 0 us
  starting transfers between devices: 0.2 us -> 37.8 us
  matrix products: 27.2 us -> 0 us
  other arithmetic: 13.8 us -> 0.01 us
  between operations: 13.9 us -> 0.81 us
  Pallas kernels: 0 us -> 10.8 us
    all_gather x3 -> x0, waiting for transfers between devices: 77.3 us -> none  [the longest x2 48.8 us: on_device(): members_row = lax.all_gather(members, 'col', axis=0, tiled=True)]
    psum x2 -> x0, blocking collectives: 77.1 us -> none  [on_device(): lax.psum((jnp.sum(members, axis=0), jnp.sum(members * scores, axis=0)), (...]
    reduce_scatter x2 -> x0, waiting for transfers between devices: 43.5 us -> none  [on_device(): lax.psum_scatter(kernel_product(column_panel, features, members_row), 'ro...]
    ppermute x0 -> x32, starting transfers between devices: none -> 37.8 us  [the longest x12 20.5 us: shift(): return lax.ppermute(x, 'row', pairs)]
    ppermute x0 -> x32, waiting for transfers between devices: none -> 32.1 us  [the longest x20 17.4 us: by_col(): return lax.ppermute(x, 'col', [(i, i ^ mask) for i in range(cols)])]
    dot_general x8 -> x0, matrix products: 27.2 us -> none  [the longest x4 14.7 us: block_product(): jnp.dot(kernel, members, precision=lax.Precision.HIGHEST, preferred_eleme...]
    pallas_call x0 -> x17, Pallas kernels: none -> 10.8 us  [call(): pl.pallas_call(body, in_specs=specs or [VMEM] * len(args), out_specs=[VME...]
    reduce_sum x9 -> x0, other arithmetic: 9.61 us -> none  [the longest x3 3.29 us: on_device(): members = raised / jnp.sum(raised, axis=1, keepdims=True)]
  transfers between devices with their start and end apart: 5 -> 32, of which waited for: 5 -> 16; matrix products, arithmetic and copies ran while one was open for 1% -> 0% of each run, Pallas kernels for 0% -> 7%
where the time goes in v3:
time: 84.5 us; the launch traced here: 84.3 us
  starting transfers between devices  37.8 us (45%)
  waiting for transfers between devices  32.1 us (38%)
  Pallas kernels  10.8 us (13%)
  local copies, waits for them, and re-layouts  2.78 us (3%)
    ppermute x12, starting transfers between devices, shift(): return lax.ppermute(x, 'row', pairs)  20.5 us
    ppermute x20, waiting for transfers between devices, by_col(): return lax.ppermute(x, 'col', [(i, i ^ mask) for i in range(cols)])  17.4 us
    ppermute x20, starting transfers between devices, by_col(): return lax.ppermute(x, 'col', [(i, i ^ mask) for i in range(cols)])  17.3 us
    ppermute x12, waiting for transfers between devices, shift(): return lax.ppermute(x, 'row', pairs)  14.6 us
    pallas_call x17, Pallas kernels, call(): pl.pallas_call(body, in_specs=specs or [VMEM] * len(args), out_specs=[VME...  10.8 us
    unnamed x6, local copies, waits for them, and re-layouts  2.78 us
  transfers between devices with their start and end apart: 32, of which 16 were waited for; matrix products, arithmetic and copies ran while one was open for 0% of the time, Pallas kernels for 7%

profile of v3, /device:TPU:0, one launch (start us, length us, event | category | flops | bytes accessed | tf_op | source)
XLA Modules:
  0.0 84.3 jit_solution(9539051386730424257)
XLA Ops:
  0.6 1.6 %copy-done = bf16[2048,512]{1,0:T(8,128)(2,1)S(1)} copy-done((bf16[2048,512]{1,0:T(8,128)(2,1)S(1)}, bf16[2048,512]{1,0:T(8,128)(2,1)}, u32[]{:S(2)}) %copy-start) | copy-done | bytes 2097176
  2.2 0.9 %copy-done.2 = f32[256,128]{1,0:T(8,128)S(1)} copy-done((f32[256,128]{1,0:T(8,128)S(1)}, f32[256,128]{1,0:T(8,128)}, u32[]{:S(2)}) %copy-start.2) | copy-done | bytes 131096
  3.1 0.2 shard_map.41
  3.3 3.1 %collective-permute-start.8 = (bf16[256,768]{1,0:T(8,128)(2,1)S(1)}, bf16[256,768]{1,0:T(8,128)(2,1)S(1)}, u32[]{:S(2)}, u32[]{:S(2)}) collective-permute-start(bf16[256,768]{1,0:T(8,128)(2,1)S(1)} %get-tuple-element.36.rows_ref), channel_id=1, source_target_pairs={{0,8},{8,0},{16,24},{24,16},{1,9},{9,1},{17,25},{25,17},{2,10},{10... | collective-permute-start | bytes 1179656 | tf_op jit(solution)/shard_map/ppermute | solution.py:311
  6.4 2.5 %collective-permute-start = (bf16[256,768]{1,0:T(8,128)(2,1)S(1)}, bf16[256,768]{1,0:T(8,128)(2,1)S(1)}, u32[]{:S(2)}, u32[]{:S(2)}) collective-permute-start(bf16[256,768]{1,0:T(8,128)(2,1)S(1)} %get-tuple-element.36.rows_ref), channel_id=1, source_target_pairs={{16,0},{8,16},{24,8},{0,24},{17,1},{9,17},{25,9},{1,25},{18,2},{10... | collective-permute-start | bytes 1179656 | tf_op jit(solution)/shard_map/ppermute | solution.py:311
  8.9 1.5 %collective-permute-start.1 = (bf16[256,256]{1,0:T(8,128)(2,1)S(1)}, bf16[256,256]{1,0:T(8,128)(2,1)S(1)}, u32[]{:S(2)}, u32[]{:S(2)}) collective-permute-start(bf16[256,256]{1,0:T(8,128)(2,1)S(1)} %get-tuple-element.37.refs_0_.own), channel_id=1, source_target_pairs={{0,2},{1,3},{2,0},{3,1},{4,6},{5,7},{6,4},{7,5},{8,10},{9,11},{10,... | collective-permute-start | bytes 393224 | tf_op jit(solution)/shard_map/ppermute | solution.py:304
  10.4 1.5 %collective-permute-start.2 = (bf16[256,256]{1,0:T(8,128)(2,1)S(1)}, bf16[256,256]{1,0:T(8,128)(2,1)S(1)}, u32[]{:S(2)}, u32[]{:S(2)}) collective-permute-start(bf16[256,256]{1,0:T(8,128)(2,1)S(1)} %get-tuple-element.37.refs_0_.own), channel_id=1, source_target_pairs={{0,4},{1,5},{2,6},{3,7},{4,0},{5,1},{6,2},{7,3},{8,12},{9,13},{10,... | collective-permute-start | bytes 393224 | tf_op jit(solution)/shard_map/ppermute | solution.py:304
  11.9 0.5 collective-permute-start.3
  12.3 2.2 %collective-permute-done.1.refs_1_ = bf16[256,256]{1,0:T(8,128)(2,1)S(1)} collective-permute-done((bf16[256,256]{1,0:T(8,128)(2,1)S(1)}, bf16[256,256]{1,0:T(8,128)(2,1)S(1)}, u32[]{:S(2)}, u32[]{:S(2)}) %collective-permute-start.1) | collective-permute-done | bytes 131104 | tf_op jit(solution)/shard_map/ppermute | solution.py:304
  14.6 3.6 %collective-permute-done.2.refs_2_ = bf16[256,256]{1,0:T(8,128)(2,1)S(1)} collective-permute-done((bf16[256,256]{1,0:T(8,128)(2,1)S(1)}, bf16[256,256]{1,0:T(8,128)(2,1)S(1)}, u32[]{:S(2)}, u32[]{:S(2)}) %collective-permute-start.2) | collective-permute-done | bytes 131104 | tf_op jit(solution)/shard_map/ppermute | solution.py:304
  18.1 1.2 %collective-permute-start.6 = (bf16[256,256]{1,0:T(8,128)(2,1)S(1)}, bf16[256,256]{1,0:T(8,128)(2,1)S(1)}, u32[]{:S(2)}, u32[]{:S(2)}) collective-permute-start(bf16[256,256]{1,0:T(8,128)(2,1)S(1)} %get-tuple-element.37.refs_0_.own), channel_id=1, source_target_pairs={{0,5},{1,4},{2,7},{3,6},{4,1},{5,0},{6,3},{7,2},{8,13},{9,12},{10,... | collective-permute-start | bytes 393224 | tf_op jit(solution)/shard_map/ppermute | solution.py:304
  19.4 4.5 %collective-permute-done.8.rows_ref.refs_3_ = bf16[256,768]{1,0:T(8,128)(2,1)S(1)} collective-permute-done((bf16[256,768]{1,0:T(8,128)(2,1)S(1)}, bf16[256,768]{1,0:T(8,128)(2,1)S(1)}, u32[]{:S(2)}, u32[]{:S(2)}) %collective-permute-start.8) | collective-permute-done | bytes 393248 | tf_op jit(solution)/shard_map/ppermute | solution.py:311
  23.8 1.2 %collective-permute-start.7 = (bf16[256,256]{1,0:T(8,128)(2,1)S(1)}, bf16[256,256]{1,0:T(8,128)(2,1)S(1)}, u32[]{:S(2)}, u32[]{:S(2)}) collective-permute-start(bf16[256,256]{1,0:T(8,128)(2,1)S(1)} %get-tuple-element.37.refs_0_.own), channel_id=1, source_target_pairs={{0,7},{1,6},{2,5},{3,4},{4,3},{5,2},{6,1},{7,0},{8,15},{9,14},{10,... | collective-permute-start | bytes 393224 | tf_op jit(solution)/shard_map/ppermute | solution.py:304
  25.0 0.9 %shard_map.42 = (bf16[256,2048]{1,0:T(8,128)(2,1)S(1)}, bf16[256,2048]{1,0:T(8,128)(2,1)S(1)}) custom-call(s32[1]{0:T(128)} %bitcast.column_ref, bf16[256,768]{1,0:T(8,128)(2,1)S(1)} %get-tuple-element.36.rows_ref, bf16[2048,512]{1,0:T(8,128)(2,1)S(1)} %copy-done), custom_call_target="tpu_custom_call" | custom-call | tf_op jit(solution)/shard_map/pallas_call | solution.py:30
  25.9 0.9 %shard_map.43 = (bf16[256,2048]{1,0:T(8,128)(2,1)S(1)}, bf16[256,2048]{1,0:T(8,128)(2,1)S(1)}) custom-call(s32[1]{0:T(128)} %bitcast.column_ref, bf16[256,768]{1,0:T(8,128)(2,1)S(1)} %collective-permute-done.8.rows_ref.refs_3_, bf16[2048,512]{1,0:T(8,128)(2,1)S(1)} %copy-done), custom_call_target="tpu_custom_call" | custom-call | tf_op jit(solution)/shard_map/pallas_call | solution.py:30
  26.8 3.5 %collective-permute-done.7.refs_7_ = bf16[256,256]{1,0:T(8,128)(2,1)S(1)} collective-permute-done((bf16[256,256]{1,0:T(8,128)(2,1)S(1)}, bf16[256,256]{1,0:T(8,128)(2,1)S(1)}, u32[]{:S(2)}, u32[]{:S(2)}) %collective-permute-start.7) | collective-permute-done | bytes 131104 | tf_op jit(solution)/shard_map/ppermute | solution.py:304
  30.2 1.3 %shard_map.44 = (f32[256,128]{1,0:T(8,128)S(1)}, f32[272,128]{1,0:T(8,128)S(1)}) custom-call(bf16[256,256]{1,0:T(8,128)(2,1)S(1)} %get-tuple-element.37.refs_0_.own, bf16[256,256]{1,0:T(8,128)(2,1)S(1)} %collective-permute-done.1.refs_1_, bf16[256,256]{1,0:T(8,128)(2,1)S(1)} %collective-permute-done.2.refs_2_, ...), custom_call_target="tpu_custom_call" | custom-call | tf_op jit(solution)/shard_map/pallas_call | solution.py:30
  31.5 0.3 copy-done.1
  31.8 0.9 %shard_map.45 = (bf16[256,2048]{1,0:T(8,128)(2,1)S(1)}, bf16[256,2048]{1,0:T(8,128)(2,1)S(1)}) custom-call(s32[1]{0:T(128)} %bitcast.column_ref, bf16[256,768]{1,0:T(8,128)(2,1)S(1)} %collective-permute-done.rows_ref.refs_4_.refs_0_, bf16[2048,512]{1,0:T(8,128)(2,1)S(1)} %copy-done.1, f32[256,128]{1,0:T(8,128)S(1)} %get-tuple-element.42.refs_0_.refs_1_, ...), custom_call_target="tpu_custom_call" | custom-call | tf_op jit(solution)/shard_map/pallas_call | solution.py:30
  32.7 0.7 shard_map.46.refs_2_
  33.4 0.1 shard_map.47.refs_3_.refs_0_
  33.5 0.8 shard_map.48
  34.3 0.2 collective-permute-start.9
  34.5 4.6 %collective-permute-start.10 = (f32[272,128]{1,0:T(8,128)S(1)}, f32[272,128]{1,0:T(8,128)S(1)}, u32[]{:S(2)}, u32[]{:S(2)}) collective-permute-start(f32[272,128]{1,0:T(8,128)S(1)} %get-tuple-element.43.refs_1_), channel_id=1, source_target_pairs={{0,8},{8,0},{16,24},{24,16},{1,9},{9,1},{17,25},{25,17},{2,10},{10... | collective-permute-start | bytes 417800 | tf_op jit(solution)/shard_map/ppermute | solution.py:311
  39.1 0.1 shard_map.49
  39.2 0.8 collective-permute-start.12
  39.9 1.0 %collective-permute-start.13 = (f32[264,128]{1,0:T(8,128)S(1)}, f32[264,128]{1,0:T(8,128)S(1)}, u32[]{:S(2)}, u32[]{:S(2)}) collective-permute-start(f32[264,128]{1,0:T(8,128)S(1)} %get-tuple-element.50), channel_id=1, source_target_pairs={{0,4},{1,5},{2,6},{3,7},{4,0},{5,1},{6,2},{7,3},{8,12},{9,13},{10,... | collective-permute-start | bytes 405512 | tf_op jit(solution)/shard_map/ppermute | solution.py:304
  40.9 1.8 %collective-permute-start.14 = (f32[264,128]{1,0:T(8,128)S(1)}, f32[264,128]{1,0:T(8,128)S(1)}, u32[]{:S(2)}, u32[]{:S(2)}) collective-permute-start(f32[264,128]{1,0:T(8,128)S(1)} %get-tuple-element.51), channel_id=1, source_target_pairs={{0,6},{1,7},{2,4},{3,5},{4,2},{5,3},{6,0},{7,1},{8,14},{9,15},{10,... | collective-permute-start | bytes 405512 | tf_op jit(solution)/shard_map/ppermute | solution.py:304
  42.7 0.3 collective-permute-done.11.refs_3_
  43.0 2.7 %collective-permute-done.10.refs_2_ = f32[272,128]{1,0:T(8,128)S(1)} collective-permute-done((f32[272,128]{1,0:T(8,128)S(1)}, f32[272,128]{1,0:T(8,128)S(1)}, u32[]{:S(2)}, u32[]{:S(2)}) %collective-permute-start.10) | collective-permute-done | bytes 139296 | tf_op jit(solution)/shard_map/ppermute | solution.py:311
  45.7 2.2 %collective-permute-done.13.refs_5_ = f32[264,128]{1,0:T(8,128)S(1)} collective-permute-done((f32[264,128]{1,0:T(8,128)S(1)}, f32[264,128]{1,0:T(8,128)S(1)}, u32[]{:S(2)}, u32[]{:S(2)}) %collective-permute-start.13) | collective-permute-done | bytes 135200 | tf_op jit(solution)/shard_map/ppermute | solution.py:304
  47.9 0.1 shard_map.50
  48.0 0.3 collective-permute-start.15
  48.3 1.8 %collective-permute-start.19 = (f32[264,128]{1,0:T(8,128)S(1)}, f32[264,128]{1,0:T(8,128)S(1)}, u32[]{:S(2)}, u32[]{:S(2)}) collective-permute-start(f32[264,128]{1,0:T(8,128)S(1)} %get-tuple-element.54), channel_id=1, source_target_pairs={{0,8},{8,0},{16,24},{24,16},{1,9},{9,1},{17,25},{25,17},{2,10},{10... | collective-permute-start | bytes 405512 | tf_op jit(solution)/shard_map/ppermute | solution.py:311
  50.1 1.7 %collective-permute-start.20 = (f32[264,128]{1,0:T(8,128)S(1)}, f32[264,128]{1,0:T(8,128)S(1)}, u32[]{:S(2)}, u32[]{:S(2)}) collective-permute-start(f32[264,128]{1,0:T(8,128)S(1)} %get-tuple-element.54), channel_id=1, source_target_pairs={{16,0},{8,16},{24,8},{0,24},{17,1},{9,17},{25,9},{1,25},{18,2},{10... | collective-permute-start | bytes 405512 | tf_op jit(solution)/shard_map/ppermute | solution.py:311
  51.9 1.3 %collective-permute-start.16 = (f32[256,128]{1,0:T(8,128)S(1)}, f32[256,128]{1,0:T(8,128)S(1)}, u32[]{:S(2)}, u32[]{:S(2)}) collective-permute-start(f32[256,128]{1,0:T(8,128)S(1)} %get-tuple-element.53.refs_2_), channel_id=1, source_target_pairs={{0,2},{1,3},{2,0},{3,1},{4,6},{5,7},{6,4},{7,5},{8,10},{9,11},{10,... | collective-permute-start | bytes 393224 | tf_op jit(solution)/shard_map/ppermute | solution.py:304
  53.2 0.7 collective-permute-start.17
  53.9 1.5 %collective-permute-start.18 = (f32[256,128]{1,0:T(8,128)S(1)}, f32[256,128]{1,0:T(8,128)S(1)}, u32[]{:S(2)}, u32[]{:S(2)}) collective-permute-start(f32[256,128]{1,0:T(8,128)S(1)} %get-tuple-element.53.refs_2_), channel_id=1, source_target_pairs={{0,6},{1,7},{2,4},{3,5},{4,2},{5,3},{6,0},{7,1},{8,14},{9,15},{10,... | collective-permute-start | bytes 393224 | tf_op jit(solution)/shard_map/ppermute | solution.py:304
  55.4 2.1 %collective-permute-done.16.refs_3_ = f32[256,128]{1,0:T(8,128)S(1)} collective-permute-done((f32[256,128]{1,0:T(8,128)S(1)}, f32[256,128]{1,0:T(8,128)S(1)}, u32[]{:S(2)}, u32[]{:S(2)}) %collective-permute-start.16) | collective-permute-done | bytes 131104 | tf_op jit(solution)/shard_map/ppermute | solution.py:304
  57.4 0.9 %collective-permute-done.17.refs_4_ = f32[256,128]{1,0:T(8,128)S(1)} collective-permute-done((f32[256,128]{1,0:T(8,128)S(1)}, f32[256,128]{1,0:T(8,128)S(1)}, u32[]{:S(2)}, u32[]{:S(2)}) %collective-permute-start.17) | collective-permute-done | bytes 131104 | tf_op jit(solution)/shard_map/ppermute | solution.py:304
  58.3 1.4 %collective-permute-done.18.refs_5_ = f32[256,128]{1,0:T(8,128)S(1)} collective-permute-done((f32[256,128]{1,0:T(8,128)S(1)}, f32[256,128]{1,0:T(8,128)S(1)}, u32[]{:S(2)}, u32[]{:S(2)}) %collective-permute-start.18) | collective-permute-done | bytes 131104 | tf_op jit(solution)/shard_map/ppermute | solution.py:304
  59.7 1.2 %shard_map.51 = (bf16[1024,256]{1,0:T(8,128)(2,1)S(1)}, bf16[256,256]{1,0:T(8,128)(2,1)S(1)}, bf16[256,256]{1,0:T(8,128)(2,1)S(1)}) custom-call(f32[8,128]{1,0:T(8,128)S(1)} %get-tuple-element.52.refs_0_, f32[8,128]{1,0:T(8,128)S(1)} %collective-permute-done.15.refs_1_, f32[256,128]{1,0:T(8,128)S(1)} %get-tuple-element.53.refs_2_, ...), custom_call_target="tpu_custom_call" | custom-call | bytes 1589248 | tf_op jit(solution)/shard_map/pallas_call | solution.py:30
  61.0 0.1 collective-permute-start.22
  61.0 0.8 shard_map.52
  61.8 0.6 collective-permute-start.21
  62.4 1.0 %shard_map.53 = (f32[256,128]{1,0:T(8,128)S(1)}, f32[272,128]{1,0:T(8,128)S(1)}, f32[272,128]{1,0:T(8,128)S(1)}) custom-call(bf16[1024,256]{1,0:T(8,128)(2,1)S(1)} %get-tuple-element.58.refs_0_.own, bf16[256,2048]{1,0:T(8,128)(2,1)S(1)} %get-tuple-element.38.refs_8_.refs_1_, bf16[256,2048]{1,0:T(8,128)(2,1)S(1)} %get-tuple-element.39.refs_9_.refs_2_, ...), custom_call_target="tpu_custom_call" | custom-call | flops 603979776 | bytes 7225344 | tf_op jit(solution)/shard_map/pallas_call | solution.py:30
  63.4 1.0 %shard_map.54 = (f32[256,128]{1,0:T(8,128)S(1)}, f32[272,128]{1,0:T(8,128)S(1)}, f32[272,128]{1,0:T(8,128)S(1)}) custom-call(bf16[1024,256]{1,0:T(8,128)(2,1)S(1)} %collective-permute-done.22.refs_0_, bf16[256,2048]{1,0:T(8,128)(2,1)S(1)} %get-tuple-element.38.refs_8_.refs_1_, bf16[256,2048]{1,0:T(8,128)(2,1)S(1)} %get-tuple-element.39.refs_9_.refs_2_, ...), custom_call_target="tpu_custom_call" | custom-call | flops 603979776 | bytes 7634944 | tf_op jit(solution)/shard_map/pallas_call | solution.py:30
  64.3 0.1 shard_map.55
  64.4 0.9 %collective-permute-start.23 = (f32[8,128]{1,0:T(8,128)S(1)}, f32[8,128]{1,0:T(8,128)S(1)}, u32[]{:S(2)}, u32[]{:S(2)}) collective-permute-start(f32[8,128]{1,0:T(8,128)S(1)} %shard_map.55), channel_id=1, source_target_pairs={{16,0},{8,16},{24,8},{0,24},{17,1},{9,17},{25,9},{1,25},{18,2},{10... | collective-permute-start | bytes 12296 | tf_op jit(solution)/shard_map/ppermute | solution.py:311
  65.3 1.0 %collective-permute-start.24 = (f32[8,128]{1,0:T(8,128)S(1)}, f32[8,128]{1,0:T(8,128)S(1)}, u32[]{:S(2)}, u32[]{:S(2)}) collective-permute-start(f32[8,128]{1,0:T(8,128)S(1)} %shard_map.55), channel_id=1, source_target_pairs={{8,0},{24,16},{0,8},{16,24},{9,1},{25,17},{1,9},{17,25},{10,2},{26... | collective-permute-start | bytes 12296 | tf_op jit(solution)/shard_map/ppermute | solution.py:311
  66.3 2.3 %collective-permute-start.25 = (f32[8,128]{1,0:T(8,128)S(1)}, f32[8,128]{1,0:T(8,128)S(1)}, u32[]{:S(2)}, u32[]{:S(2)}) collective-permute-start(f32[8,128]{1,0:T(8,128)S(1)} %shard_map.55), channel_id=1, source_target_pairs={{24,0},{0,16},{16,8},{8,24},{25,1},{1,17},{17,9},{9,25},{26,2},{2,... | collective-permute-start | bytes 12296 | tf_op jit(solution)/shard_map/ppermute | solution.py:311
  68.5 0.5 collective-permute-done.23
  69.0 2.7 %collective-permute-done.25 = f32[8,128]{1,0:T(8,128)S(1)} collective-permute-done((f32[8,128]{1,0:T(8,128)S(1)}, f32[8,128]{1,0:T(8,128)S(1)}, u32[]{:S(2)}, u32[]{:S(2)}) %collective-permute-start.25) | collective-permute-done | bytes 4128 | tf_op jit(solution)/shard_map/ppermute | solution.py:311
  71.7 0.1 collective-permute-start.27
  71.8 2.2 %collective-permute-start.28 = (f32[272,128]{1,0:T(8,128)S(1)}, f32[272,128]{1,0:T(8,128)S(1)}, u32[]{:S(2)}, u32[]{:S(2)}) collective-permute-start(f32[272,128]{1,0:T(8,128)S(1)} %get-tuple-element.64.refs_2_), channel_id=1, source_target_pairs={{24,0},{0,16},{16,8},{8,24},{25,1},{1,17},{17,9},{9,25},{26,2},{2,... | collective-permute-start | bytes 417800 | tf_op jit(solution)/shard_map/ppermute | solution.py:311
  74.0 0.1 shard_map.56
  74.1 1.2 %collective-permute-start.29 = (f32[264,128]{1,0:T(8,128)S(1)}, f32[264,128]{1,0:T(8,128)S(1)}, u32[]{:S(2)}, u32[]{:S(2)}) collective-permute-start(f32[264,128]{1,0:T(8,128)S(1)} %get-tuple-element.67), channel_id=1, source_target_pairs={{0,2},{1,3},{2,0},{3,1},{4,6},{5,7},{6,4},{7,5},{8,10},{9,11},{10,... | collective-permute-start | bytes 405512 | tf_op jit(solution)/shard_map/ppermute | solution.py:304
  75.3 0.9 %collective-permute-start.30 = (f32[264,128]{1,0:T(8,128)S(1)}, f32[264,128]{1,0:T(8,128)S(1)}, u32[]{:S(2)}, u32[]{:S(2)}) collective-permute-start(f32[264,128]{1,0:T(8,128)S(1)} %get-tuple-element.68), channel_id=1, source_target_pairs={{0,4},{1,5},{2,6},{3,7},{4,0},{5,1},{6,2},{7,3},{8,12},{9,13},{10,... | collective-permute-start | bytes 405512 | tf_op jit(solution)/shard_map/ppermute | solution.py:304
  76.2 1.4 %collective-permute-start.31 = (f32[264,128]{1,0:T(8,128)S(1)}, f32[264,128]{1,0:T(8,128)S(1)}, u32[]{:S(2)}, u32[]{:S(2)}) collective-permute-start(f32[264,128]{1,0:T(8,128)S(1)} %get-tuple-element.69), channel_id=1, source_target_pairs={{0,6},{1,7},{2,4},{3,5},{4,2},{5,3},{6,0},{7,1},{8,14},{9,15},{10,... | collective-permute-start | bytes 405512 | tf_op jit(solution)/shard_map/ppermute | solution.py:304
  77.6 0.1 collective-permute-done.27.refs_2_
  77.8 3.9 %collective-permute-done.28.refs_3_ = f32[272,128]{1,0:T(8,128)S(1)} collective-permute-done((f32[272,128]{1,0:T(8,128)S(1)}, f32[272,128]{1,0:T(8,128)S(1)}, u32[]{:S(2)}, u32[]{:S(2)}) %collective-permute-start.28) | collective-permute-done | bytes 139296 | tf_op jit(solution)/shard_map/ppermute | solution.py:311
  81.7 0.1 collective-permute-done.30.refs_5_
  81.7 1.5 %collective-permute-done.31.refs_6_ = f32[264,128]{1,0:T(8,128)S(1)} collective-permute-done((f32[264,128]{1,0:T(8,128)S(1)}, f32[264,128]{1,0:T(8,128)S(1)}, u32[]{:S(2)}, u32[]{:S(2)}) %collective-permute-start.31) | collective-permute-done | bytes 135200 | tf_op jit(solution)/shard_map/ppermute | solution.py:304
  83.2 1.0 %shard_map.57 = (f32[256,128]{1,0:T(8,128)}, f32[256,128]{1,0:T(8,128)}) custom-call(f32[264,128]{1,0:T(8,128)S(1)} %get-tuple-element.66.refs_0_, f32[256,128]{1,0:T(8,128)S(1)} %get-tuple-element.62.refs_0_.refs_1_, f32[272,128]{1,0:T(8,128)S(1)} %collective-permute-done.27.refs_2_, f32[272,128]{1,0:T(8,128)S(1)} %collective-permute-done.28.refs_3_, ...), custom_call_target="tpu_custom_call" | custom-call | bytes 1212416 | tf_op jit(solution)/shard_map/pallas_call | solution.py:30
  (24 shorter events, 0.1 us)
Async XLA Ops:
  0.6 1.6 %copy-start = (bf16[2048,512]{1,0:T(8,128)(2,1)S(1)}, bf16[2048,512]{1,0:T(8,128)(2,1)}, u32[]{:S(2)}) copy-start(bf16[2048,512]{1,0:T(8,128)(2,1)} %plane_ref.5) | copy-start | bytes 6291460
  2.2 0.9 %copy-start.2 = (f32[256,128]{1,0:T(8,128)S(1)}, f32[256,128]{1,0:T(8,128)}, u32[]{:S(2)}) copy-start(f32[256,128]{1,0:T(8,128)} %logits.1) | copy-start | bytes 393220
  3.3 20.5 %collective-permute-start.8 = (bf16[256,768]{1,0:T(8,128)(2,1)S(1)}, bf16[256,768]{1,0:T(8,128)(2,1)S(1)}, u32[]{:S(2)}, u32[]{:S(2)}) collective-permute-start(bf16[256,768]{1,0:T(8,128)(2,1)S(1)} %get-tuple-element.36.rows_ref), channel_id=1, source_target_pairs={{0,8},{8,0},{16,24},{24,16},{1,9},{9,1},{17,25},{25,17},{2,10},{10... | collective-permute-start | bytes 1179656 | tf_op jit(solution)/shard_map/ppermute | solution.py:311
  6.4 25.1 %collective-permute-start = (bf16[256,768]{1,0:T(8,128)(2,1)S(1)}, bf16[256,768]{1,0:T(8,128)(2,1)S(1)}, u32[]{:S(2)}, u32[]{:S(2)}) collective-permute-start(bf16[256,768]{1,0:T(8,128)(2,1)S(1)} %get-tuple-element.36.rows_ref), channel_id=1, source_target_pairs={{16,0},{8,16},{24,8},{0,24},{17,1},{9,17},{25,9},{1,25},{18,2},{10... | collective-permute-start | bytes 1179656 | tf_op jit(solution)/shard_map/ppermute | solution.py:311
  8.9 5.7 %collective-permute-start.1 = (bf16[256,256]{1,0:T(8,128)(2,1)S(1)}, bf16[256,256]{1,0:T(8,128)(2,1)S(1)}, u32[]{:S(2)}, u32[]{:S(2)}) collective-permute-start(bf16[256,256]{1,0:T(8,128)(2,1)S(1)} %get-tuple-element.37.refs_0_.own), channel_id=1, source_target_pairs={{0,2},{1,3},{2,0},{3,1},{4,6},{5,7},{6,4},{7,5},{8,10},{9,11},{10,... | collective-permute-start | bytes 393224 | tf_op jit(solution)/shard_map/ppermute | solution.py:304
  10.4 7.8 %collective-permute-start.2 = (bf16[256,256]{1,0:T(8,128)(2,1)S(1)}, bf16[256,256]{1,0:T(8,128)(2,1)S(1)}, u32[]{:S(2)}, u32[]{:S(2)}) collective-permute-start(bf16[256,256]{1,0:T(8,128)(2,1)S(1)} %get-tuple-element.37.refs_0_.own), channel_id=1, source_target_pairs={{0,4},{1,5},{2,6},{3,7},{4,0},{5,1},{6,2},{7,3},{8,12},{9,13},{10,... | collective-permute-start | bytes 393224 | tf_op jit(solution)/shard_map/ppermute | solution.py:304
  11.9 6.3 %collective-permute-start.3 = (bf16[256,256]{1,0:T(8,128)(2,1)S(1)}, bf16[256,256]{1,0:T(8,128)(2,1)S(1)}, u32[]{:S(2)}, u32[]{:S(2)}) collective-permute-start(bf16[256,256]{1,0:T(8,128)(2,1)S(1)} %get-tuple-element.37.refs_0_.own), channel_id=1, source_target_pairs={{0,6},{1,7},{2,4},{3,5},{4,2},{5,3},{6,0},{7,1},{8,14},{9,15},{10,... | collective-permute-start | bytes 393224 | tf_op jit(solution)/shard_map/ppermute | solution.py:304
  14.6 12.2 %collective-permute-start.4 = (bf16[256,256]{1,0:T(8,128)(2,1)S(1)}, bf16[256,256]{1,0:T(8,128)(2,1)S(1)}, u32[]{:S(2)}, u32[]{:S(2)}) collective-permute-start(bf16[256,256]{1,0:T(8,128)(2,1)S(1)} %get-tuple-element.37.refs_0_.own), channel_id=1, source_target_pairs={{0,1},{1,0},{2,3},{3,2},{4,5},{5,4},{6,7},{7,6},{8,9},{9,8},{10,11... | collective-permute-start | bytes 393224 | tf_op jit(solution)/shard_map/ppermute | solution.py:304
  18.1 8.6 %collective-permute-start.5 = (bf16[256,256]{1,0:T(8,128)(2,1)S(1)}, bf16[256,256]{1,0:T(8,128)(2,1)S(1)}, u32[]{:S(2)}, u32[]{:S(2)}) collective-permute-start(bf16[256,256]{1,0:T(8,128)(2,1)S(1)} %get-tuple-element.37.refs_0_.own), channel_id=1, source_target_pairs={{0,3},{1,2},{2,1},{3,0},{4,7},{5,6},{6,5},{7,4},{8,11},{9,10},{10,... | collective-permute-start | bytes 393224 | tf_op jit(solution)/shard_map/ppermute | solution.py:304
  18.1 8.6 %collective-permute-start.6 = (bf16[256,256]{1,0:T(8,128)(2,1)S(1)}, bf16[256,256]{1,0:T(8,128)(2,1)S(1)}, u32[]{:S(2)}, u32[]{:S(2)}) collective-permute-start(bf16[256,256]{1,0:T(8,128)(2,1)S(1)} %get-tuple-element.37.refs_0_.own), channel_id=1, source_target_pairs={{0,5},{1,4},{2,7},{3,6},{4,1},{5,0},{6,3},{7,2},{8,13},{9,12},{10,... | collective-permute-start | bytes 393224 | tf_op jit(solution)/shard_map/ppermute | solution.py:304
  23.8 6.4 %collective-permute-start.7 = (bf16[256,256]{1,0:T(8,128)(2,1)S(1)}, bf16[256,256]{1,0:T(8,128)(2,1)S(1)}, u32[]{:S(2)}, u32[]{:S(2)}) collective-permute-start(bf16[256,256]{1,0:T(8,128)(2,1)S(1)} %get-tuple-element.37.refs_0_.own), channel_id=1, source_target_pairs={{0,7},{1,6},{2,5},{3,4},{4,3},{5,2},{6,1},{7,0},{8,15},{9,14},{10,... | collective-permute-start | bytes 393224 | tf_op jit(solution)/shard_map/ppermute | solution.py:304
  30.2 1.6 %copy-start.1 = (bf16[2048,512]{1,0:T(8,128)(2,1)S(1)}, bf16[2048,512]{1,0:T(8,128)(2,1)}, u32[]{:S(2)}) copy-start(bf16[2048,512]{1,0:T(8,128)(2,1)} %plane_ref.5) | copy-start | bytes 6291460
  34.3 4.8 %collective-permute-start.9 = (f32[1032,128]{1,0:T(8,128)S(1)}, f32[1032,128]{1,0:T(8,128)S(1)}, u32[]{:S(2)}, u32[]{:S(2)}) collective-permute-start(f32[1032,128]{1,0:T(8,128)S(1)} %get-tuple-element.47), channel_id=1, source_target_pairs={{0,1},{1,0},{2,3},{3,2},{4,5},{5,4},{6,7},{7,6},{8,9},{9,8},{10,11... | collective-permute-start | bytes 1585160 | tf_op jit(solution)/shard_map/ppermute | solution.py:304
  34.5 8.6 %collective-permute-start.11 = (f32[272,128]{1,0:T(8,128)S(1)}, f32[272,128]{1,0:T(8,128)S(1)}, u32[]{:S(2)}, u32[]{:S(2)}) collective-permute-start(f32[272,128]{1,0:T(8,128)S(1)} %shard_map.46.refs_2_), channel_id=1, source_target_pairs={{24,0},{0,16},{16,8},{8,24},{25,1},{1,17},{17,9},{9,25},{26,2},{2,... | collective-permute-start | bytes 417800 | tf_op jit(solution)/shard_map/ppermute | solution.py:311
  34.5 11.3 %collective-permute-start.10 = (f32[272,128]{1,0:T(8,128)S(1)}, f32[272,128]{1,0:T(8,128)S(1)}, u32[]{:S(2)}, u32[]{:S(2)}) collective-permute-start(f32[272,128]{1,0:T(8,128)S(1)} %get-tuple-element.43.refs_1_), channel_id=1, source_target_pairs={{0,8},{8,0},{16,24},{24,16},{1,9},{9,1},{17,25},{25,17},{2,10},{10... | collective-permute-start | bytes 417800 | tf_op jit(solution)/shard_map/ppermute | solution.py:311
  39.2 6.6 %collective-permute-start.12 = (f32[264,128]{1,0:T(8,128)S(1)}, f32[264,128]{1,0:T(8,128)S(1)}, u32[]{:S(2)}, u32[]{:S(2)}) collective-permute-start(f32[264,128]{1,0:T(8,128)S(1)} %get-tuple-element.49), channel_id=1, source_target_pairs={{0,2},{1,3},{2,0},{3,1},{4,6},{5,7},{6,4},{7,5},{8,10},{9,11},{10,... | collective-permute-start | bytes 405512 | tf_op jit(solution)/shard_map/ppermute | solution.py:304
  39.9 8.0 %collective-permute-start.13 = (f32[264,128]{1,0:T(8,128)S(1)}, f32[264,128]{1,0:T(8,128)S(1)}, u32[]{:S(2)}, u32[]{:S(2)}) collective-permute-start(f32[264,128]{1,0:T(8,128)S(1)} %get-tuple-element.50), channel_id=1, source_target_pairs={{0,4},{1,5},{2,6},{3,7},{4,0},{5,1},{6,2},{7,3},{8,12},{9,13},{10,... | collective-permute-start | bytes 405512 | tf_op jit(solution)/shard_map/ppermute | solution.py:304
  40.9 7.0 %collective-permute-start.14 = (f32[264,128]{1,0:T(8,128)S(1)}, f32[264,128]{1,0:T(8,128)S(1)}, u32[]{:S(2)}, u32[]{:S(2)}) collective-permute-start(f32[264,128]{1,0:T(8,128)S(1)} %get-tuple-element.51), channel_id=1, source_target_pairs={{0,6},{1,7},{2,4},{3,5},{4,2},{5,3},{6,0},{7,1},{8,14},{9,15},{10,... | collective-permute-start | bytes 405512 | tf_op jit(solution)/shard_map/ppermute | solution.py:304
  48.0 5.9 %collective-permute-start.15 = (f32[8,128]{1,0:T(8,128)S(1)}, f32[8,128]{1,0:T(8,128)S(1)}, u32[]{:S(2)}, u32[]{:S(2)}) collective-permute-start(f32[8,128]{1,0:T(8,128)S(1)} %get-tuple-element.52.refs_0_), channel_id=1, source_target_pairs={{24,0},{0,16},{16,8},{8,24},{25,1},{1,17},{17,9},{9,25},{26,2},{2,... | collective-permute-start | bytes 12296 | tf_op jit(solution)/shard_map/ppermute | solution.py:311
  48.3 11.4 %collective-permute-start.19 = (f32[264,128]{1,0:T(8,128)S(1)}, f32[264,128]{1,0:T(8,128)S(1)}, u32[]{:S(2)}, u32[]{:S(2)}) collective-permute-start(f32[264,128]{1,0:T(8,128)S(1)} %get-tuple-element.54), channel_id=1, source_target_pairs={{0,8},{8,0},{16,24},{24,16},{1,9},{9,1},{17,25},{25,17},{2,10},{10... | collective-permute-start | bytes 405512 | tf_op jit(solution)/shard_map/ppermute | solution.py:311
  50.1 9.6 %collective-permute-start.20 = (f32[264,128]{1,0:T(8,128)S(1)}, f32[264,128]{1,0:T(8,128)S(1)}, u32[]{:S(2)}, u32[]{:S(2)}) collective-permute-start(f32[264,128]{1,0:T(8,128)S(1)} %get-tuple-element.54), channel_id=1, source_target_pairs={{16,0},{8,16},{24,8},{0,24},{17,1},{9,17},{25,9},{1,25},{18,2},{10... | collective-permute-start | bytes 405512 | tf_op jit(solution)/shard_map/ppermute | solution.py:311
  51.9 5.6 %collective-permute-start.16 = (f32[256,128]{1,0:T(8,128)S(1)}, f32[256,128]{1,0:T(8,128)S(1)}, u32[]{:S(2)}, u32[]{:S(2)}) collective-permute-start(f32[256,128]{1,0:T(8,128)S(1)} %get-tuple-element.53.refs_2_), channel_id=1, source_target_pairs={{0,2},{1,3},{2,0},{3,1},{4,6},{5,7},{6,4},{7,5},{8,10},{9,11},{10,... | collective-permute-start | bytes 393224 | tf_op jit(solution)/shard_map/ppermute | solution.py:304
  53.2 5.2 %collective-permute-start.17 = (f32[256,128]{1,0:T(8,128)S(1)}, f32[256,128]{1,0:T(8,128)S(1)}, u32[]{:S(2)}, u32[]{:S(2)}) collective-permute-start(f32[256,128]{1,0:T(8,128)S(1)} %get-tuple-element.53.refs_2_), channel_id=1, source_target_pairs={{0,4},{1,5},{2,6},{3,7},{4,0},{5,1},{6,2},{7,3},{8,12},{9,13},{10,... | collective-permute-start | bytes 393224 | tf_op jit(solution)/shard_map/ppermute | solution.py:304
  53.9 5.9 %collective-permute-start.18 = (f32[256,128]{1,0:T(8,128)S(1)}, f32[256,128]{1,0:T(8,128)S(1)}, u32[]{:S(2)}, u32[]{:S(2)}) collective-permute-start(f32[256,128]{1,0:T(8,128)S(1)} %get-tuple-element.53.refs_2_), channel_id=1, source_target_pairs={{0,6},{1,7},{2,4},{3,5},{4,2},{5,3},{6,0},{7,1},{8,14},{9,15},{10,... | collective-permute-start | bytes 393224 | tf_op jit(solution)/shard_map/ppermute | solution.py:304
  61.0 2.4 %collective-permute-start.22 = (bf16[1024,256]{1,0:T(8,128)(2,1)S(1)}, bf16[1024,256]{1,0:T(8,128)(2,1)S(1)}, u32[]{:S(2)}, u32[]{:S(2)}) collective-permute-start(bf16[1024,256]{1,0:T(8,128)(2,1)S(1)} %get-tuple-element.58.refs_0_.own), channel_id=1, source_target_pairs={{0,1},{1,0},{2,3},{3,2},{4,5},{5,4},{6,7},{7,6},{8,9},{9,8},{10,11... | collective-permute-start | bytes 1572872 | tf_op jit(solution)/shard_map/ppermute | solution.py:304
  61.8 12.2 %collective-permute-start.21 = (f32[1024,128]{1,0:T(8,128)S(1)}, f32[1024,128]{1,0:T(8,128)S(1)}, u32[]{:S(2)}, u32[]{:S(2)}) collective-permute-start(f32[1024,128]{1,0:T(8,128)S(1)} %get-tuple-element.57), channel_id=1, source_target_pairs={{0,1},{1,0},{2,3},{3,2},{4,5},{5,4},{6,7},{7,6},{8,9},{9,8},{10,11... | collective-permute-start | bytes 1572872 | tf_op jit(solution)/shard_map/ppermute | solution.py:304
  64.4 4.6 %collective-permute-start.23 = (f32[8,128]{1,0:T(8,128)S(1)}, f32[8,128]{1,0:T(8,128)S(1)}, u32[]{:S(2)}, u32[]{:S(2)}) collective-permute-start(f32[8,128]{1,0:T(8,128)S(1)} %shard_map.55), channel_id=1, source_target_pairs={{16,0},{8,16},{24,8},{0,24},{17,1},{9,17},{25,9},{1,25},{18,2},{10... | collective-permute-start | bytes 12296 | tf_op jit(solution)/shard_map/ppermute | solution.py:311
  65.3 3.7 %collective-permute-start.24 = (f32[8,128]{1,0:T(8,128)S(1)}, f32[8,128]{1,0:T(8,128)S(1)}, u32[]{:S(2)}, u32[]{:S(2)}) collective-permute-start(f32[8,128]{1,0:T(8,128)S(1)} %shard_map.55), channel_id=1, source_target_pairs={{8,0},{24,16},{0,8},{16,24},{9,1},{25,17},{1,9},{17,25},{10,2},{26... | collective-permute-start | bytes 12296 | tf_op jit(solution)/shard_map/ppermute | solution.py:311
  66.3 5.4 %collective-permute-start.25 = (f32[8,128]{1,0:T(8,128)S(1)}, f32[8,128]{1,0:T(8,128)S(1)}, u32[]{:S(2)}, u32[]{:S(2)}) collective-permute-start(f32[8,128]{1,0:T(8,128)S(1)} %shard_map.55), channel_id=1, source_target_pairs={{24,0},{0,16},{16,8},{8,24},{25,1},{1,17},{17,9},{9,25},{26,2},{2,... | collective-permute-start | bytes 12296 | tf_op jit(solution)/shard_map/ppermute | solution.py:311
  71.7 2.3 %collective-permute-start.26 = (f32[8,128]{1,0:T(8,128)S(1)}, f32[8,128]{1,0:T(8,128)S(1)}, u32[]{:S(2)}, u32[]{:S(2)}) collective-permute-start(f32[8,128]{1,0:T(8,128)S(1)} %add_add_fusion.refs_0_), channel_id=1, source_target_pairs={{0,1},{1,0},{2,3},{3,2},{4,5},{5,4},{6,7},{7,6},{8,9},{9,8},{10,11... | collective-permute-start | bytes 12296 | tf_op jit(solution)/shard_map/ppermute | solution.py:304
  71.7 6.1 %collective-permute-start.27 = (f32[272,128]{1,0:T(8,128)S(1)}, f32[272,128]{1,0:T(8,128)S(1)}, u32[]{:S(2)}, u32[]{:S(2)}) collective-permute-start(f32[272,128]{1,0:T(8,128)S(1)} %get-tuple-element.63.refs_1_), channel_id=1, source_target_pairs={{0,8},{8,0},{16,24},{24,16},{1,9},{9,1},{17,25},{25,17},{2,10},{10... | collective-permute-start | bytes 417800 | tf_op jit(solution)/shard_map/ppermute | solution.py:311
  71.8 9.9 %collective-permute-start.28 = (f32[272,128]{1,0:T(8,128)S(1)}, f32[272,128]{1,0:T(8,128)S(1)}, u32[]{:S(2)}, u32[]{:S(2)}) collective-permute-start(f32[272,128]{1,0:T(8,128)S(1)} %get-tuple-element.64.refs_2_), channel_id=1, source_target_pairs={{24,0},{0,16},{16,8},{8,24},{25,1},{1,17},{17,9},{9,25},{26,2},{2,... | collective-permute-start | bytes 417800 | tf_op jit(solution)/shard_map/ppermute | solution.py:311
  74.1 7.6 %collective-permute-start.29 = (f32[264,128]{1,0:T(8,128)S(1)}, f32[264,128]{1,0:T(8,128)S(1)}, u32[]{:S(2)}, u32[]{:S(2)}) collective-permute-start(f32[264,128]{1,0:T(8,128)S(1)} %get-tuple-element.67), channel_id=1, source_target_pairs={{0,2},{1,3},{2,0},{3,1},{4,6},{5,7},{6,4},{7,5},{8,10},{9,11},{10,... | collective-permute-start | bytes 405512 | tf_op jit(solution)/shard_map/ppermute | solution.py:304
  75.3 6.5 %collective-permute-start.30 = (f32[264,128]{1,0:T(8,128)S(1)}, f32[264,128]{1,0:T(8,128)S(1)}, u32[]{:S(2)}, u32[]{:S(2)}) collective-permute-start(f32[264,128]{1,0:T(8,128)S(1)} %get-tuple-element.68), channel_id=1, source_target_pairs={{0,4},{1,5},{2,6},{3,7},{4,0},{5,1},{6,2},{7,3},{8,12},{9,13},{10,... | collective-permute-start | bytes 405512 | tf_op jit(solution)/shard_map/ppermute | solution.py:304
  76.2 7.0 %collective-permute-start.31 = (f32[264,128]{1,0:T(8,128)S(1)}, f32[264,128]{1,0:T(8,128)S(1)}, u32[]{:S(2)}, u32[]{:S(2)}) collective-permute-start(f32[264,128]{1,0:T(8,128)S(1)} %get-tuple-element.69), channel_id=1, source_target_pairs={{0,6},{1,7},{2,4},{3,5},{4,2},{5,3},{6,0},{7,1},{8,14},{9,15},{10,... | collective-permute-start | bytes 405512 | tf_op jit(solution)/shard_map/ppermute | solution.py:304

commit v4 on v3

--- a/solution.py
+++ b/solution.py
@@ -11,6 +11,7 @@
 STAT_ROWS = 8
 BACK_ROWS = 16
 VMEM_BYTES = 24 * 1024 * 1024
+PREPARE_BYTES = 62 * 1024 * 1024
 VMEM = pl.BlockSpec(memory_space=pltpu.VMEM)
 SMEM = pl.BlockSpec(memory_space=pltpu.SMEM)
 ANY = pl.BlockSpec(memory_space=pl.ANY)
@@ -23,7 +24,7 @@
     return jax.ShapeDtypeStruct((rows, columns), dtype)
 
 
-def call(body, args, outs, specs=None, scratch=(), flops=0, hidden=False):
+def call(body, args, outs, specs=None, scratch=(), flops=0, hidden=False, vmem=None):
     bytes_accessed = sum(x.size * x.dtype.itemsize for x in list(args) + list(outs))
     if hidden:
         flops = bytes_accessed = 0
@@ -33,7 +34,7 @@
         out_specs=[VMEM] * len(outs),
         out_shape=list(outs),
         scratch_shapes=list(scratch),
-        compiler_params=pltpu.CompilerParams(vmem_limit_bytes=VMEM_BYTES),
+        compiler_params=pltpu.CompilerParams(vmem_limit_bytes=vmem or VMEM_BYTES),
         cost_estimate=pl.CostEstimate(
             flops=flops, bytes_accessed=bytes_accessed, transcendentals=0
         ),
@@ -70,27 +71,35 @@
     out[rows, clusters:] = low
 
 
-def prepare_body(column_ref, features, logits, message, pair, sem):
+def prepare_body(column_ref, features, logits, near, cross, pair, sems):
     n, clusters = logits.shape
     width = features.shape[1]
     start = pl.multiple_of(column_ref[0] * n, n)
-    copy = pltpu.make_async_copy(
-        features.at[pl.ds(start, n), :], message.at[:, pl.ds(0, width)], sem
-    )
-    copy.start()
+    copies = [
+        pltpu.make_async_copy(
+            features.at[pl.ds(start, n), :],
+            out.at[pl.ds(0, n), pl.ds(0, width)],
+            sems.at[i],
+        )
+        for i, out in enumerate((near, cross))
+    ]
+    for copy in copies:
+        copy.start()
+    rows = slice(0, n)
     high, low = split(normalize(jnp.exp(logits[...])))
-    pair[:, :clusters] = high
-    pair[:, clusters:] = low
-    message[:, width : width + clusters] = high
-    message[:, width + clusters :] = low
-    copy.wait()
+    for out, at in ((pair, 0), (near, width), (cross, width)):
+        out[rows, at : at + clusters] = high
+        out[rows, at + clusters : at + 2 * clusters] = low
+    cross[n:, :] = jnp.zeros((cross.shape[0] - n, cross.shape[1]), BF16)
+    for copy in copies:
+        copy.wait()
 
 
 def kernel_body(order, column_ref, rows_ref, plane_ref, *refs):
     high_ref, low_ref = refs[-2:]
-    n, width = rows_ref.shape[0], plane_ref.shape[1]
+    n, width = high_ref.shape[0], plane_ref.shape[1]
     column = column_ref[0]
-    rows = rows_ref[:, :width]
+    rows = rows_ref[:n, :width]
     for j, k in enumerate(order):
         start = pl.multiple_of(lax.bitwise_xor(column, k) * n, n)
         inner = lax.dot_general(
@@ -105,8 +114,8 @@
         low_ref[:, j * n : (j + 1) * n] = low
 
 
-def kernel_call(order, column, rows, plane, after=()):
-    n, total = rows.shape[0], plane.shape[0]
+def kernel_call(n, order, column, rows, plane, after=()):
+    total = plane.shape[0]
     return call(
         functools.partial(kernel_body, tuple(order)),
         [column, rows, plane, *after],
@@ -116,10 +125,10 @@
     )
 
 
-def scores_body(at, pieces, kernels, partials, *refs):
+def scores_body(at, pieces, kernels, partials, unused, *refs):
     members, refs = refs[:pieces], refs[pieces:]
     blocks, refs = refs[:kernels], refs[kernels:]
-    before, outs = refs[:partials], refs[partials:]
+    before, outs = refs[:partials], refs[partials + unused :]
     n = blocks[0].shape[0]
     clusters = members[0].shape[1] // 2
     for i, out in enumerate(outs):
@@ -143,13 +152,16 @@
             out[n:, :] = jnp.zeros((out.shape[0] - n, clusters), F32)
 
 
-def scores_call(at, members, kernels, partials, extra, hidden=False):
+def scores_call(at, members, kernels, partials, extra, hidden=False, after=()):
     n, clusters = kernels[0].shape[0], members[0].shape[1] // 2
     depth = sum(x.shape[0] for x in members)
     return call(
-        functools.partial(scores_body, at, len(members), len(kernels), len(partials)),
-        members + kernels + partials,
+        functools.partial(
+            scores_body, at, len(members), len(kernels), len(partials), len(after)
+        ),
+        [*members, *kernels, *partials, *after],
         [shaped(n + e, clusters) for e in extra],
+        [VMEM] * (len(members) + len(kernels) + len(partials)) + [ANY] * len(after),
         flops=3 * n * len(kernels) * depth * clusters,
         hidden=hidden,
     )
@@ -195,7 +207,7 @@
     total = jnp.sum(member * scores[0][...], axis=0, keepdims=True)
     for i in range(count):
         pair = pairs[i]
-        other = whole(pair[:, pair.shape[1] - 2 * clusters :])
+        other = whole(pair[:n, pair.shape[1] - 2 * clusters :])
         part = jnp.sum(other * scores[i + 1][:n, :], axis=0, keepdims=True)
         total += part if i < has_near else 2.0 * part
     size = jnp.sum(member, axis=0, keepdims=True)
@@ -212,7 +224,7 @@
     )[0]
 
 
-def other_body(count, *refs):
+def other_body(n, count, *refs):
     pairs, refs = refs[:count], refs[count:]
     kernels, refs = refs[: 2 * count], refs[2 * count :]
     stat, (even, odd) = refs[:-2], refs[-2:]
@@ -222,7 +234,7 @@
         columns = slice((1 - part) * half, (2 - part) * half)
         acc = jnp.zeros((half, clusters), F32)
         for i, pair in enumerate(pairs):
-            both = pair[:, pair.shape[1] - 2 * clusters :]
+            both = pair[:n, pair.shape[1] - 2 * clusters :]
             a = lax.dot_general(
                 kernels[2 * i][:, columns], both, over, preferred_element_type=F32
             )
@@ -238,10 +250,9 @@
         odd[half:, :] = stat[0][...]
 
 
-def other_call(half, clusters, pairs, kernels, stat):
-    n = pairs[0].shape[0] if pairs else 0
-    return call(
-        functools.partial(other_body, len(pairs)),
+def other_call(n, half, clusters, pairs, kernels, stat):
+    return call(
+        functools.partial(other_body, n, len(pairs)),
         pairs + kernels + stat,
         [shaped(half, clusters), shaped(half + STAT_ROWS * len(stat), clusters)],
         flops=12 * n * len(pairs) * half * clusters,
@@ -251,15 +262,37 @@
 def fold_body(n, count, even, received, *refs):
     stats, outs = refs[:count], refs[count:]
     half = even.shape[0]
-    stat = stats[0][...]
-    for ref in stats[1:]:
-        stat += ref[...]
-    if received.shape[0] > half:
-        stat += received[half:, :]
     for j, out in enumerate(outs):
         rows = slice(j * n, (j + 1) * n)
         out[:n, :] = even[rows, :] + received[rows, :]
+        if count:
+            out[n:, :] = stats[0][...] + received[half:, :]
+
+
+def fold_call(n, even, received, stats, extra):
+    half, clusters = even.shape
+    return call(
+        functools.partial(fold_body, n, len(stats)),
+        [even, received] + stats,
+        [shaped(n + extra, clusters)] * (half // n),
+    )
+
+
+def widen_body(n, *refs):
+    count = (len(refs) - 2) // 2
+    stat = refs[count][...] + refs[count + 1][...]
+    for ref, out in zip(refs[:count], refs[count + 2 :]):
+        out[:n, :] = ref[...]
         out[n:, :] = stat
+
+
+def widen_call(n, parts, stats):
+    clusters = parts[0].shape[1]
+    return call(
+        functools.partial(widen_body, n),
+        parts + stats,
+        [shaped(n + STAT_ROWS, clusters)] * len(parts),
+    )
 
 
 def sum_body(n, last, *refs):
@@ -311,25 +344,31 @@
         return lax.ppermute(x, "row", pairs)
 
     column = jnp.reshape(lax.axis_index("col"), (1,)).astype(jnp.int32)
-    message, pair = call(
+    message, wide, pair = call(
         prepare_body,
         [column, features, logits],
-        [shaped(n, width + 2 * clusters, BF16), shaped(n, 2 * clusters, BF16)],
-        [SMEM, HBM, VMEM],
-        [pltpu.SemaphoreType.DMA],
-    )
-    others = [shift(message, d) for d in steps]
-    members = [pair] + [by_col(pair, k) for k in order[1:]]
+        [
+            shaped(n, width + 2 * clusters, BF16),
+            shaped(n + BACK_ROWS, width + 2 * clusters, BF16),
+            shaped(n, 2 * clusters, BF16),
+        ],
+        [SMEM, ANY, VMEM],
+        [pltpu.SemaphoreType.DMA((2,))],
+        vmem=PREPARE_BYTES,
+    )
+    others = [shift(message if d == 0 else wide, d) for d in steps]
+    evens = [pair] + [by_col(pair, k) for k in masks]
+    members = evens + [by_col(x, 1) for x in evens]
     early = 1 + has_near
     extra = [0] + [BACK_ROWS] * len(steps)
     rows_of = [message] + others
     kernels = []
     for x in rows_of[:early]:
-        kernels += kernel_call(order, column, x, features)
+        kernels += kernel_call(n, order, column, x, features)
     scores = scores_call(0, members, kernels, [], extra[:early], True)
     cross = []
     for x in rows_of[early:]:
-        cross += kernel_call(order, column, x, features, scores)
+        cross += kernel_call(n, order, column, x, features, scores)
     scores += scores_call(0, members, cross, [], extra[early:], True)
     kernels += cross
     own = pair
@@ -339,25 +378,22 @@
         if iteration > 0:
             even, *others = members_call(n, stats, evens, others)
             odd = by_col(even, 1)
+            own = even
             scores = scores_call(0, [even], kernels, [], extra)
-            scores = scores_call(half, [odd], kernels, scores, extra)
-            own = even
-        stat = stat_call(has_near, own, scores, others)
-        t_even, t_odd = other_call(
-            half, clusters, others[has_near:], cross, [] if last else [stat]
-        )
         if last:
-            planes = [shift(stat, d) for d in list(range(1, rows))]
-            for x in planes:
+            t_even, t_odd = other_call(n, half, clusters, others[has_near:], cross, [])
+            sent = fold_call(n, t_even, by_col(t_odd, 1), [], 0)
+            scores = scores_call(half, [odd], kernels, scores, extra, after=sent[:1])
+            stat = stat_call(has_near, own, scores, others)
+            for x in [shift(stat, d) for d in range(1, rows)]:
                 stat = stat + x
-            stats = [stat, by_col(stat, 1)]
+            sent = widen_call(n, sent, [stat, by_col(stat, 1)])
         else:
-            stats = [stat]
-        sent = call(
-            functools.partial(fold_body, n, len(stats)),
-            [t_even, by_col(t_odd, 1)] + stats,
-            [shaped(n + STAT_ROWS, clusters)] * (1 + len(masks)),
-        )
+            if iteration > 0:
+                scores = scores_call(half, [odd], kernels, scores, extra)
+            stat = stat_call(has_near, own, scores, others)
+            t_even, t_odd = other_call(n, half, clusters, others[has_near:], cross, [stat])
+            sent = fold_call(n, t_even, by_col(t_odd, 1), [stat], STAT_ROWS)
         parts = [by_col(x, k) for k, x in zip(masks, sent[1:])]
         back = [shift(x, -d) for d, x in zip(steps, scores[1:])]
         outs = [shaped(n, clusters)] * 2

time: 84.5 us -> 86.1 us (1.019)
  Pallas kernels: 10.8 us -> 13.5 us
  waiting for transfers between devices: 32.1 us -> 30.5 us
    pallas_call x17 -> x18, Pallas kernels: 10.8 us -> 13.5 us  [call(): pl.pallas_call(body, in_specs=specs or [VMEM] * len(args), out_specs=[VME...]
    ppermute x12, starting transfers between devices: 20.5 us -> 22.3 us  [shift(): return lax.ppermute(x, 'row', pairs)]
    ppermute x20, starting transfers between devices: 17.3 us -> 15.7 us  [by_col(): return lax.ppermute(x, 'col', [(i, i ^ mask) for i in range(cols)])]
    ppermute x12, waiting for transfers between devices: 14.6 us -> 13.4 us  [shift(): return lax.ppermute(x, 'row', pairs)]
    unnamed x6 -> x8, local copies, waits for them, and re-layouts: 2.78 us -> 2.88 us
  transfers between devices with their start and end apart: 32 -> 32, of which waited for: 16 -> 14; matrix products, arithmetic and copies ran while one was open for 0% -> 0% of each run, Pallas kernels for 7% -> 5%
where the time goes in v4:
time: 86.1 us; the launch traced here: 85.9 us
  starting transfers between devices  38.1 us (44%)
  waiting for transfers between devices  30.5 us (35%)
  Pallas kernels  13.5 us (16%)
  local copies, waits for them, and re-layouts  2.88 us (3%)
    ppermute x12, starting transfers between devices, shift(): return lax.ppermute(x, 'row', pairs)  22.3 us
    ppermute x20, waiting for transfers between devices, by_col(): return lax.ppermute(x, 'col', [(i, i ^ mask) for i in range(cols)])  17.1 us
    ppermute x20, starting transfers between devices, by_col(): return lax.ppermute(x, 'col', [(i, i ^ mask) for i in range(cols)])  15.7 us
    pallas_call x18, Pallas kernels, call(): pl.pallas_call(body, in_specs=specs or [VMEM] * len(args), out_specs=[VME...  13.5 us
    ppermute x12, waiting for transfers between devices, shift(): return lax.ppermute(x, 'row', pairs)  13.4 us
    unnamed x8, local copies, waits for them, and re-layouts  2.88 us
  transfers between devices with their start and end apart: 32, of which 14 were waited for; matrix products, arithmetic and copies ran while one was open for 0% of the time, Pallas kernels for 5%

profile of v4, /device:TPU:0, one launch (start us, length us, event | category | flops | bytes accessed | tf_op | source)
XLA Modules:
  0.0 85.9 jit_solution(13015673977015158139)
XLA Ops:
  0.6 2.9 %shard_map.41 = (bf16[256,768]{1,0:T(8,128)(2,1)}, bf16[272,768]{1,0:T(8,128)(2,1)}, bf16[256,256]{1,0:T(8,128)(2,1)}) custom-call(s32[1]{0:T(128)} %bitcast.column_ref, bf16[2048,512]{1,0:T(8,128)(2,1)} %plane_ref.5, f32[256,128]{1,0:T(8,128)} %logits.1), custom_call_target="tpu_custom_call" | custom-call | bytes 3170308 | tf_op jit(solution)/shard_map/pallas_call | solution.py:31
  3.5 3.1 %collective-permute-start.8 = (bf16[256,768]{1,0:T(8,128)(2,1)}, bf16[256,768]{1,0:T(8,128)(2,1)S(1)}, u32[]{:S(2)}, u32[]{:S(2)}) collective-permute-start(bf16[256,768]{1,0:T(8,128)(2,1)} %get-tuple-element.43.rows_ref), channel_id=1, source_target_pairs={{0,8},{8,0},{16,24},{24,16},{1,9},{9,1},{17,25},{25,17},{2,10},{10... | collective-permute-start | bytes 1179656 | tf_op jit(solution)/shard_map/ppermute | solution.py:344
  6.6 2.5 %collective-permute-start = (bf16[272,768]{1,0:T(8,128)(2,1)}, bf16[272,768]{1,0:T(8,128)(2,1)S(1)}, u32[]{:S(2)}, u32[]{:S(2)}) collective-permute-start(bf16[272,768]{1,0:T(8,128)(2,1)} %get-tuple-element.41), channel_id=1, source_target_pairs={{16,0},{8,16},{24,8},{0,24},{17,1},{9,17},{25,9},{1,25},{18,2},{10... | collective-permute-start | bytes 1253384 | tf_op jit(solution)/shard_map/ppermute | solution.py:344
  9.1 1.5 %collective-permute-start.1 = (bf16[256,256]{1,0:T(8,128)(2,1)}, bf16[256,256]{1,0:T(8,128)(2,1)S(1)}, u32[]{:S(2)}, u32[]{:S(2)}) collective-permute-start(bf16[256,256]{1,0:T(8,128)(2,1)} %get-tuple-element.42.refs_0_.own), channel_id=1, source_target_pairs={{0,2},{1,3},{2,0},{3,1},{4,6},{5,7},{6,4},{7,5},{8,10},{9,11},{10,... | collective-permute-start | bytes 393224 | tf_op jit(solution)/shard_map/ppermute | solution.py:337
  10.6 1.5 %collective-permute-start.2 = (bf16[256,256]{1,0:T(8,128)(2,1)}, bf16[256,256]{1,0:T(8,128)(2,1)S(1)}, u32[]{:S(2)}, u32[]{:S(2)}) collective-permute-start(bf16[256,256]{1,0:T(8,128)(2,1)} %get-tuple-element.42.refs_0_.own), channel_id=1, source_target_pairs={{0,4},{1,5},{2,6},{3,7},{4,0},{5,1},{6,2},{7,3},{8,12},{9,13},{10,... | collective-permute-start | bytes 393224 | tf_op jit(solution)/shard_map/ppermute | solution.py:337
  12.1 0.5 collective-permute-start.3
  12.6 2.4 %collective-permute-done.1.refs_1_ = bf16[256,256]{1,0:T(8,128)(2,1)S(1)} collective-permute-done((bf16[256,256]{1,0:T(8,128)(2,1)}, bf16[256,256]{1,0:T(8,128)(2,1)S(1)}, u32[]{:S(2)}, u32[]{:S(2)}) %collective-permute-start.1) | collective-permute-done | bytes 131104 | tf_op jit(solution)/shard_map/ppermute | solution.py:337
  15.0 3.6 %collective-permute-done.2.refs_2_ = bf16[256,256]{1,0:T(8,128)(2,1)S(1)} collective-permute-done((bf16[256,256]{1,0:T(8,128)(2,1)}, bf16[256,256]{1,0:T(8,128)(2,1)S(1)}, u32[]{:S(2)}, u32[]{:S(2)}) %collective-permute-start.2) | collective-permute-done | bytes 131104 | tf_op jit(solution)/shard_map/ppermute | solution.py:337
  18.6 0.5 collective-permute-start.6
  19.1 5.2 %collective-permute-done.8.rows_ref.refs_3_ = bf16[256,768]{1,0:T(8,128)(2,1)S(1)} collective-permute-done((bf16[256,768]{1,0:T(8,128)(2,1)}, bf16[256,768]{1,0:T(8,128)(2,1)S(1)}, u32[]{:S(2)}, u32[]{:S(2)}) %collective-permute-start.8) | collective-permute-done | bytes 393248 | tf_op jit(solution)/shard_map/ppermute | solution.py:344
  24.2 0.0 collective-permute-start.7
  24.3 1.6 %copy-done = bf16[2048,512]{1,0:T(8,128)(2,1)S(1)} copy-done((bf16[2048,512]{1,0:T(8,128)(2,1)S(1)}, bf16[2048,512]{1,0:T(8,128)(2,1)}, u32[]{:S(2)}) %copy-start) | copy-done | bytes 2097176
  25.8 1.0 %copy-done.3 = bf16[256,768]{1,0:T(8,128)(2,1)S(1)} copy-done((bf16[256,768]{1,0:T(8,128)(2,1)S(1)}, bf16[256,768]{1,0:T(8,128)(2,1)}, u32[]{:S(2)}) %copy-start.3) | copy-done | bytes 393240
  26.8 0.9 %shard_map.42 = (bf16[256,2048]{1,0:T(8,128)(2,1)S(1)}, bf16[256,2048]{1,0:T(8,128)(2,1)S(1)}) custom-call(s32[1]{0:T(128)} %bitcast.column_ref, bf16[256,768]{1,0:T(8,128)(2,1)S(1)} %copy-done.3, bf16[2048,512]{1,0:T(8,128)(2,1)S(1)} %copy-done), custom_call_target="tpu_custom_call" | custom-call | tf_op jit(solution)/shard_map/pallas_call | solution.py:31
  27.7 0.9 %shard_map.43 = (bf16[256,2048]{1,0:T(8,128)(2,1)S(1)}, bf16[256,2048]{1,0:T(8,128)(2,1)S(1)}) custom-call(s32[1]{0:T(128)} %bitcast.column_ref, bf16[256,768]{1,0:T(8,128)(2,1)S(1)} %collective-permute-done.8.rows_ref.refs_3_, bf16[2048,512]{1,0:T(8,128)(2,1)S(1)} %copy-done), custom_call_target="tpu_custom_call" | custom-call | tf_op jit(solution)/shard_map/pallas_call | solution.py:31
  28.6 0.0 collective-permute-done.6.refs_6_
  28.6 0.0 copy-start.1
  28.6 1.3 %shard_map.44 = (f32[256,128]{1,0:T(8,128)S(1)}, f32[272,128]{1,0:T(8,128)S(1)}) custom-call(bf16[256,256]{1,0:T(8,128)(2,1)S(1)} %copy-done.2, bf16[256,256]{1,0:T(8,128)(2,1)S(1)} %collective-permute-done.1.refs_1_, bf16[256,256]{1,0:T(8,128)(2,1)S(1)} %collective-permute-done.2.refs_2_, bf16[256,256]{1,0:T(8,128)(2,1)S(1)} %collective-permute-done.3.refs_3_, ...), custom_call_target="tpu_custom_call" | custom-call | tf_op jit(solution)/shard_map/pallas_call | solution.py:31
  29.9 0.3 copy-done.1
  30.2 0.9 shard_map.45
  31.1 0.7 shard_map.46.refs_2_
  31.8 0.1 shard_map.47.refs_3_.refs_0_
  31.9 0.8 shard_map.48
  32.7 0.6 collective-permute-start.9
  33.3 5.0 %collective-permute-start.11 = (f32[272,128]{1,0:T(8,128)S(1)}, f32[272,128]{1,0:T(8,128)S(1)}, u32[]{:S(2)}, u32[]{:S(2)}) collective-permute-start(f32[272,128]{1,0:T(8,128)S(1)} %shard_map.46.refs_2_), channel_id=1, source_target_pairs={{24,0},{0,16},{16,8},{8,24},{25,1},{1,17},{17,9},{9,25},{26,2},{2,... | collective-permute-start | bytes 417800 | tf_op jit(solution)/shard_map/ppermute | solution.py:344
  38.2 0.1 shard_map.49
  38.3 1.6 %collective-permute-start.12 = (f32[264,128]{1,0:T(8,128)S(1)}, f32[264,128]{1,0:T(8,128)S(1)}, u32[]{:S(2)}, u32[]{:S(2)}) collective-permute-start(f32[264,128]{1,0:T(8,128)S(1)} %get-tuple-element.55), channel_id=1, source_target_pairs={{0,2},{1,3},{2,0},{3,1},{4,6},{5,7},{6,4},{7,5},{8,10},{9,11},{10,... | collective-permute-start | bytes 405512 | tf_op jit(solution)/shard_map/ppermute | solution.py:337
  39.8 1.5 %collective-permute-start.13 = (f32[264,128]{1,0:T(8,128)S(1)}, f32[264,128]{1,0:T(8,128)S(1)}, u32[]{:S(2)}, u32[]{:S(2)}) collective-permute-start(f32[264,128]{1,0:T(8,128)S(1)} %get-tuple-element.56), channel_id=1, source_target_pairs={{0,4},{1,5},{2,6},{3,7},{4,0},{5,1},{6,2},{7,3},{8,12},{9,13},{10,... | collective-permute-start | bytes 405512 | tf_op jit(solution)/shard_map/ppermute | solution.py:337
  41.4 0.5 collective-permute-start.14
  41.8 2.8 %collective-permute-done.11.refs_3_ = f32[272,128]{1,0:T(8,128)S(1)} collective-permute-done((f32[272,128]{1,0:T(8,128)S(1)}, f32[272,128]{1,0:T(8,128)S(1)}, u32[]{:S(2)}, u32[]{:S(2)}) %collective-permute-start.11) | collective-permute-done | bytes 139296 | tf_op jit(solution)/shard_map/ppermute | solution.py:344
  44.7 3.1 %collective-permute-done.13.refs_5_ = f32[264,128]{1,0:T(8,128)S(1)} collective-permute-done((f32[264,128]{1,0:T(8,128)S(1)}, f32[264,128]{1,0:T(8,128)S(1)}, u32[]{:S(2)}, u32[]{:S(2)}) %collective-permute-start.13) | collective-permute-done | bytes 135200 | tf_op jit(solution)/shard_map/ppermute | solution.py:337
  47.8 0.1 shard_map.50
  47.8 0.1 collective-permute-start.15
  47.9 2.1 %collective-permute-start.19 = (f32[264,128]{1,0:T(8,128)S(1)}, f32[264,128]{1,0:T(8,128)S(1)}, u32[]{:S(2)}, u32[]{:S(2)}) collective-permute-start(f32[264,128]{1,0:T(8,128)S(1)} %get-tuple-element.60), channel_id=1, source_target_pairs={{0,8},{8,0},{16,24},{24,16},{1,9},{9,1},{17,25},{25,17},{2,10},{10... | collective-permute-start | bytes 405512 | tf_op jit(solution)/shard_map/ppermute | solution.py:344
  50.0 1.7 %collective-permute-start.20 = (f32[264,128]{1,0:T(8,128)S(1)}, f32[264,128]{1,0:T(8,128)S(1)}, u32[]{:S(2)}, u32[]{:S(2)}) collective-permute-start(f32[264,128]{1,0:T(8,128)S(1)} %get-tuple-element.60), channel_id=1, source_target_pairs={{16,0},{8,16},{24,8},{0,24},{17,1},{9,17},{25,9},{1,25},{18,2},{10... | collective-permute-start | bytes 405512 | tf_op jit(solution)/shard_map/ppermute | solution.py:344
  51.7 0.9 %collective-permute-start.16 = (f32[256,128]{1,0:T(8,128)S(1)}, f32[256,128]{1,0:T(8,128)S(1)}, u32[]{:S(2)}, u32[]{:S(2)}) collective-permute-start(f32[256,128]{1,0:T(8,128)S(1)} %get-tuple-element.59.refs_2_), channel_id=1, source_target_pairs={{0,2},{1,3},{2,0},{3,1},{4,6},{5,7},{6,4},{7,5},{8,10},{9,11},{10,... | collective-permute-start | bytes 393224 | tf_op jit(solution)/shard_map/ppermute | solution.py:337
  52.6 0.8 collective-permute-start.17
  53.5 1.7 %collective-permute-start.18 = (f32[256,128]{1,0:T(8,128)S(1)}, f32[256,128]{1,0:T(8,128)S(1)}, u32[]{:S(2)}, u32[]{:S(2)}) collective-permute-start(f32[256,128]{1,0:T(8,128)S(1)} %get-tuple-element.59.refs_2_), channel_id=1, source_target_pairs={{0,6},{1,7},{2,4},{3,5},{4,2},{5,3},{6,0},{7,1},{8,14},{9,15},{10,... | collective-permute-start | bytes 393224 | tf_op jit(solution)/shard_map/ppermute | solution.py:337
  55.2 1.5 %collective-permute-done.16.refs_3_ = f32[256,128]{1,0:T(8,128)S(1)} collective-permute-done((f32[256,128]{1,0:T(8,128)S(1)}, f32[256,128]{1,0:T(8,128)S(1)}, u32[]{:S(2)}, u32[]{:S(2)}) %collective-permute-start.16) | collective-permute-done | bytes 131104 | tf_op jit(solution)/shard_map/ppermute | solution.py:337
  56.7 0.9 %collective-permute-done.17.refs_4_ = f32[256,128]{1,0:T(8,128)S(1)} collective-permute-done((f32[256,128]{1,0:T(8,128)S(1)}, f32[256,128]{1,0:T(8,128)S(1)}, u32[]{:S(2)}, u32[]{:S(2)}) %collective-permute-start.17) | collective-permute-done | bytes 131104 | tf_op jit(solution)/shard_map/ppermute | solution.py:337
  57.6 1.7 %collective-permute-done.18.refs_5_ = f32[256,128]{1,0:T(8,128)S(1)} collective-permute-done((f32[256,128]{1,0:T(8,128)S(1)}, f32[256,128]{1,0:T(8,128)S(1)}, u32[]{:S(2)}, u32[]{:S(2)}) %collective-permute-start.18) | collective-permute-done | bytes 131104 | tf_op jit(solution)/shard_map/ppermute | solution.py:337
  59.4 1.2 %shard_map.51 = (bf16[1024,256]{1,0:T(8,128)(2,1)S(1)}, bf16[256,256]{1,0:T(8,128)(2,1)S(1)}, bf16[256,256]{1,0:T(8,128)(2,1)S(1)}) custom-call(f32[8,128]{1,0:T(8,128)S(1)} %get-tuple-element.58.refs_0_, f32[8,128]{1,0:T(8,128)S(1)} %collective-permute-done.15.refs_1_, f32[256,128]{1,0:T(8,128)S(1)} %get-tuple-element.59.refs_2_, ...), custom_call_target="tpu_custom_call" | custom-call | bytes 1589248 | tf_op jit(solution)/shard_map/pallas_call | solution.py:31
  60.6 0.8 shard_map.52
  61.3 0.1 collective-permute-start.21
  61.4 0.5 collective-permute-start.22
  61.9 1.0 %shard_map.54 = (f32[256,128]{1,0:T(8,128)S(1)}, f32[272,128]{1,0:T(8,128)S(1)}, f32[272,128]{1,0:T(8,128)S(1)}) custom-call(bf16[1024,256]{1,0:T(8,128)(2,1)S(1)} %get-tuple-element.68.refs_0_.own, bf16[256,2048]{1,0:T(8,128)(2,1)S(1)} %get-tuple-element.44.refs_8_.refs_1_, bf16[256,2048]{1,0:T(8,128)(2,1)S(1)} %get-tuple-element.45.refs_9_.refs_2_, ...), custom_call_target="tpu_custom_call" | custom-call | flops 603979776 | bytes 7225344 | tf_op jit(solution)/shard_map/pallas_call | solution.py:31
  62.9 0.4 collective-permute-done.21.received
  63.3 0.1 shard_map.53
  63.4 0.7 collective-permute-done.22.refs_0_
  64.0 1.0 %shard_map.55 = (f32[256,128]{1,0:T(8,128)S(1)}, f32[272,128]{1,0:T(8,128)S(1)}, f32[272,128]{1,0:T(8,128)S(1)}) custom-call(bf16[1024,256]{1,0:T(8,128)(2,1)S(1)} %collective-permute-done.22.refs_0_, bf16[256,2048]{1,0:T(8,128)(2,1)S(1)} %get-tuple-element.44.refs_8_.refs_1_, bf16[256,2048]{1,0:T(8,128)(2,1)S(1)} %get-tuple-element.45.refs_9_.refs_2_, ...), custom_call_target="tpu_custom_call" | custom-call | flops 603979776 | bytes 7766016 | tf_op jit(solution)/shard_map/pallas_call | solution.py:31
  65.0 0.1 shard_map.56
  65.1 1.5 %collective-permute-start.25 = (f32[8,128]{1,0:T(8,128)S(1)}, f32[8,128]{1,0:T(8,128)S(1)}, u32[]{:S(2)}, u32[]{:S(2)}) collective-permute-start(f32[8,128]{1,0:T(8,128)S(1)} %shard_map.56), channel_id=1, source_target_pairs={{24,0},{0,16},{16,8},{8,24},{25,1},{1,17},{17,9},{9,25},{26,2},{2,... | collective-permute-start | bytes 12296 | tf_op jit(solution)/shard_map/ppermute | solution.py:344
  66.7 0.2 collective-permute-start.24
  66.9 2.3 %collective-permute-start.23 = (f32[8,128]{1,0:T(8,128)S(1)}, f32[8,128]{1,0:T(8,128)S(1)}, u32[]{:S(2)}, u32[]{:S(2)}) collective-permute-start(f32[8,128]{1,0:T(8,128)S(1)} %shard_map.56), channel_id=1, source_target_pairs={{16,0},{8,16},{24,8},{0,24},{17,1},{9,17},{25,9},{1,25},{18,2},{10... | collective-permute-start | bytes 12296 | tf_op jit(solution)/shard_map/ppermute | solution.py:344
  69.2 1.4 %collective-permute-done.25 = f32[8,128]{1,0:T(8,128)S(1)} collective-permute-done((f32[8,128]{1,0:T(8,128)S(1)}, f32[8,128]{1,0:T(8,128)S(1)}, u32[]{:S(2)}, u32[]{:S(2)}) %collective-permute-start.25) | collective-permute-done | bytes 4128 | tf_op jit(solution)/shard_map/ppermute | solution.py:344
  70.6 0.8 collective-permute-done.23
  71.4 1.8 %collective-permute-start.27 = (f32[272,128]{1,0:T(8,128)S(1)}, f32[272,128]{1,0:T(8,128)S(1)}, u32[]{:S(2)}, u32[]{:S(2)}) collective-permute-start(f32[272,128]{1,0:T(8,128)S(1)} %get-tuple-element.73.refs_1_), channel_id=1, source_target_pairs={{0,8},{8,0},{16,24},{24,16},{1,9},{9,1},{17,25},{25,17},{2,10},{10... | collective-permute-start | bytes 417800 | tf_op jit(solution)/shard_map/ppermute | solution.py:344
  73.3 2.0 %collective-permute-start.28 = (f32[272,128]{1,0:T(8,128)S(1)}, f32[272,128]{1,0:T(8,128)S(1)}, u32[]{:S(2)}, u32[]{:S(2)}) collective-permute-start(f32[272,128]{1,0:T(8,128)S(1)} %get-tuple-element.74.refs_2_), channel_id=1, source_target_pairs={{24,0},{0,16},{16,8},{8,24},{25,1},{1,17},{17,9},{9,25},{26,2},{2,... | collective-permute-start | bytes 417800 | tf_op jit(solution)/shard_map/ppermute | solution.py:344
  75.3 1.6 %collective-permute-start.29 = (f32[264,128]{1,0:T(8,128)S(1)}, f32[264,128]{1,0:T(8,128)S(1)}, u32[]{:S(2)}, u32[]{:S(2)}) collective-permute-start(f32[264,128]{1,0:T(8,128)S(1)} %get-tuple-element.77), channel_id=1, source_target_pairs={{0,2},{1,3},{2,0},{3,1},{4,6},{5,7},{6,4},{7,5},{8,10},{9,11},{10,... | collective-permute-start | bytes 405512 | tf_op jit(solution)/shard_map/ppermute | solution.py:337
  76.9 0.8 collective-permute-start.30
  77.7 1.2 %collective-permute-start.31 = (f32[264,128]{1,0:T(8,128)S(1)}, f32[264,128]{1,0:T(8,128)S(1)}, u32[]{:S(2)}, u32[]{:S(2)}) collective-permute-start(f32[264,128]{1,0:T(8,128)S(1)} %get-tuple-element.79), channel_id=1, source_target_pairs={{0,6},{1,7},{2,4},{3,5},{4,2},{5,3},{6,0},{7,1},{8,14},{9,15},{10,... | collective-permute-start | bytes 405512 | tf_op jit(solution)/shard_map/ppermute | solution.py:337
  78.9 3.2 %collective-permute-done.28.refs_3_ = f32[272,128]{1,0:T(8,128)S(1)} collective-permute-done((f32[272,128]{1,0:T(8,128)S(1)}, f32[272,128]{1,0:T(8,128)S(1)}, u32[]{:S(2)}, u32[]{:S(2)}) %collective-permute-start.28) | collective-permute-done | bytes 139296 | tf_op jit(solution)/shard_map/ppermute | solution.py:344
  82.1 2.8 %collective-permute-done.30.refs_5_ = f32[264,128]{1,0:T(8,128)S(1)} collective-permute-done((f32[264,128]{1,0:T(8,128)S(1)}, f32[264,128]{1,0:T(8,128)S(1)}, u32[]{:S(2)}, u32[]{:S(2)}) %collective-permute-start.30) | collective-permute-done | bytes 135200 | tf_op jit(solution)/shard_map/ppermute | solution.py:337
  84.9 1.0 %shard_map.58 = (f32[256,128]{1,0:T(8,128)}, f32[256,128]{1,0:T(8,128)}) custom-call(f32[264,128]{1,0:T(8,128)S(1)} %get-tuple-element.76.refs_0_, f32[256,128]{1,0:T(8,128)S(1)} %get-tuple-element.72.refs_0_.refs_1_, f32[272,128]{1,0:T(8,128)S(1)} %collective-permute-done.27.refs_2_, f32[272,128]{1,0:T(8,128)S(1)} %collective-permute-done.28.refs_3_, ...), custom_call_target="tpu_custom_call" | custom-call | bytes 1212416 | tf_op jit(solution)/shard_map/pallas_call | solution.py:31
  (27 shorter events, 0.1 us)
Async XLA Ops:
  3.5 20.7 %collective-permute-start.8 = (bf16[256,768]{1,0:T(8,128)(2,1)}, bf16[256,768]{1,0:T(8,128)(2,1)S(1)}, u32[]{:S(2)}, u32[]{:S(2)}) collective-permute-start(bf16[256,768]{1,0:T(8,128)(2,1)} %get-tuple-element.43.rows_ref), channel_id=1, source_target_pairs={{0,8},{8,0},{16,24},{24,16},{1,9},{9,1},{17,25},{25,17},{2,10},{10... | collective-permute-start | bytes 1179656 | tf_op jit(solution)/shard_map/ppermute | solution.py:344
  6.6 23.3 %collective-permute-start = (bf16[272,768]{1,0:T(8,128)(2,1)}, bf16[272,768]{1,0:T(8,128)(2,1)S(1)}, u32[]{:S(2)}, u32[]{:S(2)}) collective-permute-start(bf16[272,768]{1,0:T(8,128)(2,1)} %get-tuple-element.41), channel_id=1, source_target_pairs={{16,0},{8,16},{24,8},{0,24},{17,1},{9,17},{25,9},{1,25},{18,2},{10... | collective-permute-start | bytes 1253384 | tf_op jit(solution)/shard_map/ppermute | solution.py:344
  9.1 5.9 %collective-permute-start.1 = (bf16[256,256]{1,0:T(8,128)(2,1)}, bf16[256,256]{1,0:T(8,128)(2,1)S(1)}, u32[]{:S(2)}, u32[]{:S(2)}) collective-permute-start(bf16[256,256]{1,0:T(8,128)(2,1)} %get-tuple-element.42.refs_0_.own), channel_id=1, source_target_pairs={{0,2},{1,3},{2,0},{3,1},{4,6},{5,7},{6,4},{7,5},{8,10},{9,11},{10,... | collective-permute-start | bytes 393224 | tf_op jit(solution)/shard_map/ppermute | solution.py:337
  10.6 8.0 %collective-permute-start.2 = (bf16[256,256]{1,0:T(8,128)(2,1)}, bf16[256,256]{1,0:T(8,128)(2,1)S(1)}, u32[]{:S(2)}, u32[]{:S(2)}) collective-permute-start(bf16[256,256]{1,0:T(8,128)(2,1)} %get-tuple-element.42.refs_0_.own), channel_id=1, source_target_pairs={{0,4},{1,5},{2,6},{3,7},{4,0},{5,1},{6,2},{7,3},{8,12},{9,13},{10,... | collective-permute-start | bytes 393224 | tf_op jit(solution)/shard_map/ppermute | solution.py:337
  12.1 6.5 %collective-permute-start.3 = (bf16[256,256]{1,0:T(8,128)(2,1)}, bf16[256,256]{1,0:T(8,128)(2,1)S(1)}, u32[]{:S(2)}, u32[]{:S(2)}) collective-permute-start(bf16[256,256]{1,0:T(8,128)(2,1)} %get-tuple-element.42.refs_0_.own), channel_id=1, source_target_pairs={{0,6},{1,7},{2,4},{3,5},{4,2},{5,3},{6,0},{7,1},{8,14},{9,15},{10,... | collective-permute-start | bytes 393224 | tf_op jit(solution)/shard_map/ppermute | solution.py:337
  15.0 13.6 %collective-permute-start.4 = (bf16[256,256]{1,0:T(8,128)(2,1)}, bf16[256,256]{1,0:T(8,128)(2,1)S(1)}, u32[]{:S(2)}, u32[]{:S(2)}) collective-permute-start(bf16[256,256]{1,0:T(8,128)(2,1)} %get-tuple-element.42.refs_0_.own), channel_id=1, source_target_pairs={{0,1},{1,0},{2,3},{3,2},{4,5},{5,4},{6,7},{7,6},{8,9},{9,8},{10,11... | collective-permute-start | bytes 393224 | tf_op jit(solution)/shard_map/ppermute | solution.py:337
  18.6 10.0 %collective-permute-start.5 = (bf16[256,256]{1,0:T(8,128)(2,1)S(1)}, bf16[256,256]{1,0:T(8,128)(2,1)S(1)}, u32[]{:S(2)}, u32[]{:S(2)}) collective-permute-start(bf16[256,256]{1,0:T(8,128)(2,1)S(1)} %collective-permute-done.1.refs_1_), channel_id=1, source_target_pairs={{0,1},{1,0},{2,3},{3,2},{4,5},{5,4},{6,7},{7,6},{8,9},{9,8},{10,11... | collective-permute-start | bytes 393224 | tf_op jit(solution)/shard_map/ppermute | solution.py:337
  18.6 10.0 %collective-permute-start.6 = (bf16[256,256]{1,0:T(8,128)(2,1)S(1)}, bf16[256,256]{1,0:T(8,128)(2,1)S(1)}, u32[]{:S(2)}, u32[]{:S(2)}) collective-permute-start(bf16[256,256]{1,0:T(8,128)(2,1)S(1)} %collective-permute-done.2.refs_2_), channel_id=1, source_target_pairs={{0,1},{1,0},{2,3},{3,2},{4,5},{5,4},{6,7},{7,6},{8,9},{9,8},{10,11... | collective-permute-start | bytes 393224 | tf_op jit(solution)/shard_map/ppermute | solution.py:337
  24.2 4.4 %collective-permute-start.7 = (bf16[256,256]{1,0:T(8,128)(2,1)S(1)}, bf16[256,256]{1,0:T(8,128)(2,1)S(1)}, u32[]{:S(2)}, u32[]{:S(2)}) collective-permute-start(bf16[256,256]{1,0:T(8,128)(2,1)S(1)} %collective-permute-done.3.refs_3_), channel_id=1, source_target_pairs={{0,1},{1,0},{2,3},{3,2},{4,5},{5,4},{6,7},{7,6},{8,9},{9,8},{10,11... | collective-permute-start | bytes 393224 | tf_op jit(solution)/shard_map/ppermute | solution.py:337
  24.2 1.6 %copy-start = (bf16[2048,512]{1,0:T(8,128)(2,1)S(1)}, bf16[2048,512]{1,0:T(8,128)(2,1)}, u32[]{:S(2)}) copy-start(bf16[2048,512]{1,0:T(8,128)(2,1)} %plane_ref.5) | copy-start | bytes 6291460
  25.8 1.0 %copy-start.3 = (bf16[256,768]{1,0:T(8,128)(2,1)S(1)}, bf16[256,768]{1,0:T(8,128)(2,1)}, u32[]{:S(2)}) copy-start(bf16[256,768]{1,0:T(8,128)(2,1)} %get-tuple-element.43.rows_ref) | copy-start | bytes 1179652
  26.8 1.8 %copy-start.2 = (bf16[256,256]{1,0:T(8,128)(2,1)S(1)}, bf16[256,256]{1,0:T(8,128)(2,1)}, u32[]{:S(2)}) copy-start(bf16[256,256]{1,0:T(8,128)(2,1)} %get-tuple-element.42.refs_0_.own) | copy-start | bytes 393220
  28.6 1.6 %copy-start.1 = (bf16[2048,512]{1,0:T(8,128)(2,1)S(1)}, bf16[2048,512]{1,0:T(8,128)(2,1)}, u32[]{:S(2)}) copy-start(bf16[2048,512]{1,0:T(8,128)(2,1)} %plane_ref.5) | copy-start | bytes 6291460
  32.7 5.5 %collective-permute-start.9 = (f32[1032,128]{1,0:T(8,128)S(1)}, f32[1032,128]{1,0:T(8,128)S(1)}, u32[]{:S(2)}, u32[]{:S(2)}) collective-permute-start(f32[1032,128]{1,0:T(8,128)S(1)} %get-tuple-element.53), channel_id=1, source_target_pairs={{0,1},{1,0},{2,3},{3,2},{4,5},{5,4},{6,7},{7,6},{8,9},{9,8},{10,11... | collective-permute-start | bytes 1585160 | tf_op jit(solution)/shard_map/ppermute | solution.py:337
  33.3 8.6 %collective-permute-start.10 = (f32[272,128]{1,0:T(8,128)S(1)}, f32[272,128]{1,0:T(8,128)S(1)}, u32[]{:S(2)}, u32[]{:S(2)}) collective-permute-start(f32[272,128]{1,0:T(8,128)S(1)} %get-tuple-element.49.refs_1_), channel_id=1, source_target_pairs={{0,8},{8,0},{16,24},{24,16},{1,9},{9,1},{17,25},{25,17},{2,10},{10... | collective-permute-start | bytes 417800 | tf_op jit(solution)/shard_map/ppermute | solution.py:344
  33.3 11.4 %collective-permute-start.11 = (f32[272,128]{1,0:T(8,128)S(1)}, f32[272,128]{1,0:T(8,128)S(1)}, u32[]{:S(2)}, u32[]{:S(2)}) collective-permute-start(f32[272,128]{1,0:T(8,128)S(1)} %shard_map.46.refs_2_), channel_id=1, source_target_pairs={{24,0},{0,16},{16,8},{8,24},{25,1},{1,17},{17,9},{9,25},{26,2},{2,... | collective-permute-start | bytes 417800 | tf_op jit(solution)/shard_map/ppermute | solution.py:344
  38.3 6.4 %collective-permute-start.12 = (f32[264,128]{1,0:T(8,128)S(1)}, f32[264,128]{1,0:T(8,128)S(1)}, u32[]{:S(2)}, u32[]{:S(2)}) collective-permute-start(f32[264,128]{1,0:T(8,128)S(1)} %get-tuple-element.55), channel_id=1, source_target_pairs={{0,2},{1,3},{2,0},{3,1},{4,6},{5,7},{6,4},{7,5},{8,10},{9,11},{10,... | collective-permute-start | bytes 405512 | tf_op jit(solution)/shard_map/ppermute | solution.py:337
  39.8 7.9 %collective-permute-start.13 = (f32[264,128]{1,0:T(8,128)S(1)}, f32[264,128]{1,0:T(8,128)S(1)}, u32[]{:S(2)}, u32[]{:S(2)}) collective-permute-start(f32[264,128]{1,0:T(8,128)S(1)} %get-tuple-element.56), channel_id=1, source_target_pairs={{0,4},{1,5},{2,6},{3,7},{4,0},{5,1},{6,2},{7,3},{8,12},{9,13},{10,... | collective-permute-start | bytes 405512 | tf_op jit(solution)/shard_map/ppermute | solution.py:337
  41.4 6.4 %collective-permute-start.14 = (f32[264,128]{1,0:T(8,128)S(1)}, f32[264,128]{1,0:T(8,128)S(1)}, u32[]{:S(2)}, u32[]{:S(2)}) collective-permute-start(f32[264,128]{1,0:T(8,128)S(1)} %get-tuple-element.57), channel_id=1, source_target_pairs={{0,6},{1,7},{2,4},{3,5},{4,2},{5,3},{6,0},{7,1},{8,14},{9,15},{10,... | collective-permute-start | bytes 405512 | tf_op jit(solution)/shard_map/ppermute | solution.py:337
  47.8 5.7 %collective-permute-start.15 = (f32[8,128]{1,0:T(8,128)S(1)}, f32[8,128]{1,0:T(8,128)S(1)}, u32[]{:S(2)}, u32[]{:S(2)}) collective-permute-start(f32[8,128]{1,0:T(8,128)S(1)} %get-tuple-element.58.refs_0_), channel_id=1, source_target_pairs={{24,0},{0,16},{16,8},{8,24},{25,1},{1,17},{17,9},{9,25},{26,2},{2,... | collective-permute-start | bytes 12296 | tf_op jit(solution)/shard_map/ppermute | solution.py:344
  47.9 11.5 %collective-permute-start.19 = (f32[264,128]{1,0:T(8,128)S(1)}, f32[264,128]{1,0:T(8,128)S(1)}, u32[]{:S(2)}, u32[]{:S(2)}) collective-permute-start(f32[264,128]{1,0:T(8,128)S(1)} %get-tuple-element.60), channel_id=1, source_target_pairs={{0,8},{8,0},{16,24},{24,16},{1,9},{9,1},{17,25},{25,17},{2,10},{10... | collective-permute-start | bytes 405512 | tf_op jit(solution)/shard_map/ppermute | solution.py:344
  50.0 9.4 %collective-permute-start.20 = (f32[264,128]{1,0:T(8,128)S(1)}, f32[264,128]{1,0:T(8,128)S(1)}, u32[]{:S(2)}, u32[]{:S(2)}) collective-permute-start(f32[264,128]{1,0:T(8,128)S(1)} %get-tuple-element.60), channel_id=1, source_target_pairs={{16,0},{8,16},{24,8},{0,24},{17,1},{9,17},{25,9},{1,25},{18,2},{10... | collective-permute-start | bytes 405512 | tf_op jit(solution)/shard_map/ppermute | solution.py:344
  51.7 5.0 %collective-permute-start.16 = (f32[256,128]{1,0:T(8,128)S(1)}, f32[256,128]{1,0:T(8,128)S(1)}, u32[]{:S(2)}, u32[]{:S(2)}) collective-permute-start(f32[256,128]{1,0:T(8,128)S(1)} %get-tuple-element.59.refs_2_), channel_id=1, source_target_pairs={{0,2},{1,3},{2,0},{3,1},{4,6},{5,7},{6,4},{7,5},{8,10},{9,11},{10,... | collective-permute-start | bytes 393224 | tf_op jit(solution)/shard_map/ppermute | solution.py:337
  52.6 5.0 %collective-permute-start.17 = (f32[256,128]{1,0:T(8,128)S(1)}, f32[256,128]{1,0:T(8,128)S(1)}, u32[]{:S(2)}, u32[]{:S(2)}) collective-permute-start(f32[256,128]{1,0:T(8,128)S(1)} %get-tuple-element.59.refs_2_), channel_id=1, source_target_pairs={{0,4},{1,5},{2,6},{3,7},{4,0},{5,1},{6,2},{7,3},{8,12},{9,13},{10,... | collective-permute-start | bytes 393224 | tf_op jit(solution)/shard_map/ppermute | solution.py:337
  53.5 5.9 %collective-permute-start.18 = (f32[256,128]{1,0:T(8,128)S(1)}, f32[256,128]{1,0:T(8,128)S(1)}, u32[]{:S(2)}, u32[]{:S(2)}) collective-permute-start(f32[256,128]{1,0:T(8,128)S(1)} %get-tuple-element.59.refs_2_), channel_id=1, source_target_pairs={{0,6},{1,7},{2,4},{3,5},{4,2},{5,3},{6,0},{7,1},{8,14},{9,15},{10,... | collective-permute-start | bytes 393224 | tf_op jit(solution)/shard_map/ppermute | solution.py:337
  61.3 2.0 %collective-permute-start.21 = (f32[1024,128]{1,0:T(8,128)S(1)}, f32[1024,128]{1,0:T(8,128)S(1)}, u32[]{:S(2)}, u32[]{:S(2)}) collective-permute-start(f32[1024,128]{1,0:T(8,128)S(1)} %get-tuple-element.63), channel_id=1, source_target_pairs={{0,1},{1,0},{2,3},{3,2},{4,5},{5,4},{6,7},{7,6},{8,9},{9,8},{10,11... | collective-permute-start | bytes 1572872 | tf_op jit(solution)/shard_map/ppermute | solution.py:337
  61.4 2.6 %collective-permute-start.22 = (bf16[1024,256]{1,0:T(8,128)(2,1)S(1)}, bf16[1024,256]{1,0:T(8,128)(2,1)S(1)}, u32[]{:S(2)}, u32[]{:S(2)}) collective-permute-start(bf16[1024,256]{1,0:T(8,128)(2,1)S(1)} %get-tuple-element.68.refs_0_.own), channel_id=1, source_target_pairs={{0,1},{1,0},{2,3},{3,2},{4,5},{5,4},{6,7},{7,6},{8,9},{9,8},{10,11... | collective-permute-start | bytes 1572872 | tf_op jit(solution)/shard_map/ppermute | solution.py:337
  65.1 5.5 %collective-permute-start.25 = (f32[8,128]{1,0:T(8,128)S(1)}, f32[8,128]{1,0:T(8,128)S(1)}, u32[]{:S(2)}, u32[]{:S(2)}) collective-permute-start(f32[8,128]{1,0:T(8,128)S(1)} %shard_map.56), channel_id=1, source_target_pairs={{24,0},{0,16},{16,8},{8,24},{25,1},{1,17},{17,9},{9,25},{26,2},{2,... | collective-permute-start | bytes 12296 | tf_op jit(solution)/shard_map/ppermute | solution.py:344
  66.7 3.9 %collective-permute-start.24 = (f32[8,128]{1,0:T(8,128)S(1)}, f32[8,128]{1,0:T(8,128)S(1)}, u32[]{:S(2)}, u32[]{:S(2)}) collective-permute-start(f32[8,128]{1,0:T(8,128)S(1)} %shard_map.56), channel_id=1, source_target_pairs={{8,0},{24,16},{0,8},{16,24},{9,1},{25,17},{1,9},{17,25},{10,2},{26... | collective-permute-start | bytes 12296 | tf_op jit(solution)/shard_map/ppermute | solution.py:344
  66.9 4.5 %collective-permute-start.23 = (f32[8,128]{1,0:T(8,128)S(1)}, f32[8,128]{1,0:T(8,128)S(1)}, u32[]{:S(2)}, u32[]{:S(2)}) collective-permute-start(f32[8,128]{1,0:T(8,128)S(1)} %shard_map.56), channel_id=1, source_target_pairs={{16,0},{8,16},{24,8},{0,24},{17,1},{9,17},{25,9},{1,25},{18,2},{10... | collective-permute-start | bytes 12296 | tf_op jit(solution)/shard_map/ppermute | solution.py:344
  71.4 3.9 %collective-permute-start.26 = (f32[8,128]{1,0:T(8,128)S(1)}, f32[8,128]{1,0:T(8,128)S(1)}, u32[]{:S(2)}, u32[]{:S(2)}) collective-permute-start(f32[8,128]{1,0:T(8,128)S(1)} %add_add_fusion.refs_4_), channel_id=1, source_target_pairs={{0,1},{1,0},{2,3},{3,2},{4,5},{5,4},{6,7},{7,6},{8,9},{9,8},{10,11... | collective-permute-start | bytes 12296 | tf_op jit(solution)/shard_map/ppermute | solution.py:337
  71.4 7.4 %collective-permute-start.27 = (f32[272,128]{1,0:T(8,128)S(1)}, f32[272,128]{1,0:T(8,128)S(1)}, u32[]{:S(2)}, u32[]{:S(2)}) collective-permute-start(f32[272,128]{1,0:T(8,128)S(1)} %get-tuple-element.73.refs_1_), channel_id=1, source_target_pairs={{0,8},{8,0},{16,24},{24,16},{1,9},{9,1},{17,25},{25,17},{2,10},{10... | collective-permute-start | bytes 417800 | tf_op jit(solution)/shard_map/ppermute | solution.py:344
  73.3 8.8 %collective-permute-start.28 = (f32[272,128]{1,0:T(8,128)S(1)}, f32[272,128]{1,0:T(8,128)S(1)}, u32[]{:S(2)}, u32[]{:S(2)}) collective-permute-start(f32[272,128]{1,0:T(8,128)S(1)} %get-tuple-element.74.refs_2_), channel_id=1, source_target_pairs={{24,0},{0,16},{16,8},{8,24},{25,1},{1,17},{17,9},{9,25},{26,2},{2,... | collective-permute-start | bytes 417800 | tf_op jit(solution)/shard_map/ppermute | solution.py:344
  75.3 6.8 %collective-permute-start.29 = (f32[264,128]{1,0:T(8,128)S(1)}, f32[264,128]{1,0:T(8,128)S(1)}, u32[]{:S(2)}, u32[]{:S(2)}) collective-permute-start(f32[264,128]{1,0:T(8,128)S(1)} %get-tuple-element.77), channel_id=1, source_target_pairs={{0,2},{1,3},{2,0},{3,1},{4,6},{5,7},{6,4},{7,5},{8,10},{9,11},{10,... | collective-permute-start | bytes 405512 | tf_op jit(solution)/shard_map/ppermute | solution.py:337
  76.9 8.0 %collective-permute-start.30 = (f32[264,128]{1,0:T(8,128)S(1)}, f32[264,128]{1,0:T(8,128)S(1)}, u32[]{:S(2)}, u32[]{:S(2)}) collective-permute-start(f32[264,128]{1,0:T(8,128)S(1)} %get-tuple-element.78), channel_id=1, source_target_pairs={{0,4},{1,5},{2,6},{3,7},{4,0},{5,1},{6,2},{7,3},{8,12},{9,13},{10,... | collective-permute-start | bytes 405512 | tf_op jit(solution)/shard_map/ppermute | solution.py:337
  77.7 7.2 %collective-permute-start.31 = (f32[264,128]{1,0:T(8,128)S(1)}, f32[264,128]{1,0:T(8,128)S(1)}, u32[]{:S(2)}, u32[]{:S(2)}) collective-permute-start(f32[264,128]{1,0:T(8,128)S(1)} %get-tuple-element.79), channel_id=1, source_target_pairs={{0,6},{1,7},{2,4},{3,5},{4,2},{5,3},{6,0},{7,1},{8,14},{9,15},{10,... | collective-permute-start | bytes 405512 | tf_op jit(solution)/shard_map/ppermute | solution.py:337

commit v5 on v4

--- a/solution.py
+++ b/solution.py
@@ -9,13 +9,13 @@
 
 ITERS = 2
 STAT_ROWS = 8
+WIDE_ROWS = 16
 BACK_ROWS = 16
 VMEM_BYTES = 24 * 1024 * 1024
-PREPARE_BYTES = 62 * 1024 * 1024
+KERNEL_FLOPS = 5.4
 VMEM = pl.BlockSpec(memory_space=pltpu.VMEM)
 SMEM = pl.BlockSpec(memory_space=pltpu.SMEM)
 ANY = pl.BlockSpec(memory_space=pl.ANY)
-HBM = pl.BlockSpec(memory_space=pltpu.HBM)
 BF16 = jnp.bfloat16
 F32 = jnp.float32
 
@@ -24,7 +24,7 @@
     return jax.ShapeDtypeStruct((rows, columns), dtype)
 
 
-def call(body, args, outs, specs=None, scratch=(), flops=0, hidden=False, vmem=None):
+def call(body, args, outs, specs=None, scratch=(), flops=0, hidden=False):
     bytes_accessed = sum(x.size * x.dtype.itemsize for x in list(args) + list(outs))
     if hidden:
         flops = bytes_accessed = 0
@@ -34,7 +34,7 @@
         out_specs=[VMEM] * len(outs),
         out_shape=list(outs),
         scratch_shapes=list(scratch),
-        compiler_params=pltpu.CompilerParams(vmem_limit_bytes=vmem or VMEM_BYTES),
+        compiler_params=pltpu.CompilerParams(vmem_limit_bytes=VMEM_BYTES),
         cost_estimate=pl.CostEstimate(
             flops=flops, bytes_accessed=bytes_accessed, transcendentals=0
         ),
@@ -71,28 +71,12 @@
     out[rows, clusters:] = low
 
 
-def prepare_body(column_ref, features, logits, near, cross, pair, sems):
-    n, clusters = logits.shape
-    width = features.shape[1]
-    start = pl.multiple_of(column_ref[0] * n, n)
-    copies = [
-        pltpu.make_async_copy(
-            features.at[pl.ds(start, n), :],
-            out.at[pl.ds(0, n), pl.ds(0, width)],
-            sems.at[i],
-        )
-        for i, out in enumerate((near, cross))
-    ]
-    for copy in copies:
-        copy.start()
-    rows = slice(0, n)
-    high, low = split(normalize(jnp.exp(logits[...])))
-    for out, at in ((pair, 0), (near, width), (cross, width)):
-        out[rows, at : at + clusters] = high
-        out[rows, at + clusters : at + 2 * clusters] = low
-    cross[n:, :] = jnp.zeros((cross.shape[0] - n, cross.shape[1]), BF16)
-    for copy in copies:
-        copy.wait()
+def prepare_body(logits, unused, pair, wide):
+    n = logits.shape[0]
+    member = normalize(jnp.exp(logits[...]))
+    store_pair(pair, slice(0, n), member)
+    store_pair(wide, slice(0, n), member)
+    wide[n:, :] = jnp.zeros((wide.shape[0] - n, wide.shape[1]), BF16)
 
 
 def kernel_body(order, column_ref, rows_ref, plane_ref, *refs):
@@ -121,17 +105,18 @@
         [column, rows, plane, *after],
         [shaped(n, total, BF16)] * 2,
         [SMEM, VMEM, VMEM] + [ANY] * len(after),
-        hidden=True,
-    )
-
-
-def scores_body(at, pieces, kernels, partials, unused, *refs):
+        flops=int(KERNEL_FLOPS * n) * total * plane.shape[1],
+    )
+
+
+def scores_body(at, pieces, kernels, partials, unused, weights, has_near, *refs):
     members, refs = refs[:pieces], refs[pieces:]
     blocks, refs = refs[:kernels], refs[kernels:]
-    before, outs = refs[:partials], refs[partials + unused :]
+    before, refs = refs[:partials], refs[partials:]
+    own, outs = refs[:weights], refs[weights + unused :]
     n = blocks[0].shape[0]
     clusters = members[0].shape[1] // 2
-    for i, out in enumerate(outs):
+    for i, out in enumerate(outs[: kernels // 2]):
         both, rest, start = None, None, at
         for piece in members:
             columns = slice(start, start + piece.shape[0])
@@ -150,18 +135,35 @@
         out[:n, :] = s
         if out.shape[0] > n:
             out[n:, :] = jnp.zeros((out.shape[0] - n, clusters), F32)
-
-
-def scores_call(at, members, kernels, partials, extra, hidden=False, after=()):
+    if weights:
+        count = len(outs) - 1
+        stat = outs[count]
+        stat_body(has_near, *own[:1], *outs[:count], *own[1:], stat)
+        for out in outs[1:count]:
+            out[n : n + STAT_ROWS, :] = stat[...]
+
+
+def scores_call(
+    at, members, kernels, partials, extra, hidden=False, after=(), weights=(), has_near=0
+):
     n, clusters = kernels[0].shape[0], members[0].shape[1] // 2
     depth = sum(x.shape[0] for x in members)
     return call(
         functools.partial(
-            scores_body, at, len(members), len(kernels), len(partials), len(after)
+            scores_body,
+            at,
+            len(members),
+            len(kernels),
+            len(partials),
+            len(after),
+            len(weights),
+            has_near,
         ),
-        [*members, *kernels, *partials, *after],
-        [shaped(n + e, clusters) for e in extra],
-        [VMEM] * (len(members) + len(kernels) + len(partials)) + [ANY] * len(after),
+        [*members, *kernels, *partials, *weights, *after],
+        [shaped(n + e, clusters) for e in extra]
+        + [shaped(STAT_ROWS, clusters)] * (len(weights) > 0),
+        [VMEM] * (len(members) + len(kernels) + len(partials) + len(weights))
+        + [ANY] * len(after),
         flops=3 * n * len(kernels) * depth * clusters,
         hidden=hidden,
     )
@@ -278,30 +280,34 @@
     )
 
 
-def widen_body(n, *refs):
-    count = (len(refs) - 2) // 2
-    stat = refs[count][...] + refs[count + 1][...]
-    for ref, out in zip(refs[:count], refs[count + 2 :]):
-        out[:n, :] = ref[...]
-        out[n:, :] = stat
-
-
-def widen_call(n, parts, stats):
-    clusters = parts[0].shape[1]
-    return call(
-        functools.partial(widen_body, n),
-        parts + stats,
-        [shaped(n + STAT_ROWS, clusters)] * len(parts),
-    )
+def add_body(*refs):
+    refs, out = refs[:-1], refs[-1]
+    n = out.shape[0]
+    total = refs[0][:n, :]
+    for ref in refs[1:]:
+        total += ref[:n, :]
+    out[...] = total
+
+
+def plane_body(count, *refs):
+    total = refs[0][...]
+    for ref in refs[1:count]:
+        total += ref[...]
+    refs[-1][...] = total
 
 
 def sum_body(n, last, *refs):
     many = 2 if last else 3
     refs, outs = refs[:-many], refs[-many:]
-    total, stat = refs[0][:n, :], refs[0][n:, :]
+    if last:
+        stat = refs[0][...] + refs[1][...]
+        refs = refs[2:]
+    else:
+        stat = refs[0][n:, :]
+    total = refs[0][:n, :]
     for ref in refs[1:]:
         total += ref[:n, :]
-        if ref.shape[0] == n + STAT_ROWS:
+        if not last and ref.shape[0] == n + STAT_ROWS:
             stat += ref[n:, :]
     if last:
         members, standardized = outs
@@ -344,33 +350,27 @@
         return lax.ppermute(x, "row", pairs)
 
     column = jnp.reshape(lax.axis_index("col"), (1,)).astype(jnp.int32)
-    message, wide, pair = call(
+    own_rows = lax.dynamic_slice_in_dim(features, lax.axis_index("col") * n, n, 0)
+    pair, wide = call(
         prepare_body,
-        [column, features, logits],
-        [
-            shaped(n, width + 2 * clusters, BF16),
-            shaped(n + BACK_ROWS, width + 2 * clusters, BF16),
-            shaped(n, 2 * clusters, BF16),
-        ],
-        [SMEM, ANY, VMEM],
-        [pltpu.SemaphoreType.DMA((2,))],
-        vmem=PREPARE_BYTES,
-    )
-    others = [shift(message if d == 0 else wide, d) for d in steps]
+        [logits, own_rows],
+        [shaped(n, 2 * clusters, BF16), shaped(n + WIDE_ROWS, 2 * clusters, BF16)],
+        [VMEM, ANY],
+        hidden=True,
+    )
+    far_rows = [shift(own_rows, d) for d in steps]
+    others = [shift(wide if d else pair, d) for d in steps]
     evens = [pair] + [by_col(pair, k) for k in masks]
     members = evens + [by_col(x, 1) for x in evens]
     early = 1 + has_near
     extra = [0] + [BACK_ROWS] * len(steps)
-    rows_of = [message] + others
-    kernels = []
-    for x in rows_of[:early]:
-        kernels += kernel_call(n, order, column, x, features)
-    scores = scores_call(0, members, kernels, [], extra[:early], True)
-    cross = []
-    for x in rows_of[early:]:
-        cross += kernel_call(n, order, column, x, features, scores)
-    scores += scores_call(0, members, cross, [], extra[early:], True)
-    kernels += cross
+    blocks = [kernel_call(n, order, column, own_rows, features)]
+    for x in reversed(far_rows):
+        blocks.append(kernel_call(n, order, column, x, features, blocks[-1][:1]))
+    blocks = blocks[:1] + blocks[:0:-1]
+    kernels = [x for block in blocks for x in block]
+    cross = kernels[2 * early :]
+    scores = scores_call(0, members, kernels, [], extra, True)
     own = pair
 
     for iteration in range(ITERS):
@@ -383,11 +383,9 @@
         if last:
             t_even, t_odd = other_call(n, half, clusters, others[has_near:], cross, [])
             sent = fold_call(n, t_even, by_col(t_odd, 1), [], 0)
-            scores = scores_call(half, [odd], kernels, scores, extra, after=sent[:1])
-            stat = stat_call(has_near, own, scores, others)
-            for x in [shift(stat, d) for d in range(1, rows)]:
-                stat = stat + x
-            sent = widen_call(n, sent, [stat, by_col(stat, 1)])
+            *scores, stat = scores_call(
+                half, [odd], kernels, scores, extra, False, sent[:1], [own] + others, has_near
+            )
         else:
             if iteration > 0:
                 scores = scores_call(half, [odd], kernels, scores, extra)
@@ -396,12 +394,29 @@
             sent = fold_call(n, t_even, by_col(t_odd, 1), [stat], STAT_ROWS)
         parts = [by_col(x, k) for k, x in zip(masks, sent[1:])]
         back = [shift(x, -d) for d, x in zip(steps, scores[1:])]
+        total = []
+        if last:
+            for x in [shift(stat, d) for d in offsets]:
+                stat = stat + x
+            for x in back:
+                stat = stat + x[n : n + STAT_ROWS]
+            plane = stat
+            sent = call(add_body, [sent[0], scores[0]] + parts, [shaped(n, clusters)])
+            stats = [plane] + [by_col(plane, k) for k in masks]
+            stat = call(
+                functools.partial(plane_body, len(stats)),
+                stats + sent,
+                [shaped(STAT_ROWS, clusters)],
+                [VMEM] * len(stats) + [ANY],
+            )[0]
+            total = [stat, by_col(stat, 1)]
+            parts = []
         outs = [shaped(n, clusters)] * 2
         if not last:
             outs = [shaped(n + STAT_ROWS, clusters), outs[0], shaped(STAT_ROWS, clusters)]
         done = call(
             functools.partial(sum_body, n, last),
-            [sent[0], scores[0]] + back + parts,
+            total + ([sent[0]] if last else [sent[0], scores[0]]) + back + parts,
             outs,
         )
         if not last:

time: 86.1 us -> 77.2 us (0.90)
  waiting for transfers between devices: 30.5 us -> 24.6 us
  Pallas kernels: 13.5 us -> 10.6 us
    ppermute x20 -> x23, waiting for transfers between devices: 17.1 us -> 12.7 us  [by_col(): return lax.ppermute(x, 'col', [(i, i ^ mask) for i in range(cols)])]
    ppermute x12, starting transfers between devices: 22.3 us -> 18.7 us  [shift(): return lax.ppermute(x, 'row', pairs)]
    ppermute x20 -> x23, starting transfers between devices: 15.7 us -> 18.9 us  [by_col(): return lax.ppermute(x, 'col', [(i, i ^ mask) for i in range(cols)])]
    pallas_call x18 -> x17, Pallas kernels: 13.5 us -> 10.6 us  [call(): pl.pallas_call(body, in_specs=specs or [VMEM] * len(args), out_specs=[VME...]
    ppermute x12, waiting for transfers between devices: 13.4 us -> 11.9 us  [shift(): return lax.ppermute(x, 'row', pairs)]
    dynamic_slice x0 -> x1, local copies, waits for them, and re-layouts: none -> 0.97 us  [on_device(): lax.dynamic_slice_in_dim(features, lax.axis_index('col') * n, n, 0)]
    unnamed x8 -> x6, local copies, waits for them, and re-layouts: 2.88 us -> 2.5 us
  transfers between devices with their start and end apart: 32 -> 35, of which waited for: 14 -> 16; matrix products, arithmetic and copies ran while one was open for 0% -> 0% of each run, Pallas kernels for 5% -> 7%
where the time goes in v5:
time: 77.2 us; the launch traced here: 77 us
  starting transfers between devices  37.6 us (49%)
  waiting for transfers between devices  24.6 us (32%)
  Pallas kernels  10.6 us (14%)
  local copies, waits for them, and re-layouts  3.47 us (4%)
  between operations  0.82 us (1%)
    ppermute x23, starting transfers between devices, by_col(): return lax.ppermute(x, 'col', [(i, i ^ mask) for i in range(cols)])  18.9 us
    ppermute x12, starting transfers between devices, shift(): return lax.ppermute(x, 'row', pairs)  18.7 us
    ppermute x23, waiting for transfers between devices, by_col(): return lax.ppermute(x, 'col', [(i, i ^ mask) for i in range(cols)])  12.7 us
    ppermute x12, waiting for transfers between devices, shift(): return lax.ppermute(x, 'row', pairs)  11.9 us
    pallas_call x17, Pallas kernels, call(): pl.pallas_call(body, in_specs=specs or [VMEM] * len(args), out_specs=[VME...  10.6 us
    unnamed x6, local copies, waits for them, and re-layouts  2.5 us
  transfers between devices with their start and end apart: 35, of which 16 were waited for; matrix products, arithmetic and copies ran while one was open for 0% of the time, Pallas kernels for 7%

profile of v5, /device:TPU:0, one launch (start us, length us, event | category | flops | bytes accessed | tf_op | source)
XLA Modules:
  0.0 77.0 jit_solution(14924746977664388791)
XLA Ops:
  0.6 1.0 %constant_dynamic-slice_fusion.unused.rows_ref = bf16[256,512]{1,0:T(8,128)(2,1)S(1)} fusion(bf16[2048,512]{1,0:T(8,128)(2,1)} %plane_ref.5, s32[]{:T(128)S(6)} %select_n.3), kind=kLoop, calls=%fused_computation.2 | loop fusion | bytes 524292 | tf_op jit(solution)/shard_map/dynamic_slice | solution.py:353
  1.6 5.1 %collective-permute-start.1 = (bf16[256,512]{1,0:T(8,128)(2,1)S(1)}, bf16[256,512]{1,0:T(8,128)(2,1)S(1)}, u32[]{:S(2)}, u32[]{:S(2)}) collective-permute-start(bf16[256,512]{1,0:T(8,128)(2,1)S(1)} %constant_dynamic-slice_fusion.unused.rows_ref), channel_id=1, source_target_pairs={{16,0},{8,16},{24,8},{0,24},{17,1},{9,17},{25,9},{1,25},{18,2},{10... | collective-permute-start | bytes 786440 | tf_op jit(solution)/shard_map/ppermute | solution.py:350
  6.7 0.9 %copy-done = f32[256,128]{1,0:T(8,128)S(1)} copy-done((f32[256,128]{1,0:T(8,128)S(1)}, f32[256,128]{1,0:T(8,128)}, u32[]{:S(2)}) %copy-start) | copy-done | bytes 131096
  7.6 0.1 shard_map.41
  7.7 1.6 %collective-permute-start.2 = (bf16[256,256]{1,0:T(8,128)(2,1)S(1)}, bf16[256,256]{1,0:T(8,128)(2,1)S(1)}, u32[]{:S(2)}, u32[]{:S(2)}) collective-permute-start(bf16[256,256]{1,0:T(8,128)(2,1)S(1)} %get-tuple-element.42.refs_0_.own), channel_id=1, source_target_pairs={{0,2},{1,3},{2,0},{3,1},{4,6},{5,7},{6,4},{7,5},{8,10},{9,11},{10,... | collective-permute-start | bytes 393224 | tf_op jit(solution)/shard_map/ppermute | solution.py:343
  9.3 1.5 %collective-permute-start.3 = (bf16[256,256]{1,0:T(8,128)(2,1)S(1)}, bf16[256,256]{1,0:T(8,128)(2,1)S(1)}, u32[]{:S(2)}, u32[]{:S(2)}) collective-permute-start(bf16[256,256]{1,0:T(8,128)(2,1)S(1)} %get-tuple-element.42.refs_0_.own), channel_id=1, source_target_pairs={{0,4},{1,5},{2,6},{3,7},{4,0},{5,1},{6,2},{7,3},{8,12},{9,13},{10,... | collective-permute-start | bytes 393224 | tf_op jit(solution)/shard_map/ppermute | solution.py:343
  10.8 0.5 collective-permute-start.4
  11.3 1.6 %copy-done.1 = bf16[2048,512]{1,0:T(8,128)(2,1)S(1)} copy-done((bf16[2048,512]{1,0:T(8,128)(2,1)S(1)}, bf16[2048,512]{1,0:T(8,128)(2,1)}, u32[]{:S(2)}) %copy-start.1) | copy-done | bytes 2097176
  12.9 0.9 %shard_map.42 = (bf16[256,2048]{1,0:T(8,128)(2,1)S(1)}, bf16[256,2048]{1,0:T(8,128)(2,1)S(1)}) custom-call(s32[1]{0:T(128)} %bitcast.column_ref, bf16[256,512]{1,0:T(8,128)(2,1)S(1)} %constant_dynamic-slice_fusion.unused.rows_ref, bf16[2048,512]{1,0:T(8,128)(2,1)S(1)} %copy-done.1), custom_call_target="tpu_custom_call" | custom-call | flops 1449132032 | bytes 4456452 | tf_op jit(solution)/shard_map/pallas_call | solution.py:31
  13.8 0.1 collective-permute-start.5
  13.9 3.9 %collective-permute-done.1.rows_ref = bf16[256,512]{1,0:T(8,128)(2,1)S(1)} collective-permute-done((bf16[256,512]{1,0:T(8,128)(2,1)S(1)}, bf16[256,512]{1,0:T(8,128)(2,1)S(1)}, u32[]{:S(2)}, u32[]{:S(2)}) %collective-permute-start.1) | collective-permute-done | bytes 262176 | tf_op jit(solution)/shard_map/ppermute | solution.py:350
  17.7 0.9 %shard_map.43 = (bf16[256,2048]{1,0:T(8,128)(2,1)S(1)}, bf16[256,2048]{1,0:T(8,128)(2,1)S(1)}) custom-call(s32[1]{0:T(128)} %bitcast.column_ref, bf16[256,512]{1,0:T(8,128)(2,1)S(1)} %collective-permute-done.1.rows_ref, bf16[2048,512]{1,0:T(8,128)(2,1)S(1)} %copy-done.2, bf16[256,2048]{1,0:T(8,128)(2,1)S(1)} %get-tuple-element.39.refs_0_.refs_8_.refs_1_), custom_call_target="tpu_custom_call" | custom-call | flops 1449132032 | bytes 5505028 | tf_op jit(solution)/shard_map/pallas_call | solution.py:31
  18.6 2.3 %collective-permute-start.10 = (bf16[256,256]{1,0:T(8,128)(2,1)S(1)}, bf16[256,256]{1,0:T(8,128)(2,1)S(1)}, u32[]{:S(2)}, u32[]{:S(2)}) collective-permute-start(bf16[256,256]{1,0:T(8,128)(2,1)S(1)} %get-tuple-element.42.refs_0_.own), channel_id=1, source_target_pairs={{0,8},{8,0},{16,24},{24,16},{1,9},{9,1},{17,25},{25,17},{2,10},{10... | collective-permute-start | bytes 393224 | tf_op jit(solution)/shard_map/ppermute | solution.py:350
  20.9 0.5 collective-permute-start.7
  21.4 0.1 collective-permute-start.8
  21.5 0.9 %shard_map.44 = (bf16[256,2048]{1,0:T(8,128)(2,1)S(1)}, bf16[256,2048]{1,0:T(8,128)(2,1)S(1)}) custom-call(s32[1]{0:T(128)} %bitcast.column_ref, bf16[256,512]{1,0:T(8,128)(2,1)S(1)} %collective-permute-done.9.rows_ref, bf16[2048,512]{1,0:T(8,128)(2,1)S(1)} %copy-done.2, bf16[256,2048]{1,0:T(8,128)(2,1)S(1)} %get-tuple-element.40.refs_0_.refs_12_.refs_1_.refs_5_), custom_call_target="tpu_custom_call" | custom-call | flops 1449132032 | bytes 5505028 | tf_op jit(solution)/shard_map/pallas_call | solution.py:31
  22.4 0.3 collective-permute-done.8.refs_7_
  22.7 1.8 %shard_map.45 = (f32[256,128]{1,0:T(8,128)S(1)}, f32[272,128]{1,0:T(8,128)S(1)}, f32[272,128]{1,0:T(8,128)S(1)}) custom-call(bf16[256,256]{1,0:T(8,128)(2,1)S(1)} %get-tuple-element.42.refs_0_.own, bf16[256,256]{1,0:T(8,128)(2,1)S(1)} %collective-permute-done.2.refs_1_, bf16[256,256]{1,0:T(8,128)(2,1)S(1)} %collective-permute-done.3.refs_2_, ...), custom_call_target="tpu_custom_call" | custom-call | tf_op jit(solution)/shard_map/pallas_call | solution.py:31
  24.6 1.7 %collective-permute-done.10.refs_3_ = bf16[256,256]{1,0:T(8,128)(2,1)S(1)} collective-permute-done((bf16[256,256]{1,0:T(8,128)(2,1)S(1)}, bf16[256,256]{1,0:T(8,128)(2,1)S(1)}, u32[]{:S(2)}, u32[]{:S(2)}) %collective-permute-start.10) | collective-permute-done | bytes 131104 | tf_op jit(solution)/shard_map/ppermute | solution.py:350
  26.3 0.1 shard_map.46.refs_3_.refs_0_
  26.4 0.8 %shard_map.47 = (f32[1024,128]{1,0:T(8,128)S(1)}, f32[1032,128]{1,0:T(8,128)S(1)}) custom-call(bf16[272,256]{1,0:T(8,128)(2,1)S(1)} %collective-permute-done.refs_4_.refs_0_, bf16[256,2048]{1,0:T(8,128)(2,1)S(1)} %get-tuple-element.40.refs_0_.refs_12_.refs_1_.refs_5_, bf16[256,2048]{1,0:T(8,128)(2,1)S(1)} %get-tuple-element.41.refs_13_.refs_2_.refs_6_, ...), custom_call_target="tpu_custom_call" | custom-call | flops 402653184 | bytes 3293184 | tf_op jit(solution)/shard_map/pallas_call | solution.py:31
  27.2 0.1 collective-permute-start.11
  27.3 0.1 collective-permute-start.12
  27.3 2.4 %collective-permute-start.13 = (f32[272,128]{1,0:T(8,128)S(1)}, f32[272,128]{1,0:T(8,128)S(1)}, u32[]{:S(2)}, u32[]{:S(2)}) collective-permute-start(f32[272,128]{1,0:T(8,128)S(1)} %get-tuple-element.48.refs_2_), channel_id=1, source_target_pairs={{24,0},{0,16},{16,8},{8,24},{25,1},{1,17},{17,9},{9,25},{26,2},{2,... | collective-permute-start | bytes 417800 | tf_op jit(solution)/shard_map/ppermute | solution.py:350
  29.7 0.1 shard_map.48
  29.8 1.3 %collective-permute-start.14 = (f32[264,128]{1,0:T(8,128)S(1)}, f32[264,128]{1,0:T(8,128)S(1)}, u32[]{:S(2)}, u32[]{:S(2)}) collective-permute-start(f32[264,128]{1,0:T(8,128)S(1)} %get-tuple-element.52), channel_id=1, source_target_pairs={{0,2},{1,3},{2,0},{3,1},{4,6},{5,7},{6,4},{7,5},{8,10},{9,11},{10,... | collective-permute-start | bytes 405512 | tf_op jit(solution)/shard_map/ppermute | solution.py:343
  31.0 1.5 %collective-permute-start.15 = (f32[264,128]{1,0:T(8,128)S(1)}, f32[264,128]{1,0:T(8,128)S(1)}, u32[]{:S(2)}, u32[]{:S(2)}) collective-permute-start(f32[264,128]{1,0:T(8,128)S(1)} %get-tuple-element.53), channel_id=1, source_target_pairs={{0,4},{1,5},{2,6},{3,7},{4,0},{5,1},{6,2},{7,3},{8,12},{9,13},{10,... | collective-permute-start | bytes 405512 | tf_op jit(solution)/shard_map/ppermute | solution.py:343
  32.6 0.8 collective-permute-start.16
  33.3 0.3 collective-permute-done.12.refs_2_
  33.6 2.9 %collective-permute-done.13.refs_3_ = f32[272,128]{1,0:T(8,128)S(1)} collective-permute-done((f32[272,128]{1,0:T(8,128)S(1)}, f32[272,128]{1,0:T(8,128)S(1)}, u32[]{:S(2)}, u32[]{:S(2)}) %collective-permute-start.13) | collective-permute-done | bytes 139296 | tf_op jit(solution)/shard_map/ppermute | solution.py:350
  36.5 2.5 %collective-permute-done.15.refs_5_ = f32[264,128]{1,0:T(8,128)S(1)} collective-permute-done((f32[264,128]{1,0:T(8,128)S(1)}, f32[264,128]{1,0:T(8,128)S(1)}, u32[]{:S(2)}, u32[]{:S(2)}) %collective-permute-start.15) | collective-permute-done | bytes 135200 | tf_op jit(solution)/shard_map/ppermute | solution.py:343
  39.0 0.1 shard_map.49
  39.1 1.5 %collective-permute-start.17 = (f32[8,128]{1,0:T(8,128)S(1)}, f32[8,128]{1,0:T(8,128)S(1)}, u32[]{:S(2)}, u32[]{:S(2)}) collective-permute-start(f32[8,128]{1,0:T(8,128)S(1)} %get-tuple-element.55.refs_0_), channel_id=1, source_target_pairs={{24,0},{0,16},{16,8},{8,24},{25,1},{1,17},{17,9},{9,25},{26,2},{2,... | collective-permute-start | bytes 12296 | tf_op jit(solution)/shard_map/ppermute | solution.py:350
  40.6 1.2 %collective-permute-start.21 = (f32[264,128]{1,0:T(8,128)S(1)}, f32[264,128]{1,0:T(8,128)S(1)}, u32[]{:S(2)}, u32[]{:S(2)}) collective-permute-start(f32[264,128]{1,0:T(8,128)S(1)} %get-tuple-element.57), channel_id=1, source_target_pairs={{0,8},{8,0},{16,24},{24,16},{1,9},{9,1},{17,25},{25,17},{2,10},{10... | collective-permute-start | bytes 405512 | tf_op jit(solution)/shard_map/ppermute | solution.py:350
  41.7 1.3 %collective-permute-start.22 = (f32[264,128]{1,0:T(8,128)S(1)}, f32[264,128]{1,0:T(8,128)S(1)}, u32[]{:S(2)}, u32[]{:S(2)}) collective-permute-start(f32[264,128]{1,0:T(8,128)S(1)} %get-tuple-element.57), channel_id=1, source_target_pairs={{16,0},{8,16},{24,8},{0,24},{17,1},{9,17},{25,9},{1,25},{18,2},{10... | collective-permute-start | bytes 405512 | tf_op jit(solution)/shard_map/ppermute | solution.py:350
  43.0 1.2 %collective-permute-start.18 = (f32[256,128]{1,0:T(8,128)S(1)}, f32[256,128]{1,0:T(8,128)S(1)}, u32[]{:S(2)}, u32[]{:S(2)}) collective-permute-start(f32[256,128]{1,0:T(8,128)S(1)} %get-tuple-element.56.refs_2_), channel_id=1, source_target_pairs={{0,2},{1,3},{2,0},{3,1},{4,6},{5,7},{6,4},{7,5},{8,10},{9,11},{10,... | collective-permute-start | bytes 393224 | tf_op jit(solution)/shard_map/ppermute | solution.py:343
  44.2 0.8 %collective-permute-start.19 = (f32[256,128]{1,0:T(8,128)S(1)}, f32[256,128]{1,0:T(8,128)S(1)}, u32[]{:S(2)}, u32[]{:S(2)}) collective-permute-start(f32[256,128]{1,0:T(8,128)S(1)} %get-tuple-element.56.refs_2_), channel_id=1, source_target_pairs={{0,4},{1,5},{2,6},{3,7},{4,0},{5,1},{6,2},{7,3},{8,12},{9,13},{10,... | collective-permute-start | bytes 393224 | tf_op jit(solution)/shard_map/ppermute | solution.py:343
  45.1 1.4 %collective-permute-start.20 = (f32[256,128]{1,0:T(8,128)S(1)}, f32[256,128]{1,0:T(8,128)S(1)}, u32[]{:S(2)}, u32[]{:S(2)}) collective-permute-start(f32[256,128]{1,0:T(8,128)S(1)} %get-tuple-element.56.refs_2_), channel_id=1, source_target_pairs={{0,6},{1,7},{2,4},{3,5},{4,2},{5,3},{6,0},{7,1},{8,14},{9,15},{10,... | collective-permute-start | bytes 393224 | tf_op jit(solution)/shard_map/ppermute | solution.py:343
  46.5 2.5 %collective-permute-done.18.refs_3_ = f32[256,128]{1,0:T(8,128)S(1)} collective-permute-done((f32[256,128]{1,0:T(8,128)S(1)}, f32[256,128]{1,0:T(8,128)S(1)}, u32[]{:S(2)}, u32[]{:S(2)}) %collective-permute-start.18) | collective-permute-done | bytes 131104 | tf_op jit(solution)/shard_map/ppermute | solution.py:343
  49.0 0.2 collective-permute-done.19.refs_4_
  49.2 1.7 %collective-permute-done.20.refs_5_ = f32[256,128]{1,0:T(8,128)S(1)} collective-permute-done((f32[256,128]{1,0:T(8,128)S(1)}, f32[256,128]{1,0:T(8,128)S(1)}, u32[]{:S(2)}, u32[]{:S(2)}) %collective-permute-start.20) | collective-permute-done | bytes 131104 | tf_op jit(solution)/shard_map/ppermute | solution.py:343
  50.9 1.2 %shard_map.50 = (bf16[1024,256]{1,0:T(8,128)(2,1)S(1)}, bf16[256,256]{1,0:T(8,128)(2,1)S(1)}, bf16[256,256]{1,0:T(8,128)(2,1)S(1)}) custom-call(f32[8,128]{1,0:T(8,128)S(1)} %get-tuple-element.55.refs_0_, f32[8,128]{1,0:T(8,128)S(1)} %collective-permute-done.17.refs_1_, f32[256,128]{1,0:T(8,128)S(1)} %get-tuple-element.56.refs_2_, ...), custom_call_target="tpu_custom_call" | custom-call | bytes 1589248 | tf_op jit(solution)/shard_map/pallas_call | solution.py:31
  52.1 0.8 %shard_map.52 = (f32[1024,128]{1,0:T(8,128)S(1)}, f32[1024,128]{1,0:T(8,128)S(1)}) custom-call(bf16[256,256]{1,0:T(8,128)(2,1)S(1)} %get-tuple-element.63.refs_0_.refs_12_, bf16[256,2048]{1,0:T(8,128)(2,1)S(1)} %get-tuple-element.40.refs_0_.refs_12_.refs_1_.refs_5_, bf16[256,2048]{1,0:T(8,128)(2,1)S(1)} %get-tuple-element.41.refs_13_.refs_2_.refs_6_), custom_call_target="tpu_custom_call" | custom-call | flops 402653184 | bytes 3276800 | tf_op jit(solution)/shard_map/pallas_call | solution.py:31
  52.9 0.1 collective-permute-start.24
  53.0 0.5 collective-permute-start.23
  53.5 1.0 %shard_map.51 = (f32[256,128]{1,0:T(8,128)S(1)}, f32[272,128]{1,0:T(8,128)S(1)}, f32[272,128]{1,0:T(8,128)S(1)}) custom-call(bf16[1024,256]{1,0:T(8,128)(2,1)S(1)} %get-tuple-element.58.refs_0_.refs_10_, bf16[256,2048]{1,0:T(8,128)(2,1)S(1)} %get-tuple-element.39.refs_0_.refs_8_.refs_1_, bf16[256,2048]{1,0:T(8,128)(2,1)S(1)} %get-tuple-element.43.refs_9_.refs_2_, ...), custom_call_target="tpu_custom_call" | custom-call | flops 603979776 | bytes 7225344 | tf_op jit(solution)/shard_map/pallas_call | solution.py:31
  54.5 0.4 collective-permute-done.24.received
  55.0 0.7 collective-permute-done.23.refs_0_
  55.6 1.0 %shard_map.54 = (f32[256,128]{1,0:T(8,128)S(1)}, f32[272,128]{1,0:T(8,128)S(1)}, f32[272,128]{1,0:T(8,128)S(1)}, f32[8,128]{1,0:T(8,128)S(1)}) custom-call(bf16[1024,256]{1,0:T(8,128)(2,1)S(1)} %collective-permute-done.23.refs_0_, bf16[256,2048]{1,0:T(8,128)(2,1)S(1)} %get-tuple-element.39.refs_0_.refs_8_.refs_1_, ...), custom_call_target="tpu_custom_call" | custom-call | flops 603979776 | bytes 8556544 | tf_op jit(solution)/shard_map/pallas_call | solution.py:31
  56.7 1.2 %collective-permute-start.26 = (f32[272,128]{1,0:T(8,128)S(1)}, f32[272,128]{1,0:T(8,128)S(1)}, u32[]{:S(2)}, u32[]{:S(2)}) collective-permute-start(f32[272,128]{1,0:T(8,128)S(1)} %get-tuple-element.68), channel_id=1, source_target_pairs={{0,8},{8,0},{16,24},{24,16},{1,9},{9,1},{17,25},{25,17},{2,10},{10... | collective-permute-start | bytes 417800 | tf_op jit(solution)/shard_map/ppermute | solution.py:350
  57.9 1.3 %collective-permute-start.27 = (f32[272,128]{1,0:T(8,128)S(1)}, f32[272,128]{1,0:T(8,128)S(1)}, u32[]{:S(2)}, u32[]{:S(2)}) collective-permute-start(f32[272,128]{1,0:T(8,128)S(1)} %get-tuple-element.69), channel_id=1, source_target_pairs={{24,0},{0,16},{16,8},{8,24},{25,1},{1,17},{17,9},{9,25},{26,2},{2,... | collective-permute-start | bytes 417800 | tf_op jit(solution)/shard_map/ppermute | solution.py:350
  59.2 2.5 %collective-permute-start.25 = (f32[8,128]{1,0:T(8,128)S(1)}, f32[8,128]{1,0:T(8,128)S(1)}, u32[]{:S(2)}, u32[]{:S(2)}) collective-permute-start(f32[8,128]{1,0:T(8,128)S(1)} %get-tuple-element.67), channel_id=1, source_target_pairs={{16,0},{8,16},{24,8},{0,24},{17,1},{9,17},{25,9},{1,25},{18,2},{10... | collective-permute-start | bytes 12296 | tf_op jit(solution)/shard_map/ppermute | solution.py:350
  61.7 1.5 %collective-permute-start.31 = (f32[256,128]{1,0:T(8,128)S(1)}, f32[256,128]{1,0:T(8,128)S(1)}, u32[]{:S(2)}, u32[]{:S(2)}) collective-permute-start(f32[256,128]{1,0:T(8,128)S(1)} %get-tuple-element.71), channel_id=1, source_target_pairs={{0,2},{1,3},{2,0},{3,1},{4,6},{5,7},{6,4},{7,5},{8,10},{9,11},{10,... | collective-permute-start | bytes 393224 | tf_op jit(solution)/shard_map/ppermute | solution.py:343
  63.2 0.5 collective-permute-start.32
  63.7 3.1 %collective-permute-done.25 = f32[8,128]{1,0:T(8,128)S(1)} collective-permute-done((f32[8,128]{1,0:T(8,128)S(1)}, f32[8,128]{1,0:T(8,128)S(1)}, u32[]{:S(2)}, u32[]{:S(2)}) %collective-permute-start.25) | collective-permute-done | bytes 4128 | tf_op jit(solution)/shard_map/ppermute | solution.py:350
  66.8 1.4 %collective-permute-start.33 = (f32[256,128]{1,0:T(8,128)S(1)}, f32[256,128]{1,0:T(8,128)S(1)}, u32[]{:S(2)}, u32[]{:S(2)}) collective-permute-start(f32[256,128]{1,0:T(8,128)S(1)} %get-tuple-element.73), channel_id=1, source_target_pairs={{0,6},{1,7},{2,4},{3,5},{4,2},{5,3},{6,0},{7,1},{8,14},{9,15},{10,... | collective-permute-start | bytes 393224 | tf_op jit(solution)/shard_map/ppermute | solution.py:343
  68.2 1.4 %collective-permute-start.28 = (f32[8,128]{1,0:T(8,128)S(1)}, f32[8,128]{1,0:T(8,128)S(1)}, u32[]{:S(2)}, u32[]{:S(2)}) collective-permute-start(f32[8,128]{1,0:T(8,128)S(1)} %slice_add_fusion.refs_0_), channel_id=1, source_target_pairs={{0,2},{1,3},{2,0},{3,1},{4,6},{5,7},{6,4},{7,5},{8,10},{9,11},{10,... | collective-permute-start | bytes 12296 | tf_op jit(solution)/shard_map/ppermute | solution.py:343
  69.6 0.7 collective-permute-start.29
  70.4 1.4 %collective-permute-start.30 = (f32[8,128]{1,0:T(8,128)S(1)}, f32[8,128]{1,0:T(8,128)S(1)}, u32[]{:S(2)}, u32[]{:S(2)}) collective-permute-start(f32[8,128]{1,0:T(8,128)S(1)} %slice_add_fusion.refs_0_), channel_id=1, source_target_pairs={{0,6},{1,7},{2,4},{3,5},{4,2},{5,3},{6,0},{7,1},{8,14},{9,15},{10,... | collective-permute-start | bytes 12296 | tf_op jit(solution)/shard_map/ppermute | solution.py:343
  71.8 0.9 %collective-permute-done.33.refs_4_ = f32[256,128]{1,0:T(8,128)S(1)} collective-permute-done((f32[256,128]{1,0:T(8,128)S(1)}, f32[256,128]{1,0:T(8,128)S(1)}, u32[]{:S(2)}, u32[]{:S(2)}) %collective-permute-start.33) | collective-permute-done | bytes 131104 | tf_op jit(solution)/shard_map/ppermute | solution.py:343
  72.7 0.5 collective-permute-done.29.refs_2_
  73.2 1.6 %collective-permute-done.30.refs_3_ = f32[8,128]{1,0:T(8,128)S(1)} collective-permute-done((f32[8,128]{1,0:T(8,128)S(1)}, f32[8,128]{1,0:T(8,128)S(1)}, u32[]{:S(2)}, u32[]{:S(2)}) %collective-permute-start.30) | collective-permute-done | bytes 4128 | tf_op jit(solution)/shard_map/ppermute | solution.py:343
  74.9 1.2 %collective-permute-done.34.refs_1_ = f32[8,128]{1,0:T(8,128)S(1)} collective-permute-done((f32[8,128]{1,0:T(8,128)S(1)}, f32[8,128]{1,0:T(8,128)S(1)}, u32[]{:S(2)}, u32[]{:S(2)}) %collective-permute-start.34) | collective-permute-done | bytes 4128 | tf_op jit(solution)/shard_map/ppermute | solution.py:343
  76.0 1.0 %shard_map.57 = (f32[256,128]{1,0:T(8,128)}, f32[256,128]{1,0:T(8,128)}) custom-call(f32[8,128]{1,0:T(8,128)S(1)} %shard_map.56.refs_0_, f32[8,128]{1,0:T(8,128)S(1)} %collective-permute-done.34.refs_1_, f32[256,128]{1,0:T(8,128)S(1)} %shard_map.55.refs_4_.refs_2_, f32[272,128]{1,0:T(8,128)S(1)} %collective-permute-done.26.refs_3_, ...), custom_call_target="tpu_custom_call" | custom-call | bytes 679936 | tf_op jit(solution)/shard_map/pallas_call | solution.py:31
  (31 shorter events, 0.2 us)
Async XLA Ops:
  1.6 16.1 %collective-permute-start.1 = (bf16[256,512]{1,0:T(8,128)(2,1)S(1)}, bf16[256,512]{1,0:T(8,128)(2,1)S(1)}, u32[]{:S(2)}, u32[]{:S(2)}) collective-permute-start(bf16[256,512]{1,0:T(8,128)(2,1)S(1)} %constant_dynamic-slice_fusion.unused.rows_ref), channel_id=1, source_target_pairs={{16,0},{8,16},{24,8},{0,24},{17,1},{9,17},{25,9},{1,25},{18,2},{10... | collective-permute-start | bytes 786440 | tf_op jit(solution)/shard_map/ppermute | solution.py:350
  6.7 14.7 %collective-permute-start.9 = (bf16[256,512]{1,0:T(8,128)(2,1)S(1)}, bf16[256,512]{1,0:T(8,128)(2,1)S(1)}, u32[]{:S(2)}, u32[]{:S(2)}) collective-permute-start(bf16[256,512]{1,0:T(8,128)(2,1)S(1)} %constant_dynamic-slice_fusion.unused.rows_ref), channel_id=1, source_target_pairs={{0,8},{8,0},{16,24},{24,16},{1,9},{9,1},{17,25},{25,17},{2,10},{10... | collective-permute-start | bytes 786440 | tf_op jit(solution)/shard_map/ppermute | solution.py:350
  6.7 0.9 %copy-start = (f32[256,128]{1,0:T(8,128)S(1)}, f32[256,128]{1,0:T(8,128)}, u32[]{:S(2)}) copy-start(f32[256,128]{1,0:T(8,128)} %logits.1) | copy-start | bytes 393220
  7.7 6.0 %collective-permute-start.2 = (bf16[256,256]{1,0:T(8,128)(2,1)S(1)}, bf16[256,256]{1,0:T(8,128)(2,1)S(1)}, u32[]{:S(2)}, u32[]{:S(2)}) collective-permute-start(bf16[256,256]{1,0:T(8,128)(2,1)S(1)} %get-tuple-element.42.refs_0_.own), channel_id=1, source_target_pairs={{0,2},{1,3},{2,0},{3,1},{4,6},{5,7},{6,4},{7,5},{8,10},{9,11},{10,... | collective-permute-start | bytes 393224 | tf_op jit(solution)/shard_map/ppermute | solution.py:343
  9.3 9.3 %collective-permute-start.3 = (bf16[256,256]{1,0:T(8,128)(2,1)S(1)}, bf16[256,256]{1,0:T(8,128)(2,1)S(1)}, u32[]{:S(2)}, u32[]{:S(2)}) collective-permute-start(bf16[256,256]{1,0:T(8,128)(2,1)S(1)} %get-tuple-element.42.refs_0_.own), channel_id=1, source_target_pairs={{0,4},{1,5},{2,6},{3,7},{4,0},{5,1},{6,2},{7,3},{8,12},{9,13},{10,... | collective-permute-start | bytes 393224 | tf_op jit(solution)/shard_map/ppermute | solution.py:343
  10.8 10.1 %collective-permute-start.4 = (bf16[256,256]{1,0:T(8,128)(2,1)S(1)}, bf16[256,256]{1,0:T(8,128)(2,1)S(1)}, u32[]{:S(2)}, u32[]{:S(2)}) collective-permute-start(bf16[256,256]{1,0:T(8,128)(2,1)S(1)} %get-tuple-element.42.refs_0_.own), channel_id=1, source_target_pairs={{0,6},{1,7},{2,4},{3,5},{4,2},{5,3},{6,0},{7,1},{8,14},{9,15},{10,... | collective-permute-start | bytes 393224 | tf_op jit(solution)/shard_map/ppermute | solution.py:343
  11.3 1.6 %copy-start.1 = (bf16[2048,512]{1,0:T(8,128)(2,1)S(1)}, bf16[2048,512]{1,0:T(8,128)(2,1)}, u32[]{:S(2)}) copy-start(bf16[2048,512]{1,0:T(8,128)(2,1)} %plane_ref.5) | copy-start | bytes 6291460
  12.9 4.8 %copy-start.2 = (bf16[2048,512]{1,0:T(8,128)(2,1)S(1)}, bf16[2048,512]{1,0:T(8,128)(2,1)}, u32[]{:S(2)}) copy-start(bf16[2048,512]{1,0:T(8,128)(2,1)} %plane_ref.5) | copy-start | bytes 6291460
  13.8 7.1 %collective-permute-start.5 = (bf16[256,256]{1,0:T(8,128)(2,1)S(1)}, bf16[256,256]{1,0:T(8,128)(2,1)S(1)}, u32[]{:S(2)}, u32[]{:S(2)}) collective-permute-start(bf16[256,256]{1,0:T(8,128)(2,1)S(1)} %get-tuple-element.42.refs_0_.own), channel_id=1, source_target_pairs={{0,1},{1,0},{2,3},{3,2},{4,5},{5,4},{6,7},{7,6},{8,9},{9,8},{10,11... | collective-permute-start | bytes 393224 | tf_op jit(solution)/shard_map/ppermute | solution.py:343
  17.7 8.6 %collective-permute-start = (bf16[272,256]{1,0:T(8,128)(2,1)S(1)}, bf16[272,256]{1,0:T(8,128)(2,1)S(1)}, u32[]{:S(2)}, u32[]{:S(2)}) collective-permute-start(bf16[272,256]{1,0:T(8,128)(2,1)S(1)} %get-tuple-element.38), channel_id=1, source_target_pairs={{16,0},{8,16},{24,8},{0,24},{17,1},{9,17},{25,9},{1,25},{18,2},{10... | collective-permute-start | bytes 417800 | tf_op jit(solution)/shard_map/ppermute | solution.py:350
  18.6 7.7 %collective-permute-start.10 = (bf16[256,256]{1,0:T(8,128)(2,1)S(1)}, bf16[256,256]{1,0:T(8,128)(2,1)S(1)}, u32[]{:S(2)}, u32[]{:S(2)}) collective-permute-start(bf16[256,256]{1,0:T(8,128)(2,1)S(1)} %get-tuple-element.42.refs_0_.own), channel_id=1, source_target_pairs={{0,8},{8,0},{16,24},{24,16},{1,9},{9,1},{17,25},{25,17},{2,10},{10... | collective-permute-start | bytes 393224 | tf_op jit(solution)/shard_map/ppermute | solution.py:350
  20.9 1.5 %collective-permute-start.6 = (bf16[256,256]{1,0:T(8,128)(2,1)S(1)}, bf16[256,256]{1,0:T(8,128)(2,1)S(1)}, u32[]{:S(2)}, u32[]{:S(2)}) collective-permute-start(bf16[256,256]{1,0:T(8,128)(2,1)S(1)} %collective-permute-done.2.refs_1_), channel_id=1, source_target_pairs={{0,1},{1,0},{2,3},{3,2},{4,5},{5,4},{6,7},{7,6},{8,9},{9,8},{10,11... | collective-permute-start | bytes 393224 | tf_op jit(solution)/shard_map/ppermute | solution.py:343
  20.9 1.5 %collective-permute-start.7 = (bf16[256,256]{1,0:T(8,128)(2,1)S(1)}, bf16[256,256]{1,0:T(8,128)(2,1)S(1)}, u32[]{:S(2)}, u32[]{:S(2)}) collective-permute-start(bf16[256,256]{1,0:T(8,128)(2,1)S(1)} %collective-permute-done.3.refs_2_), channel_id=1, source_target_pairs={{0,1},{1,0},{2,3},{3,2},{4,5},{5,4},{6,7},{7,6},{8,9},{9,8},{10,11... | collective-permute-start | bytes 393224 | tf_op jit(solution)/shard_map/ppermute | solution.py:343
  21.4 1.3 %collective-permute-start.8 = (bf16[256,256]{1,0:T(8,128)(2,1)S(1)}, bf16[256,256]{1,0:T(8,128)(2,1)S(1)}, u32[]{:S(2)}, u32[]{:S(2)}) collective-permute-start(bf16[256,256]{1,0:T(8,128)(2,1)S(1)} %collective-permute-done.4.refs_3_), channel_id=1, source_target_pairs={{0,1},{1,0},{2,3},{3,2},{4,5},{5,4},{6,7},{7,6},{8,9},{9,8},{10,11... | collective-permute-start | bytes 393224 | tf_op jit(solution)/shard_map/ppermute | solution.py:343
  27.2 2.5 %collective-permute-start.11 = (f32[1032,128]{1,0:T(8,128)S(1)}, f32[1032,128]{1,0:T(8,128)S(1)}, u32[]{:S(2)}, u32[]{:S(2)}) collective-permute-start(f32[1032,128]{1,0:T(8,128)S(1)} %get-tuple-element.50), channel_id=1, source_target_pairs={{0,1},{1,0},{2,3},{3,2},{4,5},{5,4},{6,7},{7,6},{8,9},{9,8},{10,11... | collective-permute-start | bytes 1585160 | tf_op jit(solution)/shard_map/ppermute | solution.py:343
  27.3 6.4 %collective-permute-start.12 = (f32[272,128]{1,0:T(8,128)S(1)}, f32[272,128]{1,0:T(8,128)S(1)}, u32[]{:S(2)}, u32[]{:S(2)}) collective-permute-start(f32[272,128]{1,0:T(8,128)S(1)} %get-tuple-element.47.refs_1_), channel_id=1, source_target_pairs={{0,8},{8,0},{16,24},{24,16},{1,9},{9,1},{17,25},{25,17},{2,10},{10... | collective-permute-start | bytes 417800 | tf_op jit(solution)/shard_map/ppermute | solution.py:350
  27.3 9.2 %collective-permute-start.13 = (f32[272,128]{1,0:T(8,128)S(1)}, f32[272,128]{1,0:T(8,128)S(1)}, u32[]{:S(2)}, u32[]{:S(2)}) collective-permute-start(f32[272,128]{1,0:T(8,128)S(1)} %get-tuple-element.48.refs_2_), channel_id=1, source_target_pairs={{24,0},{0,16},{16,8},{8,24},{25,1},{1,17},{17,9},{9,25},{26,2},{2,... | collective-permute-start | bytes 417800 | tf_op jit(solution)/shard_map/ppermute | solution.py:350
  29.8 6.7 %collective-permute-start.14 = (f32[264,128]{1,0:T(8,128)S(1)}, f32[264,128]{1,0:T(8,128)S(1)}, u32[]{:S(2)}, u32[]{:S(2)}) collective-permute-start(f32[264,128]{1,0:T(8,128)S(1)} %get-tuple-element.52), channel_id=1, source_target_pairs={{0,2},{1,3},{2,0},{3,1},{4,6},{5,7},{6,4},{7,5},{8,10},{9,11},{10,... | collective-permute-start | bytes 405512 | tf_op jit(solution)/shard_map/ppermute | solution.py:343
  31.0 8.0 %collective-permute-start.15 = (f32[264,128]{1,0:T(8,128)S(1)}, f32[264,128]{1,0:T(8,128)S(1)}, u32[]{:S(2)}, u32[]{:S(2)}) collective-permute-start(f32[264,128]{1,0:T(8,128)S(1)} %get-tuple-element.53), channel_id=1, source_target_pairs={{0,4},{1,5},{2,6},{3,7},{4,0},{5,1},{6,2},{7,3},{8,12},{9,13},{10,... | collective-permute-start | bytes 405512 | tf_op jit(solution)/shard_map/ppermute | solution.py:343
  32.6 6.5 %collective-permute-start.16 = (f32[264,128]{1,0:T(8,128)S(1)}, f32[264,128]{1,0:T(8,128)S(1)}, u32[]{:S(2)}, u32[]{:S(2)}) collective-permute-start(f32[264,128]{1,0:T(8,128)S(1)} %get-tuple-element.54), channel_id=1, source_target_pairs={{0,6},{1,7},{2,4},{3,5},{4,2},{5,3},{6,0},{7,1},{8,14},{9,15},{10,... | collective-permute-start | bytes 405512 | tf_op jit(solution)/shard_map/ppermute | solution.py:343
  39.1 5.9 %collective-permute-start.17 = (f32[8,128]{1,0:T(8,128)S(1)}, f32[8,128]{1,0:T(8,128)S(1)}, u32[]{:S(2)}, u32[]{:S(2)}) collective-permute-start(f32[8,128]{1,0:T(8,128)S(1)} %get-tuple-element.55.refs_0_), channel_id=1, source_target_pairs={{24,0},{0,16},{16,8},{8,24},{25,1},{1,17},{17,9},{9,25},{26,2},{2,... | collective-permute-start | bytes 12296 | tf_op jit(solution)/shard_map/ppermute | solution.py:350
  40.6 10.4 %collective-permute-start.21 = (f32[264,128]{1,0:T(8,128)S(1)}, f32[264,128]{1,0:T(8,128)S(1)}, u32[]{:S(2)}, u32[]{:S(2)}) collective-permute-start(f32[264,128]{1,0:T(8,128)S(1)} %get-tuple-element.57), channel_id=1, source_target_pairs={{0,8},{8,0},{16,24},{24,16},{1,9},{9,1},{17,25},{25,17},{2,10},{10... | collective-permute-start | bytes 405512 | tf_op jit(solution)/shard_map/ppermute | solution.py:350
  41.7 9.2 %collective-permute-start.22 = (f32[264,128]{1,0:T(8,128)S(1)}, f32[264,128]{1,0:T(8,128)S(1)}, u32[]{:S(2)}, u32[]{:S(2)}) collective-permute-start(f32[264,128]{1,0:T(8,128)S(1)} %get-tuple-element.57), channel_id=1, source_target_pairs={{16,0},{8,16},{24,8},{0,24},{17,1},{9,17},{25,9},{1,25},{18,2},{10... | collective-permute-start | bytes 405512 | tf_op jit(solution)/shard_map/ppermute | solution.py:350
  43.0 6.0 %collective-permute-start.18 = (f32[256,128]{1,0:T(8,128)S(1)}, f32[256,128]{1,0:T(8,128)S(1)}, u32[]{:S(2)}, u32[]{:S(2)}) collective-permute-start(f32[256,128]{1,0:T(8,128)S(1)} %get-tuple-element.56.refs_2_), channel_id=1, source_target_pairs={{0,2},{1,3},{2,0},{3,1},{4,6},{5,7},{6,4},{7,5},{8,10},{9,11},{10,... | collective-permute-start | bytes 393224 | tf_op jit(solution)/shard_map/ppermute | solution.py:343
  44.2 5.0 %collective-permute-start.19 = (f32[256,128]{1,0:T(8,128)S(1)}, f32[256,128]{1,0:T(8,128)S(1)}, u32[]{:S(2)}, u32[]{:S(2)}) collective-permute-start(f32[256,128]{1,0:T(8,128)S(1)} %get-tuple-element.56.refs_2_), channel_id=1, source_target_pairs={{0,4},{1,5},{2,6},{3,7},{4,0},{5,1},{6,2},{7,3},{8,12},{9,13},{10,... | collective-permute-start | bytes 393224 | tf_op jit(solution)/shard_map/ppermute | solution.py:343
  45.1 5.9 %collective-permute-start.20 = (f32[256,128]{1,0:T(8,128)S(1)}, f32[256,128]{1,0:T(8,128)S(1)}, u32[]{:S(2)}, u32[]{:S(2)}) collective-permute-start(f32[256,128]{1,0:T(8,128)S(1)} %get-tuple-element.56.refs_2_), channel_id=1, source_target_pairs={{0,6},{1,7},{2,4},{3,5},{4,2},{5,3},{6,0},{7,1},{8,14},{9,15},{10,... | collective-permute-start | bytes 393224 | tf_op jit(solution)/shard_map/ppermute | solution.py:343
  52.9 2.0 %collective-permute-start.24 = (f32[1024,128]{1,0:T(8,128)S(1)}, f32[1024,128]{1,0:T(8,128)S(1)}, u32[]{:S(2)}, u32[]{:S(2)}) collective-permute-start(f32[1024,128]{1,0:T(8,128)S(1)} %get-tuple-element.65), channel_id=1, source_target_pairs={{0,1},{1,0},{2,3},{3,2},{4,5},{5,4},{6,7},{7,6},{8,9},{9,8},{10,11... | collective-permute-start | bytes 1572872 | tf_op jit(solution)/shard_map/ppermute | solution.py:343
  53.0 2.6 %collective-permute-start.23 = (bf16[1024,256]{1,0:T(8,128)(2,1)S(1)}, bf16[1024,256]{1,0:T(8,128)(2,1)S(1)}, u32[]{:S(2)}, u32[]{:S(2)}) collective-permute-start(bf16[1024,256]{1,0:T(8,128)(2,1)S(1)} %get-tuple-element.58.refs_0_.refs_10_), channel_id=1, source_target_pairs={{0,1},{1,0},{2,3},{3,2},{4,5},{5,4},{6,7},{7,6},{8,9},{9,8},{10,11... | collective-permute-start | bytes 1572872 | tf_op jit(solution)/shard_map/ppermute | solution.py:343
  56.7 11.6 %collective-permute-start.26 = (f32[272,128]{1,0:T(8,128)S(1)}, f32[272,128]{1,0:T(8,128)S(1)}, u32[]{:S(2)}, u32[]{:S(2)}) collective-permute-start(f32[272,128]{1,0:T(8,128)S(1)} %get-tuple-element.68), channel_id=1, source_target_pairs={{0,8},{8,0},{16,24},{24,16},{1,9},{9,1},{17,25},{25,17},{2,10},{10... | collective-permute-start | bytes 417800 | tf_op jit(solution)/shard_map/ppermute | solution.py:350
  57.9 10.4 %collective-permute-start.27 = (f32[272,128]{1,0:T(8,128)S(1)}, f32[272,128]{1,0:T(8,128)S(1)}, u32[]{:S(2)}, u32[]{:S(2)}) collective-permute-start(f32[272,128]{1,0:T(8,128)S(1)} %get-tuple-element.69), channel_id=1, source_target_pairs={{24,0},{0,16},{16,8},{8,24},{25,1},{1,17},{17,9},{9,25},{26,2},{2,... | collective-permute-start | bytes 417800 | tf_op jit(solution)/shard_map/ppermute | solution.py:350
  59.2 7.6 %collective-permute-start.25 = (f32[8,128]{1,0:T(8,128)S(1)}, f32[8,128]{1,0:T(8,128)S(1)}, u32[]{:S(2)}, u32[]{:S(2)}) collective-permute-start(f32[8,128]{1,0:T(8,128)S(1)} %get-tuple-element.67), channel_id=1, source_target_pairs={{16,0},{8,16},{24,8},{0,24},{17,1},{9,17},{25,9},{1,25},{18,2},{10... | collective-permute-start | bytes 12296 | tf_op jit(solution)/shard_map/ppermute | solution.py:350
  61.7 8.7 %collective-permute-start.31 = (f32[256,128]{1,0:T(8,128)S(1)}, f32[256,128]{1,0:T(8,128)S(1)}, u32[]{:S(2)}, u32[]{:S(2)}) collective-permute-start(f32[256,128]{1,0:T(8,128)S(1)} %get-tuple-element.71), channel_id=1, source_target_pairs={{0,2},{1,3},{2,0},{3,1},{4,6},{5,7},{6,4},{7,5},{8,10},{9,11},{10,... | collective-permute-start | bytes 393224 | tf_op jit(solution)/shard_map/ppermute | solution.py:343
  63.2 8.6 %collective-permute-start.32 = (f32[256,128]{1,0:T(8,128)S(1)}, f32[256,128]{1,0:T(8,128)S(1)}, u32[]{:S(2)}, u32[]{:S(2)}) collective-permute-start(f32[256,128]{1,0:T(8,128)S(1)} %get-tuple-element.72), channel_id=1, source_target_pairs={{0,4},{1,5},{2,6},{3,7},{4,0},{5,1},{6,2},{7,3},{8,12},{9,13},{10,... | collective-permute-start | bytes 393224 | tf_op jit(solution)/shard_map/ppermute | solution.py:343
  66.8 5.9 %collective-permute-start.33 = (f32[256,128]{1,0:T(8,128)S(1)}, f32[256,128]{1,0:T(8,128)S(1)}, u32[]{:S(2)}, u32[]{:S(2)}) collective-permute-start(f32[256,128]{1,0:T(8,128)S(1)} %get-tuple-element.73), channel_id=1, source_target_pairs={{0,6},{1,7},{2,4},{3,5},{4,2},{5,3},{6,0},{7,1},{8,14},{9,15},{10,... | collective-permute-start | bytes 393224 | tf_op jit(solution)/shard_map/ppermute | solution.py:343
  68.2 4.5 %collective-permute-start.28 = (f32[8,128]{1,0:T(8,128)S(1)}, f32[8,128]{1,0:T(8,128)S(1)}, u32[]{:S(2)}, u32[]{:S(2)}) collective-permute-start(f32[8,128]{1,0:T(8,128)S(1)} %slice_add_fusion.refs_0_), channel_id=1, source_target_pairs={{0,2},{1,3},{2,0},{3,1},{4,6},{5,7},{6,4},{7,5},{8,10},{9,11},{10,... | collective-permute-start | bytes 12296 | tf_op jit(solution)/shard_map/ppermute | solution.py:343
  69.6 3.6 %collective-permute-start.29 = (f32[8,128]{1,0:T(8,128)S(1)}, f32[8,128]{1,0:T(8,128)S(1)}, u32[]{:S(2)}, u32[]{:S(2)}) collective-permute-start(f32[8,128]{1,0:T(8,128)S(1)} %slice_add_fusion.refs_0_), channel_id=1, source_target_pairs={{0,4},{1,5},{2,6},{3,7},{4,0},{5,1},{6,2},{7,3},{8,12},{9,13},{10,... | collective-permute-start | bytes 12296 | tf_op jit(solution)/shard_map/ppermute | solution.py:343
  70.4 4.5 %collective-permute-start.30 = (f32[8,128]{1,0:T(8,128)S(1)}, f32[8,128]{1,0:T(8,128)S(1)}, u32[]{:S(2)}, u32[]{:S(2)}) collective-permute-start(f32[8,128]{1,0:T(8,128)S(1)} %slice_add_fusion.refs_0_), channel_id=1, source_target_pairs={{0,6},{1,7},{2,4},{3,5},{4,2},{5,3},{6,0},{7,1},{8,14},{9,15},{10,... | collective-permute-start | bytes 12296 | tf_op jit(solution)/shard_map/ppermute | solution.py:343
  74.9 1.2 %collective-permute-start.34 = (f32[8,128]{1,0:T(8,128)S(1)}, f32[8,128]{1,0:T(8,128)S(1)}, u32[]{:S(2)}, u32[]{:S(2)}) collective-permute-start(f32[8,128]{1,0:T(8,128)S(1)} %shard_map.56.refs_0_), channel_id=1, source_target_pairs={{0,1},{1,0},{2,3},{3,2},{4,5},{5,4},{6,7},{7,6},{8,9},{9,8},{10,11... | collective-permute-start | bytes 12296 | tf_op jit(solution)/shard_map/ppermute | solution.py:343

commit v6 on v5

--- a/solution.py
+++ b/solution.py
@@ -9,10 +9,11 @@
 
 ITERS = 2
 STAT_ROWS = 8
+GATHER_ROWS = (8, 16, 24)
 WIDE_ROWS = 16
 BACK_ROWS = 16
 VMEM_BYTES = 24 * 1024 * 1024
-KERNEL_FLOPS = 5.4
+CROSS_COST = 6
 VMEM = pl.BlockSpec(memory_space=pltpu.VMEM)
 SMEM = pl.BlockSpec(memory_space=pltpu.SMEM)
 ANY = pl.BlockSpec(memory_space=pl.ANY)
@@ -71,12 +72,14 @@
     out[rows, clusters:] = low
 
 
-def prepare_body(logits, unused, pair, wide):
-    n = logits.shape[0]
+def prepare_body(logits, rows, pair, wide, message):
+    n, width = rows.shape
     member = normalize(jnp.exp(logits[...]))
     store_pair(pair, slice(0, n), member)
     store_pair(wide, slice(0, n), member)
     wide[n:, :] = jnp.zeros((wide.shape[0] - n, wide.shape[1]), BF16)
+    message[:, :width] = rows[...]
+    message[:, width:] = pair[...]
 
 
 def kernel_body(order, column_ref, rows_ref, plane_ref, *refs):
@@ -98,14 +101,14 @@
         low_ref[:, j * n : (j + 1) * n] = low
 
 
-def kernel_call(n, order, column, rows, plane, after=()):
+def kernel_call(n, order, column, rows, plane, after=(), cost=1):
     total = plane.shape[0]
     return call(
         functools.partial(kernel_body, tuple(order)),
         [column, rows, plane, *after],
         [shaped(n, total, BF16)] * 2,
         [SMEM, VMEM, VMEM] + [ANY] * len(after),
-        flops=int(KERNEL_FLOPS * n) * total * plane.shape[1],
+        flops=int(2 * cost * n) * total * plane.shape[1],
     )
 
 
@@ -178,14 +181,14 @@
     for ref in stats[1:]:
         stat += ref[...]
     for ref in rest:
-        stat += ref[n:, :]
+        stat += ref[n : n + STAT_ROWS, :]
     weighted, size = stat[0:1, :], stat[1:2, :]
 
     def member_of(x):
         return normalize(jnp.exp(-2.0 * standardize(x, size, weighted)))
 
     for j, ref in enumerate(own):
-        store_pair(even, slice(j * n, (j + 1) * n), member_of(ref[...]))
+        store_pair(even, slice(j * n, (j + 1) * n), member_of(ref[:n, :]))
     for pair, ref in zip(pairs, rest):
         store_pair(pair, slice(0, n), member_of(ref[:n, :]))
 
@@ -261,22 +264,25 @@
     )
 
 
-def fold_body(n, count, even, received, *refs):
-    stats, outs = refs[:count], refs[count:]
+def fold_body(n, count, unused, even, received, *refs):
+    stats, outs = refs[:count], refs[count + unused :]
     half = even.shape[0]
     for j, out in enumerate(outs):
         rows = slice(j * n, (j + 1) * n)
         out[:n, :] = even[rows, :] + received[rows, :]
         if count:
             out[n:, :] = stats[0][...] + received[half:, :]
-
-
-def fold_call(n, even, received, stats, extra):
+        else:
+            out[n:, :] = jnp.zeros((out.shape[0] - n, out.shape[1]), F32)
+
+
+def fold_call(n, even, received, stats, extra, after=()):
     half, clusters = even.shape
     return call(
-        functools.partial(fold_body, n, len(stats)),
-        [even, received] + stats,
+        functools.partial(fold_body, n, len(stats), len(after)),
+        [even, received, *stats, *after],
         [shaped(n + extra, clusters)] * (half // n),
+        [VMEM] * (2 + len(stats)) + [ANY] * len(after),
     )
 
 
@@ -289,6 +295,13 @@
     out[...] = total
 
 
+def column_body(n, *refs):
+    total = refs[0][...]
+    for ref in refs[1:-1]:
+        total += ref[...] if ref.shape[0] < n else ref[n : n + STAT_ROWS, :]
+    refs[-1][...] = total
+
+
 def plane_body(count, *refs):
     total = refs[0][...]
     for ref in refs[1:count]:
@@ -297,7 +310,7 @@
 
 
 def sum_body(n, last, *refs):
-    many = 2 if last else 3
+    many = 2 if last else 1 + len(GATHER_ROWS)
     refs, outs = refs[:-many], refs[-many:]
     if last:
         stat = refs[0][...] + refs[1][...]
@@ -315,11 +328,14 @@
         standardized[...] = x
         members[...] = normalize(jnp.exp(-2.0 * x))
     else:
-        full, scores, stats = outs
-        full[:n, :] = total
-        full[n:, :] = stat
-        scores[...] = total
+        stats, fulls = outs[0], outs[1:]
         stats[...] = stat
+        for full in fulls:
+            full[:n, :] = total
+            full[n : n + STAT_ROWS, :] = stat
+            rest = full.shape[0] - n - STAT_ROWS
+            if rest:
+                full[n + STAT_ROWS :, :] = jnp.zeros((rest, full.shape[1]), F32)
 
 
 def on_device(rows, cols, features, logits):
@@ -351,26 +367,35 @@
 
     column = jnp.reshape(lax.axis_index("col"), (1,)).astype(jnp.int32)
     own_rows = lax.dynamic_slice_in_dim(features, lax.axis_index("col") * n, n, 0)
-    pair, wide = call(
+    pair, wide, message = call(
         prepare_body,
         [logits, own_rows],
-        [shaped(n, 2 * clusters, BF16), shaped(n + WIDE_ROWS, 2 * clusters, BF16)],
-        [VMEM, ANY],
+        [
+            shaped(n, 2 * clusters, BF16),
+            shaped(n + WIDE_ROWS, 2 * clusters, BF16),
+            shaped(n, width + 2 * clusters, BF16),
+        ],
         hidden=True,
     )
-    far_rows = [shift(own_rows, d) for d in steps]
-    others = [shift(wide if d else pair, d) for d in steps]
+    far_rows = [shift(own_rows if d else message, d) for d in steps]
+    others = [shift(wide, d) if d else far_rows[0] for d in steps]
     evens = [pair] + [by_col(pair, k) for k in masks]
     members = evens + [by_col(x, 1) for x in evens]
     early = 1 + has_near
     extra = [0] + [BACK_ROWS] * len(steps)
-    blocks = [kernel_call(n, order, column, own_rows, features)]
-    for x in reversed(far_rows):
-        blocks.append(kernel_call(n, order, column, x, features, blocks[-1][:1]))
-    blocks = blocks[:1] + blocks[:0:-1]
-    kernels = [x for block in blocks for x in block]
-    cross = kernels[2 * early :]
-    scores = scores_call(0, members, kernels, [], extra, True)
+    kernels = kernel_call(n, order, column, own_rows, features)
+    cross = []
+    for x in far_rows[has_near:]:
+        after = (cross or kernels)[-2:]
+        cross += kernel_call(n, order, column, x, features, after, CROSS_COST)
+    scores = scores_call(
+        0, members, kernels + cross, [], extra[:1] + extra[early:], hidden=True
+    )
+    if has_near:
+        near = kernel_call(n, order, column, far_rows[0], features, scores[-1:])
+        kernels += near
+        scores[1:1] = scores_call(0, members, near, [], extra[1:2], hidden=True)
+    kernels += cross
     own = pair
 
     for iteration in range(ITERS):
@@ -382,10 +407,12 @@
             scores = scores_call(0, [even], kernels, [], extra)
         if last:
             t_even, t_odd = other_call(n, half, clusters, others[has_near:], cross, [])
-            sent = fold_call(n, t_even, by_col(t_odd, 1), [], 0)
+            extra = [0] + [STAT_ROWS] * len(steps)
             *scores, stat = scores_call(
-                half, [odd], kernels, scores, extra, False, sent[:1], [own] + others, has_near
+                half, [odd], kernels, scores, extra, False, (), [own] + others, has_near
             )
+            small = [shift(stat, d) for d in offsets]
+            sent = fold_call(n, t_even, by_col(t_odd, 1), [], STAT_ROWS, small)
         else:
             if iteration > 0:
                 scores = scores_call(half, [odd], kernels, scores, extra)
@@ -396,11 +423,11 @@
         back = [shift(x, -d) for d, x in zip(steps, scores[1:])]
         total = []
         if last:
-            for x in [shift(stat, d) for d in offsets]:
-                stat = stat + x
-            for x in back:
-                stat = stat + x[n : n + STAT_ROWS]
-            plane = stat
+            plane = call(
+                functools.partial(column_body, n),
+                [stat] + back + small,
+                [shaped(STAT_ROWS, clusters)],
+            )[0]
             sent = call(add_body, [sent[0], scores[0]] + parts, [shaped(n, clusters)])
             stats = [plane] + [by_col(plane, k) for k in masks]
             stat = call(
@@ -413,16 +440,17 @@
             parts = []
         outs = [shaped(n, clusters)] * 2
         if not last:
-            outs = [shaped(n + STAT_ROWS, clusters), outs[0], shaped(STAT_ROWS, clusters)]
+            outs = [shaped(STAT_ROWS, clusters)]
+            outs += [shaped(n + r, clusters) for r in GATHER_ROWS]
         done = call(
             functools.partial(sum_body, n, last),
             total + ([sent[0]] if last else [sent[0], scores[0]]) + back + parts,
             outs,
         )
         if not last:
-            full, total, stats = done
-            evens = [total] + [by_col(total, k) for k in masks]
-            others = [shift(full, d) for d in steps]
+            stats, near_full, part_full, cross_full = done
+            evens = [part_full] + [by_col(part_full, k) for k in masks]
+            others = [shift(cross_full if d else near_full, d) for d in steps]
             stats = [stats] + [shift(stats, -d) for d in offsets]
     return tuple(done)
 

time: 77.2 us -> 81.3 us (1.053)
  waiting for transfers between devices: 24.6 us -> 32.6 us
  starting transfers between devices: 37.6 us -> 33.3 us
    ppermute x12 -> x11, waiting for transfers between devices: 11.9 us -> 20.2 us  [shift(): return lax.ppermute(x, 'row', pairs)]
    ppermute x12 -> x11, starting transfers between devices: 18.7 us -> 14.3 us  [shift(): return lax.ppermute(x, 'row', pairs)]
    pallas_call x17 -> x19, Pallas kernels: 10.6 us -> 11 us  [call(): pl.pallas_call(body, in_specs=specs or [VMEM] * len(args), out_specs=[VME...]
  transfers between devices with their start and end apart: 35 -> 34, of which waited for: 16 -> 17; matrix products, arithmetic and copies ran while one was open for 0% -> 0% of each run, Pallas kernels for 7% -> 10%
where the time goes in v6:
time: 81.3 us; the launch traced here: 81.1 us
  starting transfers between devices  33.3 us (41%)
  waiting for transfers between devices  32.6 us (40%)
  Pallas kernels  11 us (14%)
  local copies, waits for them, and re-layouts  3.47 us (4%)
    ppermute x11, waiting for transfers between devices, shift(): return lax.ppermute(x, 'row', pairs)  20.2 us
    ppermute x23, starting transfers between devices, by_col(): return lax.ppermute(x, 'col', [(i, i ^ mask) for i in range(cols)])  19 us
    ppermute x11, starting transfers between devices, shift(): return lax.ppermute(x, 'row', pairs)  14.3 us
    ppermute x23, waiting for transfers between devices, by_col(): return lax.ppermute(x, 'col', [(i, i ^ mask) for i in range(cols)])  12.4 us
    pallas_call x19, Pallas kernels, call(): pl.pallas_call(body, in_specs=specs or [VMEM] * len(args), out_specs=[VME...  11 us
    unnamed x6, local copies, waits for them, and re-layouts  2.5 us
  transfers between devices with their start and end apart: 34, of which 17 were waited for; matrix products, arithmetic and copies ran while one was open for 0% of the time, Pallas kernels for 10%

profile of v6, /device:TPU:0, one launch (start us, length us, event | category | flops | bytes accessed | tf_op | source)
XLA Modules:
  0.0 81.1 jit_solution(3627943232822334380)
XLA Ops:
  0.6 1.0 %constant_dynamic-slice_fusion.rows.rows_ref = bf16[256,512]{1,0:T(8,128)(2,1)S(1)} fusion(bf16[2048,512]{1,0:T(8,128)(2,1)} %plane_ref.5, s32[]{:T(128)S(6)} %select_n.3), kind=kLoop, calls=%fused_computation | loop fusion | bytes 524292 | tf_op jit(solution)/shard_map/dynamic_slice | solution.py:369
  1.6 5.1 %collective-permute-start.1 = (bf16[256,512]{1,0:T(8,128)(2,1)S(1)}, bf16[256,512]{1,0:T(8,128)(2,1)S(1)}, u32[]{:S(2)}, u32[]{:S(2)}) collective-permute-start(bf16[256,512]{1,0:T(8,128)(2,1)S(1)} %constant_dynamic-slice_fusion.rows.rows_ref), channel_id=1, source_target_pairs={{16,0},{8,16},{24,8},{0,24},{17,1},{9,17},{25,9},{1,25},{18,2},{10... | collective-permute-start | bytes 786440 | tf_op jit(solution)/shard_map/ppermute | solution.py:366
  6.7 0.9 %copy-done.2 = f32[256,128]{1,0:T(8,128)S(1)} copy-done((f32[256,128]{1,0:T(8,128)S(1)}, f32[256,128]{1,0:T(8,128)}, u32[]{:S(2)}) %copy-start.2) | copy-done | bytes 131096
  7.6 0.1 shard_map.41
  7.8 1.6 %collective-permute-start.2 = (bf16[256,256]{1,0:T(8,128)(2,1)S(1)}, bf16[256,256]{1,0:T(8,128)(2,1)S(1)}, u32[]{:S(2)}, u32[]{:S(2)}) collective-permute-start(bf16[256,256]{1,0:T(8,128)(2,1)S(1)} %get-tuple-element.44.refs_0_.own), channel_id=1, source_target_pairs={{0,2},{1,3},{2,0},{3,1},{4,6},{5,7},{6,4},{7,5},{8,10},{9,11},{10,... | collective-permute-start | bytes 393224 | tf_op jit(solution)/shard_map/ppermute | solution.py:359
  9.3 1.5 %collective-permute-start.3 = (bf16[256,256]{1,0:T(8,128)(2,1)S(1)}, bf16[256,256]{1,0:T(8,128)(2,1)S(1)}, u32[]{:S(2)}, u32[]{:S(2)}) collective-permute-start(bf16[256,256]{1,0:T(8,128)(2,1)S(1)} %get-tuple-element.44.refs_0_.own), channel_id=1, source_target_pairs={{0,4},{1,5},{2,6},{3,7},{4,0},{5,1},{6,2},{7,3},{8,12},{9,13},{10,... | collective-permute-start | bytes 393224 | tf_op jit(solution)/shard_map/ppermute | solution.py:359
  10.8 0.5 collective-permute-start.4
  11.3 1.9 %collective-permute-done.2.refs_1_ = bf16[256,256]{1,0:T(8,128)(2,1)S(1)} collective-permute-done((bf16[256,256]{1,0:T(8,128)(2,1)S(1)}, bf16[256,256]{1,0:T(8,128)(2,1)S(1)}, u32[]{:S(2)}, u32[]{:S(2)}) %collective-permute-start.2) | collective-permute-done | bytes 131104 | tf_op jit(solution)/shard_map/ppermute | solution.py:359
  13.2 1.6 %copy-done = bf16[2048,512]{1,0:T(8,128)(2,1)S(1)} copy-done((bf16[2048,512]{1,0:T(8,128)(2,1)S(1)}, bf16[2048,512]{1,0:T(8,128)(2,1)}, u32[]{:S(2)}) %copy-start) | copy-done | bytes 2097176
  14.8 0.9 %shard_map.42 = (bf16[256,2048]{1,0:T(8,128)(2,1)S(1)}, bf16[256,2048]{1,0:T(8,128)(2,1)S(1)}) custom-call(s32[1]{0:T(128)} %bitcast.column_ref, bf16[256,512]{1,0:T(8,128)(2,1)S(1)} %constant_dynamic-slice_fusion.rows.rows_ref, bf16[2048,512]{1,0:T(8,128)(2,1)S(1)} %copy-done), custom_call_target="tpu_custom_call" | custom-call | flops 536870912 | bytes 4456452 | tf_op jit(solution)/shard_map/pallas_call | solution.py:32
  15.7 1.4 %collective-permute-done.3.refs_2_ = bf16[256,256]{1,0:T(8,128)(2,1)S(1)} collective-permute-done((bf16[256,256]{1,0:T(8,128)(2,1)S(1)}, bf16[256,256]{1,0:T(8,128)(2,1)S(1)}, u32[]{:S(2)}, u32[]{:S(2)}) %collective-permute-start.3) | collective-permute-done | bytes 131104 | tf_op jit(solution)/shard_map/ppermute | solution.py:359
  17.1 0.3 collective-permute-start
  17.4 0.5 collective-permute-start.7
  18.0 0.1 collective-permute-start.8
  18.0 0.9 %shard_map.43 = (bf16[256,2048]{1,0:T(8,128)(2,1)S(1)}, bf16[256,2048]{1,0:T(8,128)(2,1)S(1)}) custom-call(s32[1]{0:T(128)} %bitcast.column_ref, bf16[256,512]{1,0:T(8,128)(2,1)S(1)} %collective-permute-done.1.rows_ref, bf16[2048,512]{1,0:T(8,128)(2,1)S(1)} %copy-done.1, bf16[256,2048]{1,0:T(8,128)(2,1)S(1)} %get-tuple-element.40.refs_0_.refs_8_.refs_1_, ...), custom_call_target="tpu_custom_call" | custom-call | flops 3221225472 | bytes 6553604 | tf_op jit(solution)/shard_map/pallas_call | solution.py:32
  19.0 0.3 collective-permute-done.8.refs_7_
  19.3 1.3 %shard_map.44 = (f32[256,128]{1,0:T(8,128)S(1)}, f32[272,128]{1,0:T(8,128)S(1)}) custom-call(bf16[256,256]{1,0:T(8,128)(2,1)S(1)} %get-tuple-element.44.refs_0_.own, bf16[256,256]{1,0:T(8,128)(2,1)S(1)} %collective-permute-done.2.refs_1_, bf16[256,256]{1,0:T(8,128)(2,1)S(1)} %collective-permute-done.3.refs_2_, ...), custom_call_target="tpu_custom_call" | custom-call | tf_op jit(solution)/shard_map/pallas_call | solution.py:32
  20.6 8.4 %collective-permute-done.9.rows_ref.refs_3_ = bf16[256,768]{1,0:T(8,128)(2,1)S(1)} collective-permute-done((bf16[256,768]{1,0:T(8,128)(2,1)S(1)}, bf16[256,768]{1,0:T(8,128)(2,1)S(1)}, u32[]{:S(2)}, u32[]{:S(2)}) %collective-permute-start.9) | collective-permute-done | bytes 393248 | tf_op jit(solution)/shard_map/ppermute | solution.py:366
  29.0 0.9 %shard_map.45 = (bf16[256,2048]{1,0:T(8,128)(2,1)S(1)}, bf16[256,2048]{1,0:T(8,128)(2,1)S(1)}) custom-call(s32[1]{0:T(128)} %bitcast.column_ref, bf16[256,768]{1,0:T(8,128)(2,1)S(1)} %collective-permute-done.9.rows_ref.refs_3_, bf16[2048,512]{1,0:T(8,128)(2,1)S(1)} %copy-done.1, f32[272,128]{1,0:T(8,128)S(1)} %get-tuple-element.47.refs_0_.refs_2_), custom_call_target="tpu_custom_call" | custom-call | flops 536870912 | bytes 4726788 | tf_op jit(solution)/shard_map/pallas_call | solution.py:32
  29.9 0.7 shard_map.46.refs_1_
  30.6 0.1 shard_map.47.refs_3_.refs_0_
  30.7 0.8 shard_map.48
  31.5 0.1 collective-permute-start.10
  31.6 0.1 collective-permute-start.12
  31.7 0.1 collective-permute-start.11
  31.8 1.8 %collective-permute-done.10.received = f32[1032,128]{1,0:T(8,128)S(1)} collective-permute-done((f32[1032,128]{1,0:T(8,128)S(1)}, f32[1032,128]{1,0:T(8,128)S(1)}, u32[]{:S(2)}, u32[]{:S(2)}) %collective-permute-start.10) | collective-permute-done | bytes 528416 | tf_op jit(solution)/shard_map/ppermute | solution.py:359
  33.5 0.1 shard_map.49
  33.6 1.6 %collective-permute-start.13 = (f32[264,128]{1,0:T(8,128)S(1)}, f32[264,128]{1,0:T(8,128)S(1)}, u32[]{:S(2)}, u32[]{:S(2)}) collective-permute-start(f32[264,128]{1,0:T(8,128)S(1)} %get-tuple-element.53), channel_id=1, source_target_pairs={{0,2},{1,3},{2,0},{3,1},{4,6},{5,7},{6,4},{7,5},{8,10},{9,11},{10,... | collective-permute-start | bytes 405512 | tf_op jit(solution)/shard_map/ppermute | solution.py:359
  35.2 1.5 %collective-permute-start.14 = (f32[264,128]{1,0:T(8,128)S(1)}, f32[264,128]{1,0:T(8,128)S(1)}, u32[]{:S(2)}, u32[]{:S(2)}) collective-permute-start(f32[264,128]{1,0:T(8,128)S(1)} %get-tuple-element.54), channel_id=1, source_target_pairs={{0,4},{1,5},{2,6},{3,7},{4,0},{5,1},{6,2},{7,3},{8,12},{9,13},{10,... | collective-permute-start | bytes 405512 | tf_op jit(solution)/shard_map/ppermute | solution.py:359
  36.7 0.4 collective-permute-start.15
  37.1 2.8 %collective-permute-done.12.refs_3_ = f32[272,128]{1,0:T(8,128)S(1)} collective-permute-done((f32[272,128]{1,0:T(8,128)S(1)}, f32[272,128]{1,0:T(8,128)S(1)}, u32[]{:S(2)}, u32[]{:S(2)}) %collective-permute-start.12) | collective-permute-done | bytes 139296 | tf_op jit(solution)/shard_map/ppermute | solution.py:366
  40.0 0.7 collective-permute-done.11.refs_2_
  40.7 2.8 %collective-permute-done.14.refs_5_ = f32[264,128]{1,0:T(8,128)S(1)} collective-permute-done((f32[264,128]{1,0:T(8,128)S(1)}, f32[264,128]{1,0:T(8,128)S(1)}, u32[]{:S(2)}, u32[]{:S(2)}) %collective-permute-start.14) | collective-permute-done | bytes 135200 | tf_op jit(solution)/shard_map/ppermute | solution.py:359
  43.4 0.1 shard_map.50
  43.5 2.1 %collective-permute-start.21 = (f32[280,128]{1,0:T(8,128)S(1)}, f32[280,128]{1,0:T(8,128)S(1)}, u32[]{:S(2)}, u32[]{:S(2)}) collective-permute-start(f32[280,128]{1,0:T(8,128)S(1)} %get-tuple-element.59), channel_id=1, source_target_pairs={{16,0},{8,16},{24,8},{0,24},{17,1},{9,17},{25,9},{1,25},{18,2},{10... | collective-permute-start | bytes 430088 | tf_op jit(solution)/shard_map/ppermute | solution.py:366
  45.6 0.9 %collective-permute-start.16 = (f32[8,128]{1,0:T(8,128)S(1)}, f32[8,128]{1,0:T(8,128)S(1)}, u32[]{:S(2)}, u32[]{:S(2)}) collective-permute-start(f32[8,128]{1,0:T(8,128)S(1)} %get-tuple-element.56.refs_0_), channel_id=1, source_target_pairs={{24,0},{0,16},{16,8},{8,24},{25,1},{1,17},{17,9},{9,25},{26,2},{2,... | collective-permute-start | bytes 12296 | tf_op jit(solution)/shard_map/ppermute | solution.py:366
  46.5 1.2 %collective-permute-start.17 = (f32[272,128]{1,0:T(8,128)S(1)}, f32[272,128]{1,0:T(8,128)S(1)}, u32[]{:S(2)}, u32[]{:S(2)}) collective-permute-start(f32[272,128]{1,0:T(8,128)S(1)} %get-tuple-element.57.refs_2_), channel_id=1, source_target_pairs={{0,2},{1,3},{2,0},{3,1},{4,6},{5,7},{6,4},{7,5},{8,10},{9,11},{10,... | collective-permute-start | bytes 417800 | tf_op jit(solution)/shard_map/ppermute | solution.py:359
  47.7 0.8 %collective-permute-start.18 = (f32[272,128]{1,0:T(8,128)S(1)}, f32[272,128]{1,0:T(8,128)S(1)}, u32[]{:S(2)}, u32[]{:S(2)}) collective-permute-start(f32[272,128]{1,0:T(8,128)S(1)} %get-tuple-element.57.refs_2_), channel_id=1, source_target_pairs={{0,4},{1,5},{2,6},{3,7},{4,0},{5,1},{6,2},{7,3},{8,12},{9,13},{10,... | collective-permute-start | bytes 417800 | tf_op jit(solution)/shard_map/ppermute | solution.py:359
  48.5 1.4 %collective-permute-start.19 = (f32[272,128]{1,0:T(8,128)S(1)}, f32[272,128]{1,0:T(8,128)S(1)}, u32[]{:S(2)}, u32[]{:S(2)}) collective-permute-start(f32[272,128]{1,0:T(8,128)S(1)} %get-tuple-element.57.refs_2_), channel_id=1, source_target_pairs={{0,6},{1,7},{2,4},{3,5},{4,2},{5,3},{6,0},{7,1},{8,14},{9,15},{10,... | collective-permute-start | bytes 417800 | tf_op jit(solution)/shard_map/ppermute | solution.py:359
  50.0 1.1 %collective-permute-done.16.refs_1_ = f32[8,128]{1,0:T(8,128)S(1)} collective-permute-done((f32[8,128]{1,0:T(8,128)S(1)}, f32[8,128]{1,0:T(8,128)S(1)}, u32[]{:S(2)}, u32[]{:S(2)}) %collective-permute-start.16) | collective-permute-done | bytes 4128 | tf_op jit(solution)/shard_map/ppermute | solution.py:366
  51.1 1.4 %collective-permute-start.20 = (f32[264,128]{1,0:T(8,128)S(1)}, f32[264,128]{1,0:T(8,128)S(1)}, u32[]{:S(2)}, u32[]{:S(2)}) collective-permute-start(f32[264,128]{1,0:T(8,128)S(1)} %get-tuple-element.58), channel_id=1, source_target_pairs={{0,8},{8,0},{16,24},{24,16},{1,9},{9,1},{17,25},{25,17},{2,10},{10... | collective-permute-start | bytes 405512 | tf_op jit(solution)/shard_map/ppermute | solution.py:366
  52.5 3.6 %collective-permute-done.20.refs_6_ = f32[264,128]{1,0:T(8,128)S(1)} collective-permute-done((f32[264,128]{1,0:T(8,128)S(1)}, f32[264,128]{1,0:T(8,128)S(1)}, u32[]{:S(2)}, u32[]{:S(2)}) %collective-permute-start.20) | collective-permute-done | bytes 135200 | tf_op jit(solution)/shard_map/ppermute | solution.py:366
  56.1 1.2 %shard_map.51 = (bf16[1024,256]{1,0:T(8,128)(2,1)S(1)}, bf16[256,256]{1,0:T(8,128)(2,1)S(1)}, bf16[256,256]{1,0:T(8,128)(2,1)S(1)}) custom-call(f32[8,128]{1,0:T(8,128)S(1)} %get-tuple-element.56.refs_0_, f32[8,128]{1,0:T(8,128)S(1)} %collective-permute-done.16.refs_1_, f32[272,128]{1,0:T(8,128)S(1)} %get-tuple-element.57.refs_2_, ...), custom_call_target="tpu_custom_call" | custom-call | bytes 1630208 | tf_op jit(solution)/shard_map/pallas_call | solution.py:32
  57.3 0.1 collective-permute-start.22
  57.4 0.8 shard_map.55
  58.2 0.6 collective-permute-start.29
  58.8 1.0 %shard_map.52 = (f32[256,128]{1,0:T(8,128)S(1)}, f32[272,128]{1,0:T(8,128)S(1)}, f32[272,128]{1,0:T(8,128)S(1)}) custom-call(bf16[1024,256]{1,0:T(8,128)(2,1)S(1)} %get-tuple-element.60.refs_0_.refs_10_, bf16[256,2048]{1,0:T(8,128)(2,1)S(1)} %get-tuple-element.40.refs_0_.refs_8_.refs_1_, bf16[256,2048]{1,0:T(8,128)(2,1)S(1)} %get-tuple-element.41.refs_1_.refs_9_.refs_2_, ...), custom_call_target="tpu_custom_call" | custom-call | flops 603979776 | bytes 7225344 | tf_op jit(solution)/shard_map/pallas_call | solution.py:32
  59.8 1.0 %shard_map.53 = (f32[256,128]{1,0:T(8,128)S(1)}, f32[264,128]{1,0:T(8,128)S(1)}, f32[264,128]{1,0:T(8,128)S(1)}, f32[8,128]{1,0:T(8,128)S(1)}) custom-call(bf16[1024,256]{1,0:T(8,128)(2,1)S(1)} %collective-permute-done.22.refs_0_, bf16[256,2048]{1,0:T(8,128)(2,1)S(1)} %get-tuple-element.40.refs_0_.refs_8_.refs_1_, ...), custom_call_target="tpu_custom_call" | custom-call | flops 603979776 | bytes 8417280 | tf_op jit(solution)/shard_map/pallas_call | solution.py:32
  60.8 3.3 %collective-permute-start.25 = (f32[8,128]{1,0:T(8,128)S(1)}, f32[8,128]{1,0:T(8,128)S(1)}, u32[]{:S(2)}, u32[]{:S(2)}) collective-permute-start(f32[8,128]{1,0:T(8,128)S(1)} %get-tuple-element.66.refs_0_), channel_id=1, source_target_pairs={{16,0},{8,16},{24,8},{0,24},{17,1},{9,17},{25,9},{1,25},{18,2},{10... | collective-permute-start | bytes 12296 | tf_op jit(solution)/shard_map/ppermute | solution.py:366
  64.1 1.0 %collective-permute-start.24 = (f32[264,128]{1,0:T(8,128)S(1)}, f32[264,128]{1,0:T(8,128)S(1)}, u32[]{:S(2)}, u32[]{:S(2)}) collective-permute-start(f32[264,128]{1,0:T(8,128)S(1)} %get-tuple-element.68), channel_id=1, source_target_pairs={{24,0},{0,16},{16,8},{8,24},{25,1},{1,17},{17,9},{9,25},{26,2},{2,... | collective-permute-start | bytes 405512 | tf_op jit(solution)/shard_map/ppermute | solution.py:366
  65.2 0.3 collective-permute-done.25.refs_3_.refs_0_
  65.5 0.1 shard_map.56
  65.5 1.8 %collective-permute-start.30 = (f32[264,128]{1,0:T(8,128)S(1)}, f32[264,128]{1,0:T(8,128)S(1)}, u32[]{:S(2)}, u32[]{:S(2)}) collective-permute-start(f32[264,128]{1,0:T(8,128)S(1)} %get-tuple-element.73), channel_id=1, source_target_pairs={{0,2},{1,3},{2,0},{3,1},{4,6},{5,7},{6,4},{7,5},{8,10},{9,11},{10,... | collective-permute-start | bytes 405512 | tf_op jit(solution)/shard_map/ppermute | solution.py:359
  67.3 0.4 collective-permute-start.31
  67.7 1.4 %collective-permute-start.32 = (f32[264,128]{1,0:T(8,128)S(1)}, f32[264,128]{1,0:T(8,128)S(1)}, u32[]{:S(2)}, u32[]{:S(2)}) collective-permute-start(f32[264,128]{1,0:T(8,128)S(1)} %get-tuple-element.75), channel_id=1, source_target_pairs={{0,6},{1,7},{2,4},{3,5},{4,2},{5,3},{6,0},{7,1},{8,14},{9,15},{10,... | collective-permute-start | bytes 405512 | tf_op jit(solution)/shard_map/ppermute | solution.py:359
  69.1 3.2 %collective-permute-done.23.refs_1_.refs_3_ = f32[264,128]{1,0:T(8,128)S(1)} collective-permute-done((f32[264,128]{1,0:T(8,128)S(1)}, f32[264,128]{1,0:T(8,128)S(1)}, u32[]{:S(2)}, u32[]{:S(2)}) %collective-permute-start.23) | collective-permute-done | bytes 135200 | tf_op jit(solution)/shard_map/ppermute | solution.py:366
  72.3 1.6 %collective-permute-start.26 = (f32[8,128]{1,0:T(8,128)S(1)}, f32[8,128]{1,0:T(8,128)S(1)}, u32[]{:S(2)}, u32[]{:S(2)}) collective-permute-start(f32[8,128]{1,0:T(8,128)S(1)} %shard_map.54.refs_0_), channel_id=1, source_target_pairs={{0,2},{1,3},{2,0},{3,1},{4,6},{5,7},{6,4},{7,5},{8,10},{9,11},{10,... | collective-permute-start | bytes 12296 | tf_op jit(solution)/shard_map/ppermute | solution.py:359
  73.9 0.5 collective-permute-start.27
  74.4 1.4 %collective-permute-start.28 = (f32[8,128]{1,0:T(8,128)S(1)}, f32[8,128]{1,0:T(8,128)S(1)}, u32[]{:S(2)}, u32[]{:S(2)}) collective-permute-start(f32[8,128]{1,0:T(8,128)S(1)} %shard_map.54.refs_0_), channel_id=1, source_target_pairs={{0,6},{1,7},{2,4},{3,5},{4,2},{5,3},{6,0},{7,1},{8,14},{9,15},{10,... | collective-permute-start | bytes 12296 | tf_op jit(solution)/shard_map/ppermute | solution.py:359
  75.8 0.1 shard_map.57.refs_4_.refs_2_
  75.9 1.6 %collective-permute-done.27.refs_2_ = f32[8,128]{1,0:T(8,128)S(1)} collective-permute-done((f32[8,128]{1,0:T(8,128)S(1)}, f32[8,128]{1,0:T(8,128)S(1)}, u32[]{:S(2)}, u32[]{:S(2)}) %collective-permute-start.27) | collective-permute-done | bytes 4128 | tf_op jit(solution)/shard_map/ppermute | solution.py:359
  77.5 1.4 %collective-permute-done.28.refs_3_ = f32[8,128]{1,0:T(8,128)S(1)} collective-permute-done((f32[8,128]{1,0:T(8,128)S(1)}, f32[8,128]{1,0:T(8,128)S(1)}, u32[]{:S(2)}, u32[]{:S(2)}) %collective-permute-start.28) | collective-permute-done | bytes 4128 | tf_op jit(solution)/shard_map/ppermute | solution.py:359
  78.9 1.2 %collective-permute-done.33.refs_1_ = f32[8,128]{1,0:T(8,128)S(1)} collective-permute-done((f32[8,128]{1,0:T(8,128)S(1)}, f32[8,128]{1,0:T(8,128)S(1)}, u32[]{:S(2)}, u32[]{:S(2)}) %collective-permute-start.33) | collective-permute-done | bytes 4128 | tf_op jit(solution)/shard_map/ppermute | solution.py:359
  80.1 1.0 %shard_map.59 = (f32[256,128]{1,0:T(8,128)}, f32[256,128]{1,0:T(8,128)}) custom-call(f32[8,128]{1,0:T(8,128)S(1)} %shard_map.58.refs_0_, f32[8,128]{1,0:T(8,128)S(1)} %collective-permute-done.33.refs_1_, f32[256,128]{1,0:T(8,128)S(1)} %shard_map.57.refs_4_.refs_2_, f32[264,128]{1,0:T(8,128)S(1)} %collective-permute-done.23.refs_1_.refs_3_, ...), custom_call_target="tpu_custom_call" | custom-call | bytes 671744 | tf_op jit(solution)/shard_map/pallas_call | solution.py:32
  (30 shorter events, 0.2 us)
Async XLA Ops:
  1.6 16.3 %collective-permute-start.1 = (bf16[256,512]{1,0:T(8,128)(2,1)S(1)}, bf16[256,512]{1,0:T(8,128)(2,1)S(1)}, u32[]{:S(2)}, u32[]{:S(2)}) collective-permute-start(bf16[256,512]{1,0:T(8,128)(2,1)S(1)} %constant_dynamic-slice_fusion.rows.rows_ref), channel_id=1, source_target_pairs={{16,0},{8,16},{24,8},{0,24},{17,1},{9,17},{25,9},{1,25},{18,2},{10... | collective-permute-start | bytes 786440 | tf_op jit(solution)/shard_map/ppermute | solution.py:366
  6.7 0.9 %copy-start.2 = (f32[256,128]{1,0:T(8,128)S(1)}, f32[256,128]{1,0:T(8,128)}, u32[]{:S(2)}) copy-start(f32[256,128]{1,0:T(8,128)} %logits.1) | copy-start | bytes 393220
  7.8 5.5 %collective-permute-start.2 = (bf16[256,256]{1,0:T(8,128)(2,1)S(1)}, bf16[256,256]{1,0:T(8,128)(2,1)S(1)}, u32[]{:S(2)}, u32[]{:S(2)}) collective-permute-start(bf16[256,256]{1,0:T(8,128)(2,1)S(1)} %get-tuple-element.44.refs_0_.own), channel_id=1, source_target_pairs={{0,2},{1,3},{2,0},{3,1},{4,6},{5,7},{6,4},{7,5},{8,10},{9,11},{10,... | collective-permute-start | bytes 393224 | tf_op jit(solution)/shard_map/ppermute | solution.py:359
  9.3 7.8 %collective-permute-start.3 = (bf16[256,256]{1,0:T(8,128)(2,1)S(1)}, bf16[256,256]{1,0:T(8,128)(2,1)S(1)}, u32[]{:S(2)}, u32[]{:S(2)}) collective-permute-start(bf16[256,256]{1,0:T(8,128)(2,1)S(1)} %get-tuple-element.44.refs_0_.own), channel_id=1, source_target_pairs={{0,4},{1,5},{2,6},{3,7},{4,0},{5,1},{6,2},{7,3},{8,12},{9,13},{10,... | collective-permute-start | bytes 393224 | tf_op jit(solution)/shard_map/ppermute | solution.py:359
  10.8 6.6 %collective-permute-start.4 = (bf16[256,256]{1,0:T(8,128)(2,1)S(1)}, bf16[256,256]{1,0:T(8,128)(2,1)S(1)}, u32[]{:S(2)}, u32[]{:S(2)}) collective-permute-start(bf16[256,256]{1,0:T(8,128)(2,1)S(1)} %get-tuple-element.44.refs_0_.own), channel_id=1, source_target_pairs={{0,6},{1,7},{2,4},{3,5},{4,2},{5,3},{6,0},{7,1},{8,14},{9,15},{10,... | collective-permute-start | bytes 393224 | tf_op jit(solution)/shard_map/ppermute | solution.py:359
  11.3 6.1 %collective-permute-start.5 = (bf16[256,256]{1,0:T(8,128)(2,1)S(1)}, bf16[256,256]{1,0:T(8,128)(2,1)S(1)}, u32[]{:S(2)}, u32[]{:S(2)}) collective-permute-start(bf16[256,256]{1,0:T(8,128)(2,1)S(1)} %get-tuple-element.44.refs_0_.own), channel_id=1, source_target_pairs={{0,1},{1,0},{2,3},{3,2},{4,5},{5,4},{6,7},{7,6},{8,9},{9,8},{10,11... | collective-permute-start | bytes 393224 | tf_op jit(solution)/shard_map/ppermute | solution.py:359
  13.2 15.8 %collective-permute-start.9 = (bf16[256,768]{1,0:T(8,128)(2,1)S(1)}, bf16[256,768]{1,0:T(8,128)(2,1)S(1)}, u32[]{:S(2)}, u32[]{:S(2)}) collective-permute-start(bf16[256,768]{1,0:T(8,128)(2,1)S(1)} %get-tuple-element.46), channel_id=1, source_target_pairs={{0,8},{8,0},{16,24},{24,16},{1,9},{9,1},{17,25},{25,17},{2,10},{10... | collective-permute-start | bytes 1179656 | tf_op jit(solution)/shard_map/ppermute | solution.py:366
  13.2 1.6 %copy-start = (bf16[2048,512]{1,0:T(8,128)(2,1)S(1)}, bf16[2048,512]{1,0:T(8,128)(2,1)}, u32[]{:S(2)}) copy-start(bf16[2048,512]{1,0:T(8,128)(2,1)} %plane_ref.5) | copy-start | bytes 6291460
  14.8 3.2 %copy-start.1 = (bf16[2048,512]{1,0:T(8,128)(2,1)S(1)}, bf16[2048,512]{1,0:T(8,128)(2,1)}, u32[]{:S(2)}) copy-start(bf16[2048,512]{1,0:T(8,128)(2,1)} %plane_ref.5) | copy-start | bytes 6291460
  17.1 13.5 %collective-permute-start = (bf16[272,256]{1,0:T(8,128)(2,1)S(1)}, bf16[272,256]{1,0:T(8,128)(2,1)S(1)}, u32[]{:S(2)}, u32[]{:S(2)}) collective-permute-start(bf16[272,256]{1,0:T(8,128)(2,1)S(1)} %get-tuple-element.39), channel_id=1, source_target_pairs={{16,0},{8,16},{24,8},{0,24},{17,1},{9,17},{25,9},{1,25},{18,2},{10... | collective-permute-start | bytes 417800 | tf_op jit(solution)/shard_map/ppermute | solution.py:366
  17.4 1.5 %collective-permute-start.6 = (bf16[256,256]{1,0:T(8,128)(2,1)S(1)}, bf16[256,256]{1,0:T(8,128)(2,1)S(1)}, u32[]{:S(2)}, u32[]{:S(2)}) collective-permute-start(bf16[256,256]{1,0:T(8,128)(2,1)S(1)} %collective-permute-done.2.refs_1_), channel_id=1, source_target_pairs={{0,1},{1,0},{2,3},{3,2},{4,5},{5,4},{6,7},{7,6},{8,9},{9,8},{10,11... | collective-permute-start | bytes 393224 | tf_op jit(solution)/shard_map/ppermute | solution.py:359
  17.4 1.5 %collective-permute-start.7 = (bf16[256,256]{1,0:T(8,128)(2,1)S(1)}, bf16[256,256]{1,0:T(8,128)(2,1)S(1)}, u32[]{:S(2)}, u32[]{:S(2)}) collective-permute-start(bf16[256,256]{1,0:T(8,128)(2,1)S(1)} %collective-permute-done.3.refs_2_), channel_id=1, source_target_pairs={{0,1},{1,0},{2,3},{3,2},{4,5},{5,4},{6,7},{7,6},{8,9},{9,8},{10,11... | collective-permute-start | bytes 393224 | tf_op jit(solution)/shard_map/ppermute | solution.py:359
  18.0 1.3 %collective-permute-start.8 = (bf16[256,256]{1,0:T(8,128)(2,1)S(1)}, bf16[256,256]{1,0:T(8,128)(2,1)S(1)}, u32[]{:S(2)}, u32[]{:S(2)}) collective-permute-start(bf16[256,256]{1,0:T(8,128)(2,1)S(1)} %collective-permute-done.4.refs_3_), channel_id=1, source_target_pairs={{0,1},{1,0},{2,3},{3,2},{4,5},{5,4},{6,7},{7,6},{8,9},{9,8},{10,11... | collective-permute-start | bytes 393224 | tf_op jit(solution)/shard_map/ppermute | solution.py:359
  31.5 2.0 %collective-permute-start.10 = (f32[1032,128]{1,0:T(8,128)S(1)}, f32[1032,128]{1,0:T(8,128)S(1)}, u32[]{:S(2)}, u32[]{:S(2)}) collective-permute-start(f32[1032,128]{1,0:T(8,128)S(1)} %get-tuple-element.51), channel_id=1, source_target_pairs={{0,1},{1,0},{2,3},{3,2},{4,5},{5,4},{6,7},{7,6},{8,9},{9,8},{10,11... | collective-permute-start | bytes 1585160 | tf_op jit(solution)/shard_map/ppermute | solution.py:359
  31.6 8.4 %collective-permute-start.12 = (f32[272,128]{1,0:T(8,128)S(1)}, f32[272,128]{1,0:T(8,128)S(1)}, u32[]{:S(2)}, u32[]{:S(2)}) collective-permute-start(f32[272,128]{1,0:T(8,128)S(1)} %get-tuple-element.47.refs_0_.refs_2_), channel_id=1, source_target_pairs={{24,0},{0,16},{16,8},{8,24},{25,1},{1,17},{17,9},{9,25},{26,2},{2,... | collective-permute-start | bytes 417800 | tf_op jit(solution)/shard_map/ppermute | solution.py:366
  31.7 9.0 %collective-permute-start.11 = (f32[272,128]{1,0:T(8,128)S(1)}, f32[272,128]{1,0:T(8,128)S(1)}, u32[]{:S(2)}, u32[]{:S(2)}) collective-permute-start(f32[272,128]{1,0:T(8,128)S(1)} %shard_map.46.refs_1_), channel_id=1, source_target_pairs={{0,8},{8,0},{16,24},{24,16},{1,9},{9,1},{17,25},{25,17},{2,10},{10... | collective-permute-start | bytes 417800 | tf_op jit(solution)/shard_map/ppermute | solution.py:366
  33.6 7.1 %collective-permute-start.13 = (f32[264,128]{1,0:T(8,128)S(1)}, f32[264,128]{1,0:T(8,128)S(1)}, u32[]{:S(2)}, u32[]{:S(2)}) collective-permute-start(f32[264,128]{1,0:T(8,128)S(1)} %get-tuple-element.53), channel_id=1, source_target_pairs={{0,2},{1,3},{2,0},{3,1},{4,6},{5,7},{6,4},{7,5},{8,10},{9,11},{10,... | collective-permute-start | bytes 405512 | tf_op jit(solution)/shard_map/ppermute | solution.py:359
  35.2 8.2 %collective-permute-start.14 = (f32[264,128]{1,0:T(8,128)S(1)}, f32[264,128]{1,0:T(8,128)S(1)}, u32[]{:S(2)}, u32[]{:S(2)}) collective-permute-start(f32[264,128]{1,0:T(8,128)S(1)} %get-tuple-element.54), channel_id=1, source_target_pairs={{0,4},{1,5},{2,6},{3,7},{4,0},{5,1},{6,2},{7,3},{8,12},{9,13},{10,... | collective-permute-start | bytes 405512 | tf_op jit(solution)/shard_map/ppermute | solution.py:359
  36.7 6.7 %collective-permute-start.15 = (f32[264,128]{1,0:T(8,128)S(1)}, f32[264,128]{1,0:T(8,128)S(1)}, u32[]{:S(2)}, u32[]{:S(2)}) collective-permute-start(f32[264,128]{1,0:T(8,128)S(1)} %get-tuple-element.55), channel_id=1, source_target_pairs={{0,6},{1,7},{2,4},{3,5},{4,2},{5,3},{6,0},{7,1},{8,14},{9,15},{10,... | collective-permute-start | bytes 405512 | tf_op jit(solution)/shard_map/ppermute | solution.py:359
  43.5 12.6 %collective-permute-start.21 = (f32[280,128]{1,0:T(8,128)S(1)}, f32[280,128]{1,0:T(8,128)S(1)}, u32[]{:S(2)}, u32[]{:S(2)}) collective-permute-start(f32[280,128]{1,0:T(8,128)S(1)} %get-tuple-element.59), channel_id=1, source_target_pairs={{16,0},{8,16},{24,8},{0,24},{17,1},{9,17},{25,9},{1,25},{18,2},{10... | collective-permute-start | bytes 430088 | tf_op jit(solution)/shard_map/ppermute | solution.py:366
  45.6 5.5 %collective-permute-start.16 = (f32[8,128]{1,0:T(8,128)S(1)}, f32[8,128]{1,0:T(8,128)S(1)}, u32[]{:S(2)}, u32[]{:S(2)}) collective-permute-start(f32[8,128]{1,0:T(8,128)S(1)} %get-tuple-element.56.refs_0_), channel_id=1, source_target_pairs={{24,0},{0,16},{16,8},{8,24},{25,1},{1,17},{17,9},{9,25},{26,2},{2,... | collective-permute-start | bytes 12296 | tf_op jit(solution)/shard_map/ppermute | solution.py:366
  46.5 9.6 %collective-permute-start.17 = (f32[272,128]{1,0:T(8,128)S(1)}, f32[272,128]{1,0:T(8,128)S(1)}, u32[]{:S(2)}, u32[]{:S(2)}) collective-permute-start(f32[272,128]{1,0:T(8,128)S(1)} %get-tuple-element.57.refs_2_), channel_id=1, source_target_pairs={{0,2},{1,3},{2,0},{3,1},{4,6},{5,7},{6,4},{7,5},{8,10},{9,11},{10,... | collective-permute-start | bytes 417800 | tf_op jit(solution)/shard_map/ppermute | solution.py:359
  47.7 8.4 %collective-permute-start.18 = (f32[272,128]{1,0:T(8,128)S(1)}, f32[272,128]{1,0:T(8,128)S(1)}, u32[]{:S(2)}, u32[]{:S(2)}) collective-permute-start(f32[272,128]{1,0:T(8,128)S(1)} %get-tuple-element.57.refs_2_), channel_id=1, source_target_pairs={{0,4},{1,5},{2,6},{3,7},{4,0},{5,1},{6,2},{7,3},{8,12},{9,13},{10,... | collective-permute-start | bytes 417800 | tf_op jit(solution)/shard_map/ppermute | solution.py:359
  48.5 7.6 %collective-permute-start.19 = (f32[272,128]{1,0:T(8,128)S(1)}, f32[272,128]{1,0:T(8,128)S(1)}, u32[]{:S(2)}, u32[]{:S(2)}) collective-permute-start(f32[272,128]{1,0:T(8,128)S(1)} %get-tuple-element.57.refs_2_), channel_id=1, source_target_pairs={{0,6},{1,7},{2,4},{3,5},{4,2},{5,3},{6,0},{7,1},{8,14},{9,15},{10,... | collective-permute-start | bytes 417800 | tf_op jit(solution)/shard_map/ppermute | solution.py:359
  51.1 5.0 %collective-permute-start.20 = (f32[264,128]{1,0:T(8,128)S(1)}, f32[264,128]{1,0:T(8,128)S(1)}, u32[]{:S(2)}, u32[]{:S(2)}) collective-permute-start(f32[264,128]{1,0:T(8,128)S(1)} %get-tuple-element.58), channel_id=1, source_target_pairs={{0,8},{8,0},{16,24},{24,16},{1,9},{9,1},{17,25},{25,17},{2,10},{10... | collective-permute-start | bytes 405512 | tf_op jit(solution)/shard_map/ppermute | solution.py:366
  57.3 2.4 %collective-permute-start.22 = (bf16[1024,256]{1,0:T(8,128)(2,1)S(1)}, bf16[1024,256]{1,0:T(8,128)(2,1)S(1)}, u32[]{:S(2)}, u32[]{:S(2)}) collective-permute-start(bf16[1024,256]{1,0:T(8,128)(2,1)S(1)} %get-tuple-element.60.refs_0_.refs_10_), channel_id=1, source_target_pairs={{0,1},{1,0},{2,3},{3,2},{4,5},{5,4},{6,7},{7,6},{8,9},{9,8},{10,11... | collective-permute-start | bytes 1572872 | tf_op jit(solution)/shard_map/ppermute | solution.py:359
  58.2 7.0 %collective-permute-start.29 = (f32[1024,128]{1,0:T(8,128)S(1)}, f32[1024,128]{1,0:T(8,128)S(1)}, u32[]{:S(2)}, u32[]{:S(2)}) collective-permute-start(f32[1024,128]{1,0:T(8,128)S(1)} %get-tuple-element.70), channel_id=1, source_target_pairs={{0,1},{1,0},{2,3},{3,2},{4,5},{5,4},{6,7},{7,6},{8,9},{9,8},{10,11... | collective-permute-start | bytes 1572872 | tf_op jit(solution)/shard_map/ppermute | solution.py:359
  60.8 4.6 %collective-permute-start.25 = (f32[8,128]{1,0:T(8,128)S(1)}, f32[8,128]{1,0:T(8,128)S(1)}, u32[]{:S(2)}, u32[]{:S(2)}) collective-permute-start(f32[8,128]{1,0:T(8,128)S(1)} %get-tuple-element.66.refs_0_), channel_id=1, source_target_pairs={{16,0},{8,16},{24,8},{0,24},{17,1},{9,17},{25,9},{1,25},{18,2},{10... | collective-permute-start | bytes 12296 | tf_op jit(solution)/shard_map/ppermute | solution.py:366
  64.1 8.1 %collective-permute-start.23 = (f32[264,128]{1,0:T(8,128)S(1)}, f32[264,128]{1,0:T(8,128)S(1)}, u32[]{:S(2)}, u32[]{:S(2)}) collective-permute-start(f32[264,128]{1,0:T(8,128)S(1)} %get-tuple-element.67), channel_id=1, source_target_pairs={{0,8},{8,0},{16,24},{24,16},{1,9},{9,1},{17,25},{25,17},{2,10},{10... | collective-permute-start | bytes 405512 | tf_op jit(solution)/shard_map/ppermute | solution.py:366
  64.1 8.1 %collective-permute-start.24 = (f32[264,128]{1,0:T(8,128)S(1)}, f32[264,128]{1,0:T(8,128)S(1)}, u32[]{:S(2)}, u32[]{:S(2)}) collective-permute-start(f32[264,128]{1,0:T(8,128)S(1)} %get-tuple-element.68), channel_id=1, source_target_pairs={{24,0},{0,16},{16,8},{8,24},{25,1},{1,17},{17,9},{9,25},{26,2},{2,... | collective-permute-start | bytes 405512 | tf_op jit(solution)/shard_map/ppermute | solution.py:366
  65.5 8.9 %collective-permute-start.30 = (f32[264,128]{1,0:T(8,128)S(1)}, f32[264,128]{1,0:T(8,128)S(1)}, u32[]{:S(2)}, u32[]{:S(2)}) collective-permute-start(f32[264,128]{1,0:T(8,128)S(1)} %get-tuple-element.73), channel_id=1, source_target_pairs={{0,2},{1,3},{2,0},{3,1},{4,6},{5,7},{6,4},{7,5},{8,10},{9,11},{10,... | collective-permute-start | bytes 405512 | tf_op jit(solution)/shard_map/ppermute | solution.py:359
  67.3 8.5 %collective-permute-start.31 = (f32[264,128]{1,0:T(8,128)S(1)}, f32[264,128]{1,0:T(8,128)S(1)}, u32[]{:S(2)}, u32[]{:S(2)}) collective-permute-start(f32[264,128]{1,0:T(8,128)S(1)} %get-tuple-element.74), channel_id=1, source_target_pairs={{0,4},{1,5},{2,6},{3,7},{4,0},{5,1},{6,2},{7,3},{8,12},{9,13},{10,... | collective-permute-start | bytes 405512 | tf_op jit(solution)/shard_map/ppermute | solution.py:359
  67.7 8.2 %collective-permute-start.32 = (f32[264,128]{1,0:T(8,128)S(1)}, f32[264,128]{1,0:T(8,128)S(1)}, u32[]{:S(2)}, u32[]{:S(2)}) collective-permute-start(f32[264,128]{1,0:T(8,128)S(1)} %get-tuple-element.75), channel_id=1, source_target_pairs={{0,6},{1,7},{2,4},{3,5},{4,2},{5,3},{6,0},{7,1},{8,14},{9,15},{10,... | collective-permute-start | bytes 405512 | tf_op jit(solution)/shard_map/ppermute | solution.py:359
  72.3 3.7 %collective-permute-start.26 = (f32[8,128]{1,0:T(8,128)S(1)}, f32[8,128]{1,0:T(8,128)S(1)}, u32[]{:S(2)}, u32[]{:S(2)}) collective-permute-start(f32[8,128]{1,0:T(8,128)S(1)} %shard_map.54.refs_0_), channel_id=1, source_target_pairs={{0,2},{1,3},{2,0},{3,1},{4,6},{5,7},{6,4},{7,5},{8,10},{9,11},{10,... | collective-permute-start | bytes 12296 | tf_op jit(solution)/shard_map/ppermute | solution.py:359
  73.9 3.6 %collective-permute-start.27 = (f32[8,128]{1,0:T(8,128)S(1)}, f32[8,128]{1,0:T(8,128)S(1)}, u32[]{:S(2)}, u32[]{:S(2)}) collective-permute-start(f32[8,128]{1,0:T(8,128)S(1)} %shard_map.54.refs_0_), channel_id=1, source_target_pairs={{0,4},{1,5},{2,6},{3,7},{4,0},{5,1},{6,2},{7,3},{8,12},{9,13},{10,... | collective-permute-start | bytes 12296 | tf_op jit(solution)/shard_map/ppermute | solution.py:359
  74.4 4.5 %collective-permute-start.28 = (f32[8,128]{1,0:T(8,128)S(1)}, f32[8,128]{1,0:T(8,128)S(1)}, u32[]{:S(2)}, u32[]{:S(2)}) collective-permute-start(f32[8,128]{1,0:T(8,128)S(1)} %shard_map.54.refs_0_), channel_id=1, source_target_pairs={{0,6},{1,7},{2,4},{3,5},{4,2},{5,3},{6,0},{7,1},{8,14},{9,15},{10,... | collective-permute-start | bytes 12296 | tf_op jit(solution)/shard_map/ppermute | solution.py:359
  78.9 1.2 %collective-permute-start.33 = (f32[8,128]{1,0:T(8,128)S(1)}, f32[8,128]{1,0:T(8,128)S(1)}, u32[]{:S(2)}, u32[]{:S(2)}) collective-permute-start(f32[8,128]{1,0:T(8,128)S(1)} %shard_map.58.refs_0_), channel_id=1, source_target_pairs={{0,1},{1,0},{2,3},{3,2},{4,5},{5,4},{6,7},{7,6},{8,9},{9,8},{10,11... | collective-permute-start | bytes 12296 | tf_op jit(solution)/shard_map/ppermute | solution.py:359

commit v7 on v6

--- a/solution.py
+++ b/solution.py
@@ -9,11 +9,12 @@
 
 ITERS = 2
 STAT_ROWS = 8
-GATHER_ROWS = (8, 16, 24)
+GATHER_ROWS = (STAT_ROWS, 0)
 WIDE_ROWS = 16
+LAST_ROWS = 32
 BACK_ROWS = 16
 VMEM_BYTES = 24 * 1024 * 1024
-CROSS_COST = 6
+CROSS_COST = 2.7
 VMEM = pl.BlockSpec(memory_space=pltpu.VMEM)
 SMEM = pl.BlockSpec(memory_space=pltpu.SMEM)
 ANY = pl.BlockSpec(memory_space=pl.ANY)
@@ -142,8 +143,6 @@
         count = len(outs) - 1
         stat = outs[count]
         stat_body(has_near, *own[:1], *outs[:count], *own[1:], stat)
-        for out in outs[1:count]:
-            out[n : n + STAT_ROWS, :] = stat[...]
 
 
 def scores_call(
@@ -264,63 +263,36 @@
     )
 
 
-def fold_body(n, count, unused, even, received, *refs):
-    stats, outs = refs[:count], refs[count + unused :]
+def fold_body(n, count, even, received, *refs):
+    stats, outs = refs[:count], refs[count:]
     half = even.shape[0]
+    stat = stats[0][...]
+    for ref in stats[1:]:
+        stat += ref[...]
+    if received.shape[0] > half:
+        stat += received[half:, :]
     for j, out in enumerate(outs):
         rows = slice(j * n, (j + 1) * n)
         out[:n, :] = even[rows, :] + received[rows, :]
-        if count:
-            out[n:, :] = stats[0][...] + received[half:, :]
-        else:
-            out[n:, :] = jnp.zeros((out.shape[0] - n, out.shape[1]), F32)
-
-
-def fold_call(n, even, received, stats, extra, after=()):
+        out[n:, :] = stat
+
+
+def fold_call(n, even, received, stats, extra):
     half, clusters = even.shape
     return call(
-        functools.partial(fold_body, n, len(stats), len(after)),
-        [even, received, *stats, *after],
+        functools.partial(fold_body, n, len(stats)),
+        [even, received] + stats,
         [shaped(n + extra, clusters)] * (half // n),
-        [VMEM] * (2 + len(stats)) + [ANY] * len(after),
-    )
-
-
-def add_body(*refs):
-    refs, out = refs[:-1], refs[-1]
-    n = out.shape[0]
-    total = refs[0][:n, :]
-    for ref in refs[1:]:
-        total += ref[:n, :]
-    out[...] = total
-
-
-def column_body(n, *refs):
-    total = refs[0][...]
-    for ref in refs[1:-1]:
-        total += ref[...] if ref.shape[0] < n else ref[n : n + STAT_ROWS, :]
-    refs[-1][...] = total
-
-
-def plane_body(count, *refs):
-    total = refs[0][...]
-    for ref in refs[1:count]:
-        total += ref[...]
-    refs[-1][...] = total
+    )
 
 
 def sum_body(n, last, *refs):
     many = 2 if last else 1 + len(GATHER_ROWS)
     refs, outs = refs[:-many], refs[-many:]
-    if last:
-        stat = refs[0][...] + refs[1][...]
-        refs = refs[2:]
-    else:
-        stat = refs[0][n:, :]
-    total = refs[0][:n, :]
+    total, stat = refs[0][:n, :], refs[0][n:, :]
     for ref in refs[1:]:
         total += ref[:n, :]
-        if not last and ref.shape[0] == n + STAT_ROWS:
+        if ref.shape[0] == n + STAT_ROWS:
             stat += ref[n:, :]
     if last:
         members, standardized = outs
@@ -332,10 +304,8 @@
         stats[...] = stat
         for full in fulls:
             full[:n, :] = total
-            full[n : n + STAT_ROWS, :] = stat
-            rest = full.shape[0] - n - STAT_ROWS
-            if rest:
-                full[n + STAT_ROWS :, :] = jnp.zeros((rest, full.shape[1]), F32)
+            if full.shape[0] > n:
+                full[n:, :] = stat
 
 
 def on_device(rows, cols, features, logits):
@@ -383,19 +353,15 @@
     members = evens + [by_col(x, 1) for x in evens]
     early = 1 + has_near
     extra = [0] + [BACK_ROWS] * len(steps)
-    kernels = kernel_call(n, order, column, own_rows, features)
-    cross = []
-    for x in far_rows[has_near:]:
-        after = (cross or kernels)[-2:]
-        cross += kernel_call(n, order, column, x, features, after, CROSS_COST)
-    scores = scores_call(
-        0, members, kernels + cross, [], extra[:1] + extra[early:], hidden=True
-    )
-    if has_near:
-        near = kernel_call(n, order, column, far_rows[0], features, scores[-1:])
-        kernels += near
-        scores[1:1] = scores_call(0, members, near, [], extra[1:2], hidden=True)
-    kernels += cross
+    blocks = [kernel_call(n, order, column, own_rows, features)]
+    for x in reversed(far_rows):
+        blocks.append(
+            kernel_call(n, order, column, x, features, blocks[-1][:1], CROSS_COST)
+        )
+    blocks = blocks[:1] + blocks[:0:-1]
+    kernels = [x for block in blocks for x in block]
+    cross = kernels[2 * early :]
+    scores = scores_call(0, members, kernels, [], extra, hidden=True)
     own = pair
 
     for iteration in range(ITERS):
@@ -407,12 +373,15 @@
             scores = scores_call(0, [even], kernels, [], extra)
         if last:
             t_even, t_odd = other_call(n, half, clusters, others[has_near:], cross, [])
-            extra = [0] + [STAT_ROWS] * len(steps)
+            extra = [0] + [LAST_ROWS] * len(steps)
             *scores, stat = scores_call(
                 half, [odd], kernels, scores, extra, False, (), [own] + others, has_near
             )
-            small = [shift(stat, d) for d in offsets]
-            sent = fold_call(n, t_even, by_col(t_odd, 1), [], STAT_ROWS, small)
+            for x in [shift(stat, d) for d in range(1, rows)]:
+                stat = stat + x
+            sent = fold_call(
+                n, t_even, by_col(t_odd, 1), [stat, by_col(stat, 1)], STAT_ROWS
+            )
         else:
             if iteration > 0:
                 scores = scores_call(half, [odd], kernels, scores, extra)
@@ -421,36 +390,19 @@
             sent = fold_call(n, t_even, by_col(t_odd, 1), [stat], STAT_ROWS)
         parts = [by_col(x, k) for k, x in zip(masks, sent[1:])]
         back = [shift(x, -d) for d, x in zip(steps, scores[1:])]
-        total = []
-        if last:
-            plane = call(
-                functools.partial(column_body, n),
-                [stat] + back + small,
-                [shaped(STAT_ROWS, clusters)],
-            )[0]
-            sent = call(add_body, [sent[0], scores[0]] + parts, [shaped(n, clusters)])
-            stats = [plane] + [by_col(plane, k) for k in masks]
-            stat = call(
-                functools.partial(plane_body, len(stats)),
-                stats + sent,
-                [shaped(STAT_ROWS, clusters)],
-                [VMEM] * len(stats) + [ANY],
-            )[0]
-            total = [stat, by_col(stat, 1)]
-            parts = []
         outs = [shaped(n, clusters)] * 2
         if not last:
             outs = [shaped(STAT_ROWS, clusters)]
             outs += [shaped(n + r, clusters) for r in GATHER_ROWS]
         done = call(
             functools.partial(sum_body, n, last),
-            total + ([sent[0]] if last else [sent[0], scores[0]]) + back + parts,
+            [sent[0], scores[0]] + back + parts,
             outs,
         )
         if not last:
-            stats, near_full, part_full, cross_full = done
-            evens = [part_full] + [by_col(part_full, k) for k in masks]
-            others = [shift(cross_full if d else near_full, d) for d in steps]
+            stats, full, total = done
+            evens = [total] + [by_col(total, k) for k in masks]
+            others = [shift(full, d) for d in steps]
             stats = [stats] + [shift(stats, -d) for d in offsets]
     return tuple(done)
 

time: 81.3 us -> 75.4 us (0.927)
  waiting for transfers between devices: 32.6 us -> 28 us
  starting transfers between devices: 33.3 us -> 32.2 us
    ppermute x11 -> x13, waiting for transfers between devices: 20.2 us -> 13.1 us  [shift(): return lax.ppermute(x, 'row', pairs)]
    ppermute x23 -> x20, starting transfers between devices: 19 us -> 15.6 us  [by_col(): return lax.ppermute(x, 'col', [(i, i ^ mask) for i in range(cols)])]
    ppermute x23 -> x20, waiting for transfers between devices: 12.4 us -> 14.9 us  [by_col(): return lax.ppermute(x, 'col', [(i, i ^ mask) for i in range(cols)])]
    ppermute x11 -> x13, starting transfers between devices: 14.3 us -> 16.5 us  [shift(): return lax.ppermute(x, 'row', pairs)]
    pallas_call x19 -> x15, Pallas kernels: 11 us -> 10.7 us  [call(): pl.pallas_call(body, in_specs=specs or [VMEM] * len(args), out_specs=[VME...]
    unnamed x6 -> x4, local copies, waits for them, and re-layouts: 2.5 us -> 2.49 us
  transfers between devices with their start and end apart: 34 -> 33, of which waited for: 17 -> 15; matrix products, arithmetic and copies ran while one was open for 0% -> 0% of each run, Pallas kernels for 10% -> 10%
where the time goes in v7:
time: 75.4 us; the launch traced here: 75.2 us
  starting transfers between devices  32.2 us (43%)
  waiting for transfers between devices  28 us (37%)
  Pallas kernels  10.7 us (14%)
  local copies, waits for them, and re-layouts  3.47 us (5%)
  between operations  0.82 us (1%)
    ppermute x13, starting transfers between devices, shift(): return lax.ppermute(x, 'row', pairs)  16.5 us
    ppermute x20, starting transfers between devices, by_col(): return lax.ppermute(x, 'col', [(i, i ^ mask) for i in range(cols)])  15.6 us
    ppermute x20, waiting for transfers between devices, by_col(): return lax.ppermute(x, 'col', [(i, i ^ mask) for i in range(cols)])  14.9 us
    ppermute x13, waiting for transfers between devices, shift(): return lax.ppermute(x, 'row', pairs)  13.1 us
    pallas_call x15, Pallas kernels, call(): pl.pallas_call(body, in_specs=specs or [VMEM] * len(args), out_specs=[VME...  10.7 us
    unnamed x4, local copies, waits for them, and re-layouts  2.49 us
  transfers between devices with their start and end apart: 33, of which 15 were waited for; matrix products, arithmetic and copies ran while one was open for 0% of the time, Pallas kernels for 10%

profile of v7, /device:TPU:0, one launch (start us, length us, event | category | flops | bytes accessed | tf_op | source)
XLA Modules:
  0.0 75.2 jit_solution(7309951265090870187)
XLA Ops:
  0.6 1.0 %constant_dynamic-slice_fusion.rows.rows_ref = bf16[256,512]{1,0:T(8,128)(2,1)S(1)} fusion(bf16[2048,512]{1,0:T(8,128)(2,1)} %plane_ref.5, s32[]{:T(128)S(6)} %select_n.3), kind=kLoop, calls=%fused_computation.1 | loop fusion | bytes 524292 | tf_op jit(solution)/shard_map/dynamic_slice | solution.py:339
  1.6 5.1 %collective-permute-start.1 = (bf16[256,512]{1,0:T(8,128)(2,1)S(1)}, bf16[256,512]{1,0:T(8,128)(2,1)S(1)}, u32[]{:S(2)}, u32[]{:S(2)}) collective-permute-start(bf16[256,512]{1,0:T(8,128)(2,1)S(1)} %constant_dynamic-slice_fusion.rows.rows_ref), channel_id=1, source_target_pairs={{16,0},{8,16},{24,8},{0,24},{17,1},{9,17},{25,9},{1,25},{18,2},{10... | collective-permute-start | bytes 786440 | tf_op jit(solution)/shard_map/ppermute | solution.py:336
  6.7 0.9 %copy-done.1 = f32[256,128]{1,0:T(8,128)S(1)} copy-done((f32[256,128]{1,0:T(8,128)S(1)}, f32[256,128]{1,0:T(8,128)}, u32[]{:S(2)}) %copy-start.1) | copy-done | bytes 131096
  7.6 0.1 shard_map.41
  7.8 0.1 collective-permute-start.9
  7.8 2.5 %collective-permute-start.4 = (bf16[256,256]{1,0:T(8,128)(2,1)S(1)}, bf16[256,256]{1,0:T(8,128)(2,1)S(1)}, u32[]{:S(2)}, u32[]{:S(2)}) collective-permute-start(bf16[256,256]{1,0:T(8,128)(2,1)S(1)} %get-tuple-element.43.refs_0_.own), channel_id=1, source_target_pairs={{0,6},{1,7},{2,4},{3,5},{4,2},{5,3},{6,0},{7,1},{8,14},{9,15},{10,... | collective-permute-start | bytes 393224 | tf_op jit(solution)/shard_map/ppermute | solution.py:329
  10.4 0.5 collective-permute-start.3
  10.9 0.5 collective-permute-start.2
  11.4 1.6 %copy-done = bf16[2048,512]{1,0:T(8,128)(2,1)S(1)} copy-done((bf16[2048,512]{1,0:T(8,128)(2,1)S(1)}, bf16[2048,512]{1,0:T(8,128)(2,1)}, u32[]{:S(2)}) %copy-start) | copy-done | bytes 2097176
  13.0 0.9 %shard_map.42 = (bf16[256,2048]{1,0:T(8,128)(2,1)S(1)}, bf16[256,2048]{1,0:T(8,128)(2,1)S(1)}) custom-call(s32[1]{0:T(128)} %bitcast.column_ref, bf16[256,512]{1,0:T(8,128)(2,1)S(1)} %constant_dynamic-slice_fusion.rows.rows_ref, bf16[2048,512]{1,0:T(8,128)(2,1)S(1)} %copy-done), custom_call_target="tpu_custom_call" | custom-call | flops 536870912 | bytes 4456452 | tf_op jit(solution)/shard_map/pallas_call | solution.py:33
  13.9 3.9 %collective-permute-done.1.rows_ref = bf16[256,512]{1,0:T(8,128)(2,1)S(1)} collective-permute-done((bf16[256,512]{1,0:T(8,128)(2,1)S(1)}, bf16[256,512]{1,0:T(8,128)(2,1)S(1)}, u32[]{:S(2)}, u32[]{:S(2)}) %collective-permute-start.1) | collective-permute-done | bytes 262176 | tf_op jit(solution)/shard_map/ppermute | solution.py:336
  17.7 0.9 %shard_map.43 = (bf16[256,2048]{1,0:T(8,128)(2,1)S(1)}, bf16[256,2048]{1,0:T(8,128)(2,1)S(1)}) custom-call(s32[1]{0:T(128)} %bitcast.column_ref, bf16[256,512]{1,0:T(8,128)(2,1)S(1)} %collective-permute-done.1.rows_ref, bf16[2048,512]{1,0:T(8,128)(2,1)S(1)} %copy-done, bf16[256,2048]{1,0:T(8,128)(2,1)S(1)} %get-tuple-element.40.refs_0_.refs_8_.refs_1_), custom_call_target="tpu_custom_call" | custom-call | flops 1449132032 | bytes 5505028 | tf_op jit(solution)/shard_map/pallas_call | solution.py:33
  18.6 0.0 collective-permute-done.4.refs_3_
  18.6 0.1 collective-permute-start.5
  18.7 0.0 collective-permute-done.3.refs_2_
  18.7 0.5 collective-permute-start.8
  19.2 0.1 collective-permute-start.7
  19.3 4.8 %collective-permute-done.9.rows_ref.refs_3_ = bf16[256,768]{1,0:T(8,128)(2,1)S(1)} collective-permute-done((bf16[256,768]{1,0:T(8,128)(2,1)S(1)}, bf16[256,768]{1,0:T(8,128)(2,1)S(1)}, u32[]{:S(2)}, u32[]{:S(2)}) %collective-permute-start.9) | collective-permute-done | bytes 393248 | tf_op jit(solution)/shard_map/ppermute | solution.py:336
  24.1 0.9 %shard_map.44 = (bf16[256,2048]{1,0:T(8,128)(2,1)S(1)}, bf16[256,2048]{1,0:T(8,128)(2,1)S(1)}) custom-call(s32[1]{0:T(128)} %bitcast.column_ref, bf16[256,768]{1,0:T(8,128)(2,1)S(1)} %collective-permute-done.9.rows_ref.refs_3_, bf16[2048,512]{1,0:T(8,128)(2,1)S(1)} %copy-done, bf16[256,2048]{1,0:T(8,128)(2,1)S(1)} %get-tuple-element.41.refs_0_.refs_12_.refs_1_.refs_5_), custom_call_target="tpu_custom_call" | custom-call | flops 1449132032 | bytes 5636100 | tf_op jit(solution)/shard_map/pallas_call | solution.py:33
  25.0 0.4 collective-permute-done.6.refs_5_
  25.4 1.8 %shard_map.45 = (f32[256,128]{1,0:T(8,128)S(1)}, f32[272,128]{1,0:T(8,128)S(1)}, f32[272,128]{1,0:T(8,128)S(1)}) custom-call(bf16[256,256]{1,0:T(8,128)(2,1)S(1)} %get-tuple-element.43.refs_0_.own, bf16[256,256]{1,0:T(8,128)(2,1)S(1)} %collective-permute-done.2.refs_1_, bf16[256,256]{1,0:T(8,128)(2,1)S(1)} %collective-permute-done.3.refs_2_, ...), custom_call_target="tpu_custom_call" | custom-call | tf_op jit(solution)/shard_map/pallas_call | solution.py:33
  27.2 0.1 shard_map.46.refs_3_.refs_0_
  27.3 0.8 %shard_map.47 = (f32[1024,128]{1,0:T(8,128)S(1)}, f32[1032,128]{1,0:T(8,128)S(1)}) custom-call(bf16[272,256]{1,0:T(8,128)(2,1)S(1)} %collective-permute-done.refs_4_.refs_0_, bf16[256,2048]{1,0:T(8,128)(2,1)S(1)} %get-tuple-element.41.refs_0_.refs_12_.refs_1_.refs_5_, bf16[256,2048]{1,0:T(8,128)(2,1)S(1)} %get-tuple-element.42.refs_13_.refs_2_.refs_6_, ...), custom_call_target="tpu_custom_call" | custom-call | flops 402653184 | bytes 3293184 | tf_op jit(solution)/shard_map/pallas_call | solution.py:33
  28.1 0.2 collective-permute-start.10
  28.4 0.3 collective-permute-start.11
  28.6 1.1 %collective-permute-start.12 = (f32[272,128]{1,0:T(8,128)S(1)}, f32[272,128]{1,0:T(8,128)S(1)}, u32[]{:S(2)}, u32[]{:S(2)}) collective-permute-start(f32[272,128]{1,0:T(8,128)S(1)} %get-tuple-element.50.refs_2_), channel_id=1, source_target_pairs={{24,0},{0,16},{16,8},{8,24},{25,1},{1,17},{17,9},{9,25},{26,2},{2,... | collective-permute-start | bytes 417800 | tf_op jit(solution)/shard_map/ppermute | solution.py:336
  29.7 0.4 collective-permute-done.10.received
  30.1 0.1 shard_map.48
  30.2 1.8 %collective-permute-start.13 = (f32[264,128]{1,0:T(8,128)S(1)}, f32[264,128]{1,0:T(8,128)S(1)}, u32[]{:S(2)}, u32[]{:S(2)}) collective-permute-start(f32[264,128]{1,0:T(8,128)S(1)} %get-tuple-element.54), channel_id=1, source_target_pairs={{0,2},{1,3},{2,0},{3,1},{4,6},{5,7},{6,4},{7,5},{8,10},{9,11},{10,... | collective-permute-start | bytes 405512 | tf_op jit(solution)/shard_map/ppermute | solution.py:329
  32.0 1.5 %collective-permute-start.14 = (f32[264,128]{1,0:T(8,128)S(1)}, f32[264,128]{1,0:T(8,128)S(1)}, u32[]{:S(2)}, u32[]{:S(2)}) collective-permute-start(f32[264,128]{1,0:T(8,128)S(1)} %get-tuple-element.55), channel_id=1, source_target_pairs={{0,4},{1,5},{2,6},{3,7},{4,0},{5,1},{6,2},{7,3},{8,12},{9,13},{10,... | collective-permute-start | bytes 405512 | tf_op jit(solution)/shard_map/ppermute | solution.py:329
  33.5 0.2 collective-permute-start.15
  33.7 3.5 %collective-permute-done.11.refs_2_ = f32[272,128]{1,0:T(8,128)S(1)} collective-permute-done((f32[272,128]{1,0:T(8,128)S(1)}, f32[272,128]{1,0:T(8,128)S(1)}, u32[]{:S(2)}, u32[]{:S(2)}) %collective-permute-start.11) | collective-permute-done | bytes 139296 | tf_op jit(solution)/shard_map/ppermute | solution.py:336
  37.3 3.0 %collective-permute-done.14.refs_5_ = f32[264,128]{1,0:T(8,128)S(1)} collective-permute-done((f32[264,128]{1,0:T(8,128)S(1)}, f32[264,128]{1,0:T(8,128)S(1)}, u32[]{:S(2)}, u32[]{:S(2)}) %collective-permute-start.14) | collective-permute-done | bytes 135200 | tf_op jit(solution)/shard_map/ppermute | solution.py:329
  40.3 0.1 shard_map.49
  40.4 1.4 %collective-permute-start.16 = (f32[8,128]{1,0:T(8,128)S(1)}, f32[8,128]{1,0:T(8,128)S(1)}, u32[]{:S(2)}, u32[]{:S(2)}) collective-permute-start(f32[8,128]{1,0:T(8,128)S(1)} %get-tuple-element.57.refs_0_), channel_id=1, source_target_pairs={{24,0},{0,16},{16,8},{8,24},{25,1},{1,17},{17,9},{9,25},{26,2},{2,... | collective-permute-start | bytes 12296 | tf_op jit(solution)/shard_map/ppermute | solution.py:336
  41.8 2.4 %collective-permute-start.21 = (f32[264,128]{1,0:T(8,128)S(1)}, f32[264,128]{1,0:T(8,128)S(1)}, u32[]{:S(2)}, u32[]{:S(2)}) collective-permute-start(f32[264,128]{1,0:T(8,128)S(1)} %get-tuple-element.59), channel_id=1, source_target_pairs={{16,0},{8,16},{24,8},{0,24},{17,1},{9,17},{25,9},{1,25},{18,2},{10... | collective-permute-start | bytes 405512 | tf_op jit(solution)/shard_map/ppermute | solution.py:336
  44.2 1.5 %collective-permute-start.19 = (f32[256,128]{1,0:T(8,128)S(1)}, f32[256,128]{1,0:T(8,128)S(1)}, u32[]{:S(2)}, u32[]{:S(2)}) collective-permute-start(f32[256,128]{1,0:T(8,128)S(1)} %get-tuple-element.58.refs_2_), channel_id=1, source_target_pairs={{0,6},{1,7},{2,4},{3,5},{4,2},{5,3},{6,0},{7,1},{8,14},{9,15},{10,... | collective-permute-start | bytes 393224 | tf_op jit(solution)/shard_map/ppermute | solution.py:329
  45.7 1.2 %collective-permute-start.18 = (f32[256,128]{1,0:T(8,128)S(1)}, f32[256,128]{1,0:T(8,128)S(1)}, u32[]{:S(2)}, u32[]{:S(2)}) collective-permute-start(f32[256,128]{1,0:T(8,128)S(1)} %get-tuple-element.58.refs_2_), channel_id=1, source_target_pairs={{0,4},{1,5},{2,6},{3,7},{4,0},{5,1},{6,2},{7,3},{8,12},{9,13},{10,... | collective-permute-start | bytes 393224 | tf_op jit(solution)/shard_map/ppermute | solution.py:329
  46.9 0.8 %collective-permute-start.17 = (f32[256,128]{1,0:T(8,128)S(1)}, f32[256,128]{1,0:T(8,128)S(1)}, u32[]{:S(2)}, u32[]{:S(2)}) collective-permute-start(f32[256,128]{1,0:T(8,128)S(1)} %get-tuple-element.58.refs_2_), channel_id=1, source_target_pairs={{0,2},{1,3},{2,0},{3,1},{4,6},{5,7},{6,4},{7,5},{8,10},{9,11},{10,... | collective-permute-start | bytes 393224 | tf_op jit(solution)/shard_map/ppermute | solution.py:329
  47.7 2.9 %collective-permute-done.19.refs_5_ = f32[256,128]{1,0:T(8,128)S(1)} collective-permute-done((f32[256,128]{1,0:T(8,128)S(1)}, f32[256,128]{1,0:T(8,128)S(1)}, u32[]{:S(2)}, u32[]{:S(2)}) %collective-permute-start.19) | collective-permute-done | bytes 131104 | tf_op jit(solution)/shard_map/ppermute | solution.py:329
  50.6 1.2 %collective-permute-done.18.refs_4_ = f32[256,128]{1,0:T(8,128)S(1)} collective-permute-done((f32[256,128]{1,0:T(8,128)S(1)}, f32[256,128]{1,0:T(8,128)S(1)}, u32[]{:S(2)}, u32[]{:S(2)}) %collective-permute-start.18) | collective-permute-done | bytes 131104 | tf_op jit(solution)/shard_map/ppermute | solution.py:329
  51.8 0.2 collective-permute-done.17.refs_3_
  52.0 1.2 %shard_map.50 = (bf16[1024,256]{1,0:T(8,128)(2,1)S(1)}, bf16[256,256]{1,0:T(8,128)(2,1)S(1)}, bf16[256,256]{1,0:T(8,128)(2,1)S(1)}) custom-call(f32[8,128]{1,0:T(8,128)S(1)} %get-tuple-element.57.refs_0_, f32[8,128]{1,0:T(8,128)S(1)} %collective-permute-done.16.refs_1_, f32[256,128]{1,0:T(8,128)S(1)} %get-tuple-element.58.refs_2_, ...), custom_call_target="tpu_custom_call" | custom-call | bytes 1589248 | tf_op jit(solution)/shard_map/pallas_call | solution.py:33
  53.2 0.1 collective-permute-start.23
  53.3 0.8 %shard_map.51 = (f32[1024,128]{1,0:T(8,128)S(1)}, f32[1024,128]{1,0:T(8,128)S(1)}) custom-call(bf16[256,256]{1,0:T(8,128)(2,1)S(1)} %get-tuple-element.60.refs_0_.refs_12_, bf16[256,2048]{1,0:T(8,128)(2,1)S(1)} %get-tuple-element.41.refs_0_.refs_12_.refs_1_.refs_5_, bf16[256,2048]{1,0:T(8,128)(2,1)S(1)} %get-tuple-element.42.refs_13_.refs_2_.refs_6_), custom_call_target="tpu_custom_call" | custom-call | flops 402653184 | bytes 3276800 | tf_op jit(solution)/shard_map/pallas_call | solution.py:33
  54.1 0.6 collective-permute-start.22
  54.6 1.0 %shard_map.52 = (f32[256,128]{1,0:T(8,128)S(1)}, f32[272,128]{1,0:T(8,128)S(1)}, f32[272,128]{1,0:T(8,128)S(1)}) custom-call(bf16[1024,256]{1,0:T(8,128)(2,1)S(1)} %get-tuple-element.63.refs_0_.refs_10_, bf16[256,2048]{1,0:T(8,128)(2,1)S(1)} %get-tuple-element.40.refs_0_.refs_8_.refs_1_, bf16[256,2048]{1,0:T(8,128)(2,1)S(1)} %get-tuple-element.44.refs_9_.refs_2_, ...), custom_call_target="tpu_custom_call" | custom-call | flops 603979776 | bytes 7225344 | tf_op jit(solution)/shard_map/pallas_call | solution.py:33
  55.6 1.0 %shard_map.53 = (f32[256,128]{1,0:T(8,128)S(1)}, f32[288,128]{1,0:T(8,128)S(1)}, f32[288,128]{1,0:T(8,128)S(1)}, f32[8,128]{1,0:T(8,128)S(1)}) custom-call(bf16[1024,256]{1,0:T(8,128)(2,1)S(1)} %collective-permute-done.23.refs_0_, bf16[256,2048]{1,0:T(8,128)(2,1)S(1)} %get-tuple-element.40.refs_0_.refs_8_.refs_1_, ...), custom_call_target="tpu_custom_call" | custom-call | flops 603979776 | bytes 8441856 | tf_op jit(solution)/shard_map/pallas_call | solution.py:33
  56.7 1.6 %collective-permute-start.26 = (f32[8,128]{1,0:T(8,128)S(1)}, f32[8,128]{1,0:T(8,128)S(1)}, u32[]{:S(2)}, u32[]{:S(2)}) collective-permute-start(f32[8,128]{1,0:T(8,128)S(1)} %get-tuple-element.68), channel_id=1, source_target_pairs={{24,0},{0,16},{16,8},{8,24},{25,1},{1,17},{17,9},{9,25},{26,2},{2,... | collective-permute-start | bytes 12296 | tf_op jit(solution)/shard_map/ppermute | solution.py:336
  58.3 0.8 %collective-permute-start.25 = (f32[8,128]{1,0:T(8,128)S(1)}, f32[8,128]{1,0:T(8,128)S(1)}, u32[]{:S(2)}, u32[]{:S(2)}) collective-permute-start(f32[8,128]{1,0:T(8,128)S(1)} %get-tuple-element.68), channel_id=1, source_target_pairs={{8,0},{24,16},{0,8},{16,24},{9,1},{25,17},{1,9},{17,25},{10,2},{26... | collective-permute-start | bytes 12296 | tf_op jit(solution)/shard_map/ppermute | solution.py:336
  59.1 2.4 %collective-permute-start.24 = (f32[8,128]{1,0:T(8,128)S(1)}, f32[8,128]{1,0:T(8,128)S(1)}, u32[]{:S(2)}, u32[]{:S(2)}) collective-permute-start(f32[8,128]{1,0:T(8,128)S(1)} %get-tuple-element.68), channel_id=1, source_target_pairs={{16,0},{8,16},{24,8},{0,24},{17,1},{9,17},{25,9},{1,25},{18,2},{10... | collective-permute-start | bytes 12296 | tf_op jit(solution)/shard_map/ppermute | solution.py:336
  61.6 0.1 collective-permute-start.28
  61.7 0.5 collective-permute-done.26
  62.1 1.1 %collective-permute-start.29 = (f32[288,128]{1,0:T(8,128)S(1)}, f32[288,128]{1,0:T(8,128)S(1)}, u32[]{:S(2)}, u32[]{:S(2)}) collective-permute-start(f32[288,128]{1,0:T(8,128)S(1)} %get-tuple-element.72), channel_id=1, source_target_pairs={{24,0},{0,16},{16,8},{8,24},{25,1},{1,17},{17,9},{9,25},{26,2},{2,... | collective-permute-start | bytes 442376 | tf_op jit(solution)/shard_map/ppermute | solution.py:336
  63.3 0.5 collective-permute-done.24
  63.8 1.2 %collective-permute-done.27.refs_1_ = f32[8,128]{1,0:T(8,128)S(1)} collective-permute-done((f32[8,128]{1,0:T(8,128)S(1)}, f32[8,128]{1,0:T(8,128)S(1)}, u32[]{:S(2)}, u32[]{:S(2)}) %collective-permute-start.27) | collective-permute-done | bytes 4128 | tf_op jit(solution)/shard_map/ppermute | solution.py:329
  64.9 0.1 shard_map.54
  65.0 0.9 %collective-permute-start.30 = (f32[264,128]{1,0:T(8,128)S(1)}, f32[264,128]{1,0:T(8,128)S(1)}, u32[]{:S(2)}, u32[]{:S(2)}) collective-permute-start(f32[264,128]{1,0:T(8,128)S(1)} %get-tuple-element.73), channel_id=1, source_target_pairs={{0,2},{1,3},{2,0},{3,1},{4,6},{5,7},{6,4},{7,5},{8,10},{9,11},{10,... | collective-permute-start | bytes 405512 | tf_op jit(solution)/shard_map/ppermute | solution.py:329
  65.9 1.5 %collective-permute-start.31 = (f32[264,128]{1,0:T(8,128)S(1)}, f32[264,128]{1,0:T(8,128)S(1)}, u32[]{:S(2)}, u32[]{:S(2)}) collective-permute-start(f32[264,128]{1,0:T(8,128)S(1)} %get-tuple-element.74), channel_id=1, source_target_pairs={{0,4},{1,5},{2,6},{3,7},{4,0},{5,1},{6,2},{7,3},{8,12},{9,13},{10,... | collective-permute-start | bytes 405512 | tf_op jit(solution)/shard_map/ppermute | solution.py:329
  67.4 1.2 %collective-permute-start.32 = (f32[264,128]{1,0:T(8,128)S(1)}, f32[264,128]{1,0:T(8,128)S(1)}, u32[]{:S(2)}, u32[]{:S(2)}) collective-permute-start(f32[264,128]{1,0:T(8,128)S(1)} %get-tuple-element.75), channel_id=1, source_target_pairs={{0,6},{1,7},{2,4},{3,5},{4,2},{5,3},{6,0},{7,1},{8,14},{9,15},{10,... | collective-permute-start | bytes 405512 | tf_op jit(solution)/shard_map/ppermute | solution.py:329
  68.6 2.9 %collective-permute-done.30.refs_4_ = f32[264,128]{1,0:T(8,128)S(1)} collective-permute-done((f32[264,128]{1,0:T(8,128)S(1)}, f32[264,128]{1,0:T(8,128)S(1)}, u32[]{:S(2)}, u32[]{:S(2)}) %collective-permute-start.30) | collective-permute-done | bytes 135200 | tf_op jit(solution)/shard_map/ppermute | solution.py:329
  71.5 1.7 %collective-permute-done.31.refs_5_ = f32[264,128]{1,0:T(8,128)S(1)} collective-permute-done((f32[264,128]{1,0:T(8,128)S(1)}, f32[264,128]{1,0:T(8,128)S(1)}, u32[]{:S(2)}, u32[]{:S(2)}) %collective-permute-start.31) | collective-permute-done | bytes 135200 | tf_op jit(solution)/shard_map/ppermute | solution.py:329
  73.2 1.0 %collective-permute-done.32.refs_6_ = f32[264,128]{1,0:T(8,128)S(1)} collective-permute-done((f32[264,128]{1,0:T(8,128)S(1)}, f32[264,128]{1,0:T(8,128)S(1)}, u32[]{:S(2)}, u32[]{:S(2)}) %collective-permute-start.32) | collective-permute-done | bytes 135200 | tf_op jit(solution)/shard_map/ppermute | solution.py:329
  74.2 1.0 %shard_map.55 = (f32[256,128]{1,0:T(8,128)}, f32[256,128]{1,0:T(8,128)}) custom-call(f32[264,128]{1,0:T(8,128)S(1)} %get-tuple-element.69.refs_0_, f32[256,128]{1,0:T(8,128)S(1)} %get-tuple-element.70.refs_1_, f32[288,128]{1,0:T(8,128)S(1)} %collective-permute-done.28.refs_2_, f32[288,128]{1,0:T(8,128)S(1)} %collective-permute-done.29.refs_3_, ...), custom_call_target="tpu_custom_call" | custom-call | bytes 1228800 | tf_op jit(solution)/shard_map/pallas_call | solution.py:33
  (23 shorter events, 0.1 us)
Async XLA Ops:
  1.6 16.1 %collective-permute-start.1 = (bf16[256,512]{1,0:T(8,128)(2,1)S(1)}, bf16[256,512]{1,0:T(8,128)(2,1)S(1)}, u32[]{:S(2)}, u32[]{:S(2)}) collective-permute-start(bf16[256,512]{1,0:T(8,128)(2,1)S(1)} %constant_dynamic-slice_fusion.rows.rows_ref), channel_id=1, source_target_pairs={{16,0},{8,16},{24,8},{0,24},{17,1},{9,17},{25,9},{1,25},{18,2},{10... | collective-permute-start | bytes 786440 | tf_op jit(solution)/shard_map/ppermute | solution.py:336
  6.7 0.9 %copy-start.1 = (f32[256,128]{1,0:T(8,128)S(1)}, f32[256,128]{1,0:T(8,128)}, u32[]{:S(2)}) copy-start(f32[256,128]{1,0:T(8,128)} %logits.1) | copy-start | bytes 393220
  7.8 16.3 %collective-permute-start.9 = (bf16[256,768]{1,0:T(8,128)(2,1)S(1)}, bf16[256,768]{1,0:T(8,128)(2,1)S(1)}, u32[]{:S(2)}, u32[]{:S(2)}) collective-permute-start(bf16[256,768]{1,0:T(8,128)(2,1)S(1)} %get-tuple-element.45), channel_id=1, source_target_pairs={{0,8},{8,0},{16,24},{24,16},{1,9},{9,1},{17,25},{25,17},{2,10},{10... | collective-permute-start | bytes 1179656 | tf_op jit(solution)/shard_map/ppermute | solution.py:336
  7.8 10.8 %collective-permute-start.4 = (bf16[256,256]{1,0:T(8,128)(2,1)S(1)}, bf16[256,256]{1,0:T(8,128)(2,1)S(1)}, u32[]{:S(2)}, u32[]{:S(2)}) collective-permute-start(bf16[256,256]{1,0:T(8,128)(2,1)S(1)} %get-tuple-element.43.refs_0_.own), channel_id=1, source_target_pairs={{0,6},{1,7},{2,4},{3,5},{4,2},{5,3},{6,0},{7,1},{8,14},{9,15},{10,... | collective-permute-start | bytes 393224 | tf_op jit(solution)/shard_map/ppermute | solution.py:329
  10.4 8.4 %collective-permute-start.3 = (bf16[256,256]{1,0:T(8,128)(2,1)S(1)}, bf16[256,256]{1,0:T(8,128)(2,1)S(1)}, u32[]{:S(2)}, u32[]{:S(2)}) collective-permute-start(bf16[256,256]{1,0:T(8,128)(2,1)S(1)} %get-tuple-element.43.refs_0_.own), channel_id=1, source_target_pairs={{0,4},{1,5},{2,6},{3,7},{4,0},{5,1},{6,2},{7,3},{8,12},{9,13},{10,... | collective-permute-start | bytes 393224 | tf_op jit(solution)/shard_map/ppermute | solution.py:329
  10.9 8.4 %collective-permute-start.2 = (bf16[256,256]{1,0:T(8,128)(2,1)S(1)}, bf16[256,256]{1,0:T(8,128)(2,1)S(1)}, u32[]{:S(2)}, u32[]{:S(2)}) collective-permute-start(bf16[256,256]{1,0:T(8,128)(2,1)S(1)} %get-tuple-element.43.refs_0_.own), channel_id=1, source_target_pairs={{0,2},{1,3},{2,0},{3,1},{4,6},{5,7},{6,4},{7,5},{8,10},{9,11},{10,... | collective-permute-start | bytes 393224 | tf_op jit(solution)/shard_map/ppermute | solution.py:329
  11.4 1.6 %copy-start = (bf16[2048,512]{1,0:T(8,128)(2,1)S(1)}, bf16[2048,512]{1,0:T(8,128)(2,1)}, u32[]{:S(2)}) copy-start(bf16[2048,512]{1,0:T(8,128)(2,1)} %plane_ref.5) | copy-start | bytes 6291460
  17.7 9.5 %collective-permute-start = (bf16[272,256]{1,0:T(8,128)(2,1)S(1)}, bf16[272,256]{1,0:T(8,128)(2,1)S(1)}, u32[]{:S(2)}, u32[]{:S(2)}) collective-permute-start(bf16[272,256]{1,0:T(8,128)(2,1)S(1)} %get-tuple-element.39), channel_id=1, source_target_pairs={{16,0},{8,16},{24,8},{0,24},{17,1},{9,17},{25,9},{1,25},{18,2},{10... | collective-permute-start | bytes 417800 | tf_op jit(solution)/shard_map/ppermute | solution.py:336
  18.6 6.3 %collective-permute-start.5 = (bf16[256,256]{1,0:T(8,128)(2,1)S(1)}, bf16[256,256]{1,0:T(8,128)(2,1)S(1)}, u32[]{:S(2)}, u32[]{:S(2)}) collective-permute-start(bf16[256,256]{1,0:T(8,128)(2,1)S(1)} %get-tuple-element.43.refs_0_.own), channel_id=1, source_target_pairs={{0,1},{1,0},{2,3},{3,2},{4,5},{5,4},{6,7},{7,6},{8,9},{9,8},{10,11... | collective-permute-start | bytes 393224 | tf_op jit(solution)/shard_map/ppermute | solution.py:329
  18.7 6.2 %collective-permute-start.8 = (bf16[256,256]{1,0:T(8,128)(2,1)S(1)}, bf16[256,256]{1,0:T(8,128)(2,1)S(1)}, u32[]{:S(2)}, u32[]{:S(2)}) collective-permute-start(bf16[256,256]{1,0:T(8,128)(2,1)S(1)} %collective-permute-done.4.refs_3_), channel_id=1, source_target_pairs={{0,1},{1,0},{2,3},{3,2},{4,5},{5,4},{6,7},{7,6},{8,9},{9,8},{10,11... | collective-permute-start | bytes 393224 | tf_op jit(solution)/shard_map/ppermute | solution.py:329
  19.2 5.7 %collective-permute-start.7 = (bf16[256,256]{1,0:T(8,128)(2,1)S(1)}, bf16[256,256]{1,0:T(8,128)(2,1)S(1)}, u32[]{:S(2)}, u32[]{:S(2)}) collective-permute-start(bf16[256,256]{1,0:T(8,128)(2,1)S(1)} %collective-permute-done.3.refs_2_), channel_id=1, source_target_pairs={{0,1},{1,0},{2,3},{3,2},{4,5},{5,4},{6,7},{7,6},{8,9},{9,8},{10,11... | collective-permute-start | bytes 393224 | tf_op jit(solution)/shard_map/ppermute | solution.py:329
  24.1 1.3 %collective-permute-start.6 = (bf16[256,256]{1,0:T(8,128)(2,1)S(1)}, bf16[256,256]{1,0:T(8,128)(2,1)S(1)}, u32[]{:S(2)}, u32[]{:S(2)}) collective-permute-start(bf16[256,256]{1,0:T(8,128)(2,1)S(1)} %collective-permute-done.2.refs_1_), channel_id=1, source_target_pairs={{0,1},{1,0},{2,3},{3,2},{4,5},{5,4},{6,7},{7,6},{8,9},{9,8},{10,11... | collective-permute-start | bytes 393224 | tf_op jit(solution)/shard_map/ppermute | solution.py:329
  28.1 2.0 %collective-permute-start.10 = (f32[1032,128]{1,0:T(8,128)S(1)}, f32[1032,128]{1,0:T(8,128)S(1)}, u32[]{:S(2)}, u32[]{:S(2)}) collective-permute-start(f32[1032,128]{1,0:T(8,128)S(1)} %get-tuple-element.52), channel_id=1, source_target_pairs={{0,1},{1,0},{2,3},{3,2},{4,5},{5,4},{6,7},{7,6},{8,9},{9,8},{10,11... | collective-permute-start | bytes 1585160 | tf_op jit(solution)/shard_map/ppermute | solution.py:329
  28.4 8.9 %collective-permute-start.11 = (f32[272,128]{1,0:T(8,128)S(1)}, f32[272,128]{1,0:T(8,128)S(1)}, u32[]{:S(2)}, u32[]{:S(2)}) collective-permute-start(f32[272,128]{1,0:T(8,128)S(1)} %get-tuple-element.49.refs_1_), channel_id=1, source_target_pairs={{0,8},{8,0},{16,24},{24,16},{1,9},{9,1},{17,25},{25,17},{2,10},{10... | collective-permute-start | bytes 417800 | tf_op jit(solution)/shard_map/ppermute | solution.py:336
  28.6 8.6 %collective-permute-start.12 = (f32[272,128]{1,0:T(8,128)S(1)}, f32[272,128]{1,0:T(8,128)S(1)}, u32[]{:S(2)}, u32[]{:S(2)}) collective-permute-start(f32[272,128]{1,0:T(8,128)S(1)} %get-tuple-element.50.refs_2_), channel_id=1, source_target_pairs={{24,0},{0,16},{16,8},{8,24},{25,1},{1,17},{17,9},{9,25},{26,2},{2,... | collective-permute-start | bytes 417800 | tf_op jit(solution)/shard_map/ppermute | solution.py:336
  30.2 7.1 %collective-permute-start.13 = (f32[264,128]{1,0:T(8,128)S(1)}, f32[264,128]{1,0:T(8,128)S(1)}, u32[]{:S(2)}, u32[]{:S(2)}) collective-permute-start(f32[264,128]{1,0:T(8,128)S(1)} %get-tuple-element.54), channel_id=1, source_target_pairs={{0,2},{1,3},{2,0},{3,1},{4,6},{5,7},{6,4},{7,5},{8,10},{9,11},{10,... | collective-permute-start | bytes 405512 | tf_op jit(solution)/shard_map/ppermute | solution.py:329
  32.0 8.3 %collective-permute-start.14 = (f32[264,128]{1,0:T(8,128)S(1)}, f32[264,128]{1,0:T(8,128)S(1)}, u32[]{:S(2)}, u32[]{:S(2)}) collective-permute-start(f32[264,128]{1,0:T(8,128)S(1)} %get-tuple-element.55), channel_id=1, source_target_pairs={{0,4},{1,5},{2,6},{3,7},{4,0},{5,1},{6,2},{7,3},{8,12},{9,13},{10,... | collective-permute-start | bytes 405512 | tf_op jit(solution)/shard_map/ppermute | solution.py:329
  33.5 6.7 %collective-permute-start.15 = (f32[264,128]{1,0:T(8,128)S(1)}, f32[264,128]{1,0:T(8,128)S(1)}, u32[]{:S(2)}, u32[]{:S(2)}) collective-permute-start(f32[264,128]{1,0:T(8,128)S(1)} %get-tuple-element.56), channel_id=1, source_target_pairs={{0,6},{1,7},{2,4},{3,5},{4,2},{5,3},{6,0},{7,1},{8,14},{9,15},{10,... | collective-permute-start | bytes 405512 | tf_op jit(solution)/shard_map/ppermute | solution.py:329
  40.4 6.6 %collective-permute-start.16 = (f32[8,128]{1,0:T(8,128)S(1)}, f32[8,128]{1,0:T(8,128)S(1)}, u32[]{:S(2)}, u32[]{:S(2)}) collective-permute-start(f32[8,128]{1,0:T(8,128)S(1)} %get-tuple-element.57.refs_0_), channel_id=1, source_target_pairs={{24,0},{0,16},{16,8},{8,24},{25,1},{1,17},{17,9},{9,25},{26,2},{2,... | collective-permute-start | bytes 12296 | tf_op jit(solution)/shard_map/ppermute | solution.py:336
  41.8 10.2 %collective-permute-start.21 = (f32[264,128]{1,0:T(8,128)S(1)}, f32[264,128]{1,0:T(8,128)S(1)}, u32[]{:S(2)}, u32[]{:S(2)}) collective-permute-start(f32[264,128]{1,0:T(8,128)S(1)} %get-tuple-element.59), channel_id=1, source_target_pairs={{16,0},{8,16},{24,8},{0,24},{17,1},{9,17},{25,9},{1,25},{18,2},{10... | collective-permute-start | bytes 405512 | tf_op jit(solution)/shard_map/ppermute | solution.py:336
  44.2 7.8 %collective-permute-start.20 = (f32[264,128]{1,0:T(8,128)S(1)}, f32[264,128]{1,0:T(8,128)S(1)}, u32[]{:S(2)}, u32[]{:S(2)}) collective-permute-start(f32[264,128]{1,0:T(8,128)S(1)} %get-tuple-element.59), channel_id=1, source_target_pairs={{0,8},{8,0},{16,24},{24,16},{1,9},{9,1},{17,25},{25,17},{2,10},{10... | collective-permute-start | bytes 405512 | tf_op jit(solution)/shard_map/ppermute | solution.py:336
  44.2 6.3 %collective-permute-start.19 = (f32[256,128]{1,0:T(8,128)S(1)}, f32[256,128]{1,0:T(8,128)S(1)}, u32[]{:S(2)}, u32[]{:S(2)}) collective-permute-start(f32[256,128]{1,0:T(8,128)S(1)} %get-tuple-element.58.refs_2_), channel_id=1, source_target_pairs={{0,6},{1,7},{2,4},{3,5},{4,2},{5,3},{6,0},{7,1},{8,14},{9,15},{10,... | collective-permute-start | bytes 393224 | tf_op jit(solution)/shard_map/ppermute | solution.py:329
  45.7 6.1 %collective-permute-start.18 = (f32[256,128]{1,0:T(8,128)S(1)}, f32[256,128]{1,0:T(8,128)S(1)}, u32[]{:S(2)}, u32[]{:S(2)}) collective-permute-start(f32[256,128]{1,0:T(8,128)S(1)} %get-tuple-element.58.refs_2_), channel_id=1, source_target_pairs={{0,4},{1,5},{2,6},{3,7},{4,0},{5,1},{6,2},{7,3},{8,12},{9,13},{10,... | collective-permute-start | bytes 393224 | tf_op jit(solution)/shard_map/ppermute | solution.py:329
  46.9 5.1 %collective-permute-start.17 = (f32[256,128]{1,0:T(8,128)S(1)}, f32[256,128]{1,0:T(8,128)S(1)}, u32[]{:S(2)}, u32[]{:S(2)}) collective-permute-start(f32[256,128]{1,0:T(8,128)S(1)} %get-tuple-element.58.refs_2_), channel_id=1, source_target_pairs={{0,2},{1,3},{2,0},{3,1},{4,6},{5,7},{6,4},{7,5},{8,10},{9,11},{10,... | collective-permute-start | bytes 393224 | tf_op jit(solution)/shard_map/ppermute | solution.py:329
  53.2 2.4 %collective-permute-start.23 = (bf16[1024,256]{1,0:T(8,128)(2,1)S(1)}, bf16[1024,256]{1,0:T(8,128)(2,1)S(1)}, u32[]{:S(2)}, u32[]{:S(2)}) collective-permute-start(bf16[1024,256]{1,0:T(8,128)(2,1)S(1)} %get-tuple-element.63.refs_0_.refs_10_), channel_id=1, source_target_pairs={{0,1},{1,0},{2,3},{3,2},{4,5},{5,4},{6,7},{7,6},{8,9},{9,8},{10,11... | collective-permute-start | bytes 1572872 | tf_op jit(solution)/shard_map/ppermute | solution.py:329
  54.1 9.7 %collective-permute-start.22 = (f32[1024,128]{1,0:T(8,128)S(1)}, f32[1024,128]{1,0:T(8,128)S(1)}, u32[]{:S(2)}, u32[]{:S(2)}) collective-permute-start(f32[1024,128]{1,0:T(8,128)S(1)} %get-tuple-element.62), channel_id=1, source_target_pairs={{0,1},{1,0},{2,3},{3,2},{4,5},{5,4},{6,7},{7,6},{8,9},{9,8},{10,11... | collective-permute-start | bytes 1572872 | tf_op jit(solution)/shard_map/ppermute | solution.py:329
  56.7 5.5 %collective-permute-start.26 = (f32[8,128]{1,0:T(8,128)S(1)}, f32[8,128]{1,0:T(8,128)S(1)}, u32[]{:S(2)}, u32[]{:S(2)}) collective-permute-start(f32[8,128]{1,0:T(8,128)S(1)} %get-tuple-element.68), channel_id=1, source_target_pairs={{24,0},{0,16},{16,8},{8,24},{25,1},{1,17},{17,9},{9,25},{26,2},{2,... | collective-permute-start | bytes 12296 | tf_op jit(solution)/shard_map/ppermute | solution.py:336
  58.3 5.0 %collective-permute-start.25 = (f32[8,128]{1,0:T(8,128)S(1)}, f32[8,128]{1,0:T(8,128)S(1)}, u32[]{:S(2)}, u32[]{:S(2)}) collective-permute-start(f32[8,128]{1,0:T(8,128)S(1)} %get-tuple-element.68), channel_id=1, source_target_pairs={{8,0},{24,16},{0,8},{16,24},{9,1},{25,17},{1,9},{17,25},{10,2},{26... | collective-permute-start | bytes 12296 | tf_op jit(solution)/shard_map/ppermute | solution.py:336
  59.1 4.6 %collective-permute-start.24 = (f32[8,128]{1,0:T(8,128)S(1)}, f32[8,128]{1,0:T(8,128)S(1)}, u32[]{:S(2)}, u32[]{:S(2)}) collective-permute-start(f32[8,128]{1,0:T(8,128)S(1)} %get-tuple-element.68), channel_id=1, source_target_pairs={{16,0},{8,16},{24,8},{0,24},{17,1},{9,17},{25,9},{1,25},{18,2},{10... | collective-permute-start | bytes 12296 | tf_op jit(solution)/shard_map/ppermute | solution.py:336
  61.6 12.6 %collective-permute-start.28 = (f32[288,128]{1,0:T(8,128)S(1)}, f32[288,128]{1,0:T(8,128)S(1)}, u32[]{:S(2)}, u32[]{:S(2)}) collective-permute-start(f32[288,128]{1,0:T(8,128)S(1)} %get-tuple-element.71), channel_id=1, source_target_pairs={{0,8},{8,0},{16,24},{24,16},{1,9},{9,1},{17,25},{25,17},{2,10},{10... | collective-permute-start | bytes 442376 | tf_op jit(solution)/shard_map/ppermute | solution.py:336
  62.1 12.1 %collective-permute-start.29 = (f32[288,128]{1,0:T(8,128)S(1)}, f32[288,128]{1,0:T(8,128)S(1)}, u32[]{:S(2)}, u32[]{:S(2)}) collective-permute-start(f32[288,128]{1,0:T(8,128)S(1)} %get-tuple-element.72), channel_id=1, source_target_pairs={{24,0},{0,16},{16,8},{8,24},{25,1},{1,17},{17,9},{9,25},{26,2},{2,... | collective-permute-start | bytes 442376 | tf_op jit(solution)/shard_map/ppermute | solution.py:336
  63.8 1.2 %collective-permute-start.27 = (f32[8,128]{1,0:T(8,128)S(1)}, f32[8,128]{1,0:T(8,128)S(1)}, u32[]{:S(2)}, u32[]{:S(2)}) collective-permute-start(f32[8,128]{1,0:T(8,128)S(1)} %add_add_fusion.refs_0_), channel_id=1, source_target_pairs={{0,1},{1,0},{2,3},{3,2},{4,5},{5,4},{6,7},{7,6},{8,9},{9,8},{10,11... | collective-permute-start | bytes 12296 | tf_op jit(solution)/shard_map/ppermute | solution.py:329
  65.0 6.5 %collective-permute-start.30 = (f32[264,128]{1,0:T(8,128)S(1)}, f32[264,128]{1,0:T(8,128)S(1)}, u32[]{:S(2)}, u32[]{:S(2)}) collective-permute-start(f32[264,128]{1,0:T(8,128)S(1)} %get-tuple-element.73), channel_id=1, source_target_pairs={{0,2},{1,3},{2,0},{3,1},{4,6},{5,7},{6,4},{7,5},{8,10},{9,11},{10,... | collective-permute-start | bytes 405512 | tf_op jit(solution)/shard_map/ppermute | solution.py:329
  65.9 7.3 %collective-permute-start.31 = (f32[264,128]{1,0:T(8,128)S(1)}, f32[264,128]{1,0:T(8,128)S(1)}, u32[]{:S(2)}, u32[]{:S(2)}) collective-permute-start(f32[264,128]{1,0:T(8,128)S(1)} %get-tuple-element.74), channel_id=1, source_target_pairs={{0,4},{1,5},{2,6},{3,7},{4,0},{5,1},{6,2},{7,3},{8,12},{9,13},{10,... | collective-permute-start | bytes 405512 | tf_op jit(solution)/shard_map/ppermute | solution.py:329
  67.4 6.8 %collective-permute-start.32 = (f32[264,128]{1,0:T(8,128)S(1)}, f32[264,128]{1,0:T(8,128)S(1)}, u32[]{:S(2)}, u32[]{:S(2)}) collective-permute-start(f32[264,128]{1,0:T(8,128)S(1)} %get-tuple-element.75), channel_id=1, source_target_pairs={{0,6},{1,7},{2,4},{3,5},{4,2},{5,3},{6,0},{7,1},{8,14},{9,15},{10,... | collective-permute-start | bytes 405512 | tf_op jit(solution)/shard_map/ppermute | solution.py:329

commit v8 on v7

--- a/solution.py
+++ b/solution.py
@@ -7,14 +7,14 @@
 from jax.experimental.pallas import tpu as pltpu
 from jax.sharding import PartitionSpec as P
 
-ITERS = 2
 STAT_ROWS = 8
-GATHER_ROWS = (STAT_ROWS, 0)
+FAR_ROWS = 16
 WIDE_ROWS = 16
 LAST_ROWS = 32
 BACK_ROWS = 16
 VMEM_BYTES = 24 * 1024 * 1024
-CROSS_COST = 2.7
+NEAR_COST = 10
+CROSS_COST = 4
 VMEM = pl.BlockSpec(memory_space=pltpu.VMEM)
 SMEM = pl.BlockSpec(memory_space=pltpu.SMEM)
 ANY = pl.BlockSpec(memory_space=pl.ANY)
@@ -142,7 +142,7 @@
     if weights:
         count = len(outs) - 1
         stat = outs[count]
-        stat_body(has_near, *own[:1], *outs[:count], *own[1:], stat)
+        stat_body(has_near, count - 1, *own[:1], *outs[:count], *own[1:], stat)
 
 
 def scores_call(
@@ -171,16 +171,13 @@
     )
 
 
-def members_body(n, smalls, evens, others, *refs):
-    stats, refs = refs[:smalls], refs[smalls:]
+def members_body(n, evens, *refs):
     own, refs = refs[:evens], refs[evens:]
-    rest, refs = refs[:others], refs[others:]
-    even, pairs = refs[0], refs[1:]
-    stat = stats[0][...]
-    for ref in stats[1:]:
-        stat += ref[...]
-    for ref in rest:
-        stat += ref[n : n + STAT_ROWS, :]
+    others = (len(refs) - 1) // 2
+    rest, even, pairs = refs[:others], refs[others], refs[others + 1 :]
+    stat = own[0][n:, :]
+    for ref in own[1:]:
+        stat += ref[n:, :]
     weighted, size = stat[0:1, :], stat[1:2, :]
 
     def member_of(x):
@@ -192,20 +189,19 @@
         store_pair(pair, slice(0, n), member_of(ref[:n, :]))
 
 
-def members_call(n, stats, evens, others):
+def members_call(n, evens, others):
     clusters = evens[0].shape[1]
     return call(
-        functools.partial(members_body, n, len(stats), len(evens), len(others)),
-        stats + evens + others,
+        functools.partial(members_body, n, len(evens)),
+        evens + others,
         [shaped(n * len(evens), 2 * clusters, BF16)]
         + [shaped(n, 2 * clusters, BF16)] * len(others),
     )
 
 
-def stat_body(has_near, own, *refs):
-    out, refs = refs[-1], refs[:-1]
-    count = len(refs) // 2
-    scores, pairs = refs[: count + 1], refs[count + 1 :]
+def stat_body(has_near, count, own, *refs):
+    scores, refs = refs[: count + 1], refs[count + 1 :]
+    pairs, out, wide = refs[:count], refs[count], refs[count + 1 :]
     n, clusters = scores[0].shape
     member = whole(own[:n, :])
     total = jnp.sum(member * scores[0][...], axis=0, keepdims=True)
@@ -216,22 +212,29 @@
         total += part if i < has_near else 2.0 * part
     size = jnp.sum(member, axis=0, keepdims=True)
     row = lax.broadcasted_iota(jnp.int32, out.shape, 0)
-    out[...] = jnp.where(row == 0, total, jnp.where(row == 1, size, 0.0))
-
-
-def stat_call(has_near, own, scores, pairs):
-    clusters = scores[0].shape[1]
-    return call(
-        functools.partial(stat_body, has_near),
+    stat = jnp.where(row == 0, total, jnp.where(row == 1, size, 0.0))
+    out[...] = stat
+    for back, score in zip(wide, scores[1:]):
+        back[:n, :] = score[:n, :]
+        back[n : n + STAT_ROWS, :] = stat
+        rest = back.shape[0] - n - STAT_ROWS
+        if rest:
+            back[n + STAT_ROWS :, :] = jnp.zeros((rest, clusters), F32)
+
+
+def stat_call(has_near, own, scores, pairs, extra):
+    n, clusters = scores[0].shape
+    return call(
+        functools.partial(stat_body, has_near, len(pairs)),
         [own] + scores + pairs,
-        [shaped(STAT_ROWS, clusters)],
-    )[0]
+        [shaped(STAT_ROWS, clusters)] + [shaped(n + extra, clusters)] * len(pairs),
+    )
 
 
 def other_body(n, count, *refs):
     pairs, refs = refs[:count], refs[count:]
     kernels, refs = refs[: 2 * count], refs[2 * count :]
-    stat, (even, odd) = refs[:-2], refs[-2:]
+    even, odd = refs[-2:]
     half, clusters = even.shape
     over = (((0,), (0,)), ((), ()))
     for part, out in enumerate((odd, even)):
@@ -249,36 +252,31 @@
                 preferred_element_type=F32,
             )
             acc += a[:, :clusters] + (a[:, clusters:] + b)
-        out[:half, :] = acc
-    if stat:
-        odd[half:, :] = stat[0][...]
-
-
-def other_call(n, half, clusters, pairs, kernels, stat):
+        out[...] = acc
+
+
+def other_call(n, half, clusters, pairs, kernels, after=()):
     return call(
         functools.partial(other_body, n, len(pairs)),
-        pairs + kernels + stat,
-        [shaped(half, clusters), shaped(half + STAT_ROWS * len(stat), clusters)],
+        [*pairs, *kernels, *after],
+        [shaped(half, clusters)] * 2,
+        [VMEM] * (len(pairs) + len(kernels)) + [ANY] * len(after),
         flops=12 * n * len(pairs) * half * clusters,
     )
 
 
 def fold_body(n, count, even, received, *refs):
     stats, outs = refs[:count], refs[count:]
-    half = even.shape[0]
-    stat = stats[0][...]
-    for ref in stats[1:]:
-        stat += ref[...]
-    if received.shape[0] > half:
-        stat += received[half:, :]
     for j, out in enumerate(outs):
         rows = slice(j * n, (j + 1) * n)
         out[:n, :] = even[rows, :] + received[rows, :]
-        out[n:, :] = stat
-
-
-def fold_call(n, even, received, stats, extra):
+        if count:
+            out[n:, :] = stats[0][...] + stats[1][...]
+
+
+def fold_call(n, even, received, stats):
     half, clusters = even.shape
+    extra = STAT_ROWS if stats else 0
     return call(
         functools.partial(fold_body, n, len(stats)),
         [even, received] + stats,
@@ -286,26 +284,39 @@
     )
 
 
-def sum_body(n, last, *refs):
-    many = 2 if last else 1 + len(GATHER_ROWS)
-    refs, outs = refs[:-many], refs[-many:]
-    total, stat = refs[0][:n, :], refs[0][n:, :]
-    for ref in refs[1:]:
+def first_body(n, stats, backs, *refs):
+    smalls, refs = refs[:stats], refs[stats:]
+    (*parts, far, out, stat_out) = refs
+    stat = smalls[0][...]
+    for ref in smalls[1:]:
+        stat += ref[...]
+    total = parts[0][:n, :]
+    for ref in parts[1:]:
+        total += ref[:n, :]
+    for ref in parts[len(parts) - backs :]:
+        stat += ref[n : n + STAT_ROWS, :]
+    out[...] = total
+    far[:n, :] = total
+    far[n:, :] = jnp.zeros((far.shape[0] - n, far.shape[1]), F32)
+    stat_out[...] = stat
+
+
+def widen_body(scores, stat, other, out):
+    n = scores.shape[0]
+    out[:n, :] = scores[...]
+    out[n:, :] = stat[...] + other[...]
+
+
+def last_body(n, *refs):
+    parts, (members, standardized) = refs[:-2], refs[-2:]
+    total, stat = parts[0][:n, :], parts[0][n:, :]
+    for ref in parts[1:]:
         total += ref[:n, :]
         if ref.shape[0] == n + STAT_ROWS:
             stat += ref[n:, :]
-    if last:
-        members, standardized = outs
-        x = standardize(total, stat[1:2, :], stat[0:1, :])
-        standardized[...] = x
-        members[...] = normalize(jnp.exp(-2.0 * x))
-    else:
-        stats, fulls = outs[0], outs[1:]
-        stats[...] = stat
-        for full in fulls:
-            full[:n, :] = total
-            if full.shape[0] > n:
-                full[n:, :] = stat
+    x = standardize(total, stat[1:2, :], stat[0:1, :])
+    standardized[...] = x
+    members[...] = normalize(jnp.exp(-2.0 * x))
 
 
 def on_device(rows, cols, features, logits):
@@ -351,60 +362,60 @@
     others = [shift(wide, d) if d else far_rows[0] for d in steps]
     evens = [pair] + [by_col(pair, k) for k in masks]
     members = evens + [by_col(x, 1) for x in evens]
-    early = 1 + has_near
-    extra = [0] + [BACK_ROWS] * len(steps)
-    blocks = [kernel_call(n, order, column, own_rows, features)]
-    for x in reversed(far_rows):
-        blocks.append(
-            kernel_call(n, order, column, x, features, blocks[-1][:1], CROSS_COST)
+    half = n * len(evens)
+    odds = members[len(evens) :]
+    diag = kernel_call(n, order, column, own_rows, features)
+    cross = []
+    for x in far_rows[has_near:]:
+        after = (cross or diag)[-1:]
+        cross += kernel_call(n, order, column, x, features, after, CROSS_COST)
+    extra = [0] + [BACK_ROWS] * len(offsets)
+    scores = scores_call(0, evens, diag + cross, [], extra, hidden=True)
+    near = []
+    scores = scores_call(half, odds, diag + cross, scores, extra, hidden=True)
+    t_even, t_odd = other_call(n, half, clusters, others[has_near:], cross, scores[:1])
+    if has_near:
+        near = kernel_call(n, order, column, far_rows[0], features, cross[-1:], NEAR_COST)
+        scores[1:1] = scores_call(
+            0, members, near, [], [BACK_ROWS], hidden=True, after=[t_even]
         )
-    blocks = blocks[:1] + blocks[:0:-1]
-    kernels = [x for block in blocks for x in block]
-    cross = kernels[2 * early :]
-    scores = scores_call(0, members, kernels, [], extra, hidden=True)
-    own = pair
-
-    for iteration in range(ITERS):
-        last = iteration == ITERS - 1
-        if iteration > 0:
-            even, *others = members_call(n, stats, evens, others)
-            odd = by_col(even, 1)
-            own = even
-            scores = scores_call(0, [even], kernels, [], extra)
-        if last:
-            t_even, t_odd = other_call(n, half, clusters, others[has_near:], cross, [])
-            extra = [0] + [LAST_ROWS] * len(steps)
-            *scores, stat = scores_call(
-                half, [odd], kernels, scores, extra, False, (), [own] + others, has_near
-            )
-            for x in [shift(stat, d) for d in range(1, rows)]:
-                stat = stat + x
-            sent = fold_call(
-                n, t_even, by_col(t_odd, 1), [stat, by_col(stat, 1)], STAT_ROWS
-            )
-        else:
-            if iteration > 0:
-                scores = scores_call(half, [odd], kernels, scores, extra)
-            stat = stat_call(has_near, own, scores, others)
-            t_even, t_odd = other_call(n, half, clusters, others[has_near:], cross, [stat])
-            sent = fold_call(n, t_even, by_col(t_odd, 1), [stat], STAT_ROWS)
-        parts = [by_col(x, k) for k, x in zip(masks, sent[1:])]
-        back = [shift(x, -d) for d, x in zip(steps, scores[1:])]
-        outs = [shaped(n, clusters)] * 2
-        if not last:
-            outs = [shaped(STAT_ROWS, clusters)]
-            outs += [shaped(n + r, clusters) for r in GATHER_ROWS]
-        done = call(
-            functools.partial(sum_body, n, last),
-            [sent[0], scores[0]] + back + parts,
-            outs,
+    stat, *backs = stat_call(has_near, pair, scores, others, BACK_ROWS)
+    sent = fold_call(n, t_even, by_col(t_odd, 1), [])
+    parts = [by_col(x, k) for k, x in zip(masks, sent[1:])]
+    backs = [shift(x, -d) for d, x in zip(steps, backs)]
+    stats = [stat] + [shift(stat, d) for d in offsets]
+    far, total, stat = call(
+        functools.partial(first_body, n, len(stats), len(backs)),
+        stats + [sent[0], scores[0]] + parts + backs,
+        [shaped(n + FAR_ROWS, clusters), shaped(n, clusters), shaped(STAT_ROWS, clusters)],
+    )
+
+    kernels = diag + near + cross
+    others = [shift(far, d) for d in steps]
+    (full,) = call(
+        widen_body, [total, stat, by_col(stat, 1)], [shaped(n + STAT_ROWS, clusters)]
+    )
+    evens = [full] + [by_col(full, k) for k in masks]
+    even, *others = members_call(n, evens, others)
+    odd = by_col(even, 1)
+    extra = [0] + [LAST_ROWS] * len(steps)
+    scores = scores_call(0, [even], kernels, [], extra)
+    t_even, t_odd = other_call(n, half, clusters, others[has_near:], cross)
+    *scores, stat = scores_call(
+        half, [odd], kernels, scores, extra, weights=[even] + others, has_near=has_near
+    )
+    for x in [shift(stat, d) for d in range(1, rows)]:
+        stat = stat + x
+    sent = fold_call(n, t_even, by_col(t_odd, 1), [stat, by_col(stat, 1)])
+    parts = [by_col(x, k) for k, x in zip(masks, sent[1:])]
+    backs = [shift(x, -d) for d, x in zip(steps, scores[1:])]
+    return tuple(
+        call(
+            functools.partial(last_body, n),
+            [sent[0], scores[0]] + backs + parts,
+            [shaped(n, clusters)] * 2,
         )
-        if not last:
-            stats, full, total = done
-            evens = [total] + [by_col(total, k) for k in masks]
-            others = [shift(full, d) for d in steps]
-            stats = [stats] + [shift(stats, -d) for d in offsets]
-    return tuple(done)
+    )
 
 
 def solution(mesh):

time: 75.4 us -> 82.6 us (1.095)
  waiting for transfers between devices: 28 us -> 34 us
  starting transfers between devices: 32.2 us -> 33.1 us
    ppermute x20 -> x21, waiting for transfers between devices: 14.9 us -> 19 us  [by_col(): return lax.ppermute(x, 'col', [(i, i ^ mask) for i in range(cols)])]
    ppermute x13, waiting for transfers between devices: 13.1 us -> 15 us  [shift(): return lax.ppermute(x, 'row', pairs)]
    ppermute x13, starting transfers between devices: 16.5 us -> 18.1 us  [shift(): return lax.ppermute(x, 'row', pairs)]
    ppermute x20 -> x21, starting transfers between devices: 15.6 us -> 15 us  [by_col(): return lax.ppermute(x, 'col', [(i, i ^ mask) for i in range(cols)])]
    pallas_call x15 -> x18, Pallas kernels: 10.7 us -> 11 us  [call(): pl.pallas_call(body, in_specs=specs or [VMEM] * len(args), out_specs=[VME...]
    unnamed x4 -> x6, local copies, waits for them, and re-layouts: 2.49 us -> 2.5 us
  transfers between devices with their start and end apart: 33 -> 34, of which waited for: 15 -> 13; matrix products, arithmetic and copies ran while one was open for 0% -> 0% of each run, Pallas kernels for 10% -> 10%
where the time goes in v8:
time: 82.6 us; the launch traced here: 82.4 us
  waiting for transfers between devices  34 us (41%)
  starting transfers between devices  33.1 us (40%)
  Pallas kernels  11 us (13%)
  local copies, waits for them, and re-layouts  3.47 us (4%)
  between operations  0.85 us (1%)
    ppermute x21, waiting for transfers between devices, by_col(): return lax.ppermute(x, 'col', [(i, i ^ mask) for i in range(cols)])  19 us
    ppermute x13, starting transfers between devices, shift(): return lax.ppermute(x, 'row', pairs)  18.1 us
    ppermute x21, starting transfers between devices, by_col(): return lax.ppermute(x, 'col', [(i, i ^ mask) for i in range(cols)])  15 us
    ppermute x13, waiting for transfers between devices, shift(): return lax.ppermute(x, 'row', pairs)  15 us
    pallas_call x18, Pallas kernels, call(): pl.pallas_call(body, in_specs=specs or [VMEM] * len(args), out_specs=[VME...  11 us
    unnamed x6, local copies, waits for them, and re-layouts  2.5 us
  transfers between devices with their start and end apart: 34, of which 13 were waited for; matrix products, arithmetic and copies ran while one was open for 0% of the time, Pallas kernels for 10%

profile of v8, /device:TPU:0, one launch (start us, length us, event | category | flops | bytes accessed | tf_op | source)
XLA Modules:
  0.0 82.4 jit_solution(13161015134363844610)
XLA Ops:
  0.6 1.0 %constant_dynamic-slice_fusion.rows.rows_ref = bf16[256,512]{1,0:T(8,128)(2,1)S(1)} fusion(bf16[2048,512]{1,0:T(8,128)(2,1)} %plane_ref.5, s32[]{:T(128)S(6)} %select_n.3), kind=kLoop, calls=%fused_computation.1 | loop fusion | bytes 524292 | tf_op jit(solution)/shard_map/dynamic_slice | solution.py:350
  1.6 0.9 %copy-done.2 = f32[256,128]{1,0:T(8,128)S(1)} copy-done((f32[256,128]{1,0:T(8,128)S(1)}, f32[256,128]{1,0:T(8,128)}, u32[]{:S(2)}) %copy-start.2) | copy-done | bytes 131096
  2.5 0.1 shard_map.41
  2.7 4.0 %collective-permute-start.5 = (bf16[256,256]{1,0:T(8,128)(2,1)S(1)}, bf16[256,256]{1,0:T(8,128)(2,1)S(1)}, u32[]{:S(2)}, u32[]{:S(2)}) collective-permute-start(bf16[256,256]{1,0:T(8,128)(2,1)S(1)} %get-tuple-element.43.refs_0_.own), channel_id=1, source_target_pairs={{0,6},{1,7},{2,4},{3,5},{4,2},{5,3},{6,0},{7,1},{8,14},{9,15},{10,... | collective-permute-start | bytes 393224 | tf_op jit(solution)/shard_map/ppermute | solution.py:340
  6.6 3.6 %collective-permute-start.7 = (bf16[256,512]{1,0:T(8,128)(2,1)S(1)}, bf16[256,512]{1,0:T(8,128)(2,1)S(1)}, u32[]{:S(2)}, u32[]{:S(2)}) collective-permute-start(bf16[256,512]{1,0:T(8,128)(2,1)S(1)} %constant_dynamic-slice_fusion.rows.rows_ref), channel_id=1, source_target_pairs={{16,0},{8,16},{24,8},{0,24},{17,1},{9,17},{25,9},{1,25},{18,2},{10... | collective-permute-start | bytes 786440 | tf_op jit(solution)/shard_map/ppermute | solution.py:347
  10.2 0.5 collective-permute-start.3
  10.7 0.5 collective-permute-start.1
  11.3 1.6 %copy-done = bf16[2048,512]{1,0:T(8,128)(2,1)S(1)} copy-done((bf16[2048,512]{1,0:T(8,128)(2,1)S(1)}, bf16[2048,512]{1,0:T(8,128)(2,1)}, u32[]{:S(2)}) %copy-start) | copy-done | bytes 2097176
  12.9 0.9 %shard_map.42 = (bf16[256,2048]{1,0:T(8,128)(2,1)S(1)}, bf16[256,2048]{1,0:T(8,128)(2,1)S(1)}) custom-call(s32[1]{0:T(128)} %bitcast.column_ref, bf16[256,512]{1,0:T(8,128)(2,1)S(1)} %constant_dynamic-slice_fusion.rows.rows_ref, bf16[2048,512]{1,0:T(8,128)(2,1)S(1)} %copy-done), custom_call_target="tpu_custom_call" | custom-call | flops 536870912 | bytes 4456452 | tf_op jit(solution)/shard_map/pallas_call | solution.py:33
  13.7 1.5 %collective-permute-done.3.refs_2_ = bf16[256,256]{1,0:T(8,128)(2,1)S(1)} collective-permute-done((bf16[256,256]{1,0:T(8,128)(2,1)S(1)}, bf16[256,256]{1,0:T(8,128)(2,1)S(1)}, u32[]{:S(2)}, u32[]{:S(2)}) %collective-permute-start.3) | collective-permute-done | bytes 131104 | tf_op jit(solution)/shard_map/ppermute | solution.py:340
  15.2 1.5 %collective-permute-start.9 = (bf16[272,256]{1,0:T(8,128)(2,1)S(1)}, bf16[272,256]{1,0:T(8,128)(2,1)S(1)}, u32[]{:S(2)}, u32[]{:S(2)}) collective-permute-start(bf16[272,256]{1,0:T(8,128)(2,1)S(1)} %get-tuple-element.54), channel_id=1, source_target_pairs={{16,0},{8,16},{24,8},{0,24},{17,1},{9,17},{25,9},{1,25},{18,2},{10... | collective-permute-start | bytes 417800 | tf_op jit(solution)/shard_map/ppermute | solution.py:347
  16.7 0.2 collective-permute-start.6
  16.9 0.3 collective-permute-start.4
  17.2 4.9 %collective-permute-done.7.rows_ref = bf16[256,512]{1,0:T(8,128)(2,1)S(1)} collective-permute-done((bf16[256,512]{1,0:T(8,128)(2,1)S(1)}, bf16[256,512]{1,0:T(8,128)(2,1)S(1)}, u32[]{:S(2)}, u32[]{:S(2)}) %collective-permute-start.7) | collective-permute-done | bytes 262176 | tf_op jit(solution)/shard_map/ppermute | solution.py:347
  22.2 0.9 %shard_map.43 = (bf16[256,2048]{1,0:T(8,128)(2,1)S(1)}, bf16[256,2048]{1,0:T(8,128)(2,1)S(1)}) custom-call(s32[1]{0:T(128)} %bitcast.column_ref, bf16[256,512]{1,0:T(8,128)(2,1)S(1)} %collective-permute-done.7.rows_ref, bf16[2048,512]{1,0:T(8,128)(2,1)S(1)} %copy-done, bf16[256,2048]{1,0:T(8,128)(2,1)S(1)} %get-tuple-element.45.refs_0_.refs_5_.refs_2_), custom_call_target="tpu_custom_call" | custom-call | flops 2147483648 | bytes 5505028 | tf_op jit(solution)/shard_map/pallas_call | solution.py:33
  23.1 0.7 shard_map.44
  23.8 0.7 shard_map.45
  24.5 0.0 copy-start.1
  24.5 2.4 %collective-permute-done.9.refs_0_.refs_4_ = bf16[272,256]{1,0:T(8,128)(2,1)S(1)} collective-permute-done((bf16[272,256]{1,0:T(8,128)(2,1)S(1)}, bf16[272,256]{1,0:T(8,128)(2,1)S(1)}, u32[]{:S(2)}, u32[]{:S(2)}) %collective-permute-start.9) | collective-permute-done | bytes 139296 | tf_op jit(solution)/shard_map/ppermute | solution.py:347
  27.0 0.8 shard_map.47
  27.8 0.1 collective-permute-start.11
  27.8 0.2 collective-permute-done.8.rows_ref.refs_3_
  28.0 0.9 %shard_map.46 = (bf16[256,2048]{1,0:T(8,128)(2,1)S(1)}, bf16[256,2048]{1,0:T(8,128)(2,1)S(1)}) custom-call(s32[1]{0:T(128)} %bitcast.column_ref, bf16[256,768]{1,0:T(8,128)(2,1)S(1)} %collective-permute-done.8.rows_ref.refs_3_, bf16[2048,512]{1,0:T(8,128)(2,1)S(1)} %copy-done.1, bf16[256,2048]{1,0:T(8,128)(2,1)S(1)} %get-tuple-element.47.refs_7_.refs_0_.refs_2_.refs_6_), custom_call_target="tpu_custom_call" | custom-call | flops 5368709120 | bytes 5636100 | tf_op jit(solution)/shard_map/pallas_call | solution.py:33
  28.9 0.7 shard_map.48.refs_1_
  29.6 0.1 shard_map.49
  29.7 1.3 %collective-permute-start.15 = (f32[272,128]{1,0:T(8,128)S(1)}, f32[272,128]{1,0:T(8,128)S(1)}, u32[]{:S(2)}, u32[]{:S(2)}) collective-permute-start(f32[272,128]{1,0:T(8,128)S(1)} %get-tuple-element.63), channel_id=1, source_target_pairs={{0,8},{8,0},{16,24},{24,16},{1,9},{9,1},{17,25},{25,17},{2,10},{10... | collective-permute-start | bytes 417800 | tf_op jit(solution)/shard_map/ppermute | solution.py:347
  31.0 3.5 %collective-permute-start.16 = (f32[272,128]{1,0:T(8,128)S(1)}, f32[272,128]{1,0:T(8,128)S(1)}, u32[]{:S(2)}, u32[]{:S(2)}) collective-permute-start(f32[272,128]{1,0:T(8,128)S(1)} %get-tuple-element.64), channel_id=1, source_target_pairs={{24,0},{0,16},{16,8},{8,24},{25,1},{1,17},{17,9},{9,25},{26,2},{2,... | collective-permute-start | bytes 417800 | tf_op jit(solution)/shard_map/ppermute | solution.py:347
  34.5 0.3 collective-permute-start.10
  34.8 0.1 shard_map.50
  34.9 0.6 collective-permute-start.12
  35.5 0.5 collective-permute-start.13
  36.0 5.7 %collective-permute-done.10.refs_1_ = f32[8,128]{1,0:T(8,128)S(1)} collective-permute-done((f32[8,128]{1,0:T(8,128)S(1)}, f32[8,128]{1,0:T(8,128)S(1)}, u32[]{:S(2)}, u32[]{:S(2)}) %collective-permute-start.10) | collective-permute-done | bytes 4128 | tf_op jit(solution)/shard_map/ppermute | solution.py:347
  41.7 0.5 collective-permute-start.14
  42.2 5.4 %collective-permute-done.14.refs_6_ = f32[256,128]{1,0:T(8,128)S(1)} collective-permute-done((f32[256,128]{1,0:T(8,128)S(1)}, f32[256,128]{1,0:T(8,128)S(1)}, u32[]{:S(2)}, u32[]{:S(2)}) %collective-permute-start.14) | collective-permute-done | bytes 131104 | tf_op jit(solution)/shard_map/ppermute | solution.py:340
  47.5 0.1 shard_map.51
  47.6 0.1 collective-permute-start.17
  47.7 0.6 collective-permute-start.22
  48.3 1.7 %collective-permute-start.21 = (f32[272,128]{1,0:T(8,128)S(1)}, f32[272,128]{1,0:T(8,128)S(1)}, u32[]{:S(2)}, u32[]{:S(2)}) collective-permute-start(f32[272,128]{1,0:T(8,128)S(1)} %get-tuple-element.67), channel_id=1, source_target_pairs={{0,8},{8,0},{16,24},{24,16},{1,9},{9,1},{17,25},{25,17},{2,10},{10... | collective-permute-start | bytes 417800 | tf_op jit(solution)/shard_map/ppermute | solution.py:347
  50.0 0.5 collective-permute-start.20
  50.6 1.5 %collective-permute-start.19 = (f32[264,128]{1,0:T(8,128)S(1)}, f32[264,128]{1,0:T(8,128)S(1)}, u32[]{:S(2)}, u32[]{:S(2)}) collective-permute-start(f32[264,128]{1,0:T(8,128)S(1)} %shard_map.52.refs_0_), channel_id=1, source_target_pairs={{0,4},{1,5},{2,6},{3,7},{4,0},{5,1},{6,2},{7,3},{8,12},{9,13},{10,... | collective-permute-start | bytes 405512 | tf_op jit(solution)/shard_map/ppermute | solution.py:340
  52.1 1.5 %collective-permute-start.18 = (f32[264,128]{1,0:T(8,128)S(1)}, f32[264,128]{1,0:T(8,128)S(1)}, u32[]{:S(2)}, u32[]{:S(2)}) collective-permute-start(f32[264,128]{1,0:T(8,128)S(1)} %shard_map.52.refs_0_), channel_id=1, source_target_pairs={{0,2},{1,3},{2,0},{3,1},{4,6},{5,7},{6,4},{7,5},{8,10},{9,11},{10,... | collective-permute-start | bytes 405512 | tf_op jit(solution)/shard_map/ppermute | solution.py:340
  53.6 3.9 %collective-permute-done.20.refs_3_ = f32[264,128]{1,0:T(8,128)S(1)} collective-permute-done((f32[264,128]{1,0:T(8,128)S(1)}, f32[264,128]{1,0:T(8,128)S(1)}, u32[]{:S(2)}, u32[]{:S(2)}) %collective-permute-start.20) | collective-permute-done | bytes 135200 | tf_op jit(solution)/shard_map/ppermute | solution.py:340
  57.5 1.1 %collective-permute-done.19.refs_2_ = f32[264,128]{1,0:T(8,128)S(1)} collective-permute-done((f32[264,128]{1,0:T(8,128)S(1)}, f32[264,128]{1,0:T(8,128)S(1)}, u32[]{:S(2)}, u32[]{:S(2)}) %collective-permute-start.19) | collective-permute-done | bytes 135200 | tf_op jit(solution)/shard_map/ppermute | solution.py:340
  58.6 1.2 %shard_map.53 = (bf16[1024,256]{1,0:T(8,128)(2,1)S(1)}, bf16[256,256]{1,0:T(8,128)(2,1)S(1)}, bf16[256,256]{1,0:T(8,128)(2,1)S(1)}) custom-call(f32[264,128]{1,0:T(8,128)S(1)} %shard_map.52.refs_0_, f32[264,128]{1,0:T(8,128)S(1)} %collective-permute-done.18.refs_1_, f32[264,128]{1,0:T(8,128)S(1)} %collective-permute-done.19.refs_2_, ...), custom_call_target="tpu_custom_call" | custom-call | bytes 1605632 | tf_op jit(solution)/shard_map/pallas_call | solution.py:33
  59.8 0.1 collective-permute-start.24
  59.9 0.8 shard_map.54
  60.6 0.6 collective-permute-start.23
  61.2 1.0 %shard_map.55 = (f32[256,128]{1,0:T(8,128)S(1)}, f32[288,128]{1,0:T(8,128)S(1)}, f32[288,128]{1,0:T(8,128)S(1)}) custom-call(bf16[1024,256]{1,0:T(8,128)(2,1)S(1)} %get-tuple-element.71.refs_0_.refs_10_, bf16[256,2048]{1,0:T(8,128)(2,1)S(1)} %get-tuple-element.44.refs_4_.refs_1_, bf16[256,2048]{1,0:T(8,128)(2,1)S(1)} %get-tuple-element.45.refs_0_.refs_5_.refs_2_, ...), custom_call_target="tpu_custom_call" | custom-call | flops 603979776 | bytes 7241728 | tf_op jit(solution)/shard_map/pallas_call | solution.py:33
  62.2 1.0 %shard_map.56 = (f32[256,128]{1,0:T(8,128)S(1)}, f32[288,128]{1,0:T(8,128)S(1)}, f32[288,128]{1,0:T(8,128)S(1)}, f32[8,128]{1,0:T(8,128)S(1)}) custom-call(bf16[1024,256]{1,0:T(8,128)(2,1)S(1)} %collective-permute-done.24.refs_0_, bf16[256,2048]{1,0:T(8,128)(2,1)S(1)} %get-tuple-element.44.refs_4_.refs_1_, ...), custom_call_target="tpu_custom_call" | custom-call | flops 603979776 | bytes 8458240 | tf_op jit(solution)/shard_map/pallas_call | solution.py:33
  63.3 1.1 %collective-permute-start.27 = (f32[8,128]{1,0:T(8,128)S(1)}, f32[8,128]{1,0:T(8,128)S(1)}, u32[]{:S(2)}, u32[]{:S(2)}) collective-permute-start(f32[8,128]{1,0:T(8,128)S(1)} %get-tuple-element.76), channel_id=1, source_target_pairs={{24,0},{0,16},{16,8},{8,24},{25,1},{1,17},{17,9},{9,25},{26,2},{2,... | collective-permute-start | bytes 12296 | tf_op jit(solution)/shard_map/ppermute | solution.py:347
  64.3 1.7 %collective-permute-start.26 = (f32[8,128]{1,0:T(8,128)S(1)}, f32[8,128]{1,0:T(8,128)S(1)}, u32[]{:S(2)}, u32[]{:S(2)}) collective-permute-start(f32[8,128]{1,0:T(8,128)S(1)} %get-tuple-element.76), channel_id=1, source_target_pairs={{8,0},{24,16},{0,8},{16,24},{9,1},{25,17},{1,9},{17,25},{10,2},{26... | collective-permute-start | bytes 12296 | tf_op jit(solution)/shard_map/ppermute | solution.py:347
  66.0 1.1 %collective-permute-start.25 = (f32[8,128]{1,0:T(8,128)S(1)}, f32[8,128]{1,0:T(8,128)S(1)}, u32[]{:S(2)}, u32[]{:S(2)}) collective-permute-start(f32[8,128]{1,0:T(8,128)S(1)} %get-tuple-element.76), channel_id=1, source_target_pairs={{16,0},{8,16},{24,8},{0,24},{17,1},{9,17},{25,9},{1,25},{18,2},{10... | collective-permute-start | bytes 12296 | tf_op jit(solution)/shard_map/ppermute | solution.py:347
  67.2 1.1 %collective-permute-start.29 = (f32[288,128]{1,0:T(8,128)S(1)}, f32[288,128]{1,0:T(8,128)S(1)}, u32[]{:S(2)}, u32[]{:S(2)}) collective-permute-start(f32[288,128]{1,0:T(8,128)S(1)} %get-tuple-element.79), channel_id=1, source_target_pairs={{0,8},{8,0},{16,24},{24,16},{1,9},{9,1},{17,25},{25,17},{2,10},{10... | collective-permute-start | bytes 442376 | tf_op jit(solution)/shard_map/ppermute | solution.py:347
  68.3 0.5 collective-permute-done.27
  68.7 0.6 collective-permute-start.30
  69.3 1.3 %collective-permute-done.25 = f32[8,128]{1,0:T(8,128)S(1)} collective-permute-done((f32[8,128]{1,0:T(8,128)S(1)}, f32[8,128]{1,0:T(8,128)S(1)}, u32[]{:S(2)}, u32[]{:S(2)}) %collective-permute-start.25) | collective-permute-done | bytes 4128 | tf_op jit(solution)/shard_map/ppermute | solution.py:347
  70.6 1.2 %collective-permute-done.28.refs_1_ = f32[8,128]{1,0:T(8,128)S(1)} collective-permute-done((f32[8,128]{1,0:T(8,128)S(1)}, f32[8,128]{1,0:T(8,128)S(1)}, u32[]{:S(2)}, u32[]{:S(2)}) %collective-permute-start.28) | collective-permute-done | bytes 4128 | tf_op jit(solution)/shard_map/ppermute | solution.py:340
  71.7 0.1 shard_map.57
  71.8 1.3 %collective-permute-start.31 = (f32[264,128]{1,0:T(8,128)S(1)}, f32[264,128]{1,0:T(8,128)S(1)}, u32[]{:S(2)}, u32[]{:S(2)}) collective-permute-start(f32[264,128]{1,0:T(8,128)S(1)} %get-tuple-element.81), channel_id=1, source_target_pairs={{0,2},{1,3},{2,0},{3,1},{4,6},{5,7},{6,4},{7,5},{8,10},{9,11},{10,... | collective-permute-start | bytes 405512 | tf_op jit(solution)/shard_map/ppermute | solution.py:340
  73.1 0.6 collective-permute-start.32
  73.7 1.7 %collective-permute-start.33 = (f32[264,128]{1,0:T(8,128)S(1)}, f32[264,128]{1,0:T(8,128)S(1)}, u32[]{:S(2)}, u32[]{:S(2)}) collective-permute-start(f32[264,128]{1,0:T(8,128)S(1)} %get-tuple-element.83), channel_id=1, source_target_pairs={{0,6},{1,7},{2,4},{3,5},{4,2},{5,3},{6,0},{7,1},{8,14},{9,15},{10,... | collective-permute-start | bytes 405512 | tf_op jit(solution)/shard_map/ppermute | solution.py:340
  75.4 2.9 %collective-permute-done.31.refs_4_ = f32[264,128]{1,0:T(8,128)S(1)} collective-permute-done((f32[264,128]{1,0:T(8,128)S(1)}, f32[264,128]{1,0:T(8,128)S(1)}, u32[]{:S(2)}, u32[]{:S(2)}) %collective-permute-start.31) | collective-permute-done | bytes 135200 | tf_op jit(solution)/shard_map/ppermute | solution.py:340
  78.3 3.1 %collective-permute-done.32.refs_5_ = f32[264,128]{1,0:T(8,128)S(1)} collective-permute-done((f32[264,128]{1,0:T(8,128)S(1)}, f32[264,128]{1,0:T(8,128)S(1)}, u32[]{:S(2)}, u32[]{:S(2)}) %collective-permute-start.32) | collective-permute-done | bytes 135200 | tf_op jit(solution)/shard_map/ppermute | solution.py:340
  81.4 1.0 %shard_map.58 = (f32[256,128]{1,0:T(8,128)}, f32[256,128]{1,0:T(8,128)}) custom-call(f32[264,128]{1,0:T(8,128)S(1)} %get-tuple-element.77.refs_0_, f32[256,128]{1,0:T(8,128)S(1)} %get-tuple-element.78.refs_1_, f32[288,128]{1,0:T(8,128)S(1)} %collective-permute-done.29.refs_2_, f32[288,128]{1,0:T(8,128)S(1)} %collective-permute-done.30.refs_3_, ...), custom_call_target="tpu_custom_call" | custom-call | bytes 1228800 | tf_op jit(solution)/shard_map/pallas_call | solution.py:33
  (30 shorter events, 0.1 us)
Async XLA Ops:
  1.6 0.9 %copy-start.2 = (f32[256,128]{1,0:T(8,128)S(1)}, f32[256,128]{1,0:T(8,128)}, u32[]{:S(2)}) copy-start(f32[256,128]{1,0:T(8,128)} %logits.1) | copy-start | bytes 393220
  2.7 8.6 %collective-permute-start.5 = (bf16[256,256]{1,0:T(8,128)(2,1)S(1)}, bf16[256,256]{1,0:T(8,128)(2,1)S(1)}, u32[]{:S(2)}, u32[]{:S(2)}) collective-permute-start(bf16[256,256]{1,0:T(8,128)(2,1)S(1)} %get-tuple-element.43.refs_0_.own), channel_id=1, source_target_pairs={{0,6},{1,7},{2,4},{3,5},{4,2},{5,3},{6,0},{7,1},{8,14},{9,15},{10,... | collective-permute-start | bytes 393224 | tf_op jit(solution)/shard_map/ppermute | solution.py:340
  6.6 15.5 %collective-permute-start.7 = (bf16[256,512]{1,0:T(8,128)(2,1)S(1)}, bf16[256,512]{1,0:T(8,128)(2,1)S(1)}, u32[]{:S(2)}, u32[]{:S(2)}) collective-permute-start(bf16[256,512]{1,0:T(8,128)(2,1)S(1)} %constant_dynamic-slice_fusion.rows.rows_ref), channel_id=1, source_target_pairs={{16,0},{8,16},{24,8},{0,24},{17,1},{9,17},{25,9},{1,25},{18,2},{10... | collective-permute-start | bytes 786440 | tf_op jit(solution)/shard_map/ppermute | solution.py:347
  10.2 17.8 %collective-permute-start.8 = (bf16[256,768]{1,0:T(8,128)(2,1)S(1)}, bf16[256,768]{1,0:T(8,128)(2,1)S(1)}, u32[]{:S(2)}, u32[]{:S(2)}) collective-permute-start(bf16[256,768]{1,0:T(8,128)(2,1)S(1)} %get-tuple-element.51), channel_id=1, source_target_pairs={{0,8},{8,0},{16,24},{24,16},{1,9},{9,1},{17,25},{25,17},{2,10},{10... | collective-permute-start | bytes 1179656 | tf_op jit(solution)/shard_map/ppermute | solution.py:347
  10.2 5.0 %collective-permute-start.3 = (bf16[256,256]{1,0:T(8,128)(2,1)S(1)}, bf16[256,256]{1,0:T(8,128)(2,1)S(1)}, u32[]{:S(2)}, u32[]{:S(2)}) collective-permute-start(bf16[256,256]{1,0:T(8,128)(2,1)S(1)} %get-tuple-element.43.refs_0_.own), channel_id=1, source_target_pairs={{0,4},{1,5},{2,6},{3,7},{4,0},{5,1},{6,2},{7,3},{8,12},{9,13},{10,... | collective-permute-start | bytes 393224 | tf_op jit(solution)/shard_map/ppermute | solution.py:340
  10.7 6.0 %collective-permute-start.1 = (bf16[256,256]{1,0:T(8,128)(2,1)S(1)}, bf16[256,256]{1,0:T(8,128)(2,1)S(1)}, u32[]{:S(2)}, u32[]{:S(2)}) collective-permute-start(bf16[256,256]{1,0:T(8,128)(2,1)S(1)} %get-tuple-element.43.refs_0_.own), channel_id=1, source_target_pairs={{0,2},{1,3},{2,0},{3,1},{4,6},{5,7},{6,4},{7,5},{8,10},{9,11},{10,... | collective-permute-start | bytes 393224 | tf_op jit(solution)/shard_map/ppermute | solution.py:340
  11.3 5.6 %collective-permute-start = (bf16[256,256]{1,0:T(8,128)(2,1)S(1)}, bf16[256,256]{1,0:T(8,128)(2,1)S(1)}, u32[]{:S(2)}, u32[]{:S(2)}) collective-permute-start(bf16[256,256]{1,0:T(8,128)(2,1)S(1)} %get-tuple-element.43.refs_0_.own), channel_id=1, source_target_pairs={{0,1},{1,0},{2,3},{3,2},{4,5},{5,4},{6,7},{7,6},{8,9},{9,8},{10,11... | collective-permute-start | bytes 393224 | tf_op jit(solution)/shard_map/ppermute | solution.py:340
  11.3 1.6 %copy-start = (bf16[2048,512]{1,0:T(8,128)(2,1)S(1)}, bf16[2048,512]{1,0:T(8,128)(2,1)}, u32[]{:S(2)}) copy-start(bf16[2048,512]{1,0:T(8,128)(2,1)} %plane_ref.5) | copy-start | bytes 6291460
  15.2 11.8 %collective-permute-start.9 = (bf16[272,256]{1,0:T(8,128)(2,1)S(1)}, bf16[272,256]{1,0:T(8,128)(2,1)S(1)}, u32[]{:S(2)}, u32[]{:S(2)}) collective-permute-start(bf16[272,256]{1,0:T(8,128)(2,1)S(1)} %get-tuple-element.54), channel_id=1, source_target_pairs={{16,0},{8,16},{24,8},{0,24},{17,1},{9,17},{25,9},{1,25},{18,2},{10... | collective-permute-start | bytes 417800 | tf_op jit(solution)/shard_map/ppermute | solution.py:347
  16.7 7.0 %collective-permute-start.6 = (bf16[256,256]{1,0:T(8,128)(2,1)S(1)}, bf16[256,256]{1,0:T(8,128)(2,1)S(1)}, u32[]{:S(2)}, u32[]{:S(2)}) collective-permute-start(bf16[256,256]{1,0:T(8,128)(2,1)S(1)} %collective-permute-done.5.refs_3_), channel_id=1, source_target_pairs={{0,1},{1,0},{2,3},{3,2},{4,5},{5,4},{6,7},{7,6},{8,9},{9,8},{10,11... | collective-permute-start | bytes 393224 | tf_op jit(solution)/shard_map/ppermute | solution.py:340
  16.9 6.9 %collective-permute-start.4 = (bf16[256,256]{1,0:T(8,128)(2,1)S(1)}, bf16[256,256]{1,0:T(8,128)(2,1)S(1)}, u32[]{:S(2)}, u32[]{:S(2)}) collective-permute-start(bf16[256,256]{1,0:T(8,128)(2,1)S(1)} %collective-permute-done.3.refs_2_), channel_id=1, source_target_pairs={{0,1},{1,0},{2,3},{3,2},{4,5},{5,4},{6,7},{7,6},{8,9},{9,8},{10,11... | collective-permute-start | bytes 393224 | tf_op jit(solution)/shard_map/ppermute | solution.py:340
  22.2 1.6 %collective-permute-start.2 = (bf16[256,256]{1,0:T(8,128)(2,1)S(1)}, bf16[256,256]{1,0:T(8,128)(2,1)S(1)}, u32[]{:S(2)}, u32[]{:S(2)}) collective-permute-start(bf16[256,256]{1,0:T(8,128)(2,1)S(1)} %collective-permute-done.1.refs_1_), channel_id=1, source_target_pairs={{0,1},{1,0},{2,3},{3,2},{4,5},{5,4},{6,7},{7,6},{8,9},{9,8},{10,11... | collective-permute-start | bytes 393224 | tf_op jit(solution)/shard_map/ppermute | solution.py:340
  24.5 3.5 %copy-start.1 = (bf16[2048,512]{1,0:T(8,128)(2,1)S(1)}, bf16[2048,512]{1,0:T(8,128)(2,1)}, u32[]{:S(2)}) copy-start(bf16[2048,512]{1,0:T(8,128)(2,1)} %plane_ref.5) | copy-start | bytes 6291460
  27.8 7.1 %collective-permute-start.11 = (f32[1024,128]{1,0:T(8,128)S(1)}, f32[1024,128]{1,0:T(8,128)S(1)}, u32[]{:S(2)}, u32[]{:S(2)}) collective-permute-start(f32[1024,128]{1,0:T(8,128)S(1)} %get-tuple-element.58), channel_id=1, source_target_pairs={{0,1},{1,0},{2,3},{3,2},{4,5},{5,4},{6,7},{7,6},{8,9},{9,8},{10,11... | collective-permute-start | bytes 1572872 | tf_op jit(solution)/shard_map/ppermute | solution.py:340
  29.7 12.4 %collective-permute-start.15 = (f32[272,128]{1,0:T(8,128)S(1)}, f32[272,128]{1,0:T(8,128)S(1)}, u32[]{:S(2)}, u32[]{:S(2)}) collective-permute-start(f32[272,128]{1,0:T(8,128)S(1)} %get-tuple-element.63), channel_id=1, source_target_pairs={{0,8},{8,0},{16,24},{24,16},{1,9},{9,1},{17,25},{25,17},{2,10},{10... | collective-permute-start | bytes 417800 | tf_op jit(solution)/shard_map/ppermute | solution.py:347
  31.0 11.2 %collective-permute-start.16 = (f32[272,128]{1,0:T(8,128)S(1)}, f32[272,128]{1,0:T(8,128)S(1)}, u32[]{:S(2)}, u32[]{:S(2)}) collective-permute-start(f32[272,128]{1,0:T(8,128)S(1)} %get-tuple-element.64), channel_id=1, source_target_pairs={{24,0},{0,16},{16,8},{8,24},{25,1},{1,17},{17,9},{9,25},{26,2},{2,... | collective-permute-start | bytes 417800 | tf_op jit(solution)/shard_map/ppermute | solution.py:347
  34.5 7.2 %collective-permute-start.10 = (f32[8,128]{1,0:T(8,128)S(1)}, f32[8,128]{1,0:T(8,128)S(1)}, u32[]{:S(2)}, u32[]{:S(2)}) collective-permute-start(f32[8,128]{1,0:T(8,128)S(1)} %get-tuple-element.57.refs_0_), channel_id=1, source_target_pairs={{16,0},{8,16},{24,8},{0,24},{17,1},{9,17},{25,9},{1,25},{18,2},{10... | collective-permute-start | bytes 12296 | tf_op jit(solution)/shard_map/ppermute | solution.py:347
  34.9 7.3 %collective-permute-start.12 = (f32[256,128]{1,0:T(8,128)S(1)}, f32[256,128]{1,0:T(8,128)S(1)}, u32[]{:S(2)}, u32[]{:S(2)}) collective-permute-start(f32[256,128]{1,0:T(8,128)S(1)} %get-tuple-element.60), channel_id=1, source_target_pairs={{0,2},{1,3},{2,0},{3,1},{4,6},{5,7},{6,4},{7,5},{8,10},{9,11},{10,... | collective-permute-start | bytes 393224 | tf_op jit(solution)/shard_map/ppermute | solution.py:340
  35.5 6.7 %collective-permute-start.13 = (f32[256,128]{1,0:T(8,128)S(1)}, f32[256,128]{1,0:T(8,128)S(1)}, u32[]{:S(2)}, u32[]{:S(2)}) collective-permute-start(f32[256,128]{1,0:T(8,128)S(1)} %get-tuple-element.61), channel_id=1, source_target_pairs={{0,4},{1,5},{2,6},{3,7},{4,0},{5,1},{6,2},{7,3},{8,12},{9,13},{10,... | collective-permute-start | bytes 393224 | tf_op jit(solution)/shard_map/ppermute | solution.py:340
  41.7 5.9 %collective-permute-start.14 = (f32[256,128]{1,0:T(8,128)S(1)}, f32[256,128]{1,0:T(8,128)S(1)}, u32[]{:S(2)}, u32[]{:S(2)}) collective-permute-start(f32[256,128]{1,0:T(8,128)S(1)} %get-tuple-element.62), channel_id=1, source_target_pairs={{0,6},{1,7},{2,4},{3,5},{4,2},{5,3},{6,0},{7,1},{8,14},{9,15},{10,... | collective-permute-start | bytes 393224 | tf_op jit(solution)/shard_map/ppermute | solution.py:340
  47.6 2.4 %collective-permute-start.17 = (f32[8,128]{1,0:T(8,128)S(1)}, f32[8,128]{1,0:T(8,128)S(1)}, u32[]{:S(2)}, u32[]{:S(2)}) collective-permute-start(f32[8,128]{1,0:T(8,128)S(1)} %get-tuple-element.66.stat), channel_id=1, source_target_pairs={{0,1},{1,0},{2,3},{3,2},{4,5},{5,4},{6,7},{7,6},{8,9},{9,8},{10,11... | collective-permute-start | bytes 12296 | tf_op jit(solution)/shard_map/ppermute | solution.py:340
  47.7 10.9 %collective-permute-start.22 = (f32[272,128]{1,0:T(8,128)S(1)}, f32[272,128]{1,0:T(8,128)S(1)}, u32[]{:S(2)}, u32[]{:S(2)}) collective-permute-start(f32[272,128]{1,0:T(8,128)S(1)} %get-tuple-element.67), channel_id=1, source_target_pairs={{16,0},{8,16},{24,8},{0,24},{17,1},{9,17},{25,9},{1,25},{18,2},{10... | collective-permute-start | bytes 417800 | tf_op jit(solution)/shard_map/ppermute | solution.py:347
  48.3 10.3 %collective-permute-start.21 = (f32[272,128]{1,0:T(8,128)S(1)}, f32[272,128]{1,0:T(8,128)S(1)}, u32[]{:S(2)}, u32[]{:S(2)}) collective-permute-start(f32[272,128]{1,0:T(8,128)S(1)} %get-tuple-element.67), channel_id=1, source_target_pairs={{0,8},{8,0},{16,24},{24,16},{1,9},{9,1},{17,25},{25,17},{2,10},{10... | collective-permute-start | bytes 417800 | tf_op jit(solution)/shard_map/ppermute | solution.py:347
  50.0 7.4 %collective-permute-start.20 = (f32[264,128]{1,0:T(8,128)S(1)}, f32[264,128]{1,0:T(8,128)S(1)}, u32[]{:S(2)}, u32[]{:S(2)}) collective-permute-start(f32[264,128]{1,0:T(8,128)S(1)} %shard_map.52.refs_0_), channel_id=1, source_target_pairs={{0,6},{1,7},{2,4},{3,5},{4,2},{5,3},{6,0},{7,1},{8,14},{9,15},{10,... | collective-permute-start | bytes 405512 | tf_op jit(solution)/shard_map/ppermute | solution.py:340
  50.6 8.0 %collective-permute-start.19 = (f32[264,128]{1,0:T(8,128)S(1)}, f32[264,128]{1,0:T(8,128)S(1)}, u32[]{:S(2)}, u32[]{:S(2)}) collective-permute-start(f32[264,128]{1,0:T(8,128)S(1)} %shard_map.52.refs_0_), channel_id=1, source_target_pairs={{0,4},{1,5},{2,6},{3,7},{4,0},{5,1},{6,2},{7,3},{8,12},{9,13},{10,... | collective-permute-start | bytes 405512 | tf_op jit(solution)/shard_map/ppermute | solution.py:340
  52.1 6.5 %collective-permute-start.18 = (f32[264,128]{1,0:T(8,128)S(1)}, f32[264,128]{1,0:T(8,128)S(1)}, u32[]{:S(2)}, u32[]{:S(2)}) collective-permute-start(f32[264,128]{1,0:T(8,128)S(1)} %shard_map.52.refs_0_), channel_id=1, source_target_pairs={{0,2},{1,3},{2,0},{3,1},{4,6},{5,7},{6,4},{7,5},{8,10},{9,11},{10,... | collective-permute-start | bytes 405512 | tf_op jit(solution)/shard_map/ppermute | solution.py:340
  59.8 2.4 %collective-permute-start.24 = (bf16[1024,256]{1,0:T(8,128)(2,1)S(1)}, bf16[1024,256]{1,0:T(8,128)(2,1)S(1)}, u32[]{:S(2)}, u32[]{:S(2)}) collective-permute-start(bf16[1024,256]{1,0:T(8,128)(2,1)S(1)} %get-tuple-element.71.refs_0_.refs_10_), channel_id=1, source_target_pairs={{0,1},{1,0},{2,3},{3,2},{4,5},{5,4},{6,7},{7,6},{8,9},{9,8},{10,11... | collective-permute-start | bytes 1572872 | tf_op jit(solution)/shard_map/ppermute | solution.py:340
  60.6 9.9 %collective-permute-start.23 = (f32[1024,128]{1,0:T(8,128)S(1)}, f32[1024,128]{1,0:T(8,128)S(1)}, u32[]{:S(2)}, u32[]{:S(2)}) collective-permute-start(f32[1024,128]{1,0:T(8,128)S(1)} %get-tuple-element.70), channel_id=1, source_target_pairs={{0,1},{1,0},{2,3},{3,2},{4,5},{5,4},{6,7},{7,6},{8,9},{9,8},{10,11... | collective-permute-start | bytes 1572872 | tf_op jit(solution)/shard_map/ppermute | solution.py:340
  63.3 5.5 %collective-permute-start.27 = (f32[8,128]{1,0:T(8,128)S(1)}, f32[8,128]{1,0:T(8,128)S(1)}, u32[]{:S(2)}, u32[]{:S(2)}) collective-permute-start(f32[8,128]{1,0:T(8,128)S(1)} %get-tuple-element.76), channel_id=1, source_target_pairs={{24,0},{0,16},{16,8},{8,24},{25,1},{1,17},{17,9},{9,25},{26,2},{2,... | collective-permute-start | bytes 12296 | tf_op jit(solution)/shard_map/ppermute | solution.py:347
  64.3 5.0 %collective-permute-start.26 = (f32[8,128]{1,0:T(8,128)S(1)}, f32[8,128]{1,0:T(8,128)S(1)}, u32[]{:S(2)}, u32[]{:S(2)}) collective-permute-start(f32[8,128]{1,0:T(8,128)S(1)} %get-tuple-element.76), channel_id=1, source_target_pairs={{8,0},{24,16},{0,8},{16,24},{9,1},{25,17},{1,9},{17,25},{10,2},{26... | collective-permute-start | bytes 12296 | tf_op jit(solution)/shard_map/ppermute | solution.py:347
  66.0 4.6 %collective-permute-start.25 = (f32[8,128]{1,0:T(8,128)S(1)}, f32[8,128]{1,0:T(8,128)S(1)}, u32[]{:S(2)}, u32[]{:S(2)}) collective-permute-start(f32[8,128]{1,0:T(8,128)S(1)} %get-tuple-element.76), channel_id=1, source_target_pairs={{16,0},{8,16},{24,8},{0,24},{17,1},{9,17},{25,9},{1,25},{18,2},{10... | collective-permute-start | bytes 12296 | tf_op jit(solution)/shard_map/ppermute | solution.py:347
  67.2 14.2 %collective-permute-start.29 = (f32[288,128]{1,0:T(8,128)S(1)}, f32[288,128]{1,0:T(8,128)S(1)}, u32[]{:S(2)}, u32[]{:S(2)}) collective-permute-start(f32[288,128]{1,0:T(8,128)S(1)} %get-tuple-element.79), channel_id=1, source_target_pairs={{0,8},{8,0},{16,24},{24,16},{1,9},{9,1},{17,25},{25,17},{2,10},{10... | collective-permute-start | bytes 442376 | tf_op jit(solution)/shard_map/ppermute | solution.py:347
  68.7 12.7 %collective-permute-start.30 = (f32[288,128]{1,0:T(8,128)S(1)}, f32[288,128]{1,0:T(8,128)S(1)}, u32[]{:S(2)}, u32[]{:S(2)}) collective-permute-start(f32[288,128]{1,0:T(8,128)S(1)} %get-tuple-element.80), channel_id=1, source_target_pairs={{24,0},{0,16},{16,8},{8,24},{25,1},{1,17},{17,9},{9,25},{26,2},{2,... | collective-permute-start | bytes 442376 | tf_op jit(solution)/shard_map/ppermute | solution.py:347
  70.6 1.2 %collective-permute-start.28 = (f32[8,128]{1,0:T(8,128)S(1)}, f32[8,128]{1,0:T(8,128)S(1)}, u32[]{:S(2)}, u32[]{:S(2)}) collective-permute-start(f32[8,128]{1,0:T(8,128)S(1)} %add_add_fusion.refs_0_), channel_id=1, source_target_pairs={{0,1},{1,0},{2,3},{3,2},{4,5},{5,4},{6,7},{7,6},{8,9},{9,8},{10,11... | collective-permute-start | bytes 12296 | tf_op jit(solution)/shard_map/ppermute | solution.py:340
  71.8 6.4 %collective-permute-start.31 = (f32[264,128]{1,0:T(8,128)S(1)}, f32[264,128]{1,0:T(8,128)S(1)}, u32[]{:S(2)}, u32[]{:S(2)}) collective-permute-start(f32[264,128]{1,0:T(8,128)S(1)} %get-tuple-element.81), channel_id=1, source_target_pairs={{0,2},{1,3},{2,0},{3,1},{4,6},{5,7},{6,4},{7,5},{8,10},{9,11},{10,... | collective-permute-start | bytes 405512 | tf_op jit(solution)/shard_map/ppermute | solution.py:340
  73.1 8.3 %collective-permute-start.32 = (f32[264,128]{1,0:T(8,128)S(1)}, f32[264,128]{1,0:T(8,128)S(1)}, u32[]{:S(2)}, u32[]{:S(2)}) collective-permute-start(f32[264,128]{1,0:T(8,128)S(1)} %get-tuple-element.82), channel_id=1, source_target_pairs={{0,4},{1,5},{2,6},{3,7},{4,0},{5,1},{6,2},{7,3},{8,12},{9,13},{10,... | collective-permute-start | bytes 405512 | tf_op jit(solution)/shard_map/ppermute | solution.py:340
  73.7 7.7 %collective-permute-start.33 = (f32[264,128]{1,0:T(8,128)S(1)}, f32[264,128]{1,0:T(8,128)S(1)}, u32[]{:S(2)}, u32[]{:S(2)}) collective-permute-start(f32[264,128]{1,0:T(8,128)S(1)} %get-tuple-element.83), channel_id=1, source_target_pairs={{0,6},{1,7},{2,4},{3,5},{4,2},{5,3},{6,0},{7,1},{8,14},{9,15},{10,... | collective-permute-start | bytes 405512 | tf_op jit(solution)/shard_map/ppermute | solution.py:340

commit v9 on v7

--- a/solution.py
+++ b/solution.py
@@ -14,7 +14,8 @@
 LAST_ROWS = 32
 BACK_ROWS = 16
 VMEM_BYTES = 24 * 1024 * 1024
-CROSS_COST = 2.7
+NEAR_COST = 2.7
+CROSS_COST = 3
 VMEM = pl.BlockSpec(memory_space=pltpu.VMEM)
 SMEM = pl.BlockSpec(memory_space=pltpu.SMEM)
 ANY = pl.BlockSpec(memory_space=pl.ANY)
@@ -231,7 +232,7 @@
 def other_body(n, count, *refs):
     pairs, refs = refs[:count], refs[count:]
     kernels, refs = refs[: 2 * count], refs[2 * count :]
-    stat, (even, odd) = refs[:-2], refs[-2:]
+    even, odd = refs[-2:]
     half, clusters = even.shape
     over = (((0,), (0,)), ((), ()))
     for part, out in enumerate((odd, even)):
@@ -249,16 +250,15 @@
                 preferred_element_type=F32,
             )
             acc += a[:, :clusters] + (a[:, clusters:] + b)
-        out[:half, :] = acc
-    if stat:
-        odd[half:, :] = stat[0][...]
-
-
-def other_call(n, half, clusters, pairs, kernels, stat):
+        out[...] = acc
+
+
+def other_call(n, half, clusters, pairs, kernels, stat, after=()):
     return call(
         functools.partial(other_body, n, len(pairs)),
-        pairs + kernels + stat,
+        [*pairs, *kernels, *stat, *after],
         [shaped(half, clusters), shaped(half + STAT_ROWS * len(stat), clusters)],
+        [VMEM] * (len(pairs) + len(kernels) + len(stat)) + [ANY] * len(after),
         flops=12 * n * len(pairs) * half * clusters,
     )
 
@@ -353,15 +353,21 @@
     members = evens + [by_col(x, 1) for x in evens]
     early = 1 + has_near
     extra = [0] + [BACK_ROWS] * len(steps)
-    blocks = [kernel_call(n, order, column, own_rows, features)]
-    for x in reversed(far_rows):
-        blocks.append(
-            kernel_call(n, order, column, x, features, blocks[-1][:1], CROSS_COST)
-        )
-    blocks = blocks[:1] + blocks[:0:-1]
-    kernels = [x for block in blocks for x in block]
-    cross = kernels[2 * early :]
-    scores = scores_call(0, members, kernels, [], extra, hidden=True)
+    half = n * len(evens)
+    diag = kernel_call(n, order, column, own_rows, features)
+    cross = []
+    for x in far_rows[has_near:]:
+        after = (cross or diag)[-1:]
+        cross += kernel_call(n, order, column, x, features, after, CROSS_COST)
+    some = extra[:1] + extra[early:]
+    near, far_scores = [], []
+    if has_near:
+        near = kernel_call(n, order, column, far_rows[0], features, cross[-1:], NEAR_COST)
+    scores = scores_call(0, members, diag + cross, [], some, hidden=True)
+    after = scores[:1] + near[:1]
+    if has_near:
+        scores[1:1] = scores_call(0, members, near, [], extra[1:2], hidden=True)
+    kernels = diag + near + cross
     own = pair
 
     for iteration in range(ITERS):
@@ -386,8 +392,12 @@
             if iteration > 0:
                 scores = scores_call(half, [odd], kernels, scores, extra)
             stat = stat_call(has_near, own, scores, others)
-            t_even, t_odd = other_call(n, half, clusters, others[has_near:], cross, [stat])
-            sent = fold_call(n, t_even, by_col(t_odd, 1), [stat], STAT_ROWS)
+            t_even, t_odd = other_call(
+                n, half, clusters, others[has_near:], cross, [], after
+            )
+            sent = fold_call(
+                n, t_even, by_col(t_odd, 1), [stat, by_col(stat, 1)], STAT_ROWS
+            )
         parts = [by_col(x, k) for k, x in zip(masks, sent[1:])]
         back = [shift(x, -d) for d, x in zip(steps, scores[1:])]
         outs = [shaped(n, clusters)] * 2

time: 75.4 us -> 77.3 us (1.025)
  starting transfers between devices: 32.2 us -> 33.6 us
    ppermute x20 -> x21, waiting for transfers between devices: 14.9 us -> 17.3 us  [by_col(): return lax.ppermute(x, 'col', [(i, i ^ mask) for i in range(cols)])]
    ppermute x13, waiting for transfers between devices: 13.1 us -> 11 us  [shift(): return lax.ppermute(x, 'row', pairs)]
    ppermute x13, starting transfers between devices: 16.5 us -> 17.3 us  [shift(): return lax.ppermute(x, 'row', pairs)]
    ppermute x20 -> x21, starting transfers between devices: 15.6 us -> 16.3 us  [by_col(): return lax.ppermute(x, 'col', [(i, i ^ mask) for i in range(cols)])]
    pallas_call x15 -> x16, Pallas kernels: 10.7 us -> 10.8 us  [call(): pl.pallas_call(body, in_specs=specs or [VMEM] * len(args), out_specs=[VME...]
  transfers between devices with their start and end apart: 33 -> 34, of which waited for: 15 -> 17; matrix products, arithmetic and copies ran while one was open for 0% -> 0% of each run, Pallas kernels for 10% -> 10%
where the time goes in v9:
time: 77.3 us; the launch traced here: 77.1 us
  starting transfers between devices  33.6 us (43%)
  waiting for transfers between devices  28.3 us (37%)
  Pallas kernels  10.8 us (14%)
  local copies, waits for them, and re-layouts  3.46 us (4%)
  between operations  0.81 us (1%)
    ppermute x13, starting transfers between devices, shift(): return lax.ppermute(x, 'row', pairs)  17.3 us
    ppermute x21, waiting for transfers between devices, by_col(): return lax.ppermute(x, 'col', [(i, i ^ mask) for i in range(cols)])  17.3 us
    ppermute x21, starting transfers between devices, by_col(): return lax.ppermute(x, 'col', [(i, i ^ mask) for i in range(cols)])  16.3 us
    ppermute x13, waiting for transfers between devices, shift(): return lax.ppermute(x, 'row', pairs)  11 us
    pallas_call x16, Pallas kernels, call(): pl.pallas_call(body, in_specs=specs or [VMEM] * len(args), out_specs=[VME...  10.8 us
    unnamed x4, local copies, waits for them, and re-layouts  2.49 us
  transfers between devices with their start and end apart: 34, of which 17 were waited for; matrix products, arithmetic and copies ran while one was open for 0% of the time, Pallas kernels for 10%

profile of v9, /device:TPU:0, one launch (start us, length us, event | category | flops | bytes accessed | tf_op | source)
XLA Modules:
  0.0 77.1 jit_solution(4600084738617159698)
XLA Ops:
  0.6 1.0 %constant_dynamic-slice_fusion.rows.rows_ref = bf16[256,512]{1,0:T(8,128)(2,1)S(1)} fusion(bf16[2048,512]{1,0:T(8,128)(2,1)} %plane_ref.5, s32[]{:T(128)S(6)} %select_n.3), kind=kLoop, calls=%fused_computation.1 | loop fusion | bytes 524292 | tf_op jit(solution)/shard_map/dynamic_slice | solution.py:339
  1.6 0.9 %copy-done.1 = f32[256,128]{1,0:T(8,128)S(1)} copy-done((f32[256,128]{1,0:T(8,128)S(1)}, f32[256,128]{1,0:T(8,128)}, u32[]{:S(2)}) %copy-start.1) | copy-done | bytes 131096
  2.5 0.1 shard_map.41
  2.7 0.5 collective-permute-start.5
  3.2 4.7 %collective-permute-start.1 = (bf16[256,512]{1,0:T(8,128)(2,1)S(1)}, bf16[256,512]{1,0:T(8,128)(2,1)S(1)}, u32[]{:S(2)}, u32[]{:S(2)}) collective-permute-start(bf16[256,512]{1,0:T(8,128)(2,1)S(1)} %constant_dynamic-slice_fusion.rows.rows_ref), channel_id=1, source_target_pairs={{16,0},{8,16},{24,8},{0,24},{17,1},{9,17},{25,9},{1,25},{18,2},{10... | collective-permute-start | bytes 786440 | tf_op jit(solution)/shard_map/ppermute | solution.py:336
  7.8 2.4 %collective-permute-start.4 = (bf16[256,256]{1,0:T(8,128)(2,1)S(1)}, bf16[256,256]{1,0:T(8,128)(2,1)S(1)}, u32[]{:S(2)}, u32[]{:S(2)}) collective-permute-start(bf16[256,256]{1,0:T(8,128)(2,1)S(1)} %get-tuple-element.42.refs_0_.own), channel_id=1, source_target_pairs={{0,6},{1,7},{2,4},{3,5},{4,2},{5,3},{6,0},{7,1},{8,14},{9,15},{10,... | collective-permute-start | bytes 393224 | tf_op jit(solution)/shard_map/ppermute | solution.py:329
  10.3 0.5 collective-permute-start.3
  10.8 0.5 collective-permute-start.2
  11.3 1.6 %copy-done = bf16[2048,512]{1,0:T(8,128)(2,1)S(1)} copy-done((bf16[2048,512]{1,0:T(8,128)(2,1)S(1)}, bf16[2048,512]{1,0:T(8,128)(2,1)}, u32[]{:S(2)}) %copy-start) | copy-done | bytes 2097176
  12.9 0.9 %shard_map.42 = (bf16[256,2048]{1,0:T(8,128)(2,1)S(1)}, bf16[256,2048]{1,0:T(8,128)(2,1)S(1)}) custom-call(s32[1]{0:T(128)} %bitcast.column_ref, bf16[256,512]{1,0:T(8,128)(2,1)S(1)} %constant_dynamic-slice_fusion.rows.rows_ref, bf16[2048,512]{1,0:T(8,128)(2,1)S(1)} %copy-done), custom_call_target="tpu_custom_call" | custom-call | flops 536870912 | bytes 4456452 | tf_op jit(solution)/shard_map/pallas_call | solution.py:34
  13.8 0.8 %collective-permute-done.4.refs_3_ = bf16[256,256]{1,0:T(8,128)(2,1)S(1)} collective-permute-done((bf16[256,256]{1,0:T(8,128)(2,1)S(1)}, bf16[256,256]{1,0:T(8,128)(2,1)S(1)}, u32[]{:S(2)}, u32[]{:S(2)}) %collective-permute-start.4) | collective-permute-done | bytes 131104 | tf_op jit(solution)/shard_map/ppermute | solution.py:329
  14.6 0.4 collective-permute-start
  15.0 2.1 %collective-permute-done.3.refs_2_ = bf16[256,256]{1,0:T(8,128)(2,1)S(1)} collective-permute-done((bf16[256,256]{1,0:T(8,128)(2,1)S(1)}, bf16[256,256]{1,0:T(8,128)(2,1)S(1)}, u32[]{:S(2)}, u32[]{:S(2)}) %collective-permute-start.3) | collective-permute-done | bytes 131104 | tf_op jit(solution)/shard_map/ppermute | solution.py:329
  17.1 0.0 collective-permute-start.8
  17.1 0.1 collective-permute-done.2.refs_1_
  17.2 0.4 collective-permute-start.7
  17.6 2.1 %collective-permute-done.1.rows_ref = bf16[256,512]{1,0:T(8,128)(2,1)S(1)} collective-permute-done((bf16[256,512]{1,0:T(8,128)(2,1)S(1)}, bf16[256,512]{1,0:T(8,128)(2,1)S(1)}, u32[]{:S(2)}, u32[]{:S(2)}) %collective-permute-start.1) | collective-permute-done | bytes 262176 | tf_op jit(solution)/shard_map/ppermute | solution.py:336
  19.7 0.9 %shard_map.43 = (bf16[256,2048]{1,0:T(8,128)(2,1)S(1)}, bf16[256,2048]{1,0:T(8,128)(2,1)S(1)}) custom-call(s32[1]{0:T(128)} %bitcast.column_ref, bf16[256,512]{1,0:T(8,128)(2,1)S(1)} %collective-permute-done.1.rows_ref, bf16[2048,512]{1,0:T(8,128)(2,1)S(1)} %copy-done, bf16[256,2048]{1,0:T(8,128)(2,1)S(1)} %get-tuple-element.39.refs_0_.refs_9_.refs_2_), custom_call_target="tpu_custom_call" | custom-call | flops 1610612736 | bytes 5505028 | tf_op jit(solution)/shard_map/pallas_call | solution.py:34
  20.6 0.4 collective-permute-done.6.refs_5_
  21.1 1.3 %shard_map.44 = (f32[256,128]{1,0:T(8,128)S(1)}, f32[272,128]{1,0:T(8,128)S(1)}) custom-call(bf16[256,256]{1,0:T(8,128)(2,1)S(1)} %get-tuple-element.42.refs_0_.own, bf16[256,256]{1,0:T(8,128)(2,1)S(1)} %collective-permute-done.2.refs_1_, bf16[256,256]{1,0:T(8,128)(2,1)S(1)} %collective-permute-done.3.refs_2_, ...), custom_call_target="tpu_custom_call" | custom-call | tf_op jit(solution)/shard_map/pallas_call | solution.py:34
  22.3 4.1 %collective-permute-done.9.rows_ref.refs_3_ = bf16[256,768]{1,0:T(8,128)(2,1)S(1)} collective-permute-done((bf16[256,768]{1,0:T(8,128)(2,1)S(1)}, bf16[256,768]{1,0:T(8,128)(2,1)S(1)}, u32[]{:S(2)}, u32[]{:S(2)}) %collective-permute-start.9) | collective-permute-done | bytes 393248 | tf_op jit(solution)/shard_map/ppermute | solution.py:336
  26.5 0.9 %shard_map.45 = (bf16[256,2048]{1,0:T(8,128)(2,1)S(1)}, bf16[256,2048]{1,0:T(8,128)(2,1)S(1)}) custom-call(s32[1]{0:T(128)} %bitcast.column_ref, bf16[256,768]{1,0:T(8,128)(2,1)S(1)} %collective-permute-done.9.rows_ref.refs_3_, bf16[2048,512]{1,0:T(8,128)(2,1)S(1)} %copy-done, bf16[256,2048]{1,0:T(8,128)(2,1)S(1)} %get-tuple-element.41.refs_11_.refs_0_.refs_2_.refs_6_), custom_call_target="tpu_custom_call" | custom-call | flops 1449132032 | bytes 5636100 | tf_op jit(solution)/shard_map/pallas_call | solution.py:34
  27.3 0.8 %shard_map.46 = (f32[1024,128]{1,0:T(8,128)S(1)}, f32[1024,128]{1,0:T(8,128)S(1)}) custom-call(bf16[272,256]{1,0:T(8,128)(2,1)S(1)} %collective-permute-done.refs_0_.refs_4_, bf16[256,2048]{1,0:T(8,128)(2,1)S(1)} %get-tuple-element.40.refs_10_.refs_1_.refs_5_, bf16[256,2048]{1,0:T(8,128)(2,1)S(1)} %get-tuple-element.41.refs_11_.refs_0_.refs_2_.refs_6_, ...), custom_call_target="tpu_custom_call" | custom-call | flops 402653184 | bytes 4464640 | tf_op jit(solution)/shard_map/pallas_call | solution.py:34
  28.1 0.1 collective-permute-start.10
  28.2 0.7 shard_map.47.refs_1_
  28.9 0.1 shard_map.48.refs_0_
  29.0 0.6 collective-permute-start.11
  29.6 3.0 %collective-permute-start.12 = (f32[272,128]{1,0:T(8,128)S(1)}, f32[272,128]{1,0:T(8,128)S(1)}, u32[]{:S(2)}, u32[]{:S(2)}) collective-permute-start(f32[272,128]{1,0:T(8,128)S(1)} %shard_map.47.refs_1_), channel_id=1, source_target_pairs={{0,8},{8,0},{16,24},{24,16},{1,9},{9,1},{17,25},{25,17},{2,10},{10... | collective-permute-start | bytes 417800 | tf_op jit(solution)/shard_map/ppermute | solution.py:336
  32.6 0.1 shard_map.49
  32.6 1.6 %collective-permute-start.14 = (f32[264,128]{1,0:T(8,128)S(1)}, f32[264,128]{1,0:T(8,128)S(1)}, u32[]{:S(2)}, u32[]{:S(2)}) collective-permute-start(f32[264,128]{1,0:T(8,128)S(1)} %get-tuple-element.52), channel_id=1, source_target_pairs={{0,2},{1,3},{2,0},{3,1},{4,6},{5,7},{6,4},{7,5},{8,10},{9,11},{10,... | collective-permute-start | bytes 405512 | tf_op jit(solution)/shard_map/ppermute | solution.py:329
  34.2 1.5 %collective-permute-start.15 = (f32[264,128]{1,0:T(8,128)S(1)}, f32[264,128]{1,0:T(8,128)S(1)}, u32[]{:S(2)}, u32[]{:S(2)}) collective-permute-start(f32[264,128]{1,0:T(8,128)S(1)} %get-tuple-element.53), channel_id=1, source_target_pairs={{0,4},{1,5},{2,6},{3,7},{4,0},{5,1},{6,2},{7,3},{8,12},{9,13},{10,... | collective-permute-start | bytes 405512 | tf_op jit(solution)/shard_map/ppermute | solution.py:329
  35.7 0.5 collective-permute-start.16
  36.2 1.8 %collective-permute-done.13.refs_3_ = f32[272,128]{1,0:T(8,128)S(1)} collective-permute-done((f32[272,128]{1,0:T(8,128)S(1)}, f32[272,128]{1,0:T(8,128)S(1)}, u32[]{:S(2)}, u32[]{:S(2)}) %collective-permute-start.13) | collective-permute-done | bytes 139296 | tf_op jit(solution)/shard_map/ppermute | solution.py:336
  38.0 1.2 %collective-permute-done.12.refs_2_ = f32[272,128]{1,0:T(8,128)S(1)} collective-permute-done((f32[272,128]{1,0:T(8,128)S(1)}, f32[272,128]{1,0:T(8,128)S(1)}, u32[]{:S(2)}, u32[]{:S(2)}) %collective-permute-start.12) | collective-permute-done | bytes 139296 | tf_op jit(solution)/shard_map/ppermute | solution.py:336
  39.2 2.9 %collective-permute-done.15.refs_5_ = f32[264,128]{1,0:T(8,128)S(1)} collective-permute-done((f32[264,128]{1,0:T(8,128)S(1)}, f32[264,128]{1,0:T(8,128)S(1)}, u32[]{:S(2)}, u32[]{:S(2)}) %collective-permute-start.15) | collective-permute-done | bytes 135200 | tf_op jit(solution)/shard_map/ppermute | solution.py:329
  42.1 0.1 shard_map.50
  42.2 1.5 %collective-permute-start.17 = (f32[8,128]{1,0:T(8,128)S(1)}, f32[8,128]{1,0:T(8,128)S(1)}, u32[]{:S(2)}, u32[]{:S(2)}) collective-permute-start(f32[8,128]{1,0:T(8,128)S(1)} %get-tuple-element.55.refs_0_), channel_id=1, source_target_pairs={{24,0},{0,16},{16,8},{8,24},{25,1},{1,17},{17,9},{9,25},{26,2},{2,... | collective-permute-start | bytes 12296 | tf_op jit(solution)/shard_map/ppermute | solution.py:336
  43.7 2.4 %collective-permute-start.22 = (f32[264,128]{1,0:T(8,128)S(1)}, f32[264,128]{1,0:T(8,128)S(1)}, u32[]{:S(2)}, u32[]{:S(2)}) collective-permute-start(f32[264,128]{1,0:T(8,128)S(1)} %get-tuple-element.57), channel_id=1, source_target_pairs={{16,0},{8,16},{24,8},{0,24},{17,1},{9,17},{25,9},{1,25},{18,2},{10... | collective-permute-start | bytes 405512 | tf_op jit(solution)/shard_map/ppermute | solution.py:336
  46.1 1.2 %collective-permute-start.20 = (f32[256,128]{1,0:T(8,128)S(1)}, f32[256,128]{1,0:T(8,128)S(1)}, u32[]{:S(2)}, u32[]{:S(2)}) collective-permute-start(f32[256,128]{1,0:T(8,128)S(1)} %get-tuple-element.56.refs_2_), channel_id=1, source_target_pairs={{0,6},{1,7},{2,4},{3,5},{4,2},{5,3},{6,0},{7,1},{8,14},{9,15},{10,... | collective-permute-start | bytes 393224 | tf_op jit(solution)/shard_map/ppermute | solution.py:329
  47.2 1.2 %collective-permute-start.19 = (f32[256,128]{1,0:T(8,128)S(1)}, f32[256,128]{1,0:T(8,128)S(1)}, u32[]{:S(2)}, u32[]{:S(2)}) collective-permute-start(f32[256,128]{1,0:T(8,128)S(1)} %get-tuple-element.56.refs_2_), channel_id=1, source_target_pairs={{0,4},{1,5},{2,6},{3,7},{4,0},{5,1},{6,2},{7,3},{8,12},{9,13},{10,... | collective-permute-start | bytes 393224 | tf_op jit(solution)/shard_map/ppermute | solution.py:329
  48.5 1.1 %collective-permute-start.18 = (f32[256,128]{1,0:T(8,128)S(1)}, f32[256,128]{1,0:T(8,128)S(1)}, u32[]{:S(2)}, u32[]{:S(2)}) collective-permute-start(f32[256,128]{1,0:T(8,128)S(1)} %get-tuple-element.56.refs_2_), channel_id=1, source_target_pairs={{0,2},{1,3},{2,0},{3,1},{4,6},{5,7},{6,4},{7,5},{8,10},{9,11},{10,... | collective-permute-start | bytes 393224 | tf_op jit(solution)/shard_map/ppermute | solution.py:329
  49.5 2.5 %collective-permute-done.20.refs_5_ = f32[256,128]{1,0:T(8,128)S(1)} collective-permute-done((f32[256,128]{1,0:T(8,128)S(1)}, f32[256,128]{1,0:T(8,128)S(1)}, u32[]{:S(2)}, u32[]{:S(2)}) %collective-permute-start.20) | collective-permute-done | bytes 131104 | tf_op jit(solution)/shard_map/ppermute | solution.py:329
  52.0 1.3 %collective-permute-done.19.refs_4_ = f32[256,128]{1,0:T(8,128)S(1)} collective-permute-done((f32[256,128]{1,0:T(8,128)S(1)}, f32[256,128]{1,0:T(8,128)S(1)}, u32[]{:S(2)}, u32[]{:S(2)}) %collective-permute-start.19) | collective-permute-done | bytes 131104 | tf_op jit(solution)/shard_map/ppermute | solution.py:329
  53.3 0.1 collective-permute-done.18.refs_3_
  53.4 1.2 %shard_map.51 = (bf16[1024,256]{1,0:T(8,128)(2,1)S(1)}, bf16[256,256]{1,0:T(8,128)(2,1)S(1)}, bf16[256,256]{1,0:T(8,128)(2,1)S(1)}) custom-call(f32[8,128]{1,0:T(8,128)S(1)} %get-tuple-element.55.refs_0_, f32[8,128]{1,0:T(8,128)S(1)} %collective-permute-done.17.refs_1_, f32[256,128]{1,0:T(8,128)S(1)} %get-tuple-element.56.refs_2_, ...), custom_call_target="tpu_custom_call" | custom-call | bytes 1589248 | tf_op jit(solution)/shard_map/pallas_call | solution.py:34
  54.6 0.1 collective-permute-start.24
  54.7 0.8 %shard_map.52 = (f32[1024,128]{1,0:T(8,128)S(1)}, f32[1024,128]{1,0:T(8,128)S(1)}) custom-call(bf16[256,256]{1,0:T(8,128)(2,1)S(1)} %get-tuple-element.58.refs_0_.refs_12_, bf16[256,2048]{1,0:T(8,128)(2,1)S(1)} %get-tuple-element.40.refs_10_.refs_1_.refs_5_, bf16[256,2048]{1,0:T(8,128)(2,1)S(1)} %get-tuple-element.41.refs_11_.refs_0_.refs_2_.refs_6_), custom_call_target="tpu_custom_call" | custom-call | flops 402653184 | bytes 3276800 | tf_op jit(solution)/shard_map/pallas_call | solution.py:34
  55.5 0.6 collective-permute-start.23
  56.1 1.0 %shard_map.53 = (f32[256,128]{1,0:T(8,128)S(1)}, f32[272,128]{1,0:T(8,128)S(1)}, f32[272,128]{1,0:T(8,128)S(1)}) custom-call(bf16[1024,256]{1,0:T(8,128)(2,1)S(1)} %get-tuple-element.61.refs_0_.refs_10_, bf16[256,2048]{1,0:T(8,128)(2,1)S(1)} %get-tuple-element.43.refs_8_.refs_1_, bf16[256,2048]{1,0:T(8,128)(2,1)S(1)} %get-tuple-element.39.refs_0_.refs_9_.refs_2_, ...), custom_call_target="tpu_custom_call" | custom-call | flops 603979776 | bytes 7225344 | tf_op jit(solution)/shard_map/pallas_call | solution.py:34
  57.1 1.0 %shard_map.54 = (f32[256,128]{1,0:T(8,128)S(1)}, f32[288,128]{1,0:T(8,128)S(1)}, f32[288,128]{1,0:T(8,128)S(1)}, f32[8,128]{1,0:T(8,128)S(1)}) custom-call(bf16[1024,256]{1,0:T(8,128)(2,1)S(1)} %collective-permute-done.24.refs_0_, bf16[256,2048]{1,0:T(8,128)(2,1)S(1)} %get-tuple-element.43.refs_8_.refs_1_, ...), custom_call_target="tpu_custom_call" | custom-call | flops 603979776 | bytes 8441856 | tf_op jit(solution)/shard_map/pallas_call | solution.py:34
  58.1 0.9 %collective-permute-start.27 = (f32[8,128]{1,0:T(8,128)S(1)}, f32[8,128]{1,0:T(8,128)S(1)}, u32[]{:S(2)}, u32[]{:S(2)}) collective-permute-start(f32[8,128]{1,0:T(8,128)S(1)} %get-tuple-element.66), channel_id=1, source_target_pairs={{24,0},{0,16},{16,8},{8,24},{25,1},{1,17},{17,9},{9,25},{26,2},{2,... | collective-permute-start | bytes 12296 | tf_op jit(solution)/shard_map/ppermute | solution.py:336
  59.0 1.7 %collective-permute-start.26 = (f32[8,128]{1,0:T(8,128)S(1)}, f32[8,128]{1,0:T(8,128)S(1)}, u32[]{:S(2)}, u32[]{:S(2)}) collective-permute-start(f32[8,128]{1,0:T(8,128)S(1)} %get-tuple-element.66), channel_id=1, source_target_pairs={{8,0},{24,16},{0,8},{16,24},{9,1},{25,17},{1,9},{17,25},{10,2},{26... | collective-permute-start | bytes 12296 | tf_op jit(solution)/shard_map/ppermute | solution.py:336
  60.8 2.4 %collective-permute-start.25 = (f32[8,128]{1,0:T(8,128)S(1)}, f32[8,128]{1,0:T(8,128)S(1)}, u32[]{:S(2)}, u32[]{:S(2)}) collective-permute-start(f32[8,128]{1,0:T(8,128)S(1)} %get-tuple-element.66), channel_id=1, source_target_pairs={{16,0},{8,16},{24,8},{0,24},{17,1},{9,17},{25,9},{1,25},{18,2},{10... | collective-permute-start | bytes 12296 | tf_op jit(solution)/shard_map/ppermute | solution.py:336
  63.1 0.5 collective-permute-done.27
  63.6 0.4 collective-permute-start.30
  64.0 1.4 %collective-permute-done.25 = f32[8,128]{1,0:T(8,128)S(1)} collective-permute-done((f32[8,128]{1,0:T(8,128)S(1)}, f32[8,128]{1,0:T(8,128)S(1)}, u32[]{:S(2)}, u32[]{:S(2)}) %collective-permute-start.25) | collective-permute-done | bytes 4128 | tf_op jit(solution)/shard_map/ppermute | solution.py:336
  65.4 1.2 %collective-permute-done.28.refs_1_ = f32[8,128]{1,0:T(8,128)S(1)} collective-permute-done((f32[8,128]{1,0:T(8,128)S(1)}, f32[8,128]{1,0:T(8,128)S(1)}, u32[]{:S(2)}, u32[]{:S(2)}) %collective-permute-start.28) | collective-permute-done | bytes 4128 | tf_op jit(solution)/shard_map/ppermute | solution.py:329
  66.5 0.1 shard_map.55
  66.6 1.2 %collective-permute-start.31 = (f32[264,128]{1,0:T(8,128)S(1)}, f32[264,128]{1,0:T(8,128)S(1)}, u32[]{:S(2)}, u32[]{:S(2)}) collective-permute-start(f32[264,128]{1,0:T(8,128)S(1)} %get-tuple-element.71), channel_id=1, source_target_pairs={{0,2},{1,3},{2,0},{3,1},{4,6},{5,7},{6,4},{7,5},{8,10},{9,11},{10,... | collective-permute-start | bytes 405512 | tf_op jit(solution)/shard_map/ppermute | solution.py:329
  67.8 1.2 %collective-permute-start.32 = (f32[264,128]{1,0:T(8,128)S(1)}, f32[264,128]{1,0:T(8,128)S(1)}, u32[]{:S(2)}, u32[]{:S(2)}) collective-permute-start(f32[264,128]{1,0:T(8,128)S(1)} %get-tuple-element.72), channel_id=1, source_target_pairs={{0,4},{1,5},{2,6},{3,7},{4,0},{5,1},{6,2},{7,3},{8,12},{9,13},{10,... | collective-permute-start | bytes 405512 | tf_op jit(solution)/shard_map/ppermute | solution.py:329
  69.0 1.2 %collective-permute-start.33 = (f32[264,128]{1,0:T(8,128)S(1)}, f32[264,128]{1,0:T(8,128)S(1)}, u32[]{:S(2)}, u32[]{:S(2)}) collective-permute-start(f32[264,128]{1,0:T(8,128)S(1)} %get-tuple-element.73), channel_id=1, source_target_pairs={{0,6},{1,7},{2,4},{3,5},{4,2},{5,3},{6,0},{7,1},{8,14},{9,15},{10,... | collective-permute-start | bytes 405512 | tf_op jit(solution)/shard_map/ppermute | solution.py:329
  70.2 2.9 %collective-permute-done.31.refs_4_ = f32[264,128]{1,0:T(8,128)S(1)} collective-permute-done((f32[264,128]{1,0:T(8,128)S(1)}, f32[264,128]{1,0:T(8,128)S(1)}, u32[]{:S(2)}, u32[]{:S(2)}) %collective-permute-start.31) | collective-permute-done | bytes 135200 | tf_op jit(solution)/shard_map/ppermute | solution.py:329
  73.1 2.9 %collective-permute-done.32.refs_5_ = f32[264,128]{1,0:T(8,128)S(1)} collective-permute-done((f32[264,128]{1,0:T(8,128)S(1)}, f32[264,128]{1,0:T(8,128)S(1)}, u32[]{:S(2)}, u32[]{:S(2)}) %collective-permute-start.32) | collective-permute-done | bytes 135200 | tf_op jit(solution)/shard_map/ppermute | solution.py:329
  76.1 1.0 %shard_map.56 = (f32[256,128]{1,0:T(8,128)}, f32[256,128]{1,0:T(8,128)}) custom-call(f32[264,128]{1,0:T(8,128)S(1)} %get-tuple-element.67.refs_0_, f32[256,128]{1,0:T(8,128)S(1)} %get-tuple-element.68.refs_1_, f32[288,128]{1,0:T(8,128)S(1)} %collective-permute-done.29.refs_2_, f32[288,128]{1,0:T(8,128)S(1)} %collective-permute-done.30.refs_3_, ...), custom_call_target="tpu_custom_call" | custom-call | bytes 1228800 | tf_op jit(solution)/shard_map/pallas_call | solution.py:34
  (26 shorter events, 0.1 us)
Async XLA Ops:
  1.6 0.9 %copy-start.1 = (f32[256,128]{1,0:T(8,128)S(1)}, f32[256,128]{1,0:T(8,128)}, u32[]{:S(2)}) copy-start(f32[256,128]{1,0:T(8,128)} %logits.1) | copy-start | bytes 393220
  2.7 8.1 %collective-permute-start.5 = (bf16[256,256]{1,0:T(8,128)(2,1)S(1)}, bf16[256,256]{1,0:T(8,128)(2,1)S(1)}, u32[]{:S(2)}, u32[]{:S(2)}) collective-permute-start(bf16[256,256]{1,0:T(8,128)(2,1)S(1)} %get-tuple-element.42.refs_0_.own), channel_id=1, source_target_pairs={{0,1},{1,0},{2,3},{3,2},{4,5},{5,4},{6,7},{7,6},{8,9},{9,8},{10,11... | collective-permute-start | bytes 393224 | tf_op jit(solution)/shard_map/ppermute | solution.py:329
  3.2 16.5 %collective-permute-start.1 = (bf16[256,512]{1,0:T(8,128)(2,1)S(1)}, bf16[256,512]{1,0:T(8,128)(2,1)S(1)}, u32[]{:S(2)}, u32[]{:S(2)}) collective-permute-start(bf16[256,512]{1,0:T(8,128)(2,1)S(1)} %constant_dynamic-slice_fusion.rows.rows_ref), channel_id=1, source_target_pairs={{16,0},{8,16},{24,8},{0,24},{17,1},{9,17},{25,9},{1,25},{18,2},{10... | collective-permute-start | bytes 786440 | tf_op jit(solution)/shard_map/ppermute | solution.py:336
  7.8 18.6 %collective-permute-start.9 = (bf16[256,768]{1,0:T(8,128)(2,1)S(1)}, bf16[256,768]{1,0:T(8,128)(2,1)S(1)}, u32[]{:S(2)}, u32[]{:S(2)}) collective-permute-start(bf16[256,768]{1,0:T(8,128)(2,1)S(1)} %get-tuple-element.45), channel_id=1, source_target_pairs={{0,8},{8,0},{16,24},{24,16},{1,9},{9,1},{17,25},{25,17},{2,10},{10... | collective-permute-start | bytes 1179656 | tf_op jit(solution)/shard_map/ppermute | solution.py:336
  7.8 6.8 %collective-permute-start.4 = (bf16[256,256]{1,0:T(8,128)(2,1)S(1)}, bf16[256,256]{1,0:T(8,128)(2,1)S(1)}, u32[]{:S(2)}, u32[]{:S(2)}) collective-permute-start(bf16[256,256]{1,0:T(8,128)(2,1)S(1)} %get-tuple-element.42.refs_0_.own), channel_id=1, source_target_pairs={{0,6},{1,7},{2,4},{3,5},{4,2},{5,3},{6,0},{7,1},{8,14},{9,15},{10,... | collective-permute-start | bytes 393224 | tf_op jit(solution)/shard_map/ppermute | solution.py:329
  10.3 6.8 %collective-permute-start.3 = (bf16[256,256]{1,0:T(8,128)(2,1)S(1)}, bf16[256,256]{1,0:T(8,128)(2,1)S(1)}, u32[]{:S(2)}, u32[]{:S(2)}) collective-permute-start(bf16[256,256]{1,0:T(8,128)(2,1)S(1)} %get-tuple-element.42.refs_0_.own), channel_id=1, source_target_pairs={{0,4},{1,5},{2,6},{3,7},{4,0},{5,1},{6,2},{7,3},{8,12},{9,13},{10,... | collective-permute-start | bytes 393224 | tf_op jit(solution)/shard_map/ppermute | solution.py:329
  10.8 6.4 %collective-permute-start.2 = (bf16[256,256]{1,0:T(8,128)(2,1)S(1)}, bf16[256,256]{1,0:T(8,128)(2,1)S(1)}, u32[]{:S(2)}, u32[]{:S(2)}) collective-permute-start(bf16[256,256]{1,0:T(8,128)(2,1)S(1)} %get-tuple-element.42.refs_0_.own), channel_id=1, source_target_pairs={{0,2},{1,3},{2,0},{3,1},{4,6},{5,7},{6,4},{7,5},{8,10},{9,11},{10,... | collective-permute-start | bytes 393224 | tf_op jit(solution)/shard_map/ppermute | solution.py:329
  11.3 1.6 %copy-start = (bf16[2048,512]{1,0:T(8,128)(2,1)S(1)}, bf16[2048,512]{1,0:T(8,128)(2,1)}, u32[]{:S(2)}) copy-start(bf16[2048,512]{1,0:T(8,128)(2,1)} %plane_ref.5) | copy-start | bytes 6291460
  14.6 12.7 %collective-permute-start = (bf16[272,256]{1,0:T(8,128)(2,1)S(1)}, bf16[272,256]{1,0:T(8,128)(2,1)S(1)}, u32[]{:S(2)}, u32[]{:S(2)}) collective-permute-start(bf16[272,256]{1,0:T(8,128)(2,1)S(1)} %get-tuple-element.38), channel_id=1, source_target_pairs={{16,0},{8,16},{24,8},{0,24},{17,1},{9,17},{25,9},{1,25},{18,2},{10... | collective-permute-start | bytes 417800 | tf_op jit(solution)/shard_map/ppermute | solution.py:336
  17.1 3.5 %collective-permute-start.8 = (bf16[256,256]{1,0:T(8,128)(2,1)S(1)}, bf16[256,256]{1,0:T(8,128)(2,1)S(1)}, u32[]{:S(2)}, u32[]{:S(2)}) collective-permute-start(bf16[256,256]{1,0:T(8,128)(2,1)S(1)} %collective-permute-done.4.refs_3_), channel_id=1, source_target_pairs={{0,1},{1,0},{2,3},{3,2},{4,5},{5,4},{6,7},{7,6},{8,9},{9,8},{10,11... | collective-permute-start | bytes 393224 | tf_op jit(solution)/shard_map/ppermute | solution.py:329
  17.2 3.4 %collective-permute-start.7 = (bf16[256,256]{1,0:T(8,128)(2,1)S(1)}, bf16[256,256]{1,0:T(8,128)(2,1)S(1)}, u32[]{:S(2)}, u32[]{:S(2)}) collective-permute-start(bf16[256,256]{1,0:T(8,128)(2,1)S(1)} %collective-permute-done.3.refs_2_), channel_id=1, source_target_pairs={{0,1},{1,0},{2,3},{3,2},{4,5},{5,4},{6,7},{7,6},{8,9},{9,8},{10,11... | collective-permute-start | bytes 393224 | tf_op jit(solution)/shard_map/ppermute | solution.py:329
  19.7 1.3 %collective-permute-start.6 = (bf16[256,256]{1,0:T(8,128)(2,1)S(1)}, bf16[256,256]{1,0:T(8,128)(2,1)S(1)}, u32[]{:S(2)}, u32[]{:S(2)}) collective-permute-start(bf16[256,256]{1,0:T(8,128)(2,1)S(1)} %collective-permute-done.2.refs_1_), channel_id=1, source_target_pairs={{0,1},{1,0},{2,3},{3,2},{4,5},{5,4},{6,7},{7,6},{8,9},{9,8},{10,11... | collective-permute-start | bytes 393224 | tf_op jit(solution)/shard_map/ppermute | solution.py:329
  28.1 4.4 %collective-permute-start.10 = (f32[1024,128]{1,0:T(8,128)S(1)}, f32[1024,128]{1,0:T(8,128)S(1)}, u32[]{:S(2)}, u32[]{:S(2)}) collective-permute-start(f32[1024,128]{1,0:T(8,128)S(1)} %get-tuple-element.48), channel_id=1, source_target_pairs={{0,1},{1,0},{2,3},{3,2},{4,5},{5,4},{6,7},{7,6},{8,9},{9,8},{10,11... | collective-permute-start | bytes 1572872 | tf_op jit(solution)/shard_map/ppermute | solution.py:329
  29.0 3.5 %collective-permute-start.11 = (f32[8,128]{1,0:T(8,128)S(1)}, f32[8,128]{1,0:T(8,128)S(1)}, u32[]{:S(2)}, u32[]{:S(2)}) collective-permute-start(f32[8,128]{1,0:T(8,128)S(1)} %shard_map.48.refs_0_), channel_id=1, source_target_pairs={{0,1},{1,0},{2,3},{3,2},{4,5},{5,4},{6,7},{7,6},{8,9},{9,8},{10,11... | collective-permute-start | bytes 12296 | tf_op jit(solution)/shard_map/ppermute | solution.py:329
  29.6 8.4 %collective-permute-start.13 = (f32[272,128]{1,0:T(8,128)S(1)}, f32[272,128]{1,0:T(8,128)S(1)}, u32[]{:S(2)}, u32[]{:S(2)}) collective-permute-start(f32[272,128]{1,0:T(8,128)S(1)} %get-tuple-element.50.refs_2_), channel_id=1, source_target_pairs={{24,0},{0,16},{16,8},{8,24},{25,1},{1,17},{17,9},{9,25},{26,2},{2,... | collective-permute-start | bytes 417800 | tf_op jit(solution)/shard_map/ppermute | solution.py:336
  29.6 9.6 %collective-permute-start.12 = (f32[272,128]{1,0:T(8,128)S(1)}, f32[272,128]{1,0:T(8,128)S(1)}, u32[]{:S(2)}, u32[]{:S(2)}) collective-permute-start(f32[272,128]{1,0:T(8,128)S(1)} %shard_map.47.refs_1_), channel_id=1, source_target_pairs={{0,8},{8,0},{16,24},{24,16},{1,9},{9,1},{17,25},{25,17},{2,10},{10... | collective-permute-start | bytes 417800 | tf_op jit(solution)/shard_map/ppermute | solution.py:336
  32.6 6.5 %collective-permute-start.14 = (f32[264,128]{1,0:T(8,128)S(1)}, f32[264,128]{1,0:T(8,128)S(1)}, u32[]{:S(2)}, u32[]{:S(2)}) collective-permute-start(f32[264,128]{1,0:T(8,128)S(1)} %get-tuple-element.52), channel_id=1, source_target_pairs={{0,2},{1,3},{2,0},{3,1},{4,6},{5,7},{6,4},{7,5},{8,10},{9,11},{10,... | collective-permute-start | bytes 405512 | tf_op jit(solution)/shard_map/ppermute | solution.py:329
  34.2 7.9 %collective-permute-start.15 = (f32[264,128]{1,0:T(8,128)S(1)}, f32[264,128]{1,0:T(8,128)S(1)}, u32[]{:S(2)}, u32[]{:S(2)}) collective-permute-start(f32[264,128]{1,0:T(8,128)S(1)} %get-tuple-element.53), channel_id=1, source_target_pairs={{0,4},{1,5},{2,6},{3,7},{4,0},{5,1},{6,2},{7,3},{8,12},{9,13},{10,... | collective-permute-start | bytes 405512 | tf_op jit(solution)/shard_map/ppermute | solution.py:329
  35.7 6.4 %collective-permute-start.16 = (f32[264,128]{1,0:T(8,128)S(1)}, f32[264,128]{1,0:T(8,128)S(1)}, u32[]{:S(2)}, u32[]{:S(2)}) collective-permute-start(f32[264,128]{1,0:T(8,128)S(1)} %get-tuple-element.54), channel_id=1, source_target_pairs={{0,6},{1,7},{2,4},{3,5},{4,2},{5,3},{6,0},{7,1},{8,14},{9,15},{10,... | collective-permute-start | bytes 405512 | tf_op jit(solution)/shard_map/ppermute | solution.py:329
  42.2 6.3 %collective-permute-start.17 = (f32[8,128]{1,0:T(8,128)S(1)}, f32[8,128]{1,0:T(8,128)S(1)}, u32[]{:S(2)}, u32[]{:S(2)}) collective-permute-start(f32[8,128]{1,0:T(8,128)S(1)} %get-tuple-element.55.refs_0_), channel_id=1, source_target_pairs={{24,0},{0,16},{16,8},{8,24},{25,1},{1,17},{17,9},{9,25},{26,2},{2,... | collective-permute-start | bytes 12296 | tf_op jit(solution)/shard_map/ppermute | solution.py:336
  43.7 9.7 %collective-permute-start.22 = (f32[264,128]{1,0:T(8,128)S(1)}, f32[264,128]{1,0:T(8,128)S(1)}, u32[]{:S(2)}, u32[]{:S(2)}) collective-permute-start(f32[264,128]{1,0:T(8,128)S(1)} %get-tuple-element.57), channel_id=1, source_target_pairs={{16,0},{8,16},{24,8},{0,24},{17,1},{9,17},{25,9},{1,25},{18,2},{10... | collective-permute-start | bytes 405512 | tf_op jit(solution)/shard_map/ppermute | solution.py:336
  46.0 7.4 %collective-permute-start.21 = (f32[264,128]{1,0:T(8,128)S(1)}, f32[264,128]{1,0:T(8,128)S(1)}, u32[]{:S(2)}, u32[]{:S(2)}) collective-permute-start(f32[264,128]{1,0:T(8,128)S(1)} %get-tuple-element.57), channel_id=1, source_target_pairs={{0,8},{8,0},{16,24},{24,16},{1,9},{9,1},{17,25},{25,17},{2,10},{10... | collective-permute-start | bytes 405512 | tf_op jit(solution)/shard_map/ppermute | solution.py:336
  46.1 6.0 %collective-permute-start.20 = (f32[256,128]{1,0:T(8,128)S(1)}, f32[256,128]{1,0:T(8,128)S(1)}, u32[]{:S(2)}, u32[]{:S(2)}) collective-permute-start(f32[256,128]{1,0:T(8,128)S(1)} %get-tuple-element.56.refs_2_), channel_id=1, source_target_pairs={{0,6},{1,7},{2,4},{3,5},{4,2},{5,3},{6,0},{7,1},{8,14},{9,15},{10,... | collective-permute-start | bytes 393224 | tf_op jit(solution)/shard_map/ppermute | solution.py:329
  47.2 6.1 %collective-permute-start.19 = (f32[256,128]{1,0:T(8,128)S(1)}, f32[256,128]{1,0:T(8,128)S(1)}, u32[]{:S(2)}, u32[]{:S(2)}) collective-permute-start(f32[256,128]{1,0:T(8,128)S(1)} %get-tuple-element.56.refs_2_), channel_id=1, source_target_pairs={{0,4},{1,5},{2,6},{3,7},{4,0},{5,1},{6,2},{7,3},{8,12},{9,13},{10,... | collective-permute-start | bytes 393224 | tf_op jit(solution)/shard_map/ppermute | solution.py:329
  48.5 5.0 %collective-permute-start.18 = (f32[256,128]{1,0:T(8,128)S(1)}, f32[256,128]{1,0:T(8,128)S(1)}, u32[]{:S(2)}, u32[]{:S(2)}) collective-permute-start(f32[256,128]{1,0:T(8,128)S(1)} %get-tuple-element.56.refs_2_), channel_id=1, source_target_pairs={{0,2},{1,3},{2,0},{3,1},{4,6},{5,7},{6,4},{7,5},{8,10},{9,11},{10,... | collective-permute-start | bytes 393224 | tf_op jit(solution)/shard_map/ppermute | solution.py:329
  54.6 2.4 %collective-permute-start.24 = (bf16[1024,256]{1,0:T(8,128)(2,1)S(1)}, bf16[1024,256]{1,0:T(8,128)(2,1)S(1)}, u32[]{:S(2)}, u32[]{:S(2)}) collective-permute-start(bf16[1024,256]{1,0:T(8,128)(2,1)S(1)} %get-tuple-element.61.refs_0_.refs_10_), channel_id=1, source_target_pairs={{0,1},{1,0},{2,3},{3,2},{4,5},{5,4},{6,7},{7,6},{8,9},{9,8},{10,11... | collective-permute-start | bytes 1572872 | tf_op jit(solution)/shard_map/ppermute | solution.py:329
  55.5 9.9 %collective-permute-start.23 = (f32[1024,128]{1,0:T(8,128)S(1)}, f32[1024,128]{1,0:T(8,128)S(1)}, u32[]{:S(2)}, u32[]{:S(2)}) collective-permute-start(f32[1024,128]{1,0:T(8,128)S(1)} %get-tuple-element.60), channel_id=1, source_target_pairs={{0,1},{1,0},{2,3},{3,2},{4,5},{5,4},{6,7},{7,6},{8,9},{9,8},{10,11... | collective-permute-start | bytes 1572872 | tf_op jit(solution)/shard_map/ppermute | solution.py:329
  58.1 5.5 %collective-permute-start.27 = (f32[8,128]{1,0:T(8,128)S(1)}, f32[8,128]{1,0:T(8,128)S(1)}, u32[]{:S(2)}, u32[]{:S(2)}) collective-permute-start(f32[8,128]{1,0:T(8,128)S(1)} %get-tuple-element.66), channel_id=1, source_target_pairs={{24,0},{0,16},{16,8},{8,24},{25,1},{1,17},{17,9},{9,25},{26,2},{2,... | collective-permute-start | bytes 12296 | tf_op jit(solution)/shard_map/ppermute | solution.py:336
  59.0 5.0 %collective-permute-start.26 = (f32[8,128]{1,0:T(8,128)S(1)}, f32[8,128]{1,0:T(8,128)S(1)}, u32[]{:S(2)}, u32[]{:S(2)}) collective-permute-start(f32[8,128]{1,0:T(8,128)S(1)} %get-tuple-element.66), channel_id=1, source_target_pairs={{8,0},{24,16},{0,8},{16,24},{9,1},{25,17},{1,9},{17,25},{10,2},{26... | collective-permute-start | bytes 12296 | tf_op jit(solution)/shard_map/ppermute | solution.py:336
  60.8 4.6 %collective-permute-start.25 = (f32[8,128]{1,0:T(8,128)S(1)}, f32[8,128]{1,0:T(8,128)S(1)}, u32[]{:S(2)}, u32[]{:S(2)}) collective-permute-start(f32[8,128]{1,0:T(8,128)S(1)} %get-tuple-element.66), channel_id=1, source_target_pairs={{16,0},{8,16},{24,8},{0,24},{17,1},{9,17},{25,9},{1,25},{18,2},{10... | collective-permute-start | bytes 12296 | tf_op jit(solution)/shard_map/ppermute | solution.py:336
  63.1 12.9 %collective-permute-start.29 = (f32[288,128]{1,0:T(8,128)S(1)}, f32[288,128]{1,0:T(8,128)S(1)}, u32[]{:S(2)}, u32[]{:S(2)}) collective-permute-start(f32[288,128]{1,0:T(8,128)S(1)} %get-tuple-element.69), channel_id=1, source_target_pairs={{0,8},{8,0},{16,24},{24,16},{1,9},{9,1},{17,25},{25,17},{2,10},{10... | collective-permute-start | bytes 442376 | tf_op jit(solution)/shard_map/ppermute | solution.py:336
  63.6 12.5 %collective-permute-start.30 = (f32[288,128]{1,0:T(8,128)S(1)}, f32[288,128]{1,0:T(8,128)S(1)}, u32[]{:S(2)}, u32[]{:S(2)}) collective-permute-start(f32[288,128]{1,0:T(8,128)S(1)} %get-tuple-element.70), channel_id=1, source_target_pairs={{24,0},{0,16},{16,8},{8,24},{25,1},{1,17},{17,9},{9,25},{26,2},{2,... | collective-permute-start | bytes 442376 | tf_op jit(solution)/shard_map/ppermute | solution.py:336
  65.4 1.2 %collective-permute-start.28 = (f32[8,128]{1,0:T(8,128)S(1)}, f32[8,128]{1,0:T(8,128)S(1)}, u32[]{:S(2)}, u32[]{:S(2)}) collective-permute-start(f32[8,128]{1,0:T(8,128)S(1)} %add_add_fusion.refs_0_), channel_id=1, source_target_pairs={{0,1},{1,0},{2,3},{3,2},{4,5},{5,4},{6,7},{7,6},{8,9},{9,8},{10,11... | collective-permute-start | bytes 12296 | tf_op jit(solution)/shard_map/ppermute | solution.py:329
  66.6 6.5 %collective-permute-start.31 = (f32[264,128]{1,0:T(8,128)S(1)}, f32[264,128]{1,0:T(8,128)S(1)}, u32[]{:S(2)}, u32[]{:S(2)}) collective-permute-start(f32[264,128]{1,0:T(8,128)S(1)} %get-tuple-element.71), channel_id=1, source_target_pairs={{0,2},{1,3},{2,0},{3,1},{4,6},{5,7},{6,4},{7,5},{8,10},{9,11},{10,... | collective-permute-start | bytes 405512 | tf_op jit(solution)/shard_map/ppermute | solution.py:329
  67.8 8.3 %collective-permute-start.32 = (f32[264,128]{1,0:T(8,128)S(1)}, f32[264,128]{1,0:T(8,128)S(1)}, u32[]{:S(2)}, u32[]{:S(2)}) collective-permute-start(f32[264,128]{1,0:T(8,128)S(1)} %get-tuple-element.72), channel_id=1, source_target_pairs={{0,4},{1,5},{2,6},{3,7},{4,0},{5,1},{6,2},{7,3},{8,12},{9,13},{10,... | collective-permute-start | bytes 405512 | tf_op jit(solution)/shard_map/ppermute | solution.py:329
  69.0 7.1 %collective-permute-start.33 = (f32[264,128]{1,0:T(8,128)S(1)}, f32[264,128]{1,0:T(8,128)S(1)}, u32[]{:S(2)}, u32[]{:S(2)}) collective-permute-start(f32[264,128]{1,0:T(8,128)S(1)} %get-tuple-element.73), channel_id=1, source_target_pairs={{0,6},{1,7},{2,4},{3,5},{4,2},{5,3},{6,0},{7,1},{8,14},{9,15},{10,... | collective-permute-start | bytes 405512 | tf_op jit(solution)/shard_map/ppermute | solution.py:329

commit v10 on v9

--- a/solution.py
+++ b/solution.py
@@ -14,8 +14,8 @@
 LAST_ROWS = 32
 BACK_ROWS = 16
 VMEM_BYTES = 24 * 1024 * 1024
-NEAR_COST = 2.7
-CROSS_COST = 3
+NEAR_COST = 3
+CROSS_COST = 2.7
 VMEM = pl.BlockSpec(memory_space=pltpu.VMEM)
 SMEM = pl.BlockSpec(memory_space=pltpu.SMEM)
 ANY = pl.BlockSpec(memory_space=pl.ANY)

time: 77.3 us -> 78.5 us (1.016)
  waiting for transfers between devices: 28.3 us -> 31.5 us
  starting transfers between devices: 33.6 us -> 31.7 us
    ppermute x13, waiting for transfers between devices: 11 us -> 14.5 us  [shift(): return lax.ppermute(x, 'row', pairs)]
    ppermute x13, starting transfers between devices: 17.3 us -> 15.8 us  [shift(): return lax.ppermute(x, 'row', pairs)]
  transfers between devices with their start and end apart: 34 -> 34, of which waited for: 17 -> 18; matrix products, arithmetic and copies ran while one was open for 0% -> 0% of each run, Pallas kernels for 10% -> 10%
where the time goes in v10:
time: 78.5 us; the launch traced here: 78.3 us
  starting transfers between devices  31.7 us (40%)
  waiting for transfers between devices  31.5 us (40%)
  Pallas kernels  10.9 us (14%)
  local copies, waits for them, and re-layouts  3.47 us (4%)
  between operations  0.82 us (1%)
    ppermute x21, waiting for transfers between devices, by_col(): return lax.ppermute(x, 'col', [(i, i ^ mask) for i in range(cols)])  17 us
    ppermute x21, starting transfers between devices, by_col(): return lax.ppermute(x, 'col', [(i, i ^ mask) for i in range(cols)])  15.9 us
    ppermute x13, starting transfers between devices, shift(): return lax.ppermute(x, 'row', pairs)  15.8 us
    ppermute x13, waiting for transfers between devices, shift(): return lax.ppermute(x, 'row', pairs)  14.5 us
    pallas_call x16, Pallas kernels, call(): pl.pallas_call(body, in_specs=specs or [VMEM] * len(args), out_specs=[VME...  10.9 us
    unnamed x4, local copies, waits for them, and re-layouts  2.49 us
  transfers between devices with their start and end apart: 34, of which 18 were waited for; matrix products, arithmetic and copies ran while one was open for 0% of the time, Pallas kernels for 10%

profile of v10, /device:TPU:0, one launch (start us, length us, event | category | flops | bytes accessed | tf_op | source)
XLA Modules:
  0.0 78.3 jit_solution(17180067929468544317)
XLA Ops:
  0.6 1.0 %constant_dynamic-slice_fusion.rows.rows_ref = bf16[256,512]{1,0:T(8,128)(2,1)S(1)} fusion(bf16[2048,512]{1,0:T(8,128)(2,1)} %plane_ref.5, s32[]{:T(128)S(6)} %select_n.3), kind=kLoop, calls=%fused_computation.1 | loop fusion | bytes 524292 | tf_op jit(solution)/shard_map/dynamic_slice | solution.py:339
  1.6 5.1 %collective-permute-start.1 = (bf16[256,512]{1,0:T(8,128)(2,1)S(1)}, bf16[256,512]{1,0:T(8,128)(2,1)S(1)}, u32[]{:S(2)}, u32[]{:S(2)}) collective-permute-start(bf16[256,512]{1,0:T(8,128)(2,1)S(1)} %constant_dynamic-slice_fusion.rows.rows_ref), channel_id=1, source_target_pairs={{16,0},{8,16},{24,8},{0,24},{17,1},{9,17},{25,9},{1,25},{18,2},{10... | collective-permute-start | bytes 786440 | tf_op jit(solution)/shard_map/ppermute | solution.py:336
  6.7 0.9 %copy-done.1 = f32[256,128]{1,0:T(8,128)S(1)} copy-done((f32[256,128]{1,0:T(8,128)S(1)}, f32[256,128]{1,0:T(8,128)}, u32[]{:S(2)}) %copy-start.1) | copy-done | bytes 131096
  7.6 0.1 shard_map.41
  7.8 0.1 collective-permute-start.9
  7.8 2.5 %collective-permute-start.4 = (bf16[256,256]{1,0:T(8,128)(2,1)S(1)}, bf16[256,256]{1,0:T(8,128)(2,1)S(1)}, u32[]{:S(2)}, u32[]{:S(2)}) collective-permute-start(bf16[256,256]{1,0:T(8,128)(2,1)S(1)} %get-tuple-element.42.refs_0_.own), channel_id=1, source_target_pairs={{0,6},{1,7},{2,4},{3,5},{4,2},{5,3},{6,0},{7,1},{8,14},{9,15},{10,... | collective-permute-start | bytes 393224 | tf_op jit(solution)/shard_map/ppermute | solution.py:329
  10.4 0.5 collective-permute-start.3
  10.9 0.5 collective-permute-start.2
  11.4 1.6 %copy-done = bf16[2048,512]{1,0:T(8,128)(2,1)S(1)} copy-done((bf16[2048,512]{1,0:T(8,128)(2,1)S(1)}, bf16[2048,512]{1,0:T(8,128)(2,1)}, u32[]{:S(2)}) %copy-start) | copy-done | bytes 2097176
  13.0 0.9 %shard_map.42 = (bf16[256,2048]{1,0:T(8,128)(2,1)S(1)}, bf16[256,2048]{1,0:T(8,128)(2,1)S(1)}) custom-call(s32[1]{0:T(128)} %bitcast.column_ref, bf16[256,512]{1,0:T(8,128)(2,1)S(1)} %constant_dynamic-slice_fusion.rows.rows_ref, bf16[2048,512]{1,0:T(8,128)(2,1)S(1)} %copy-done), custom_call_target="tpu_custom_call" | custom-call | flops 536870912 | bytes 4456452 | tf_op jit(solution)/shard_map/pallas_call | solution.py:34
  13.9 0.4 collective-permute-done.4.refs_3_
  14.3 2.3 %collective-permute-done.3.refs_2_ = bf16[256,256]{1,0:T(8,128)(2,1)S(1)} collective-permute-done((bf16[256,256]{1,0:T(8,128)(2,1)S(1)}, bf16[256,256]{1,0:T(8,128)(2,1)S(1)}, u32[]{:S(2)}, u32[]{:S(2)}) %collective-permute-start.3) | collective-permute-done | bytes 131104 | tf_op jit(solution)/shard_map/ppermute | solution.py:329
  16.6 0.1 collective-permute-done.2.refs_1_
  16.6 0.4 collective-permute-start.7
  17.1 0.6 collective-permute-done.1.rows_ref
  17.7 0.9 %shard_map.43 = (bf16[256,2048]{1,0:T(8,128)(2,1)S(1)}, bf16[256,2048]{1,0:T(8,128)(2,1)S(1)}) custom-call(s32[1]{0:T(128)} %bitcast.column_ref, bf16[256,512]{1,0:T(8,128)(2,1)S(1)} %collective-permute-done.1.rows_ref, bf16[2048,512]{1,0:T(8,128)(2,1)S(1)} %copy-done, bf16[256,2048]{1,0:T(8,128)(2,1)S(1)} %get-tuple-element.39.refs_0_.refs_9_.refs_2_), custom_call_target="tpu_custom_call" | custom-call | flops 1449132032 | bytes 5505028 | tf_op jit(solution)/shard_map/pallas_call | solution.py:34
  18.7 0.4 collective-permute-done.6.refs_5_
  19.1 1.3 %shard_map.44 = (f32[256,128]{1,0:T(8,128)S(1)}, f32[272,128]{1,0:T(8,128)S(1)}) custom-call(bf16[256,256]{1,0:T(8,128)(2,1)S(1)} %get-tuple-element.42.refs_0_.own, bf16[256,256]{1,0:T(8,128)(2,1)S(1)} %collective-permute-done.2.refs_1_, bf16[256,256]{1,0:T(8,128)(2,1)S(1)} %collective-permute-done.3.refs_2_, ...), custom_call_target="tpu_custom_call" | custom-call | tf_op jit(solution)/shard_map/pallas_call | solution.py:34
  20.3 3.1 %collective-permute-done.9.rows_ref.refs_3_ = bf16[256,768]{1,0:T(8,128)(2,1)S(1)} collective-permute-done((bf16[256,768]{1,0:T(8,128)(2,1)S(1)}, bf16[256,768]{1,0:T(8,128)(2,1)S(1)}, u32[]{:S(2)}, u32[]{:S(2)}) %collective-permute-start.9) | collective-permute-done | bytes 393248 | tf_op jit(solution)/shard_map/ppermute | solution.py:336
  23.4 0.9 %shard_map.45 = (bf16[256,2048]{1,0:T(8,128)(2,1)S(1)}, bf16[256,2048]{1,0:T(8,128)(2,1)S(1)}) custom-call(s32[1]{0:T(128)} %bitcast.column_ref, bf16[256,768]{1,0:T(8,128)(2,1)S(1)} %collective-permute-done.9.rows_ref.refs_3_, bf16[2048,512]{1,0:T(8,128)(2,1)S(1)} %copy-done, bf16[256,2048]{1,0:T(8,128)(2,1)S(1)} %get-tuple-element.41.refs_11_.refs_0_.refs_2_.refs_6_), custom_call_target="tpu_custom_call" | custom-call | flops 1610612736 | bytes 5636100 | tf_op jit(solution)/shard_map/pallas_call | solution.py:34
  24.3 4.3 %collective-permute-done.refs_0_.refs_4_ = bf16[272,256]{1,0:T(8,128)(2,1)S(1)} collective-permute-done((bf16[272,256]{1,0:T(8,128)(2,1)S(1)}, bf16[272,256]{1,0:T(8,128)(2,1)S(1)}, u32[]{:S(2)}, u32[]{:S(2)}) %collective-permute-start) | collective-permute-done | bytes 139296 | tf_op jit(solution)/shard_map/ppermute | solution.py:336
  28.7 0.8 shard_map.46
  29.4 0.1 collective-permute-start.10
  29.5 0.7 shard_map.47.refs_1_
  30.2 0.1 shard_map.48.refs_0_
  30.3 0.6 collective-permute-start.11
  30.9 0.5 collective-permute-start.13
  31.4 0.3 collective-permute-done.11.refs_1_
  31.7 0.1 shard_map.49
  31.8 1.6 %collective-permute-start.14 = (f32[264,128]{1,0:T(8,128)S(1)}, f32[264,128]{1,0:T(8,128)S(1)}, u32[]{:S(2)}, u32[]{:S(2)}) collective-permute-start(f32[264,128]{1,0:T(8,128)S(1)} %get-tuple-element.52), channel_id=1, source_target_pairs={{0,2},{1,3},{2,0},{3,1},{4,6},{5,7},{6,4},{7,5},{8,10},{9,11},{10,... | collective-permute-start | bytes 405512 | tf_op jit(solution)/shard_map/ppermute | solution.py:329
  33.4 1.2 %collective-permute-start.15 = (f32[264,128]{1,0:T(8,128)S(1)}, f32[264,128]{1,0:T(8,128)S(1)}, u32[]{:S(2)}, u32[]{:S(2)}) collective-permute-start(f32[264,128]{1,0:T(8,128)S(1)} %get-tuple-element.53), channel_id=1, source_target_pairs={{0,4},{1,5},{2,6},{3,7},{4,0},{5,1},{6,2},{7,3},{8,12},{9,13},{10,... | collective-permute-start | bytes 405512 | tf_op jit(solution)/shard_map/ppermute | solution.py:329
  34.6 0.7 collective-permute-start.16
  35.4 3.9 %collective-permute-done.13.refs_3_ = f32[272,128]{1,0:T(8,128)S(1)} collective-permute-done((f32[272,128]{1,0:T(8,128)S(1)}, f32[272,128]{1,0:T(8,128)S(1)}, u32[]{:S(2)}, u32[]{:S(2)}) %collective-permute-start.13) | collective-permute-done | bytes 139296 | tf_op jit(solution)/shard_map/ppermute | solution.py:336
  39.2 0.6 collective-permute-done.12.refs_2_
  39.8 2.1 %collective-permute-done.15.refs_5_ = f32[264,128]{1,0:T(8,128)S(1)} collective-permute-done((f32[264,128]{1,0:T(8,128)S(1)}, f32[264,128]{1,0:T(8,128)S(1)}, u32[]{:S(2)}, u32[]{:S(2)}) %collective-permute-start.15) | collective-permute-done | bytes 135200 | tf_op jit(solution)/shard_map/ppermute | solution.py:329
  41.9 0.1 shard_map.50
  41.9 3.1 %collective-permute-start.17 = (f32[8,128]{1,0:T(8,128)S(1)}, f32[8,128]{1,0:T(8,128)S(1)}, u32[]{:S(2)}, u32[]{:S(2)}) collective-permute-start(f32[8,128]{1,0:T(8,128)S(1)} %get-tuple-element.55.refs_0_), channel_id=1, source_target_pairs={{24,0},{0,16},{16,8},{8,24},{25,1},{1,17},{17,9},{9,25},{26,2},{2,... | collective-permute-start | bytes 12296 | tf_op jit(solution)/shard_map/ppermute | solution.py:336
  45.0 0.8 %collective-permute-start.22 = (f32[264,128]{1,0:T(8,128)S(1)}, f32[264,128]{1,0:T(8,128)S(1)}, u32[]{:S(2)}, u32[]{:S(2)}) collective-permute-start(f32[264,128]{1,0:T(8,128)S(1)} %get-tuple-element.57), channel_id=1, source_target_pairs={{16,0},{8,16},{24,8},{0,24},{17,1},{9,17},{25,9},{1,25},{18,2},{10... | collective-permute-start | bytes 405512 | tf_op jit(solution)/shard_map/ppermute | solution.py:336
  45.8 1.5 %collective-permute-start.20 = (f32[256,128]{1,0:T(8,128)S(1)}, f32[256,128]{1,0:T(8,128)S(1)}, u32[]{:S(2)}, u32[]{:S(2)}) collective-permute-start(f32[256,128]{1,0:T(8,128)S(1)} %get-tuple-element.56.refs_2_), channel_id=1, source_target_pairs={{0,6},{1,7},{2,4},{3,5},{4,2},{5,3},{6,0},{7,1},{8,14},{9,15},{10,... | collective-permute-start | bytes 393224 | tf_op jit(solution)/shard_map/ppermute | solution.py:329
  47.3 0.9 %collective-permute-start.19 = (f32[256,128]{1,0:T(8,128)S(1)}, f32[256,128]{1,0:T(8,128)S(1)}, u32[]{:S(2)}, u32[]{:S(2)}) collective-permute-start(f32[256,128]{1,0:T(8,128)S(1)} %get-tuple-element.56.refs_2_), channel_id=1, source_target_pairs={{0,4},{1,5},{2,6},{3,7},{4,0},{5,1},{6,2},{7,3},{8,12},{9,13},{10,... | collective-permute-start | bytes 393224 | tf_op jit(solution)/shard_map/ppermute | solution.py:329
  48.2 1.1 %collective-permute-start.18 = (f32[256,128]{1,0:T(8,128)S(1)}, f32[256,128]{1,0:T(8,128)S(1)}, u32[]{:S(2)}, u32[]{:S(2)}) collective-permute-start(f32[256,128]{1,0:T(8,128)S(1)} %get-tuple-element.56.refs_2_), channel_id=1, source_target_pairs={{0,2},{1,3},{2,0},{3,1},{4,6},{5,7},{6,4},{7,5},{8,10},{9,11},{10,... | collective-permute-start | bytes 393224 | tf_op jit(solution)/shard_map/ppermute | solution.py:329
  49.3 3.1 %collective-permute-done.20.refs_5_ = f32[256,128]{1,0:T(8,128)S(1)} collective-permute-done((f32[256,128]{1,0:T(8,128)S(1)}, f32[256,128]{1,0:T(8,128)S(1)}, u32[]{:S(2)}, u32[]{:S(2)}) %collective-permute-start.20) | collective-permute-done | bytes 131104 | tf_op jit(solution)/shard_map/ppermute | solution.py:329
  52.4 1.3 %collective-permute-done.19.refs_4_ = f32[256,128]{1,0:T(8,128)S(1)} collective-permute-done((f32[256,128]{1,0:T(8,128)S(1)}, f32[256,128]{1,0:T(8,128)S(1)}, u32[]{:S(2)}, u32[]{:S(2)}) %collective-permute-start.19) | collective-permute-done | bytes 131104 | tf_op jit(solution)/shard_map/ppermute | solution.py:329
  53.7 1.2 %shard_map.51 = (bf16[1024,256]{1,0:T(8,128)(2,1)S(1)}, bf16[256,256]{1,0:T(8,128)(2,1)S(1)}, bf16[256,256]{1,0:T(8,128)(2,1)S(1)}) custom-call(f32[8,128]{1,0:T(8,128)S(1)} %get-tuple-element.55.refs_0_, f32[8,128]{1,0:T(8,128)S(1)} %collective-permute-done.17.refs_1_, f32[256,128]{1,0:T(8,128)S(1)} %get-tuple-element.56.refs_2_, ...), custom_call_target="tpu_custom_call" | custom-call | bytes 1589248 | tf_op jit(solution)/shard_map/pallas_call | solution.py:34
  54.9 0.1 collective-permute-start.24
  55.0 0.8 %shard_map.52 = (f32[1024,128]{1,0:T(8,128)S(1)}, f32[1024,128]{1,0:T(8,128)S(1)}) custom-call(bf16[256,256]{1,0:T(8,128)(2,1)S(1)} %get-tuple-element.58.refs_0_.refs_12_, bf16[256,2048]{1,0:T(8,128)(2,1)S(1)} %get-tuple-element.40.refs_10_.refs_1_.refs_5_, bf16[256,2048]{1,0:T(8,128)(2,1)S(1)} %get-tuple-element.41.refs_11_.refs_0_.refs_2_.refs_6_), custom_call_target="tpu_custom_call" | custom-call | flops 402653184 | bytes 3276800 | tf_op jit(solution)/shard_map/pallas_call | solution.py:34
  55.8 0.6 collective-permute-start.23
  56.3 1.0 %shard_map.53 = (f32[256,128]{1,0:T(8,128)S(1)}, f32[272,128]{1,0:T(8,128)S(1)}, f32[272,128]{1,0:T(8,128)S(1)}) custom-call(bf16[1024,256]{1,0:T(8,128)(2,1)S(1)} %get-tuple-element.61.refs_0_.refs_10_, bf16[256,2048]{1,0:T(8,128)(2,1)S(1)} %get-tuple-element.43.refs_8_.refs_1_, bf16[256,2048]{1,0:T(8,128)(2,1)S(1)} %get-tuple-element.39.refs_0_.refs_9_.refs_2_, ...), custom_call_target="tpu_custom_call" | custom-call | flops 603979776 | bytes 7225344 | tf_op jit(solution)/shard_map/pallas_call | solution.py:34
  57.4 1.0 %shard_map.54 = (f32[256,128]{1,0:T(8,128)S(1)}, f32[288,128]{1,0:T(8,128)S(1)}, f32[288,128]{1,0:T(8,128)S(1)}, f32[8,128]{1,0:T(8,128)S(1)}) custom-call(bf16[1024,256]{1,0:T(8,128)(2,1)S(1)} %collective-permute-done.24.refs_0_, bf16[256,2048]{1,0:T(8,128)(2,1)S(1)} %get-tuple-element.43.refs_8_.refs_1_, ...), custom_call_target="tpu_custom_call" | custom-call | flops 603979776 | bytes 8441856 | tf_op jit(solution)/shard_map/pallas_call | solution.py:34
  58.4 1.7 %collective-permute-start.27 = (f32[8,128]{1,0:T(8,128)S(1)}, f32[8,128]{1,0:T(8,128)S(1)}, u32[]{:S(2)}, u32[]{:S(2)}) collective-permute-start(f32[8,128]{1,0:T(8,128)S(1)} %get-tuple-element.66), channel_id=1, source_target_pairs={{24,0},{0,16},{16,8},{8,24},{25,1},{1,17},{17,9},{9,25},{26,2},{2,... | collective-permute-start | bytes 12296 | tf_op jit(solution)/shard_map/ppermute | solution.py:336
  60.1 1.9 %collective-permute-start.26 = (f32[8,128]{1,0:T(8,128)S(1)}, f32[8,128]{1,0:T(8,128)S(1)}, u32[]{:S(2)}, u32[]{:S(2)}) collective-permute-start(f32[8,128]{1,0:T(8,128)S(1)} %get-tuple-element.66), channel_id=1, source_target_pairs={{8,0},{24,16},{0,8},{16,24},{9,1},{25,17},{1,9},{17,25},{10,2},{26... | collective-permute-start | bytes 12296 | tf_op jit(solution)/shard_map/ppermute | solution.py:336
  62.0 1.1 %collective-permute-start.25 = (f32[8,128]{1,0:T(8,128)S(1)}, f32[8,128]{1,0:T(8,128)S(1)}, u32[]{:S(2)}, u32[]{:S(2)}) collective-permute-start(f32[8,128]{1,0:T(8,128)S(1)} %get-tuple-element.66), channel_id=1, source_target_pairs={{16,0},{8,16},{24,8},{0,24},{17,1},{9,17},{25,9},{1,25},{18,2},{10... | collective-permute-start | bytes 12296 | tf_op jit(solution)/shard_map/ppermute | solution.py:336
  63.1 0.3 collective-permute-start.29
  63.4 0.5 collective-permute-done.27
  63.9 1.2 %collective-permute-start.30 = (f32[288,128]{1,0:T(8,128)S(1)}, f32[288,128]{1,0:T(8,128)S(1)}, u32[]{:S(2)}, u32[]{:S(2)}) collective-permute-start(f32[288,128]{1,0:T(8,128)S(1)} %get-tuple-element.70), channel_id=1, source_target_pairs={{24,0},{0,16},{16,8},{8,24},{25,1},{1,17},{17,9},{9,25},{26,2},{2,... | collective-permute-start | bytes 442376 | tf_op jit(solution)/shard_map/ppermute | solution.py:336
  65.0 1.5 %collective-permute-done.25 = f32[8,128]{1,0:T(8,128)S(1)} collective-permute-done((f32[8,128]{1,0:T(8,128)S(1)}, f32[8,128]{1,0:T(8,128)S(1)}, u32[]{:S(2)}, u32[]{:S(2)}) %collective-permute-start.25) | collective-permute-done | bytes 4128 | tf_op jit(solution)/shard_map/ppermute | solution.py:336
  66.6 1.2 %collective-permute-done.28.refs_1_ = f32[8,128]{1,0:T(8,128)S(1)} collective-permute-done((f32[8,128]{1,0:T(8,128)S(1)}, f32[8,128]{1,0:T(8,128)S(1)}, u32[]{:S(2)}, u32[]{:S(2)}) %collective-permute-start.28) | collective-permute-done | bytes 4128 | tf_op jit(solution)/shard_map/ppermute | solution.py:329
  67.7 0.1 shard_map.55
  67.8 1.2 %collective-permute-start.31 = (f32[264,128]{1,0:T(8,128)S(1)}, f32[264,128]{1,0:T(8,128)S(1)}, u32[]{:S(2)}, u32[]{:S(2)}) collective-permute-start(f32[264,128]{1,0:T(8,128)S(1)} %get-tuple-element.71), channel_id=1, source_target_pairs={{0,2},{1,3},{2,0},{3,1},{4,6},{5,7},{6,4},{7,5},{8,10},{9,11},{10,... | collective-permute-start | bytes 405512 | tf_op jit(solution)/shard_map/ppermute | solution.py:329
  69.0 1.0 %collective-permute-start.32 = (f32[264,128]{1,0:T(8,128)S(1)}, f32[264,128]{1,0:T(8,128)S(1)}, u32[]{:S(2)}, u32[]{:S(2)}) collective-permute-start(f32[264,128]{1,0:T(8,128)S(1)} %get-tuple-element.72), channel_id=1, source_target_pairs={{0,4},{1,5},{2,6},{3,7},{4,0},{5,1},{6,2},{7,3},{8,12},{9,13},{10,... | collective-permute-start | bytes 405512 | tf_op jit(solution)/shard_map/ppermute | solution.py:329
  70.1 1.3 %collective-permute-start.33 = (f32[264,128]{1,0:T(8,128)S(1)}, f32[264,128]{1,0:T(8,128)S(1)}, u32[]{:S(2)}, u32[]{:S(2)}) collective-permute-start(f32[264,128]{1,0:T(8,128)S(1)} %get-tuple-element.73), channel_id=1, source_target_pairs={{0,6},{1,7},{2,4},{3,5},{4,2},{5,3},{6,0},{7,1},{8,14},{9,15},{10,... | collective-permute-start | bytes 405512 | tf_op jit(solution)/shard_map/ppermute | solution.py:329
  71.4 2.9 %collective-permute-done.31.refs_4_ = f32[264,128]{1,0:T(8,128)S(1)} collective-permute-done((f32[264,128]{1,0:T(8,128)S(1)}, f32[264,128]{1,0:T(8,128)S(1)}, u32[]{:S(2)}, u32[]{:S(2)}) %collective-permute-start.31) | collective-permute-done | bytes 135200 | tf_op jit(solution)/shard_map/ppermute | solution.py:329
  74.3 3.0 %collective-permute-done.32.refs_5_ = f32[264,128]{1,0:T(8,128)S(1)} collective-permute-done((f32[264,128]{1,0:T(8,128)S(1)}, f32[264,128]{1,0:T(8,128)S(1)}, u32[]{:S(2)}, u32[]{:S(2)}) %collective-permute-start.32) | collective-permute-done | bytes 135200 | tf_op jit(solution)/shard_map/ppermute | solution.py:329
  77.3 1.0 %shard_map.56 = (f32[256,128]{1,0:T(8,128)}, f32[256,128]{1,0:T(8,128)}) custom-call(f32[264,128]{1,0:T(8,128)S(1)} %get-tuple-element.67.refs_0_, f32[256,128]{1,0:T(8,128)S(1)} %get-tuple-element.68.refs_1_, f32[288,128]{1,0:T(8,128)S(1)} %collective-permute-done.29.refs_2_, f32[288,128]{1,0:T(8,128)S(1)} %collective-permute-done.30.refs_3_, ...), custom_call_target="tpu_custom_call" | custom-call | bytes 1228800 | tf_op jit(solution)/shard_map/pallas_call | solution.py:34
  (26 shorter events, 0.1 us)
Async XLA Ops:
  1.6 16.1 %collective-permute-start.1 = (bf16[256,512]{1,0:T(8,128)(2,1)S(1)}, bf16[256,512]{1,0:T(8,128)(2,1)S(1)}, u32[]{:S(2)}, u32[]{:S(2)}) collective-permute-start(bf16[256,512]{1,0:T(8,128)(2,1)S(1)} %constant_dynamic-slice_fusion.rows.rows_ref), channel_id=1, source_target_pairs={{16,0},{8,16},{24,8},{0,24},{17,1},{9,17},{25,9},{1,25},{18,2},{10... | collective-permute-start | bytes 786440 | tf_op jit(solution)/shard_map/ppermute | solution.py:336
  6.7 0.9 %copy-start.1 = (f32[256,128]{1,0:T(8,128)S(1)}, f32[256,128]{1,0:T(8,128)}, u32[]{:S(2)}) copy-start(f32[256,128]{1,0:T(8,128)} %logits.1) | copy-start | bytes 393220
  7.8 15.7 %collective-permute-start.9 = (bf16[256,768]{1,0:T(8,128)(2,1)S(1)}, bf16[256,768]{1,0:T(8,128)(2,1)S(1)}, u32[]{:S(2)}, u32[]{:S(2)}) collective-permute-start(bf16[256,768]{1,0:T(8,128)(2,1)S(1)} %get-tuple-element.45), channel_id=1, source_target_pairs={{0,8},{8,0},{16,24},{24,16},{1,9},{9,1},{17,25},{25,17},{2,10},{10... | collective-permute-start | bytes 1179656 | tf_op jit(solution)/shard_map/ppermute | solution.py:336
  7.8 6.5 %collective-permute-start.4 = (bf16[256,256]{1,0:T(8,128)(2,1)S(1)}, bf16[256,256]{1,0:T(8,128)(2,1)S(1)}, u32[]{:S(2)}, u32[]{:S(2)}) collective-permute-start(bf16[256,256]{1,0:T(8,128)(2,1)S(1)} %get-tuple-element.42.refs_0_.own), channel_id=1, source_target_pairs={{0,6},{1,7},{2,4},{3,5},{4,2},{5,3},{6,0},{7,1},{8,14},{9,15},{10,... | collective-permute-start | bytes 393224 | tf_op jit(solution)/shard_map/ppermute | solution.py:329
  10.4 6.2 %collective-permute-start.3 = (bf16[256,256]{1,0:T(8,128)(2,1)S(1)}, bf16[256,256]{1,0:T(8,128)(2,1)S(1)}, u32[]{:S(2)}, u32[]{:S(2)}) collective-permute-start(bf16[256,256]{1,0:T(8,128)(2,1)S(1)} %get-tuple-element.42.refs_0_.own), channel_id=1, source_target_pairs={{0,4},{1,5},{2,6},{3,7},{4,0},{5,1},{6,2},{7,3},{8,12},{9,13},{10,... | collective-permute-start | bytes 393224 | tf_op jit(solution)/shard_map/ppermute | solution.py:329
  10.9 5.8 %collective-permute-start.2 = (bf16[256,256]{1,0:T(8,128)(2,1)S(1)}, bf16[256,256]{1,0:T(8,128)(2,1)S(1)}, u32[]{:S(2)}, u32[]{:S(2)}) collective-permute-start(bf16[256,256]{1,0:T(8,128)(2,1)S(1)} %get-tuple-element.42.refs_0_.own), channel_id=1, source_target_pairs={{0,2},{1,3},{2,0},{3,1},{4,6},{5,7},{6,4},{7,5},{8,10},{9,11},{10,... | collective-permute-start | bytes 393224 | tf_op jit(solution)/shard_map/ppermute | solution.py:329
  11.4 1.6 %copy-start = (bf16[2048,512]{1,0:T(8,128)(2,1)S(1)}, bf16[2048,512]{1,0:T(8,128)(2,1)}, u32[]{:S(2)}) copy-start(bf16[2048,512]{1,0:T(8,128)(2,1)} %plane_ref.5) | copy-start | bytes 6291460
  14.3 4.3 %collective-permute-start.5 = (bf16[256,256]{1,0:T(8,128)(2,1)S(1)}, bf16[256,256]{1,0:T(8,128)(2,1)S(1)}, u32[]{:S(2)}, u32[]{:S(2)}) collective-permute-start(bf16[256,256]{1,0:T(8,128)(2,1)S(1)} %get-tuple-element.42.refs_0_.own), channel_id=1, source_target_pairs={{0,1},{1,0},{2,3},{3,2},{4,5},{5,4},{6,7},{7,6},{8,9},{9,8},{10,11... | collective-permute-start | bytes 393224 | tf_op jit(solution)/shard_map/ppermute | solution.py:329
  16.6 2.1 %collective-permute-start.8 = (bf16[256,256]{1,0:T(8,128)(2,1)S(1)}, bf16[256,256]{1,0:T(8,128)(2,1)S(1)}, u32[]{:S(2)}, u32[]{:S(2)}) collective-permute-start(bf16[256,256]{1,0:T(8,128)(2,1)S(1)} %collective-permute-done.4.refs_3_), channel_id=1, source_target_pairs={{0,1},{1,0},{2,3},{3,2},{4,5},{5,4},{6,7},{7,6},{8,9},{9,8},{10,11... | collective-permute-start | bytes 393224 | tf_op jit(solution)/shard_map/ppermute | solution.py:329
  16.6 2.1 %collective-permute-start.7 = (bf16[256,256]{1,0:T(8,128)(2,1)S(1)}, bf16[256,256]{1,0:T(8,128)(2,1)S(1)}, u32[]{:S(2)}, u32[]{:S(2)}) collective-permute-start(bf16[256,256]{1,0:T(8,128)(2,1)S(1)} %collective-permute-done.3.refs_2_), channel_id=1, source_target_pairs={{0,1},{1,0},{2,3},{3,2},{4,5},{5,4},{6,7},{7,6},{8,9},{9,8},{10,11... | collective-permute-start | bytes 393224 | tf_op jit(solution)/shard_map/ppermute | solution.py:329
  17.7 1.3 %collective-permute-start.6 = (bf16[256,256]{1,0:T(8,128)(2,1)S(1)}, bf16[256,256]{1,0:T(8,128)(2,1)S(1)}, u32[]{:S(2)}, u32[]{:S(2)}) collective-permute-start(bf16[256,256]{1,0:T(8,128)(2,1)S(1)} %collective-permute-done.2.refs_1_), channel_id=1, source_target_pairs={{0,1},{1,0},{2,3},{3,2},{4,5},{5,4},{6,7},{7,6},{8,9},{9,8},{10,11... | collective-permute-start | bytes 393224 | tf_op jit(solution)/shard_map/ppermute | solution.py:329
  18.6 10.0 %collective-permute-start = (bf16[272,256]{1,0:T(8,128)(2,1)S(1)}, bf16[272,256]{1,0:T(8,128)(2,1)S(1)}, u32[]{:S(2)}, u32[]{:S(2)}) collective-permute-start(bf16[272,256]{1,0:T(8,128)(2,1)S(1)} %get-tuple-element.38), channel_id=1, source_target_pairs={{16,0},{8,16},{24,8},{0,24},{17,1},{9,17},{25,9},{1,25},{18,2},{10... | collective-permute-start | bytes 417800 | tf_op jit(solution)/shard_map/ppermute | solution.py:336
  29.4 2.3 %collective-permute-start.10 = (f32[1024,128]{1,0:T(8,128)S(1)}, f32[1024,128]{1,0:T(8,128)S(1)}, u32[]{:S(2)}, u32[]{:S(2)}) collective-permute-start(f32[1024,128]{1,0:T(8,128)S(1)} %get-tuple-element.48), channel_id=1, source_target_pairs={{0,1},{1,0},{2,3},{3,2},{4,5},{5,4},{6,7},{7,6},{8,9},{9,8},{10,11... | collective-permute-start | bytes 1572872 | tf_op jit(solution)/shard_map/ppermute | solution.py:329
  30.3 1.4 %collective-permute-start.11 = (f32[8,128]{1,0:T(8,128)S(1)}, f32[8,128]{1,0:T(8,128)S(1)}, u32[]{:S(2)}, u32[]{:S(2)}) collective-permute-start(f32[8,128]{1,0:T(8,128)S(1)} %shard_map.48.refs_0_), channel_id=1, source_target_pairs={{0,1},{1,0},{2,3},{3,2},{4,5},{5,4},{6,7},{7,6},{8,9},{9,8},{10,11... | collective-permute-start | bytes 12296 | tf_op jit(solution)/shard_map/ppermute | solution.py:329
  30.9 8.3 %collective-permute-start.13 = (f32[272,128]{1,0:T(8,128)S(1)}, f32[272,128]{1,0:T(8,128)S(1)}, u32[]{:S(2)}, u32[]{:S(2)}) collective-permute-start(f32[272,128]{1,0:T(8,128)S(1)} %get-tuple-element.50.refs_2_), channel_id=1, source_target_pairs={{24,0},{0,16},{16,8},{8,24},{25,1},{1,17},{17,9},{9,25},{26,2},{2,... | collective-permute-start | bytes 417800 | tf_op jit(solution)/shard_map/ppermute | solution.py:336
  31.4 8.3 %collective-permute-start.12 = (f32[272,128]{1,0:T(8,128)S(1)}, f32[272,128]{1,0:T(8,128)S(1)}, u32[]{:S(2)}, u32[]{:S(2)}) collective-permute-start(f32[272,128]{1,0:T(8,128)S(1)} %shard_map.47.refs_1_), channel_id=1, source_target_pairs={{0,8},{8,0},{16,24},{24,16},{1,9},{9,1},{17,25},{25,17},{2,10},{10... | collective-permute-start | bytes 417800 | tf_op jit(solution)/shard_map/ppermute | solution.py:336
  31.8 8.0 %collective-permute-start.14 = (f32[264,128]{1,0:T(8,128)S(1)}, f32[264,128]{1,0:T(8,128)S(1)}, u32[]{:S(2)}, u32[]{:S(2)}) collective-permute-start(f32[264,128]{1,0:T(8,128)S(1)} %get-tuple-element.52), channel_id=1, source_target_pairs={{0,2},{1,3},{2,0},{3,1},{4,6},{5,7},{6,4},{7,5},{8,10},{9,11},{10,... | collective-permute-start | bytes 405512 | tf_op jit(solution)/shard_map/ppermute | solution.py:329
  33.4 8.4 %collective-permute-start.15 = (f32[264,128]{1,0:T(8,128)S(1)}, f32[264,128]{1,0:T(8,128)S(1)}, u32[]{:S(2)}, u32[]{:S(2)}) collective-permute-start(f32[264,128]{1,0:T(8,128)S(1)} %get-tuple-element.53), channel_id=1, source_target_pairs={{0,4},{1,5},{2,6},{3,7},{4,0},{5,1},{6,2},{7,3},{8,12},{9,13},{10,... | collective-permute-start | bytes 405512 | tf_op jit(solution)/shard_map/ppermute | solution.py:329
  34.6 7.2 %collective-permute-start.16 = (f32[264,128]{1,0:T(8,128)S(1)}, f32[264,128]{1,0:T(8,128)S(1)}, u32[]{:S(2)}, u32[]{:S(2)}) collective-permute-start(f32[264,128]{1,0:T(8,128)S(1)} %get-tuple-element.54), channel_id=1, source_target_pairs={{0,6},{1,7},{2,4},{3,5},{4,2},{5,3},{6,0},{7,1},{8,14},{9,15},{10,... | collective-permute-start | bytes 405512 | tf_op jit(solution)/shard_map/ppermute | solution.py:329
  41.9 6.3 %collective-permute-start.17 = (f32[8,128]{1,0:T(8,128)S(1)}, f32[8,128]{1,0:T(8,128)S(1)}, u32[]{:S(2)}, u32[]{:S(2)}) collective-permute-start(f32[8,128]{1,0:T(8,128)S(1)} %get-tuple-element.55.refs_0_), channel_id=1, source_target_pairs={{24,0},{0,16},{16,8},{8,24},{25,1},{1,17},{17,9},{9,25},{26,2},{2,... | collective-permute-start | bytes 12296 | tf_op jit(solution)/shard_map/ppermute | solution.py:336
  45.0 8.7 %collective-permute-start.22 = (f32[264,128]{1,0:T(8,128)S(1)}, f32[264,128]{1,0:T(8,128)S(1)}, u32[]{:S(2)}, u32[]{:S(2)}) collective-permute-start(f32[264,128]{1,0:T(8,128)S(1)} %get-tuple-element.57), channel_id=1, source_target_pairs={{16,0},{8,16},{24,8},{0,24},{17,1},{9,17},{25,9},{1,25},{18,2},{10... | collective-permute-start | bytes 405512 | tf_op jit(solution)/shard_map/ppermute | solution.py:336
  45.8 7.9 %collective-permute-start.21 = (f32[264,128]{1,0:T(8,128)S(1)}, f32[264,128]{1,0:T(8,128)S(1)}, u32[]{:S(2)}, u32[]{:S(2)}) collective-permute-start(f32[264,128]{1,0:T(8,128)S(1)} %get-tuple-element.57), channel_id=1, source_target_pairs={{0,8},{8,0},{16,24},{24,16},{1,9},{9,1},{17,25},{25,17},{2,10},{10... | collective-permute-start | bytes 405512 | tf_op jit(solution)/shard_map/ppermute | solution.py:336
  45.8 6.6 %collective-permute-start.20 = (f32[256,128]{1,0:T(8,128)S(1)}, f32[256,128]{1,0:T(8,128)S(1)}, u32[]{:S(2)}, u32[]{:S(2)}) collective-permute-start(f32[256,128]{1,0:T(8,128)S(1)} %get-tuple-element.56.refs_2_), channel_id=1, source_target_pairs={{0,6},{1,7},{2,4},{3,5},{4,2},{5,3},{6,0},{7,1},{8,14},{9,15},{10,... | collective-permute-start | bytes 393224 | tf_op jit(solution)/shard_map/ppermute | solution.py:329
  47.3 6.4 %collective-permute-start.19 = (f32[256,128]{1,0:T(8,128)S(1)}, f32[256,128]{1,0:T(8,128)S(1)}, u32[]{:S(2)}, u32[]{:S(2)}) collective-permute-start(f32[256,128]{1,0:T(8,128)S(1)} %get-tuple-element.56.refs_2_), channel_id=1, source_target_pairs={{0,4},{1,5},{2,6},{3,7},{4,0},{5,1},{6,2},{7,3},{8,12},{9,13},{10,... | collective-permute-start | bytes 393224 | tf_op jit(solution)/shard_map/ppermute | solution.py:329
  48.2 5.5 %collective-permute-start.18 = (f32[256,128]{1,0:T(8,128)S(1)}, f32[256,128]{1,0:T(8,128)S(1)}, u32[]{:S(2)}, u32[]{:S(2)}) collective-permute-start(f32[256,128]{1,0:T(8,128)S(1)} %get-tuple-element.56.refs_2_), channel_id=1, source_target_pairs={{0,2},{1,3},{2,0},{3,1},{4,6},{5,7},{6,4},{7,5},{8,10},{9,11},{10,... | collective-permute-start | bytes 393224 | tf_op jit(solution)/shard_map/ppermute | solution.py:329
  54.9 2.4 %collective-permute-start.24 = (bf16[1024,256]{1,0:T(8,128)(2,1)S(1)}, bf16[1024,256]{1,0:T(8,128)(2,1)S(1)}, u32[]{:S(2)}, u32[]{:S(2)}) collective-permute-start(bf16[1024,256]{1,0:T(8,128)(2,1)S(1)} %get-tuple-element.61.refs_0_.refs_10_), channel_id=1, source_target_pairs={{0,1},{1,0},{2,3},{3,2},{4,5},{5,4},{6,7},{7,6},{8,9},{9,8},{10,11... | collective-permute-start | bytes 1572872 | tf_op jit(solution)/shard_map/ppermute | solution.py:329
  55.8 10.8 %collective-permute-start.23 = (f32[1024,128]{1,0:T(8,128)S(1)}, f32[1024,128]{1,0:T(8,128)S(1)}, u32[]{:S(2)}, u32[]{:S(2)}) collective-permute-start(f32[1024,128]{1,0:T(8,128)S(1)} %get-tuple-element.60), channel_id=1, source_target_pairs={{0,1},{1,0},{2,3},{3,2},{4,5},{5,4},{6,7},{7,6},{8,9},{9,8},{10,11... | collective-permute-start | bytes 1572872 | tf_op jit(solution)/shard_map/ppermute | solution.py:329
  58.4 5.5 %collective-permute-start.27 = (f32[8,128]{1,0:T(8,128)S(1)}, f32[8,128]{1,0:T(8,128)S(1)}, u32[]{:S(2)}, u32[]{:S(2)}) collective-permute-start(f32[8,128]{1,0:T(8,128)S(1)} %get-tuple-element.66), channel_id=1, source_target_pairs={{24,0},{0,16},{16,8},{8,24},{25,1},{1,17},{17,9},{9,25},{26,2},{2,... | collective-permute-start | bytes 12296 | tf_op jit(solution)/shard_map/ppermute | solution.py:336
  60.1 5.0 %collective-permute-start.26 = (f32[8,128]{1,0:T(8,128)S(1)}, f32[8,128]{1,0:T(8,128)S(1)}, u32[]{:S(2)}, u32[]{:S(2)}) collective-permute-start(f32[8,128]{1,0:T(8,128)S(1)} %get-tuple-element.66), channel_id=1, source_target_pairs={{8,0},{24,16},{0,8},{16,24},{9,1},{25,17},{1,9},{17,25},{10,2},{26... | collective-permute-start | bytes 12296 | tf_op jit(solution)/shard_map/ppermute | solution.py:336
  62.0 4.6 %collective-permute-start.25 = (f32[8,128]{1,0:T(8,128)S(1)}, f32[8,128]{1,0:T(8,128)S(1)}, u32[]{:S(2)}, u32[]{:S(2)}) collective-permute-start(f32[8,128]{1,0:T(8,128)S(1)} %get-tuple-element.66), channel_id=1, source_target_pairs={{16,0},{8,16},{24,8},{0,24},{17,1},{9,17},{25,9},{1,25},{18,2},{10... | collective-permute-start | bytes 12296 | tf_op jit(solution)/shard_map/ppermute | solution.py:336
  63.1 14.2 %collective-permute-start.29 = (f32[288,128]{1,0:T(8,128)S(1)}, f32[288,128]{1,0:T(8,128)S(1)}, u32[]{:S(2)}, u32[]{:S(2)}) collective-permute-start(f32[288,128]{1,0:T(8,128)S(1)} %get-tuple-element.69), channel_id=1, source_target_pairs={{0,8},{8,0},{16,24},{24,16},{1,9},{9,1},{17,25},{25,17},{2,10},{10... | collective-permute-start | bytes 442376 | tf_op jit(solution)/shard_map/ppermute | solution.py:336
  63.9 13.5 %collective-permute-start.30 = (f32[288,128]{1,0:T(8,128)S(1)}, f32[288,128]{1,0:T(8,128)S(1)}, u32[]{:S(2)}, u32[]{:S(2)}) collective-permute-start(f32[288,128]{1,0:T(8,128)S(1)} %get-tuple-element.70), channel_id=1, source_target_pairs={{24,0},{0,16},{16,8},{8,24},{25,1},{1,17},{17,9},{9,25},{26,2},{2,... | collective-permute-start | bytes 442376 | tf_op jit(solution)/shard_map/ppermute | solution.py:336
  66.6 1.2 %collective-permute-start.28 = (f32[8,128]{1,0:T(8,128)S(1)}, f32[8,128]{1,0:T(8,128)S(1)}, u32[]{:S(2)}, u32[]{:S(2)}) collective-permute-start(f32[8,128]{1,0:T(8,128)S(1)} %add_add_fusion.refs_0_), channel_id=1, source_target_pairs={{0,1},{1,0},{2,3},{3,2},{4,5},{5,4},{6,7},{7,6},{8,9},{9,8},{10,11... | collective-permute-start | bytes 12296 | tf_op jit(solution)/shard_map/ppermute | solution.py:329
  67.8 6.5 %collective-permute-start.31 = (f32[264,128]{1,0:T(8,128)S(1)}, f32[264,128]{1,0:T(8,128)S(1)}, u32[]{:S(2)}, u32[]{:S(2)}) collective-permute-start(f32[264,128]{1,0:T(8,128)S(1)} %get-tuple-element.71), channel_id=1, source_target_pairs={{0,2},{1,3},{2,0},{3,1},{4,6},{5,7},{6,4},{7,5},{8,10},{9,11},{10,... | collective-permute-start | bytes 405512 | tf_op jit(solution)/shard_map/ppermute | solution.py:329
  69.0 8.3 %collective-permute-start.32 = (f32[264,128]{1,0:T(8,128)S(1)}, f32[264,128]{1,0:T(8,128)S(1)}, u32[]{:S(2)}, u32[]{:S(2)}) collective-permute-start(f32[264,128]{1,0:T(8,128)S(1)} %get-tuple-element.72), channel_id=1, source_target_pairs={{0,4},{1,5},{2,6},{3,7},{4,0},{5,1},{6,2},{7,3},{8,12},{9,13},{10,... | collective-permute-start | bytes 405512 | tf_op jit(solution)/shard_map/ppermute | solution.py:329
  70.1 7.2 %collective-permute-start.33 = (f32[264,128]{1,0:T(8,128)S(1)}, f32[264,128]{1,0:T(8,128)S(1)}, u32[]{:S(2)}, u32[]{:S(2)}) collective-permute-start(f32[264,128]{1,0:T(8,128)S(1)} %get-tuple-element.73), channel_id=1, source_target_pairs={{0,6},{1,7},{2,4},{3,5},{4,2},{5,3},{6,0},{7,1},{8,14},{9,15},{10,... | collective-permute-start | bytes 405512 | tf_op jit(solution)/shard_map/ppermute | solution.py:329

commit v11 on v7

--- a/solution.py
+++ b/solution.py
@@ -56,10 +56,11 @@
 
 
 def standardize(scores, size, weighted):
-    distance = weighted / (size * size) - 2.0 * scores / size
+    inverse = 1.0 / size
+    distance = weighted * inverse * inverse - scores * (2.0 * inverse)
     centered = distance - jnp.mean(distance, axis=1, keepdims=True)
     spread = jnp.mean(centered * centered, axis=1, keepdims=True)
-    return centered / jnp.sqrt(spread + 1e-06)
+    return centered * lax.rsqrt(spread + 1e-06)
 
 
 def normalize(raised):

time: 75.4 us -> 75.3 us (level)
  no operation moved by 1% of the time
where the time goes in v11:
time: 75.3 us; the launch traced here: 75.1 us
  starting transfers between devices  32.2 us (43%)
  waiting for transfers between devices  28 us (37%)
  Pallas kernels  10.6 us (14%)
  local copies, waits for them, and re-layouts  3.47 us (5%)
  between operations  0.82 us (1%)
    ppermute x13, starting transfers between devices, shift(): return lax.ppermute(x, 'row', pairs)  16.5 us
    ppermute x20, starting transfers between devices, by_col(): return lax.ppermute(x, 'col', [(i, i ^ mask) for i in range(cols)])  15.6 us
    ppermute x20, waiting for transfers between devices, by_col(): return lax.ppermute(x, 'col', [(i, i ^ mask) for i in range(cols)])  14.9 us
    ppermute x13, waiting for transfers between devices, shift(): return lax.ppermute(x, 'row', pairs)  13.1 us
    pallas_call x15, Pallas kernels, call(): pl.pallas_call(body, in_specs=specs or [VMEM] * len(args), out_specs=[VME...  10.6 us
    unnamed x4, local copies, waits for them, and re-layouts  2.49 us
  transfers between devices with their start and end apart: 33, of which 15 were waited for; matrix products, arithmetic and copies ran while one was open for 0% of the time, Pallas kernels for 10%

profile of v11, /device:TPU:0, one launch (start us, length us, event | category | flops | bytes accessed | tf_op | source)
XLA Modules:
  0.0 75.1 jit_solution(13866320701742212909)
XLA Ops:
  0.6 1.0 %constant_dynamic-slice_fusion.rows.rows_ref = bf16[256,512]{1,0:T(8,128)(2,1)S(1)} fusion(bf16[2048,512]{1,0:T(8,128)(2,1)} %plane_ref.5, s32[]{:T(128)S(6)} %select_n.3), kind=kLoop, calls=%fused_computation.1 | loop fusion | bytes 524292 | tf_op jit(solution)/shard_map/dynamic_slice | solution.py:340
  1.6 5.1 %collective-permute-start.1 = (bf16[256,512]{1,0:T(8,128)(2,1)S(1)}, bf16[256,512]{1,0:T(8,128)(2,1)S(1)}, u32[]{:S(2)}, u32[]{:S(2)}) collective-permute-start(bf16[256,512]{1,0:T(8,128)(2,1)S(1)} %constant_dynamic-slice_fusion.rows.rows_ref), channel_id=1, source_target_pairs={{16,0},{8,16},{24,8},{0,24},{17,1},{9,17},{25,9},{1,25},{18,2},{10... | collective-permute-start | bytes 786440 | tf_op jit(solution)/shard_map/ppermute | solution.py:337
  6.7 0.9 %copy-done.1 = f32[256,128]{1,0:T(8,128)S(1)} copy-done((f32[256,128]{1,0:T(8,128)S(1)}, f32[256,128]{1,0:T(8,128)}, u32[]{:S(2)}) %copy-start.1) | copy-done | bytes 131096
  7.6 0.1 shard_map.41
  7.8 0.1 collective-permute-start.9
  7.8 2.5 %collective-permute-start.4 = (bf16[256,256]{1,0:T(8,128)(2,1)S(1)}, bf16[256,256]{1,0:T(8,128)(2,1)S(1)}, u32[]{:S(2)}, u32[]{:S(2)}) collective-permute-start(bf16[256,256]{1,0:T(8,128)(2,1)S(1)} %get-tuple-element.43.refs_0_.own), channel_id=1, source_target_pairs={{0,6},{1,7},{2,4},{3,5},{4,2},{5,3},{6,0},{7,1},{8,14},{9,15},{10,... | collective-permute-start | bytes 393224 | tf_op jit(solution)/shard_map/ppermute | solution.py:330
  10.4 0.5 collective-permute-start.3
  10.9 0.5 collective-permute-start.2
  11.4 1.6 %copy-done = bf16[2048,512]{1,0:T(8,128)(2,1)S(1)} copy-done((bf16[2048,512]{1,0:T(8,128)(2,1)S(1)}, bf16[2048,512]{1,0:T(8,128)(2,1)}, u32[]{:S(2)}) %copy-start) | copy-done | bytes 2097176
  13.0 0.9 %shard_map.42 = (bf16[256,2048]{1,0:T(8,128)(2,1)S(1)}, bf16[256,2048]{1,0:T(8,128)(2,1)S(1)}) custom-call(s32[1]{0:T(128)} %bitcast.column_ref, bf16[256,512]{1,0:T(8,128)(2,1)S(1)} %constant_dynamic-slice_fusion.rows.rows_ref, bf16[2048,512]{1,0:T(8,128)(2,1)S(1)} %copy-done), custom_call_target="tpu_custom_call" | custom-call | flops 536870912 | bytes 4456452 | tf_op jit(solution)/shard_map/pallas_call | solution.py:33
  13.9 3.9 %collective-permute-done.1.rows_ref = bf16[256,512]{1,0:T(8,128)(2,1)S(1)} collective-permute-done((bf16[256,512]{1,0:T(8,128)(2,1)S(1)}, bf16[256,512]{1,0:T(8,128)(2,1)S(1)}, u32[]{:S(2)}, u32[]{:S(2)}) %collective-permute-start.1) | collective-permute-done | bytes 262176 | tf_op jit(solution)/shard_map/ppermute | solution.py:337
  17.7 0.0 collective-permute-start
  17.7 0.9 %shard_map.43 = (bf16[256,2048]{1,0:T(8,128)(2,1)S(1)}, bf16[256,2048]{1,0:T(8,128)(2,1)S(1)}) custom-call(s32[1]{0:T(128)} %bitcast.column_ref, bf16[256,512]{1,0:T(8,128)(2,1)S(1)} %collective-permute-done.1.rows_ref, bf16[2048,512]{1,0:T(8,128)(2,1)S(1)} %copy-done, bf16[256,2048]{1,0:T(8,128)(2,1)S(1)} %get-tuple-element.40.refs_0_.refs_8_.refs_1_), custom_call_target="tpu_custom_call" | custom-call | flops 1449132032 | bytes 5505028 | tf_op jit(solution)/shard_map/pallas_call | solution.py:33
  18.6 0.1 collective-permute-start.5
  18.7 0.0 collective-permute-done.3.refs_2_
  18.7 0.5 collective-permute-start.8
  19.2 0.1 collective-permute-start.7
  19.3 4.8 %collective-permute-done.9.rows_ref.refs_3_ = bf16[256,768]{1,0:T(8,128)(2,1)S(1)} collective-permute-done((bf16[256,768]{1,0:T(8,128)(2,1)S(1)}, bf16[256,768]{1,0:T(8,128)(2,1)S(1)}, u32[]{:S(2)}, u32[]{:S(2)}) %collective-permute-start.9) | collective-permute-done | bytes 393248 | tf_op jit(solution)/shard_map/ppermute | solution.py:337
  24.1 0.9 %shard_map.44 = (bf16[256,2048]{1,0:T(8,128)(2,1)S(1)}, bf16[256,2048]{1,0:T(8,128)(2,1)S(1)}) custom-call(s32[1]{0:T(128)} %bitcast.column_ref, bf16[256,768]{1,0:T(8,128)(2,1)S(1)} %collective-permute-done.9.rows_ref.refs_3_, bf16[2048,512]{1,0:T(8,128)(2,1)S(1)} %copy-done, bf16[256,2048]{1,0:T(8,128)(2,1)S(1)} %get-tuple-element.41.refs_0_.refs_12_.refs_1_.refs_5_), custom_call_target="tpu_custom_call" | custom-call | flops 1449132032 | bytes 5636100 | tf_op jit(solution)/shard_map/pallas_call | solution.py:33
  25.0 0.4 collective-permute-done.6.refs_5_
  25.4 1.8 %shard_map.45 = (f32[256,128]{1,0:T(8,128)S(1)}, f32[272,128]{1,0:T(8,128)S(1)}, f32[272,128]{1,0:T(8,128)S(1)}) custom-call(bf16[256,256]{1,0:T(8,128)(2,1)S(1)} %get-tuple-element.43.refs_0_.own, bf16[256,256]{1,0:T(8,128)(2,1)S(1)} %collective-permute-done.2.refs_1_, bf16[256,256]{1,0:T(8,128)(2,1)S(1)} %collective-permute-done.3.refs_2_, ...), custom_call_target="tpu_custom_call" | custom-call | tf_op jit(solution)/shard_map/pallas_call | solution.py:33
  27.2 0.1 shard_map.46.refs_3_.refs_0_
  27.3 0.8 %shard_map.47 = (f32[1024,128]{1,0:T(8,128)S(1)}, f32[1032,128]{1,0:T(8,128)S(1)}) custom-call(bf16[272,256]{1,0:T(8,128)(2,1)S(1)} %collective-permute-done.refs_4_.refs_0_, bf16[256,2048]{1,0:T(8,128)(2,1)S(1)} %get-tuple-element.41.refs_0_.refs_12_.refs_1_.refs_5_, bf16[256,2048]{1,0:T(8,128)(2,1)S(1)} %get-tuple-element.42.refs_13_.refs_2_.refs_6_, ...), custom_call_target="tpu_custom_call" | custom-call | flops 402653184 | bytes 3293184 | tf_op jit(solution)/shard_map/pallas_call | solution.py:33
  28.1 0.2 collective-permute-start.10
  28.4 0.3 collective-permute-start.11
  28.6 1.1 %collective-permute-start.12 = (f32[272,128]{1,0:T(8,128)S(1)}, f32[272,128]{1,0:T(8,128)S(1)}, u32[]{:S(2)}, u32[]{:S(2)}) collective-permute-start(f32[272,128]{1,0:T(8,128)S(1)} %get-tuple-element.50.refs_2_), channel_id=1, source_target_pairs={{24,0},{0,16},{16,8},{8,24},{25,1},{1,17},{17,9},{9,25},{26,2},{2,... | collective-permute-start | bytes 417800 | tf_op jit(solution)/shard_map/ppermute | solution.py:337
  29.7 0.4 collective-permute-done.10.received
  30.1 0.1 shard_map.48
  30.2 1.8 %collective-permute-start.13 = (f32[264,128]{1,0:T(8,128)S(1)}, f32[264,128]{1,0:T(8,128)S(1)}, u32[]{:S(2)}, u32[]{:S(2)}) collective-permute-start(f32[264,128]{1,0:T(8,128)S(1)} %get-tuple-element.54), channel_id=1, source_target_pairs={{0,2},{1,3},{2,0},{3,1},{4,6},{5,7},{6,4},{7,5},{8,10},{9,11},{10,... | collective-permute-start | bytes 405512 | tf_op jit(solution)/shard_map/ppermute | solution.py:330
  32.0 1.5 %collective-permute-start.14 = (f32[264,128]{1,0:T(8,128)S(1)}, f32[264,128]{1,0:T(8,128)S(1)}, u32[]{:S(2)}, u32[]{:S(2)}) collective-permute-start(f32[264,128]{1,0:T(8,128)S(1)} %get-tuple-element.55), channel_id=1, source_target_pairs={{0,4},{1,5},{2,6},{3,7},{4,0},{5,1},{6,2},{7,3},{8,12},{9,13},{10,... | collective-permute-start | bytes 405512 | tf_op jit(solution)/shard_map/ppermute | solution.py:330
  33.5 0.2 collective-permute-start.15
  33.7 3.5 %collective-permute-done.11.refs_2_ = f32[272,128]{1,0:T(8,128)S(1)} collective-permute-done((f32[272,128]{1,0:T(8,128)S(1)}, f32[272,128]{1,0:T(8,128)S(1)}, u32[]{:S(2)}, u32[]{:S(2)}) %collective-permute-start.11) | collective-permute-done | bytes 139296 | tf_op jit(solution)/shard_map/ppermute | solution.py:337
  37.3 3.0 %collective-permute-done.14.refs_5_ = f32[264,128]{1,0:T(8,128)S(1)} collective-permute-done((f32[264,128]{1,0:T(8,128)S(1)}, f32[264,128]{1,0:T(8,128)S(1)}, u32[]{:S(2)}, u32[]{:S(2)}) %collective-permute-start.14) | collective-permute-done | bytes 135200 | tf_op jit(solution)/shard_map/ppermute | solution.py:330
  40.3 0.1 shard_map.49
  40.4 1.4 %collective-permute-start.16 = (f32[8,128]{1,0:T(8,128)S(1)}, f32[8,128]{1,0:T(8,128)S(1)}, u32[]{:S(2)}, u32[]{:S(2)}) collective-permute-start(f32[8,128]{1,0:T(8,128)S(1)} %get-tuple-element.57.refs_0_), channel_id=1, source_target_pairs={{24,0},{0,16},{16,8},{8,24},{25,1},{1,17},{17,9},{9,25},{26,2},{2,... | collective-permute-start | bytes 12296 | tf_op jit(solution)/shard_map/ppermute | solution.py:337
  41.8 2.4 %collective-permute-start.21 = (f32[264,128]{1,0:T(8,128)S(1)}, f32[264,128]{1,0:T(8,128)S(1)}, u32[]{:S(2)}, u32[]{:S(2)}) collective-permute-start(f32[264,128]{1,0:T(8,128)S(1)} %get-tuple-element.59), channel_id=1, source_target_pairs={{16,0},{8,16},{24,8},{0,24},{17,1},{9,17},{25,9},{1,25},{18,2},{10... | collective-permute-start | bytes 405512 | tf_op jit(solution)/shard_map/ppermute | solution.py:337
  44.2 1.5 %collective-permute-start.19 = (f32[256,128]{1,0:T(8,128)S(1)}, f32[256,128]{1,0:T(8,128)S(1)}, u32[]{:S(2)}, u32[]{:S(2)}) collective-permute-start(f32[256,128]{1,0:T(8,128)S(1)} %get-tuple-element.58.refs_2_), channel_id=1, source_target_pairs={{0,6},{1,7},{2,4},{3,5},{4,2},{5,3},{6,0},{7,1},{8,14},{9,15},{10,... | collective-permute-start | bytes 393224 | tf_op jit(solution)/shard_map/ppermute | solution.py:330
  45.7 1.2 %collective-permute-start.18 = (f32[256,128]{1,0:T(8,128)S(1)}, f32[256,128]{1,0:T(8,128)S(1)}, u32[]{:S(2)}, u32[]{:S(2)}) collective-permute-start(f32[256,128]{1,0:T(8,128)S(1)} %get-tuple-element.58.refs_2_), channel_id=1, source_target_pairs={{0,4},{1,5},{2,6},{3,7},{4,0},{5,1},{6,2},{7,3},{8,12},{9,13},{10,... | collective-permute-start | bytes 393224 | tf_op jit(solution)/shard_map/ppermute | solution.py:330
  46.9 0.8 %collective-permute-start.17 = (f32[256,128]{1,0:T(8,128)S(1)}, f32[256,128]{1,0:T(8,128)S(1)}, u32[]{:S(2)}, u32[]{:S(2)}) collective-permute-start(f32[256,128]{1,0:T(8,128)S(1)} %get-tuple-element.58.refs_2_), channel_id=1, source_target_pairs={{0,2},{1,3},{2,0},{3,1},{4,6},{5,7},{6,4},{7,5},{8,10},{9,11},{10,... | collective-permute-start | bytes 393224 | tf_op jit(solution)/shard_map/ppermute | solution.py:330
  47.7 2.9 %collective-permute-done.19.refs_5_ = f32[256,128]{1,0:T(8,128)S(1)} collective-permute-done((f32[256,128]{1,0:T(8,128)S(1)}, f32[256,128]{1,0:T(8,128)S(1)}, u32[]{:S(2)}, u32[]{:S(2)}) %collective-permute-start.19) | collective-permute-done | bytes 131104 | tf_op jit(solution)/shard_map/ppermute | solution.py:330
  50.6 1.2 %collective-permute-done.18.refs_4_ = f32[256,128]{1,0:T(8,128)S(1)} collective-permute-done((f32[256,128]{1,0:T(8,128)S(1)}, f32[256,128]{1,0:T(8,128)S(1)}, u32[]{:S(2)}, u32[]{:S(2)}) %collective-permute-start.18) | collective-permute-done | bytes 131104 | tf_op jit(solution)/shard_map/ppermute | solution.py:330
  51.8 0.2 collective-permute-done.17.refs_3_
  52.0 1.1 %shard_map.50 = (bf16[1024,256]{1,0:T(8,128)(2,1)S(1)}, bf16[256,256]{1,0:T(8,128)(2,1)S(1)}, bf16[256,256]{1,0:T(8,128)(2,1)S(1)}) custom-call(f32[8,128]{1,0:T(8,128)S(1)} %get-tuple-element.57.refs_0_, f32[8,128]{1,0:T(8,128)S(1)} %collective-permute-done.16.refs_1_, f32[256,128]{1,0:T(8,128)S(1)} %get-tuple-element.58.refs_2_, ...), custom_call_target="tpu_custom_call" | custom-call | bytes 1589248 | tf_op jit(solution)/shard_map/pallas_call | solution.py:33
  53.1 0.1 collective-permute-start.23
  53.2 0.8 %shard_map.51 = (f32[1024,128]{1,0:T(8,128)S(1)}, f32[1024,128]{1,0:T(8,128)S(1)}) custom-call(bf16[256,256]{1,0:T(8,128)(2,1)S(1)} %get-tuple-element.60.refs_0_.refs_12_, bf16[256,2048]{1,0:T(8,128)(2,1)S(1)} %get-tuple-element.41.refs_0_.refs_12_.refs_1_.refs_5_, bf16[256,2048]{1,0:T(8,128)(2,1)S(1)} %get-tuple-element.42.refs_13_.refs_2_.refs_6_), custom_call_target="tpu_custom_call" | custom-call | flops 402653184 | bytes 3276800 | tf_op jit(solution)/shard_map/pallas_call | solution.py:33
  54.0 0.6 collective-permute-start.22
  54.5 1.0 %shard_map.52 = (f32[256,128]{1,0:T(8,128)S(1)}, f32[272,128]{1,0:T(8,128)S(1)}, f32[272,128]{1,0:T(8,128)S(1)}) custom-call(bf16[1024,256]{1,0:T(8,128)(2,1)S(1)} %get-tuple-element.63.refs_0_.refs_10_, bf16[256,2048]{1,0:T(8,128)(2,1)S(1)} %get-tuple-element.40.refs_0_.refs_8_.refs_1_, bf16[256,2048]{1,0:T(8,128)(2,1)S(1)} %get-tuple-element.44.refs_9_.refs_2_, ...), custom_call_target="tpu_custom_call" | custom-call | flops 603979776 | bytes 7225344 | tf_op jit(solution)/shard_map/pallas_call | solution.py:33
  55.6 1.0 %shard_map.53 = (f32[256,128]{1,0:T(8,128)S(1)}, f32[288,128]{1,0:T(8,128)S(1)}, f32[288,128]{1,0:T(8,128)S(1)}, f32[8,128]{1,0:T(8,128)S(1)}) custom-call(bf16[1024,256]{1,0:T(8,128)(2,1)S(1)} %collective-permute-done.23.refs_0_, bf16[256,2048]{1,0:T(8,128)(2,1)S(1)} %get-tuple-element.40.refs_0_.refs_8_.refs_1_, ...), custom_call_target="tpu_custom_call" | custom-call | flops 603979776 | bytes 8441856 | tf_op jit(solution)/shard_map/pallas_call | solution.py:33
  56.6 1.6 %collective-permute-start.26 = (f32[8,128]{1,0:T(8,128)S(1)}, f32[8,128]{1,0:T(8,128)S(1)}, u32[]{:S(2)}, u32[]{:S(2)}) collective-permute-start(f32[8,128]{1,0:T(8,128)S(1)} %get-tuple-element.68), channel_id=1, source_target_pairs={{24,0},{0,16},{16,8},{8,24},{25,1},{1,17},{17,9},{9,25},{26,2},{2,... | collective-permute-start | bytes 12296 | tf_op jit(solution)/shard_map/ppermute | solution.py:337
  58.2 0.8 %collective-permute-start.25 = (f32[8,128]{1,0:T(8,128)S(1)}, f32[8,128]{1,0:T(8,128)S(1)}, u32[]{:S(2)}, u32[]{:S(2)}) collective-permute-start(f32[8,128]{1,0:T(8,128)S(1)} %get-tuple-element.68), channel_id=1, source_target_pairs={{8,0},{24,16},{0,8},{16,24},{9,1},{25,17},{1,9},{17,25},{10,2},{26... | collective-permute-start | bytes 12296 | tf_op jit(solution)/shard_map/ppermute | solution.py:337
  59.1 2.4 %collective-permute-start.24 = (f32[8,128]{1,0:T(8,128)S(1)}, f32[8,128]{1,0:T(8,128)S(1)}, u32[]{:S(2)}, u32[]{:S(2)}) collective-permute-start(f32[8,128]{1,0:T(8,128)S(1)} %get-tuple-element.68), channel_id=1, source_target_pairs={{16,0},{8,16},{24,8},{0,24},{17,1},{9,17},{25,9},{1,25},{18,2},{10... | collective-permute-start | bytes 12296 | tf_op jit(solution)/shard_map/ppermute | solution.py:337
  61.5 0.1 collective-permute-start.28
  61.6 0.5 collective-permute-done.26
  62.1 1.1 %collective-permute-start.29 = (f32[288,128]{1,0:T(8,128)S(1)}, f32[288,128]{1,0:T(8,128)S(1)}, u32[]{:S(2)}, u32[]{:S(2)}) collective-permute-start(f32[288,128]{1,0:T(8,128)S(1)} %get-tuple-element.72), channel_id=1, source_target_pairs={{24,0},{0,16},{16,8},{8,24},{25,1},{1,17},{17,9},{9,25},{26,2},{2,... | collective-permute-start | bytes 442376 | tf_op jit(solution)/shard_map/ppermute | solution.py:337
  63.2 0.5 collective-permute-done.24
  63.7 1.2 %collective-permute-done.27.refs_1_ = f32[8,128]{1,0:T(8,128)S(1)} collective-permute-done((f32[8,128]{1,0:T(8,128)S(1)}, f32[8,128]{1,0:T(8,128)S(1)}, u32[]{:S(2)}, u32[]{:S(2)}) %collective-permute-start.27) | collective-permute-done | bytes 4128 | tf_op jit(solution)/shard_map/ppermute | solution.py:330
  64.8 0.1 shard_map.54
  64.9 0.9 %collective-permute-start.30 = (f32[264,128]{1,0:T(8,128)S(1)}, f32[264,128]{1,0:T(8,128)S(1)}, u32[]{:S(2)}, u32[]{:S(2)}) collective-permute-start(f32[264,128]{1,0:T(8,128)S(1)} %get-tuple-element.73), channel_id=1, source_target_pairs={{0,2},{1,3},{2,0},{3,1},{4,6},{5,7},{6,4},{7,5},{8,10},{9,11},{10,... | collective-permute-start | bytes 405512 | tf_op jit(solution)/shard_map/ppermute | solution.py:330
  65.8 1.5 %collective-permute-start.31 = (f32[264,128]{1,0:T(8,128)S(1)}, f32[264,128]{1,0:T(8,128)S(1)}, u32[]{:S(2)}, u32[]{:S(2)}) collective-permute-start(f32[264,128]{1,0:T(8,128)S(1)} %get-tuple-element.74), channel_id=1, source_target_pairs={{0,4},{1,5},{2,6},{3,7},{4,0},{5,1},{6,2},{7,3},{8,12},{9,13},{10,... | collective-permute-start | bytes 405512 | tf_op jit(solution)/shard_map/ppermute | solution.py:330
  67.3 1.2 %collective-permute-start.32 = (f32[264,128]{1,0:T(8,128)S(1)}, f32[264,128]{1,0:T(8,128)S(1)}, u32[]{:S(2)}, u32[]{:S(2)}) collective-permute-start(f32[264,128]{1,0:T(8,128)S(1)} %get-tuple-element.75), channel_id=1, source_target_pairs={{0,6},{1,7},{2,4},{3,5},{4,2},{5,3},{6,0},{7,1},{8,14},{9,15},{10,... | collective-permute-start | bytes 405512 | tf_op jit(solution)/shard_map/ppermute | solution.py:330
  68.5 2.9 %collective-permute-done.30.refs_4_ = f32[264,128]{1,0:T(8,128)S(1)} collective-permute-done((f32[264,128]{1,0:T(8,128)S(1)}, f32[264,128]{1,0:T(8,128)S(1)}, u32[]{:S(2)}, u32[]{:S(2)}) %collective-permute-start.30) | collective-permute-done | bytes 135200 | tf_op jit(solution)/shard_map/ppermute | solution.py:330
  71.4 1.7 %collective-permute-done.31.refs_5_ = f32[264,128]{1,0:T(8,128)S(1)} collective-permute-done((f32[264,128]{1,0:T(8,128)S(1)}, f32[264,128]{1,0:T(8,128)S(1)}, u32[]{:S(2)}, u32[]{:S(2)}) %collective-permute-start.31) | collective-permute-done | bytes 135200 | tf_op jit(solution)/shard_map/ppermute | solution.py:330
  73.1 1.0 %collective-permute-done.32.refs_6_ = f32[264,128]{1,0:T(8,128)S(1)} collective-permute-done((f32[264,128]{1,0:T(8,128)S(1)}, f32[264,128]{1,0:T(8,128)S(1)}, u32[]{:S(2)}, u32[]{:S(2)}) %collective-permute-start.32) | collective-permute-done | bytes 135200 | tf_op jit(solution)/shard_map/ppermute | solution.py:330
  74.1 1.0 %shard_map.55 = (f32[256,128]{1,0:T(8,128)}, f32[256,128]{1,0:T(8,128)}) custom-call(f32[264,128]{1,0:T(8,128)S(1)} %get-tuple-element.69.refs_0_, f32[256,128]{1,0:T(8,128)S(1)} %get-tuple-element.70.refs_1_, f32[288,128]{1,0:T(8,128)S(1)} %collective-permute-done.28.refs_2_, f32[288,128]{1,0:T(8,128)S(1)} %collective-permute-done.29.refs_3_, ...), custom_call_target="tpu_custom_call" | custom-call | bytes 1228800 | tf_op jit(solution)/shard_map/pallas_call | solution.py:33
  (23 shorter events, 0.1 us)
Async XLA Ops:
  1.6 16.1 %collective-permute-start.1 = (bf16[256,512]{1,0:T(8,128)(2,1)S(1)}, bf16[256,512]{1,0:T(8,128)(2,1)S(1)}, u32[]{:S(2)}, u32[]{:S(2)}) collective-permute-start(bf16[256,512]{1,0:T(8,128)(2,1)S(1)} %constant_dynamic-slice_fusion.rows.rows_ref), channel_id=1, source_target_pairs={{16,0},{8,16},{24,8},{0,24},{17,1},{9,17},{25,9},{1,25},{18,2},{10... | collective-permute-start | bytes 786440 | tf_op jit(solution)/shard_map/ppermute | solution.py:337
  6.7 0.9 %copy-start.1 = (f32[256,128]{1,0:T(8,128)S(1)}, f32[256,128]{1,0:T(8,128)}, u32[]{:S(2)}) copy-start(f32[256,128]{1,0:T(8,128)} %logits.1) | copy-start | bytes 393220
  7.8 16.3 %collective-permute-start.9 = (bf16[256,768]{1,0:T(8,128)(2,1)S(1)}, bf16[256,768]{1,0:T(8,128)(2,1)S(1)}, u32[]{:S(2)}, u32[]{:S(2)}) collective-permute-start(bf16[256,768]{1,0:T(8,128)(2,1)S(1)} %get-tuple-element.45), channel_id=1, source_target_pairs={{0,8},{8,0},{16,24},{24,16},{1,9},{9,1},{17,25},{25,17},{2,10},{10... | collective-permute-start | bytes 1179656 | tf_op jit(solution)/shard_map/ppermute | solution.py:337
  7.8 10.8 %collective-permute-start.4 = (bf16[256,256]{1,0:T(8,128)(2,1)S(1)}, bf16[256,256]{1,0:T(8,128)(2,1)S(1)}, u32[]{:S(2)}, u32[]{:S(2)}) collective-permute-start(bf16[256,256]{1,0:T(8,128)(2,1)S(1)} %get-tuple-element.43.refs_0_.own), channel_id=1, source_target_pairs={{0,6},{1,7},{2,4},{3,5},{4,2},{5,3},{6,0},{7,1},{8,14},{9,15},{10,... | collective-permute-start | bytes 393224 | tf_op jit(solution)/shard_map/ppermute | solution.py:330
  10.4 8.4 %collective-permute-start.3 = (bf16[256,256]{1,0:T(8,128)(2,1)S(1)}, bf16[256,256]{1,0:T(8,128)(2,1)S(1)}, u32[]{:S(2)}, u32[]{:S(2)}) collective-permute-start(bf16[256,256]{1,0:T(8,128)(2,1)S(1)} %get-tuple-element.43.refs_0_.own), channel_id=1, source_target_pairs={{0,4},{1,5},{2,6},{3,7},{4,0},{5,1},{6,2},{7,3},{8,12},{9,13},{10,... | collective-permute-start | bytes 393224 | tf_op jit(solution)/shard_map/ppermute | solution.py:330
  10.9 8.4 %collective-permute-start.2 = (bf16[256,256]{1,0:T(8,128)(2,1)S(1)}, bf16[256,256]{1,0:T(8,128)(2,1)S(1)}, u32[]{:S(2)}, u32[]{:S(2)}) collective-permute-start(bf16[256,256]{1,0:T(8,128)(2,1)S(1)} %get-tuple-element.43.refs_0_.own), channel_id=1, source_target_pairs={{0,2},{1,3},{2,0},{3,1},{4,6},{5,7},{6,4},{7,5},{8,10},{9,11},{10,... | collective-permute-start | bytes 393224 | tf_op jit(solution)/shard_map/ppermute | solution.py:330
  11.4 1.6 %copy-start = (bf16[2048,512]{1,0:T(8,128)(2,1)S(1)}, bf16[2048,512]{1,0:T(8,128)(2,1)}, u32[]{:S(2)}) copy-start(bf16[2048,512]{1,0:T(8,128)(2,1)} %plane_ref.5) | copy-start | bytes 6291460
  17.7 9.5 %collective-permute-start = (bf16[272,256]{1,0:T(8,128)(2,1)S(1)}, bf16[272,256]{1,0:T(8,128)(2,1)S(1)}, u32[]{:S(2)}, u32[]{:S(2)}) collective-permute-start(bf16[272,256]{1,0:T(8,128)(2,1)S(1)} %get-tuple-element.39), channel_id=1, source_target_pairs={{16,0},{8,16},{24,8},{0,24},{17,1},{9,17},{25,9},{1,25},{18,2},{10... | collective-permute-start | bytes 417800 | tf_op jit(solution)/shard_map/ppermute | solution.py:337
  18.6 6.3 %collective-permute-start.5 = (bf16[256,256]{1,0:T(8,128)(2,1)S(1)}, bf16[256,256]{1,0:T(8,128)(2,1)S(1)}, u32[]{:S(2)}, u32[]{:S(2)}) collective-permute-start(bf16[256,256]{1,0:T(8,128)(2,1)S(1)} %get-tuple-element.43.refs_0_.own), channel_id=1, source_target_pairs={{0,1},{1,0},{2,3},{3,2},{4,5},{5,4},{6,7},{7,6},{8,9},{9,8},{10,11... | collective-permute-start | bytes 393224 | tf_op jit(solution)/shard_map/ppermute | solution.py:330
  18.7 6.2 %collective-permute-start.8 = (bf16[256,256]{1,0:T(8,128)(2,1)S(1)}, bf16[256,256]{1,0:T(8,128)(2,1)S(1)}, u32[]{:S(2)}, u32[]{:S(2)}) collective-permute-start(bf16[256,256]{1,0:T(8,128)(2,1)S(1)} %collective-permute-done.4.refs_3_), channel_id=1, source_target_pairs={{0,1},{1,0},{2,3},{3,2},{4,5},{5,4},{6,7},{7,6},{8,9},{9,8},{10,11... | collective-permute-start | bytes 393224 | tf_op jit(solution)/shard_map/ppermute | solution.py:330
  19.2 5.7 %collective-permute-start.7 = (bf16[256,256]{1,0:T(8,128)(2,1)S(1)}, bf16[256,256]{1,0:T(8,128)(2,1)S(1)}, u32[]{:S(2)}, u32[]{:S(2)}) collective-permute-start(bf16[256,256]{1,0:T(8,128)(2,1)S(1)} %collective-permute-done.3.refs_2_), channel_id=1, source_target_pairs={{0,1},{1,0},{2,3},{3,2},{4,5},{5,4},{6,7},{7,6},{8,9},{9,8},{10,11... | collective-permute-start | bytes 393224 | tf_op jit(solution)/shard_map/ppermute | solution.py:330
  24.1 1.3 %collective-permute-start.6 = (bf16[256,256]{1,0:T(8,128)(2,1)S(1)}, bf16[256,256]{1,0:T(8,128)(2,1)S(1)}, u32[]{:S(2)}, u32[]{:S(2)}) collective-permute-start(bf16[256,256]{1,0:T(8,128)(2,1)S(1)} %collective-permute-done.2.refs_1_), channel_id=1, source_target_pairs={{0,1},{1,0},{2,3},{3,2},{4,5},{5,4},{6,7},{7,6},{8,9},{9,8},{10,11... | collective-permute-start | bytes 393224 | tf_op jit(solution)/shard_map/ppermute | solution.py:330
  28.1 2.0 %collective-permute-start.10 = (f32[1032,128]{1,0:T(8,128)S(1)}, f32[1032,128]{1,0:T(8,128)S(1)}, u32[]{:S(2)}, u32[]{:S(2)}) collective-permute-start(f32[1032,128]{1,0:T(8,128)S(1)} %get-tuple-element.52), channel_id=1, source_target_pairs={{0,1},{1,0},{2,3},{3,2},{4,5},{5,4},{6,7},{7,6},{8,9},{9,8},{10,11... | collective-permute-start | bytes 1585160 | tf_op jit(solution)/shard_map/ppermute | solution.py:330
  28.4 8.9 %collective-permute-start.11 = (f32[272,128]{1,0:T(8,128)S(1)}, f32[272,128]{1,0:T(8,128)S(1)}, u32[]{:S(2)}, u32[]{:S(2)}) collective-permute-start(f32[272,128]{1,0:T(8,128)S(1)} %get-tuple-element.49.refs_1_), channel_id=1, source_target_pairs={{0,8},{8,0},{16,24},{24,16},{1,9},{9,1},{17,25},{25,17},{2,10},{10... | collective-permute-start | bytes 417800 | tf_op jit(solution)/shard_map/ppermute | solution.py:337
  28.6 8.6 %collective-permute-start.12 = (f32[272,128]{1,0:T(8,128)S(1)}, f32[272,128]{1,0:T(8,128)S(1)}, u32[]{:S(2)}, u32[]{:S(2)}) collective-permute-start(f32[272,128]{1,0:T(8,128)S(1)} %get-tuple-element.50.refs_2_), channel_id=1, source_target_pairs={{24,0},{0,16},{16,8},{8,24},{25,1},{1,17},{17,9},{9,25},{26,2},{2,... | collective-permute-start | bytes 417800 | tf_op jit(solution)/shard_map/ppermute | solution.py:337
  30.2 7.1 %collective-permute-start.13 = (f32[264,128]{1,0:T(8,128)S(1)}, f32[264,128]{1,0:T(8,128)S(1)}, u32[]{:S(2)}, u32[]{:S(2)}) collective-permute-start(f32[264,128]{1,0:T(8,128)S(1)} %get-tuple-element.54), channel_id=1, source_target_pairs={{0,2},{1,3},{2,0},{3,1},{4,6},{5,7},{6,4},{7,5},{8,10},{9,11},{10,... | collective-permute-start | bytes 405512 | tf_op jit(solution)/shard_map/ppermute | solution.py:330
  32.0 8.3 %collective-permute-start.14 = (f32[264,128]{1,0:T(8,128)S(1)}, f32[264,128]{1,0:T(8,128)S(1)}, u32[]{:S(2)}, u32[]{:S(2)}) collective-permute-start(f32[264,128]{1,0:T(8,128)S(1)} %get-tuple-element.55), channel_id=1, source_target_pairs={{0,4},{1,5},{2,6},{3,7},{4,0},{5,1},{6,2},{7,3},{8,12},{9,13},{10,... | collective-permute-start | bytes 405512 | tf_op jit(solution)/shard_map/ppermute | solution.py:330
  33.5 6.7 %collective-permute-start.15 = (f32[264,128]{1,0:T(8,128)S(1)}, f32[264,128]{1,0:T(8,128)S(1)}, u32[]{:S(2)}, u32[]{:S(2)}) collective-permute-start(f32[264,128]{1,0:T(8,128)S(1)} %get-tuple-element.56), channel_id=1, source_target_pairs={{0,6},{1,7},{2,4},{3,5},{4,2},{5,3},{6,0},{7,1},{8,14},{9,15},{10,... | collective-permute-start | bytes 405512 | tf_op jit(solution)/shard_map/ppermute | solution.py:330
  40.4 6.6 %collective-permute-start.16 = (f32[8,128]{1,0:T(8,128)S(1)}, f32[8,128]{1,0:T(8,128)S(1)}, u32[]{:S(2)}, u32[]{:S(2)}) collective-permute-start(f32[8,128]{1,0:T(8,128)S(1)} %get-tuple-element.57.refs_0_), channel_id=1, source_target_pairs={{24,0},{0,16},{16,8},{8,24},{25,1},{1,17},{17,9},{9,25},{26,2},{2,... | collective-permute-start | bytes 12296 | tf_op jit(solution)/shard_map/ppermute | solution.py:337
  41.8 10.2 %collective-permute-start.21 = (f32[264,128]{1,0:T(8,128)S(1)}, f32[264,128]{1,0:T(8,128)S(1)}, u32[]{:S(2)}, u32[]{:S(2)}) collective-permute-start(f32[264,128]{1,0:T(8,128)S(1)} %get-tuple-element.59), channel_id=1, source_target_pairs={{16,0},{8,16},{24,8},{0,24},{17,1},{9,17},{25,9},{1,25},{18,2},{10... | collective-permute-start | bytes 405512 | tf_op jit(solution)/shard_map/ppermute | solution.py:337
  44.2 7.8 %collective-permute-start.20 = (f32[264,128]{1,0:T(8,128)S(1)}, f32[264,128]{1,0:T(8,128)S(1)}, u32[]{:S(2)}, u32[]{:S(2)}) collective-permute-start(f32[264,128]{1,0:T(8,128)S(1)} %get-tuple-element.59), channel_id=1, source_target_pairs={{0,8},{8,0},{16,24},{24,16},{1,9},{9,1},{17,25},{25,17},{2,10},{10... | collective-permute-start | bytes 405512 | tf_op jit(solution)/shard_map/ppermute | solution.py:337
  44.2 6.3 %collective-permute-start.19 = (f32[256,128]{1,0:T(8,128)S(1)}, f32[256,128]{1,0:T(8,128)S(1)}, u32[]{:S(2)}, u32[]{:S(2)}) collective-permute-start(f32[256,128]{1,0:T(8,128)S(1)} %get-tuple-element.58.refs_2_), channel_id=1, source_target_pairs={{0,6},{1,7},{2,4},{3,5},{4,2},{5,3},{6,0},{7,1},{8,14},{9,15},{10,... | collective-permute-start | bytes 393224 | tf_op jit(solution)/shard_map/ppermute | solution.py:330
  45.7 6.1 %collective-permute-start.18 = (f32[256,128]{1,0:T(8,128)S(1)}, f32[256,128]{1,0:T(8,128)S(1)}, u32[]{:S(2)}, u32[]{:S(2)}) collective-permute-start(f32[256,128]{1,0:T(8,128)S(1)} %get-tuple-element.58.refs_2_), channel_id=1, source_target_pairs={{0,4},{1,5},{2,6},{3,7},{4,0},{5,1},{6,2},{7,3},{8,12},{9,13},{10,... | collective-permute-start | bytes 393224 | tf_op jit(solution)/shard_map/ppermute | solution.py:330
  46.9 5.1 %collective-permute-start.17 = (f32[256,128]{1,0:T(8,128)S(1)}, f32[256,128]{1,0:T(8,128)S(1)}, u32[]{:S(2)}, u32[]{:S(2)}) collective-permute-start(f32[256,128]{1,0:T(8,128)S(1)} %get-tuple-element.58.refs_2_), channel_id=1, source_target_pairs={{0,2},{1,3},{2,0},{3,1},{4,6},{5,7},{6,4},{7,5},{8,10},{9,11},{10,... | collective-permute-start | bytes 393224 | tf_op jit(solution)/shard_map/ppermute | solution.py:330
  53.1 2.4 %collective-permute-start.23 = (bf16[1024,256]{1,0:T(8,128)(2,1)S(1)}, bf16[1024,256]{1,0:T(8,128)(2,1)S(1)}, u32[]{:S(2)}, u32[]{:S(2)}) collective-permute-start(bf16[1024,256]{1,0:T(8,128)(2,1)S(1)} %get-tuple-element.63.refs_0_.refs_10_), channel_id=1, source_target_pairs={{0,1},{1,0},{2,3},{3,2},{4,5},{5,4},{6,7},{7,6},{8,9},{9,8},{10,11... | collective-permute-start | bytes 1572872 | tf_op jit(solution)/shard_map/ppermute | solution.py:330
  54.0 9.7 %collective-permute-start.22 = (f32[1024,128]{1,0:T(8,128)S(1)}, f32[1024,128]{1,0:T(8,128)S(1)}, u32[]{:S(2)}, u32[]{:S(2)}) collective-permute-start(f32[1024,128]{1,0:T(8,128)S(1)} %get-tuple-element.62), channel_id=1, source_target_pairs={{0,1},{1,0},{2,3},{3,2},{4,5},{5,4},{6,7},{7,6},{8,9},{9,8},{10,11... | collective-permute-start | bytes 1572872 | tf_op jit(solution)/shard_map/ppermute | solution.py:330
  56.6 5.5 %collective-permute-start.26 = (f32[8,128]{1,0:T(8,128)S(1)}, f32[8,128]{1,0:T(8,128)S(1)}, u32[]{:S(2)}, u32[]{:S(2)}) collective-permute-start(f32[8,128]{1,0:T(8,128)S(1)} %get-tuple-element.68), channel_id=1, source_target_pairs={{24,0},{0,16},{16,8},{8,24},{25,1},{1,17},{17,9},{9,25},{26,2},{2,... | collective-permute-start | bytes 12296 | tf_op jit(solution)/shard_map/ppermute | solution.py:337
  58.2 5.0 %collective-permute-start.25 = (f32[8,128]{1,0:T(8,128)S(1)}, f32[8,128]{1,0:T(8,128)S(1)}, u32[]{:S(2)}, u32[]{:S(2)}) collective-permute-start(f32[8,128]{1,0:T(8,128)S(1)} %get-tuple-element.68), channel_id=1, source_target_pairs={{8,0},{24,16},{0,8},{16,24},{9,1},{25,17},{1,9},{17,25},{10,2},{26... | collective-permute-start | bytes 12296 | tf_op jit(solution)/shard_map/ppermute | solution.py:337
  59.1 4.6 %collective-permute-start.24 = (f32[8,128]{1,0:T(8,128)S(1)}, f32[8,128]{1,0:T(8,128)S(1)}, u32[]{:S(2)}, u32[]{:S(2)}) collective-permute-start(f32[8,128]{1,0:T(8,128)S(1)} %get-tuple-element.68), channel_id=1, source_target_pairs={{16,0},{8,16},{24,8},{0,24},{17,1},{9,17},{25,9},{1,25},{18,2},{10... | collective-permute-start | bytes 12296 | tf_op jit(solution)/shard_map/ppermute | solution.py:337
  61.5 12.6 %collective-permute-start.28 = (f32[288,128]{1,0:T(8,128)S(1)}, f32[288,128]{1,0:T(8,128)S(1)}, u32[]{:S(2)}, u32[]{:S(2)}) collective-permute-start(f32[288,128]{1,0:T(8,128)S(1)} %get-tuple-element.71), channel_id=1, source_target_pairs={{0,8},{8,0},{16,24},{24,16},{1,9},{9,1},{17,25},{25,17},{2,10},{10... | collective-permute-start | bytes 442376 | tf_op jit(solution)/shard_map/ppermute | solution.py:337
  62.1 12.1 %collective-permute-start.29 = (f32[288,128]{1,0:T(8,128)S(1)}, f32[288,128]{1,0:T(8,128)S(1)}, u32[]{:S(2)}, u32[]{:S(2)}) collective-permute-start(f32[288,128]{1,0:T(8,128)S(1)} %get-tuple-element.72), channel_id=1, source_target_pairs={{24,0},{0,16},{16,8},{8,24},{25,1},{1,17},{17,9},{9,25},{26,2},{2,... | collective-permute-start | bytes 442376 | tf_op jit(solution)/shard_map/ppermute | solution.py:337
  63.7 1.2 %collective-permute-start.27 = (f32[8,128]{1,0:T(8,128)S(1)}, f32[8,128]{1,0:T(8,128)S(1)}, u32[]{:S(2)}, u32[]{:S(2)}) collective-permute-start(f32[8,128]{1,0:T(8,128)S(1)} %add_add_fusion.refs_0_), channel_id=1, source_target_pairs={{0,1},{1,0},{2,3},{3,2},{4,5},{5,4},{6,7},{7,6},{8,9},{9,8},{10,11... | collective-permute-start | bytes 12296 | tf_op jit(solution)/shard_map/ppermute | solution.py:330
  64.9 6.5 %collective-permute-start.30 = (f32[264,128]{1,0:T(8,128)S(1)}, f32[264,128]{1,0:T(8,128)S(1)}, u32[]{:S(2)}, u32[]{:S(2)}) collective-permute-start(f32[264,128]{1,0:T(8,128)S(1)} %get-tuple-element.73), channel_id=1, source_target_pairs={{0,2},{1,3},{2,0},{3,1},{4,6},{5,7},{6,4},{7,5},{8,10},{9,11},{10,... | collective-permute-start | bytes 405512 | tf_op jit(solution)/shard_map/ppermute | solution.py:330
  65.8 7.3 %collective-permute-start.31 = (f32[264,128]{1,0:T(8,128)S(1)}, f32[264,128]{1,0:T(8,128)S(1)}, u32[]{:S(2)}, u32[]{:S(2)}) collective-permute-start(f32[264,128]{1,0:T(8,128)S(1)} %get-tuple-element.74), channel_id=1, source_target_pairs={{0,4},{1,5},{2,6},{3,7},{4,0},{5,1},{6,2},{7,3},{8,12},{9,13},{10,... | collective-permute-start | bytes 405512 | tf_op jit(solution)/shard_map/ppermute | solution.py:330
  67.3 6.8 %collective-permute-start.32 = (f32[264,128]{1,0:T(8,128)S(1)}, f32[264,128]{1,0:T(8,128)S(1)}, u32[]{:S(2)}, u32[]{:S(2)}) collective-permute-start(f32[264,128]{1,0:T(8,128)S(1)} %get-tuple-element.75), channel_id=1, source_target_pairs={{0,6},{1,7},{2,4},{3,5},{4,2},{5,3},{6,0},{7,1},{8,14},{9,15},{10,... | collective-permute-start | bytes 405512 | tf_op jit(solution)/shard_map/ppermute | solution.py:330

commit v12 on v11

--- a/solution.py
+++ b/solution.py
@@ -12,7 +12,7 @@
 GATHER_ROWS = (STAT_ROWS, 0)
 WIDE_ROWS = 16
 LAST_ROWS = 32
-BACK_ROWS = 16
+BACK_ROWS = 48
 VMEM_BYTES = 24 * 1024 * 1024
 CROSS_COST = 2.7
 VMEM = pl.BlockSpec(memory_space=pltpu.VMEM)

time: 75.3 us -> 75.3 us (level)
  no operation moved by 1% of the time
where the time goes in v12:
time: 75.3 us; the launch traced here: 75.1 us
  starting transfers between devices  32.2 us (43%)
  waiting for transfers between devices  28 us (37%)
  Pallas kernels  10.6 us (14%)
  local copies, waits for them, and re-layouts  3.47 us (5%)
  between operations  0.82 us (1%)
    ppermute x13, starting transfers between devices, shift(): return lax.ppermute(x, 'row', pairs)  16.5 us
    ppermute x20, starting transfers between devices, by_col(): return lax.ppermute(x, 'col', [(i, i ^ mask) for i in range(cols)])  15.6 us
    ppermute x20, waiting for transfers between devices, by_col(): return lax.ppermute(x, 'col', [(i, i ^ mask) for i in range(cols)])  14.2 us
    ppermute x13, waiting for transfers between devices, shift(): return lax.ppermute(x, 'row', pairs)  13.8 us
    pallas_call x15, Pallas kernels, call(): pl.pallas_call(body, in_specs=specs or [VMEM] * len(args), out_specs=[VME...  10.6 us
    unnamed x4, local copies, waits for them, and re-layouts  2.49 us
  transfers between devices with their start and end apart: 33, of which 15 were waited for; matrix products, arithmetic and copies ran while one was open for 0% of the time, Pallas kernels for 10%

profile of v12, /device:TPU:0, one launch (start us, length us, event | category | flops | bytes accessed | tf_op | source)
XLA Modules:
  0.0 75.1 jit_solution(341155133332536633)
XLA Ops:
  0.6 1.0 %constant_dynamic-slice_fusion.rows.rows_ref = bf16[256,512]{1,0:T(8,128)(2,1)S(1)} fusion(bf16[2048,512]{1,0:T(8,128)(2,1)} %plane_ref.5, s32[]{:T(128)S(6)} %select_n.3), kind=kLoop, calls=%fused_computation.1 | loop fusion | bytes 524292 | tf_op jit(solution)/shard_map/dynamic_slice | solution.py:340
  1.6 5.1 %collective-permute-start.1 = (bf16[256,512]{1,0:T(8,128)(2,1)S(1)}, bf16[256,512]{1,0:T(8,128)(2,1)S(1)}, u32[]{:S(2)}, u32[]{:S(2)}) collective-permute-start(bf16[256,512]{1,0:T(8,128)(2,1)S(1)} %constant_dynamic-slice_fusion.rows.rows_ref), channel_id=1, source_target_pairs={{16,0},{8,16},{24,8},{0,24},{17,1},{9,17},{25,9},{1,25},{18,2},{10... | collective-permute-start | bytes 786440 | tf_op jit(solution)/shard_map/ppermute | solution.py:337
  6.7 0.9 %copy-done.1 = f32[256,128]{1,0:T(8,128)S(1)} copy-done((f32[256,128]{1,0:T(8,128)S(1)}, f32[256,128]{1,0:T(8,128)}, u32[]{:S(2)}) %copy-start.1) | copy-done | bytes 131096
  7.6 0.1 shard_map.41
  7.8 0.1 collective-permute-start.9
  7.8 2.5 %collective-permute-start.4 = (bf16[256,256]{1,0:T(8,128)(2,1)S(1)}, bf16[256,256]{1,0:T(8,128)(2,1)S(1)}, u32[]{:S(2)}, u32[]{:S(2)}) collective-permute-start(bf16[256,256]{1,0:T(8,128)(2,1)S(1)} %get-tuple-element.43.refs_0_.own), channel_id=1, source_target_pairs={{0,6},{1,7},{2,4},{3,5},{4,2},{5,3},{6,0},{7,1},{8,14},{9,15},{10,... | collective-permute-start | bytes 393224 | tf_op jit(solution)/shard_map/ppermute | solution.py:330
  10.4 0.5 collective-permute-start.3
  10.9 0.5 collective-permute-start.2
  11.4 1.6 %copy-done = bf16[2048,512]{1,0:T(8,128)(2,1)S(1)} copy-done((bf16[2048,512]{1,0:T(8,128)(2,1)S(1)}, bf16[2048,512]{1,0:T(8,128)(2,1)}, u32[]{:S(2)}) %copy-start) | copy-done | bytes 2097176
  13.0 0.9 %shard_map.42 = (bf16[256,2048]{1,0:T(8,128)(2,1)S(1)}, bf16[256,2048]{1,0:T(8,128)(2,1)S(1)}) custom-call(s32[1]{0:T(128)} %bitcast.column_ref, bf16[256,512]{1,0:T(8,128)(2,1)S(1)} %constant_dynamic-slice_fusion.rows.rows_ref, bf16[2048,512]{1,0:T(8,128)(2,1)S(1)} %copy-done), custom_call_target="tpu_custom_call" | custom-call | flops 536870912 | bytes 4456452 | tf_op jit(solution)/shard_map/pallas_call | solution.py:33
  13.9 3.9 %collective-permute-done.1.rows_ref = bf16[256,512]{1,0:T(8,128)(2,1)S(1)} collective-permute-done((bf16[256,512]{1,0:T(8,128)(2,1)S(1)}, bf16[256,512]{1,0:T(8,128)(2,1)S(1)}, u32[]{:S(2)}, u32[]{:S(2)}) %collective-permute-start.1) | collective-permute-done | bytes 262176 | tf_op jit(solution)/shard_map/ppermute | solution.py:337
  17.7 0.0 collective-permute-start
  17.7 0.9 %shard_map.43 = (bf16[256,2048]{1,0:T(8,128)(2,1)S(1)}, bf16[256,2048]{1,0:T(8,128)(2,1)S(1)}) custom-call(s32[1]{0:T(128)} %bitcast.column_ref, bf16[256,512]{1,0:T(8,128)(2,1)S(1)} %collective-permute-done.1.rows_ref, bf16[2048,512]{1,0:T(8,128)(2,1)S(1)} %copy-done, bf16[256,2048]{1,0:T(8,128)(2,1)S(1)} %get-tuple-element.40.refs_0_.refs_8_.refs_1_), custom_call_target="tpu_custom_call" | custom-call | flops 1449132032 | bytes 5505028 | tf_op jit(solution)/shard_map/pallas_call | solution.py:33
  18.6 0.0 collective-permute-done.4.refs_3_
  18.6 0.1 collective-permute-start.5
  18.7 0.5 collective-permute-start.8
  19.2 0.1 collective-permute-start.7
  19.3 4.8 %collective-permute-done.9.rows_ref.refs_3_ = bf16[256,768]{1,0:T(8,128)(2,1)S(1)} collective-permute-done((bf16[256,768]{1,0:T(8,128)(2,1)S(1)}, bf16[256,768]{1,0:T(8,128)(2,1)S(1)}, u32[]{:S(2)}, u32[]{:S(2)}) %collective-permute-start.9) | collective-permute-done | bytes 393248 | tf_op jit(solution)/shard_map/ppermute | solution.py:337
  24.1 0.9 %shard_map.44 = (bf16[256,2048]{1,0:T(8,128)(2,1)S(1)}, bf16[256,2048]{1,0:T(8,128)(2,1)S(1)}) custom-call(s32[1]{0:T(128)} %bitcast.column_ref, bf16[256,768]{1,0:T(8,128)(2,1)S(1)} %collective-permute-done.9.rows_ref.refs_3_, bf16[2048,512]{1,0:T(8,128)(2,1)S(1)} %copy-done, bf16[256,2048]{1,0:T(8,128)(2,1)S(1)} %get-tuple-element.41.refs_0_.refs_12_.refs_1_.refs_5_), custom_call_target="tpu_custom_call" | custom-call | flops 1449132032 | bytes 5636100 | tf_op jit(solution)/shard_map/pallas_call | solution.py:33
  25.0 0.4 collective-permute-done.6.refs_5_
  25.4 1.8 %shard_map.45 = (f32[256,128]{1,0:T(8,128)S(1)}, f32[304,128]{1,0:T(8,128)S(1)}, f32[304,128]{1,0:T(8,128)S(1)}) custom-call(bf16[256,256]{1,0:T(8,128)(2,1)S(1)} %get-tuple-element.43.refs_0_.own, bf16[256,256]{1,0:T(8,128)(2,1)S(1)} %collective-permute-done.2.refs_1_, bf16[256,256]{1,0:T(8,128)(2,1)S(1)} %collective-permute-done.3.refs_2_, ...), custom_call_target="tpu_custom_call" | custom-call | tf_op jit(solution)/shard_map/pallas_call | solution.py:33
  27.2 0.1 shard_map.46.refs_3_.refs_0_
  27.3 0.8 %shard_map.47 = (f32[1024,128]{1,0:T(8,128)S(1)}, f32[1032,128]{1,0:T(8,128)S(1)}) custom-call(bf16[272,256]{1,0:T(8,128)(2,1)S(1)} %collective-permute-done.refs_4_.refs_0_, bf16[256,2048]{1,0:T(8,128)(2,1)S(1)} %get-tuple-element.41.refs_0_.refs_12_.refs_1_.refs_5_, bf16[256,2048]{1,0:T(8,128)(2,1)S(1)} %get-tuple-element.42.refs_13_.refs_2_.refs_6_, ...), custom_call_target="tpu_custom_call" | custom-call | flops 402653184 | bytes 3293184 | tf_op jit(solution)/shard_map/pallas_call | solution.py:33
  28.1 0.2 collective-permute-start.10
  28.4 0.3 collective-permute-start.11
  28.6 1.1 %collective-permute-start.12 = (f32[304,128]{1,0:T(8,128)S(1)}, f32[304,128]{1,0:T(8,128)S(1)}, u32[]{:S(2)}, u32[]{:S(2)}) collective-permute-start(f32[304,128]{1,0:T(8,128)S(1)} %get-tuple-element.50.refs_2_), channel_id=1, source_target_pairs={{24,0},{0,16},{16,8},{8,24},{25,1},{1,17},{17,9},{9,25},{26,2},{2,... | collective-permute-start | bytes 466952 | tf_op jit(solution)/shard_map/ppermute | solution.py:337
  29.7 0.4 collective-permute-done.10.received
  30.1 0.1 shard_map.48
  30.2 1.8 %collective-permute-start.13 = (f32[264,128]{1,0:T(8,128)S(1)}, f32[264,128]{1,0:T(8,128)S(1)}, u32[]{:S(2)}, u32[]{:S(2)}) collective-permute-start(f32[264,128]{1,0:T(8,128)S(1)} %get-tuple-element.54), channel_id=1, source_target_pairs={{0,2},{1,3},{2,0},{3,1},{4,6},{5,7},{6,4},{7,5},{8,10},{9,11},{10,... | collective-permute-start | bytes 405512 | tf_op jit(solution)/shard_map/ppermute | solution.py:330
  32.0 1.5 %collective-permute-start.14 = (f32[264,128]{1,0:T(8,128)S(1)}, f32[264,128]{1,0:T(8,128)S(1)}, u32[]{:S(2)}, u32[]{:S(2)}) collective-permute-start(f32[264,128]{1,0:T(8,128)S(1)} %get-tuple-element.55), channel_id=1, source_target_pairs={{0,4},{1,5},{2,6},{3,7},{4,0},{5,1},{6,2},{7,3},{8,12},{9,13},{10,... | collective-permute-start | bytes 405512 | tf_op jit(solution)/shard_map/ppermute | solution.py:330
  33.5 0.2 collective-permute-start.15
  33.7 4.2 %collective-permute-done.11.refs_2_ = f32[304,128]{1,0:T(8,128)S(1)} collective-permute-done((f32[304,128]{1,0:T(8,128)S(1)}, f32[304,128]{1,0:T(8,128)S(1)}, u32[]{:S(2)}, u32[]{:S(2)}) %collective-permute-start.11) | collective-permute-done | bytes 155680 | tf_op jit(solution)/shard_map/ppermute | solution.py:337
  38.0 2.3 %collective-permute-done.14.refs_5_ = f32[264,128]{1,0:T(8,128)S(1)} collective-permute-done((f32[264,128]{1,0:T(8,128)S(1)}, f32[264,128]{1,0:T(8,128)S(1)}, u32[]{:S(2)}, u32[]{:S(2)}) %collective-permute-start.14) | collective-permute-done | bytes 135200 | tf_op jit(solution)/shard_map/ppermute | solution.py:330
  40.3 0.1 shard_map.49
  40.4 1.4 %collective-permute-start.16 = (f32[8,128]{1,0:T(8,128)S(1)}, f32[8,128]{1,0:T(8,128)S(1)}, u32[]{:S(2)}, u32[]{:S(2)}) collective-permute-start(f32[8,128]{1,0:T(8,128)S(1)} %get-tuple-element.57.refs_0_), channel_id=1, source_target_pairs={{24,0},{0,16},{16,8},{8,24},{25,1},{1,17},{17,9},{9,25},{26,2},{2,... | collective-permute-start | bytes 12296 | tf_op jit(solution)/shard_map/ppermute | solution.py:337
  41.8 2.4 %collective-permute-start.21 = (f32[264,128]{1,0:T(8,128)S(1)}, f32[264,128]{1,0:T(8,128)S(1)}, u32[]{:S(2)}, u32[]{:S(2)}) collective-permute-start(f32[264,128]{1,0:T(8,128)S(1)} %get-tuple-element.59), channel_id=1, source_target_pairs={{16,0},{8,16},{24,8},{0,24},{17,1},{9,17},{25,9},{1,25},{18,2},{10... | collective-permute-start | bytes 405512 | tf_op jit(solution)/shard_map/ppermute | solution.py:337
  44.2 1.5 %collective-permute-start.19 = (f32[256,128]{1,0:T(8,128)S(1)}, f32[256,128]{1,0:T(8,128)S(1)}, u32[]{:S(2)}, u32[]{:S(2)}) collective-permute-start(f32[256,128]{1,0:T(8,128)S(1)} %get-tuple-element.58.refs_2_), channel_id=1, source_target_pairs={{0,6},{1,7},{2,4},{3,5},{4,2},{5,3},{6,0},{7,1},{8,14},{9,15},{10,... | collective-permute-start | bytes 393224 | tf_op jit(solution)/shard_map/ppermute | solution.py:330
  45.7 1.2 %collective-permute-start.18 = (f32[256,128]{1,0:T(8,128)S(1)}, f32[256,128]{1,0:T(8,128)S(1)}, u32[]{:S(2)}, u32[]{:S(2)}) collective-permute-start(f32[256,128]{1,0:T(8,128)S(1)} %get-tuple-element.58.refs_2_), channel_id=1, source_target_pairs={{0,4},{1,5},{2,6},{3,7},{4,0},{5,1},{6,2},{7,3},{8,12},{9,13},{10,... | collective-permute-start | bytes 393224 | tf_op jit(solution)/shard_map/ppermute | solution.py:330
  46.9 0.8 %collective-permute-start.17 = (f32[256,128]{1,0:T(8,128)S(1)}, f32[256,128]{1,0:T(8,128)S(1)}, u32[]{:S(2)}, u32[]{:S(2)}) collective-permute-start(f32[256,128]{1,0:T(8,128)S(1)} %get-tuple-element.58.refs_2_), channel_id=1, source_target_pairs={{0,2},{1,3},{2,0},{3,1},{4,6},{5,7},{6,4},{7,5},{8,10},{9,11},{10,... | collective-permute-start | bytes 393224 | tf_op jit(solution)/shard_map/ppermute | solution.py:330
  47.7 2.9 %collective-permute-done.19.refs_5_ = f32[256,128]{1,0:T(8,128)S(1)} collective-permute-done((f32[256,128]{1,0:T(8,128)S(1)}, f32[256,128]{1,0:T(8,128)S(1)}, u32[]{:S(2)}, u32[]{:S(2)}) %collective-permute-start.19) | collective-permute-done | bytes 131104 | tf_op jit(solution)/shard_map/ppermute | solution.py:330
  50.6 1.2 %collective-permute-done.18.refs_4_ = f32[256,128]{1,0:T(8,128)S(1)} collective-permute-done((f32[256,128]{1,0:T(8,128)S(1)}, f32[256,128]{1,0:T(8,128)S(1)}, u32[]{:S(2)}, u32[]{:S(2)}) %collective-permute-start.18) | collective-permute-done | bytes 131104 | tf_op jit(solution)/shard_map/ppermute | solution.py:330
  51.8 0.2 collective-permute-done.17.refs_3_
  52.0 1.1 %shard_map.50 = (bf16[1024,256]{1,0:T(8,128)(2,1)S(1)}, bf16[256,256]{1,0:T(8,128)(2,1)S(1)}, bf16[256,256]{1,0:T(8,128)(2,1)S(1)}) custom-call(f32[8,128]{1,0:T(8,128)S(1)} %get-tuple-element.57.refs_0_, f32[8,128]{1,0:T(8,128)S(1)} %collective-permute-done.16.refs_1_, f32[256,128]{1,0:T(8,128)S(1)} %get-tuple-element.58.refs_2_, ...), custom_call_target="tpu_custom_call" | custom-call | bytes 1589248 | tf_op jit(solution)/shard_map/pallas_call | solution.py:33
  53.1 0.1 collective-permute-start.23
  53.2 0.8 %shard_map.51 = (f32[1024,128]{1,0:T(8,128)S(1)}, f32[1024,128]{1,0:T(8,128)S(1)}) custom-call(bf16[256,256]{1,0:T(8,128)(2,1)S(1)} %get-tuple-element.60.refs_0_.refs_12_, bf16[256,2048]{1,0:T(8,128)(2,1)S(1)} %get-tuple-element.41.refs_0_.refs_12_.refs_1_.refs_5_, bf16[256,2048]{1,0:T(8,128)(2,1)S(1)} %get-tuple-element.42.refs_13_.refs_2_.refs_6_), custom_call_target="tpu_custom_call" | custom-call | flops 402653184 | bytes 3276800 | tf_op jit(solution)/shard_map/pallas_call | solution.py:33
  54.0 0.6 collective-permute-start.22
  54.5 1.0 %shard_map.52 = (f32[256,128]{1,0:T(8,128)S(1)}, f32[304,128]{1,0:T(8,128)S(1)}, f32[304,128]{1,0:T(8,128)S(1)}) custom-call(bf16[1024,256]{1,0:T(8,128)(2,1)S(1)} %get-tuple-element.63.refs_0_.refs_10_, bf16[256,2048]{1,0:T(8,128)(2,1)S(1)} %get-tuple-element.40.refs_0_.refs_8_.refs_1_, bf16[256,2048]{1,0:T(8,128)(2,1)S(1)} %get-tuple-element.44.refs_9_.refs_2_, ...), custom_call_target="tpu_custom_call" | custom-call | flops 603979776 | bytes 7258112 | tf_op jit(solution)/shard_map/pallas_call | solution.py:33
  55.6 1.0 %shard_map.53 = (f32[256,128]{1,0:T(8,128)S(1)}, f32[288,128]{1,0:T(8,128)S(1)}, f32[288,128]{1,0:T(8,128)S(1)}, f32[8,128]{1,0:T(8,128)S(1)}) custom-call(bf16[1024,256]{1,0:T(8,128)(2,1)S(1)} %collective-permute-done.23.refs_0_, bf16[256,2048]{1,0:T(8,128)(2,1)S(1)} %get-tuple-element.40.refs_0_.refs_8_.refs_1_, ...), custom_call_target="tpu_custom_call" | custom-call | flops 603979776 | bytes 8474624 | tf_op jit(solution)/shard_map/pallas_call | solution.py:33
  56.6 1.6 %collective-permute-start.26 = (f32[8,128]{1,0:T(8,128)S(1)}, f32[8,128]{1,0:T(8,128)S(1)}, u32[]{:S(2)}, u32[]{:S(2)}) collective-permute-start(f32[8,128]{1,0:T(8,128)S(1)} %get-tuple-element.68), channel_id=1, source_target_pairs={{24,0},{0,16},{16,8},{8,24},{25,1},{1,17},{17,9},{9,25},{26,2},{2,... | collective-permute-start | bytes 12296 | tf_op jit(solution)/shard_map/ppermute | solution.py:337
  58.2 0.8 %collective-permute-start.25 = (f32[8,128]{1,0:T(8,128)S(1)}, f32[8,128]{1,0:T(8,128)S(1)}, u32[]{:S(2)}, u32[]{:S(2)}) collective-permute-start(f32[8,128]{1,0:T(8,128)S(1)} %get-tuple-element.68), channel_id=1, source_target_pairs={{8,0},{24,16},{0,8},{16,24},{9,1},{25,17},{1,9},{17,25},{10,2},{26... | collective-permute-start | bytes 12296 | tf_op jit(solution)/shard_map/ppermute | solution.py:337
  59.1 2.4 %collective-permute-start.24 = (f32[8,128]{1,0:T(8,128)S(1)}, f32[8,128]{1,0:T(8,128)S(1)}, u32[]{:S(2)}, u32[]{:S(2)}) collective-permute-start(f32[8,128]{1,0:T(8,128)S(1)} %get-tuple-element.68), channel_id=1, source_target_pairs={{16,0},{8,16},{24,8},{0,24},{17,1},{9,17},{25,9},{1,25},{18,2},{10... | collective-permute-start | bytes 12296 | tf_op jit(solution)/shard_map/ppermute | solution.py:337
  61.5 0.1 collective-permute-start.28
  61.6 0.5 collective-permute-done.26
  62.1 1.1 %collective-permute-start.29 = (f32[288,128]{1,0:T(8,128)S(1)}, f32[288,128]{1,0:T(8,128)S(1)}, u32[]{:S(2)}, u32[]{:S(2)}) collective-permute-start(f32[288,128]{1,0:T(8,128)S(1)} %get-tuple-element.72), channel_id=1, source_target_pairs={{24,0},{0,16},{16,8},{8,24},{25,1},{1,17},{17,9},{9,25},{26,2},{2,... | collective-permute-start | bytes 442376 | tf_op jit(solution)/shard_map/ppermute | solution.py:337
  63.2 0.5 collective-permute-done.24
  63.7 1.2 %collective-permute-done.27.refs_1_ = f32[8,128]{1,0:T(8,128)S(1)} collective-permute-done((f32[8,128]{1,0:T(8,128)S(1)}, f32[8,128]{1,0:T(8,128)S(1)}, u32[]{:S(2)}, u32[]{:S(2)}) %collective-permute-start.27) | collective-permute-done | bytes 4128 | tf_op jit(solution)/shard_map/ppermute | solution.py:330
  64.8 0.1 shard_map.54
  64.9 0.9 %collective-permute-start.30 = (f32[264,128]{1,0:T(8,128)S(1)}, f32[264,128]{1,0:T(8,128)S(1)}, u32[]{:S(2)}, u32[]{:S(2)}) collective-permute-start(f32[264,128]{1,0:T(8,128)S(1)} %get-tuple-element.73), channel_id=1, source_target_pairs={{0,2},{1,3},{2,0},{3,1},{4,6},{5,7},{6,4},{7,5},{8,10},{9,11},{10,... | collective-permute-start | bytes 405512 | tf_op jit(solution)/shard_map/ppermute | solution.py:330
  65.8 1.5 %collective-permute-start.31 = (f32[264,128]{1,0:T(8,128)S(1)}, f32[264,128]{1,0:T(8,128)S(1)}, u32[]{:S(2)}, u32[]{:S(2)}) collective-permute-start(f32[264,128]{1,0:T(8,128)S(1)} %get-tuple-element.74), channel_id=1, source_target_pairs={{0,4},{1,5},{2,6},{3,7},{4,0},{5,1},{6,2},{7,3},{8,12},{9,13},{10,... | collective-permute-start | bytes 405512 | tf_op jit(solution)/shard_map/ppermute | solution.py:330
  67.3 1.2 %collective-permute-start.32 = (f32[264,128]{1,0:T(8,128)S(1)}, f32[264,128]{1,0:T(8,128)S(1)}, u32[]{:S(2)}, u32[]{:S(2)}) collective-permute-start(f32[264,128]{1,0:T(8,128)S(1)} %get-tuple-element.75), channel_id=1, source_target_pairs={{0,6},{1,7},{2,4},{3,5},{4,2},{5,3},{6,0},{7,1},{8,14},{9,15},{10,... | collective-permute-start | bytes 405512 | tf_op jit(solution)/shard_map/ppermute | solution.py:330
  68.5 2.9 %collective-permute-done.30.refs_4_ = f32[264,128]{1,0:T(8,128)S(1)} collective-permute-done((f32[264,128]{1,0:T(8,128)S(1)}, f32[264,128]{1,0:T(8,128)S(1)}, u32[]{:S(2)}, u32[]{:S(2)}) %collective-permute-start.30) | collective-permute-done | bytes 135200 | tf_op jit(solution)/shard_map/ppermute | solution.py:330
  71.4 1.7 %collective-permute-done.31.refs_5_ = f32[264,128]{1,0:T(8,128)S(1)} collective-permute-done((f32[264,128]{1,0:T(8,128)S(1)}, f32[264,128]{1,0:T(8,128)S(1)}, u32[]{:S(2)}, u32[]{:S(2)}) %collective-permute-start.31) | collective-permute-done | bytes 135200 | tf_op jit(solution)/shard_map/ppermute | solution.py:330
  73.1 1.0 %collective-permute-done.32.refs_6_ = f32[264,128]{1,0:T(8,128)S(1)} collective-permute-done((f32[264,128]{1,0:T(8,128)S(1)}, f32[264,128]{1,0:T(8,128)S(1)}, u32[]{:S(2)}, u32[]{:S(2)}) %collective-permute-start.32) | collective-permute-done | bytes 135200 | tf_op jit(solution)/shard_map/ppermute | solution.py:330
  74.1 1.0 %shard_map.55 = (f32[256,128]{1,0:T(8,128)}, f32[256,128]{1,0:T(8,128)}) custom-call(f32[264,128]{1,0:T(8,128)S(1)} %get-tuple-element.69.refs_0_, f32[256,128]{1,0:T(8,128)S(1)} %get-tuple-element.70.refs_1_, f32[288,128]{1,0:T(8,128)S(1)} %collective-permute-done.28.refs_2_, f32[288,128]{1,0:T(8,128)S(1)} %collective-permute-done.29.refs_3_, ...), custom_call_target="tpu_custom_call" | custom-call | bytes 1228800 | tf_op jit(solution)/shard_map/pallas_call | solution.py:33
  (23 shorter events, 0.1 us)
Async XLA Ops:
  1.6 16.1 %collective-permute-start.1 = (bf16[256,512]{1,0:T(8,128)(2,1)S(1)}, bf16[256,512]{1,0:T(8,128)(2,1)S(1)}, u32[]{:S(2)}, u32[]{:S(2)}) collective-permute-start(bf16[256,512]{1,0:T(8,128)(2,1)S(1)} %constant_dynamic-slice_fusion.rows.rows_ref), channel_id=1, source_target_pairs={{16,0},{8,16},{24,8},{0,24},{17,1},{9,17},{25,9},{1,25},{18,2},{10... | collective-permute-start | bytes 786440 | tf_op jit(solution)/shard_map/ppermute | solution.py:337
  6.7 0.9 %copy-start.1 = (f32[256,128]{1,0:T(8,128)S(1)}, f32[256,128]{1,0:T(8,128)}, u32[]{:S(2)}) copy-start(f32[256,128]{1,0:T(8,128)} %logits.1) | copy-start | bytes 393220
  7.8 16.3 %collective-permute-start.9 = (bf16[256,768]{1,0:T(8,128)(2,1)S(1)}, bf16[256,768]{1,0:T(8,128)(2,1)S(1)}, u32[]{:S(2)}, u32[]{:S(2)}) collective-permute-start(bf16[256,768]{1,0:T(8,128)(2,1)S(1)} %get-tuple-element.45), channel_id=1, source_target_pairs={{0,8},{8,0},{16,24},{24,16},{1,9},{9,1},{17,25},{25,17},{2,10},{10... | collective-permute-start | bytes 1179656 | tf_op jit(solution)/shard_map/ppermute | solution.py:337
  7.8 10.8 %collective-permute-start.4 = (bf16[256,256]{1,0:T(8,128)(2,1)S(1)}, bf16[256,256]{1,0:T(8,128)(2,1)S(1)}, u32[]{:S(2)}, u32[]{:S(2)}) collective-permute-start(bf16[256,256]{1,0:T(8,128)(2,1)S(1)} %get-tuple-element.43.refs_0_.own), channel_id=1, source_target_pairs={{0,6},{1,7},{2,4},{3,5},{4,2},{5,3},{6,0},{7,1},{8,14},{9,15},{10,... | collective-permute-start | bytes 393224 | tf_op jit(solution)/shard_map/ppermute | solution.py:330
  10.4 8.4 %collective-permute-start.3 = (bf16[256,256]{1,0:T(8,128)(2,1)S(1)}, bf16[256,256]{1,0:T(8,128)(2,1)S(1)}, u32[]{:S(2)}, u32[]{:S(2)}) collective-permute-start(bf16[256,256]{1,0:T(8,128)(2,1)S(1)} %get-tuple-element.43.refs_0_.own), channel_id=1, source_target_pairs={{0,4},{1,5},{2,6},{3,7},{4,0},{5,1},{6,2},{7,3},{8,12},{9,13},{10,... | collective-permute-start | bytes 393224 | tf_op jit(solution)/shard_map/ppermute | solution.py:330
  10.9 8.4 %collective-permute-start.2 = (bf16[256,256]{1,0:T(8,128)(2,1)S(1)}, bf16[256,256]{1,0:T(8,128)(2,1)S(1)}, u32[]{:S(2)}, u32[]{:S(2)}) collective-permute-start(bf16[256,256]{1,0:T(8,128)(2,1)S(1)} %get-tuple-element.43.refs_0_.own), channel_id=1, source_target_pairs={{0,2},{1,3},{2,0},{3,1},{4,6},{5,7},{6,4},{7,5},{8,10},{9,11},{10,... | collective-permute-start | bytes 393224 | tf_op jit(solution)/shard_map/ppermute | solution.py:330
  11.4 1.6 %copy-start = (bf16[2048,512]{1,0:T(8,128)(2,1)S(1)}, bf16[2048,512]{1,0:T(8,128)(2,1)}, u32[]{:S(2)}) copy-start(bf16[2048,512]{1,0:T(8,128)(2,1)} %plane_ref.5) | copy-start | bytes 6291460
  17.7 9.5 %collective-permute-start = (bf16[272,256]{1,0:T(8,128)(2,1)S(1)}, bf16[272,256]{1,0:T(8,128)(2,1)S(1)}, u32[]{:S(2)}, u32[]{:S(2)}) collective-permute-start(bf16[272,256]{1,0:T(8,128)(2,1)S(1)} %get-tuple-element.39), channel_id=1, source_target_pairs={{16,0},{8,16},{24,8},{0,24},{17,1},{9,17},{25,9},{1,25},{18,2},{10... | collective-permute-start | bytes 417800 | tf_op jit(solution)/shard_map/ppermute | solution.py:337
  18.6 6.3 %collective-permute-start.5 = (bf16[256,256]{1,0:T(8,128)(2,1)S(1)}, bf16[256,256]{1,0:T(8,128)(2,1)S(1)}, u32[]{:S(2)}, u32[]{:S(2)}) collective-permute-start(bf16[256,256]{1,0:T(8,128)(2,1)S(1)} %get-tuple-element.43.refs_0_.own), channel_id=1, source_target_pairs={{0,1},{1,0},{2,3},{3,2},{4,5},{5,4},{6,7},{7,6},{8,9},{9,8},{10,11... | collective-permute-start | bytes 393224 | tf_op jit(solution)/shard_map/ppermute | solution.py:330
  18.7 6.2 %collective-permute-start.8 = (bf16[256,256]{1,0:T(8,128)(2,1)S(1)}, bf16[256,256]{1,0:T(8,128)(2,1)S(1)}, u32[]{:S(2)}, u32[]{:S(2)}) collective-permute-start(bf16[256,256]{1,0:T(8,128)(2,1)S(1)} %collective-permute-done.4.refs_3_), channel_id=1, source_target_pairs={{0,1},{1,0},{2,3},{3,2},{4,5},{5,4},{6,7},{7,6},{8,9},{9,8},{10,11... | collective-permute-start | bytes 393224 | tf_op jit(solution)/shard_map/ppermute | solution.py:330
  19.2 5.7 %collective-permute-start.7 = (bf16[256,256]{1,0:T(8,128)(2,1)S(1)}, bf16[256,256]{1,0:T(8,128)(2,1)S(1)}, u32[]{:S(2)}, u32[]{:S(2)}) collective-permute-start(bf16[256,256]{1,0:T(8,128)(2,1)S(1)} %collective-permute-done.3.refs_2_), channel_id=1, source_target_pairs={{0,1},{1,0},{2,3},{3,2},{4,5},{5,4},{6,7},{7,6},{8,9},{9,8},{10,11... | collective-permute-start | bytes 393224 | tf_op jit(solution)/shard_map/ppermute | solution.py:330
  24.1 1.3 %collective-permute-start.6 = (bf16[256,256]{1,0:T(8,128)(2,1)S(1)}, bf16[256,256]{1,0:T(8,128)(2,1)S(1)}, u32[]{:S(2)}, u32[]{:S(2)}) collective-permute-start(bf16[256,256]{1,0:T(8,128)(2,1)S(1)} %collective-permute-done.2.refs_1_), channel_id=1, source_target_pairs={{0,1},{1,0},{2,3},{3,2},{4,5},{5,4},{6,7},{7,6},{8,9},{9,8},{10,11... | collective-permute-start | bytes 393224 | tf_op jit(solution)/shard_map/ppermute | solution.py:330
  28.1 2.0 %collective-permute-start.10 = (f32[1032,128]{1,0:T(8,128)S(1)}, f32[1032,128]{1,0:T(8,128)S(1)}, u32[]{:S(2)}, u32[]{:S(2)}) collective-permute-start(f32[1032,128]{1,0:T(8,128)S(1)} %get-tuple-element.52), channel_id=1, source_target_pairs={{0,1},{1,0},{2,3},{3,2},{4,5},{5,4},{6,7},{7,6},{8,9},{9,8},{10,11... | collective-permute-start | bytes 1585160 | tf_op jit(solution)/shard_map/ppermute | solution.py:330
  28.4 9.6 %collective-permute-start.11 = (f32[304,128]{1,0:T(8,128)S(1)}, f32[304,128]{1,0:T(8,128)S(1)}, u32[]{:S(2)}, u32[]{:S(2)}) collective-permute-start(f32[304,128]{1,0:T(8,128)S(1)} %get-tuple-element.49.refs_1_), channel_id=1, source_target_pairs={{0,8},{8,0},{16,24},{24,16},{1,9},{9,1},{17,25},{25,17},{2,10},{10... | collective-permute-start | bytes 466952 | tf_op jit(solution)/shard_map/ppermute | solution.py:337
  28.6 9.3 %collective-permute-start.12 = (f32[304,128]{1,0:T(8,128)S(1)}, f32[304,128]{1,0:T(8,128)S(1)}, u32[]{:S(2)}, u32[]{:S(2)}) collective-permute-start(f32[304,128]{1,0:T(8,128)S(1)} %get-tuple-element.50.refs_2_), channel_id=1, source_target_pairs={{24,0},{0,16},{16,8},{8,24},{25,1},{1,17},{17,9},{9,25},{26,2},{2,... | collective-permute-start | bytes 466952 | tf_op jit(solution)/shard_map/ppermute | solution.py:337
  30.2 7.8 %collective-permute-start.13 = (f32[264,128]{1,0:T(8,128)S(1)}, f32[264,128]{1,0:T(8,128)S(1)}, u32[]{:S(2)}, u32[]{:S(2)}) collective-permute-start(f32[264,128]{1,0:T(8,128)S(1)} %get-tuple-element.54), channel_id=1, source_target_pairs={{0,2},{1,3},{2,0},{3,1},{4,6},{5,7},{6,4},{7,5},{8,10},{9,11},{10,... | collective-permute-start | bytes 405512 | tf_op jit(solution)/shard_map/ppermute | solution.py:330
  32.0 8.3 %collective-permute-start.14 = (f32[264,128]{1,0:T(8,128)S(1)}, f32[264,128]{1,0:T(8,128)S(1)}, u32[]{:S(2)}, u32[]{:S(2)}) collective-permute-start(f32[264,128]{1,0:T(8,128)S(1)} %get-tuple-element.55), channel_id=1, source_target_pairs={{0,4},{1,5},{2,6},{3,7},{4,0},{5,1},{6,2},{7,3},{8,12},{9,13},{10,... | collective-permute-start | bytes 405512 | tf_op jit(solution)/shard_map/ppermute | solution.py:330
  33.5 6.7 %collective-permute-start.15 = (f32[264,128]{1,0:T(8,128)S(1)}, f32[264,128]{1,0:T(8,128)S(1)}, u32[]{:S(2)}, u32[]{:S(2)}) collective-permute-start(f32[264,128]{1,0:T(8,128)S(1)} %get-tuple-element.56), channel_id=1, source_target_pairs={{0,6},{1,7},{2,4},{3,5},{4,2},{5,3},{6,0},{7,1},{8,14},{9,15},{10,... | collective-permute-start | bytes 405512 | tf_op jit(solution)/shard_map/ppermute | solution.py:330
  40.4 6.6 %collective-permute-start.16 = (f32[8,128]{1,0:T(8,128)S(1)}, f32[8,128]{1,0:T(8,128)S(1)}, u32[]{:S(2)}, u32[]{:S(2)}) collective-permute-start(f32[8,128]{1,0:T(8,128)S(1)} %get-tuple-element.57.refs_0_), channel_id=1, source_target_pairs={{24,0},{0,16},{16,8},{8,24},{25,1},{1,17},{17,9},{9,25},{26,2},{2,... | collective-permute-start | bytes 12296 | tf_op jit(solution)/shard_map/ppermute | solution.py:337
  41.8 10.2 %collective-permute-start.21 = (f32[264,128]{1,0:T(8,128)S(1)}, f32[264,128]{1,0:T(8,128)S(1)}, u32[]{:S(2)}, u32[]{:S(2)}) collective-permute-start(f32[264,128]{1,0:T(8,128)S(1)} %get-tuple-element.59), channel_id=1, source_target_pairs={{16,0},{8,16},{24,8},{0,24},{17,1},{9,17},{25,9},{1,25},{18,2},{10... | collective-permute-start | bytes 405512 | tf_op jit(solution)/shard_map/ppermute | solution.py:337
  44.2 7.8 %collective-permute-start.20 = (f32[264,128]{1,0:T(8,128)S(1)}, f32[264,128]{1,0:T(8,128)S(1)}, u32[]{:S(2)}, u32[]{:S(2)}) collective-permute-start(f32[264,128]{1,0:T(8,128)S(1)} %get-tuple-element.59), channel_id=1, source_target_pairs={{0,8},{8,0},{16,24},{24,16},{1,9},{9,1},{17,25},{25,17},{2,10},{10... | collective-permute-start | bytes 405512 | tf_op jit(solution)/shard_map/ppermute | solution.py:337
  44.2 6.3 %collective-permute-start.19 = (f32[256,128]{1,0:T(8,128)S(1)}, f32[256,128]{1,0:T(8,128)S(1)}, u32[]{:S(2)}, u32[]{:S(2)}) collective-permute-start(f32[256,128]{1,0:T(8,128)S(1)} %get-tuple-element.58.refs_2_), channel_id=1, source_target_pairs={{0,6},{1,7},{2,4},{3,5},{4,2},{5,3},{6,0},{7,1},{8,14},{9,15},{10,... | collective-permute-start | bytes 393224 | tf_op jit(solution)/shard_map/ppermute | solution.py:330
  45.7 6.1 %collective-permute-start.18 = (f32[256,128]{1,0:T(8,128)S(1)}, f32[256,128]{1,0:T(8,128)S(1)}, u32[]{:S(2)}, u32[]{:S(2)}) collective-permute-start(f32[256,128]{1,0:T(8,128)S(1)} %get-tuple-element.58.refs_2_), channel_id=1, source_target_pairs={{0,4},{1,5},{2,6},{3,7},{4,0},{5,1},{6,2},{7,3},{8,12},{9,13},{10,... | collective-permute-start | bytes 393224 | tf_op jit(solution)/shard_map/ppermute | solution.py:330
  46.9 5.1 %collective-permute-start.17 = (f32[256,128]{1,0:T(8,128)S(1)}, f32[256,128]{1,0:T(8,128)S(1)}, u32[]{:S(2)}, u32[]{:S(2)}) collective-permute-start(f32[256,128]{1,0:T(8,128)S(1)} %get-tuple-element.58.refs_2_), channel_id=1, source_target_pairs={{0,2},{1,3},{2,0},{3,1},{4,6},{5,7},{6,4},{7,5},{8,10},{9,11},{10,... | collective-permute-start | bytes 393224 | tf_op jit(solution)/shard_map/ppermute | solution.py:330
  53.1 2.4 %collective-permute-start.23 = (bf16[1024,256]{1,0:T(8,128)(2,1)S(1)}, bf16[1024,256]{1,0:T(8,128)(2,1)S(1)}, u32[]{:S(2)}, u32[]{:S(2)}) collective-permute-start(bf16[1024,256]{1,0:T(8,128)(2,1)S(1)} %get-tuple-element.63.refs_0_.refs_10_), channel_id=1, source_target_pairs={{0,1},{1,0},{2,3},{3,2},{4,5},{5,4},{6,7},{7,6},{8,9},{9,8},{10,11... | collective-permute-start | bytes 1572872 | tf_op jit(solution)/shard_map/ppermute | solution.py:330
  54.0 9.7 %collective-permute-start.22 = (f32[1024,128]{1,0:T(8,128)S(1)}, f32[1024,128]{1,0:T(8,128)S(1)}, u32[]{:S(2)}, u32[]{:S(2)}) collective-permute-start(f32[1024,128]{1,0:T(8,128)S(1)} %get-tuple-element.62), channel_id=1, source_target_pairs={{0,1},{1,0},{2,3},{3,2},{4,5},{5,4},{6,7},{7,6},{8,9},{9,8},{10,11... | collective-permute-start | bytes 1572872 | tf_op jit(solution)/shard_map/ppermute | solution.py:330
  56.6 5.5 %collective-permute-start.26 = (f32[8,128]{1,0:T(8,128)S(1)}, f32[8,128]{1,0:T(8,128)S(1)}, u32[]{:S(2)}, u32[]{:S(2)}) collective-permute-start(f32[8,128]{1,0:T(8,128)S(1)} %get-tuple-element.68), channel_id=1, source_target_pairs={{24,0},{0,16},{16,8},{8,24},{25,1},{1,17},{17,9},{9,25},{26,2},{2,... | collective-permute-start | bytes 12296 | tf_op jit(solution)/shard_map/ppermute | solution.py:337
  58.2 5.0 %collective-permute-start.25 = (f32[8,128]{1,0:T(8,128)S(1)}, f32[8,128]{1,0:T(8,128)S(1)}, u32[]{:S(2)}, u32[]{:S(2)}) collective-permute-start(f32[8,128]{1,0:T(8,128)S(1)} %get-tuple-element.68), channel_id=1, source_target_pairs={{8,0},{24,16},{0,8},{16,24},{9,1},{25,17},{1,9},{17,25},{10,2},{26... | collective-permute-start | bytes 12296 | tf_op jit(solution)/shard_map/ppermute | solution.py:337
  59.1 4.6 %collective-permute-start.24 = (f32[8,128]{1,0:T(8,128)S(1)}, f32[8,128]{1,0:T(8,128)S(1)}, u32[]{:S(2)}, u32[]{:S(2)}) collective-permute-start(f32[8,128]{1,0:T(8,128)S(1)} %get-tuple-element.68), channel_id=1, source_target_pairs={{16,0},{8,16},{24,8},{0,24},{17,1},{9,17},{25,9},{1,25},{18,2},{10... | collective-permute-start | bytes 12296 | tf_op jit(solution)/shard_map/ppermute | solution.py:337
  61.5 12.6 %collective-permute-start.28 = (f32[288,128]{1,0:T(8,128)S(1)}, f32[288,128]{1,0:T(8,128)S(1)}, u32[]{:S(2)}, u32[]{:S(2)}) collective-permute-start(f32[288,128]{1,0:T(8,128)S(1)} %get-tuple-element.71), channel_id=1, source_target_pairs={{0,8},{8,0},{16,24},{24,16},{1,9},{9,1},{17,25},{25,17},{2,10},{10... | collective-permute-start | bytes 442376 | tf_op jit(solution)/shard_map/ppermute | solution.py:337
  62.1 12.1 %collective-permute-start.29 = (f32[288,128]{1,0:T(8,128)S(1)}, f32[288,128]{1,0:T(8,128)S(1)}, u32[]{:S(2)}, u32[]{:S(2)}) collective-permute-start(f32[288,128]{1,0:T(8,128)S(1)} %get-tuple-element.72), channel_id=1, source_target_pairs={{24,0},{0,16},{16,8},{8,24},{25,1},{1,17},{17,9},{9,25},{26,2},{2,... | collective-permute-start | bytes 442376 | tf_op jit(solution)/shard_map/ppermute | solution.py:337
  63.7 1.2 %collective-permute-start.27 = (f32[8,128]{1,0:T(8,128)S(1)}, f32[8,128]{1,0:T(8,128)S(1)}, u32[]{:S(2)}, u32[]{:S(2)}) collective-permute-start(f32[8,128]{1,0:T(8,128)S(1)} %add_add_fusion.refs_0_), channel_id=1, source_target_pairs={{0,1},{1,0},{2,3},{3,2},{4,5},{5,4},{6,7},{7,6},{8,9},{9,8},{10,11... | collective-permute-start | bytes 12296 | tf_op jit(solution)/shard_map/ppermute | solution.py:330
  64.9 6.5 %collective-permute-start.30 = (f32[264,128]{1,0:T(8,128)S(1)}, f32[264,128]{1,0:T(8,128)S(1)}, u32[]{:S(2)}, u32[]{:S(2)}) collective-permute-start(f32[264,128]{1,0:T(8,128)S(1)} %get-tuple-element.73), channel_id=1, source_target_pairs={{0,2},{1,3},{2,0},{3,1},{4,6},{5,7},{6,4},{7,5},{8,10},{9,11},{10,... | collective-permute-start | bytes 405512 | tf_op jit(solution)/shard_map/ppermute | solution.py:330
  65.8 7.3 %collective-permute-start.31 = (f32[264,128]{1,0:T(8,128)S(1)}, f32[264,128]{1,0:T(8,128)S(1)}, u32[]{:S(2)}, u32[]{:S(2)}) collective-permute-start(f32[264,128]{1,0:T(8,128)S(1)} %get-tuple-element.74), channel_id=1, source_target_pairs={{0,4},{1,5},{2,6},{3,7},{4,0},{5,1},{6,2},{7,3},{8,12},{9,13},{10,... | collective-permute-start | bytes 405512 | tf_op jit(solution)/shard_map/ppermute | solution.py:330
  67.3 6.8 %collective-permute-start.32 = (f32[264,128]{1,0:T(8,128)S(1)}, f32[264,128]{1,0:T(8,128)S(1)}, u32[]{:S(2)}, u32[]{:S(2)}) collective-permute-start(f32[264,128]{1,0:T(8,128)S(1)} %get-tuple-element.75), channel_id=1, source_target_pairs={{0,6},{1,7},{2,4},{3,5},{4,2},{5,3},{6,0},{7,1},{8,14},{9,15},{10,... | collective-permute-start | bytes 405512 | tf_op jit(solution)/shard_map/ppermute | solution.py:330

commit v13 on v12

--- a/solution.py
+++ b/solution.py
@@ -237,20 +237,20 @@
     over = (((0,), (0,)), ((), ()))
     for part, out in enumerate((odd, even)):
         columns = slice((1 - part) * half, (2 - part) * half)
-        acc = jnp.zeros((half, clusters), F32)
+        acc = jnp.zeros((clusters, half), F32)
         for i, pair in enumerate(pairs):
             both = pair[:n, pair.shape[1] - 2 * clusters :]
             a = lax.dot_general(
-                kernels[2 * i][:, columns], both, over, preferred_element_type=F32
+                both, kernels[2 * i][:, columns], over, preferred_element_type=F32
             )
             b = lax.dot_general(
+                both[:, :clusters],
                 kernels[2 * i + 1][:, columns],
-                both[:, :clusters],
                 over,
                 preferred_element_type=F32,
             )
-            acc += a[:, :clusters] + (a[:, clusters:] + b)
-        out[:half, :] = acc
+            acc += a[:clusters, :] + (a[clusters:, :] + b)
+        out[:half, :] = acc.T
     if stat:
         odd[half:, :] = stat[0][...]
 

time: 75.3 us -> 75.2 us (level)
  no operation moved by 1% of the time
where the time goes in v13:
time: 75.2 us; the launch traced here: 75 us
  starting transfers between devices  32.2 us (43%)
  waiting for transfers between devices  28 us (37%)
  Pallas kernels  10.5 us (14%)
  local copies, waits for them, and re-layouts  3.47 us (5%)
  between operations  0.83 us (1%)
    ppermute x13, starting transfers between devices, shift(): return lax.ppermute(x, 'row', pairs)  16.5 us
    ppermute x20, starting transfers between devices, by_col(): return lax.ppermute(x, 'col', [(i, i ^ mask) for i in range(cols)])  15.6 us
    ppermute x20, waiting for transfers between devices, by_col(): return lax.ppermute(x, 'col', [(i, i ^ mask) for i in range(cols)])  14.2 us
    ppermute x13, waiting for transfers between devices, shift(): return lax.ppermute(x, 'row', pairs)  13.8 us
    pallas_call x15, Pallas kernels, call(): pl.pallas_call(body, in_specs=specs or [VMEM] * len(args), out_specs=[VME...  10.5 us
    unnamed x4, local copies, waits for them, and re-layouts  2.49 us
  transfers between devices with their start and end apart: 33, of which 15 were waited for; matrix products, arithmetic and copies ran while one was open for 0% of the time, Pallas kernels for 10%

profile of v13, /device:TPU:0, one launch (start us, length us, event | category | flops | bytes accessed | tf_op | source)
XLA Modules:
  0.0 75.0 jit_solution(16944551880379778377)
XLA Ops:
  0.6 1.0 %constant_dynamic-slice_fusion.rows.rows_ref = bf16[256,512]{1,0:T(8,128)(2,1)S(1)} fusion(bf16[2048,512]{1,0:T(8,128)(2,1)} %plane_ref.5, s32[]{:T(128)S(6)} %select_n.3), kind=kLoop, calls=%fused_computation.1 | loop fusion | bytes 524292 | tf_op jit(solution)/shard_map/dynamic_slice | solution.py:340
  1.6 5.1 %collective-permute-start.1 = (bf16[256,512]{1,0:T(8,128)(2,1)S(1)}, bf16[256,512]{1,0:T(8,128)(2,1)S(1)}, u32[]{:S(2)}, u32[]{:S(2)}) collective-permute-start(bf16[256,512]{1,0:T(8,128)(2,1)S(1)} %constant_dynamic-slice_fusion.rows.rows_ref), channel_id=1, source_target_pairs={{16,0},{8,16},{24,8},{0,24},{17,1},{9,17},{25,9},{1,25},{18,2},{10... | collective-permute-start | bytes 786440 | tf_op jit(solution)/shard_map/ppermute | solution.py:337
  6.7 0.9 %copy-done.1 = f32[256,128]{1,0:T(8,128)S(1)} copy-done((f32[256,128]{1,0:T(8,128)S(1)}, f32[256,128]{1,0:T(8,128)}, u32[]{:S(2)}) %copy-start.1) | copy-done | bytes 131096
  7.6 0.1 shard_map.41
  7.8 0.1 collective-permute-start.9
  7.8 2.5 %collective-permute-start.4 = (bf16[256,256]{1,0:T(8,128)(2,1)S(1)}, bf16[256,256]{1,0:T(8,128)(2,1)S(1)}, u32[]{:S(2)}, u32[]{:S(2)}) collective-permute-start(bf16[256,256]{1,0:T(8,128)(2,1)S(1)} %get-tuple-element.43.refs_0_.own), channel_id=1, source_target_pairs={{0,6},{1,7},{2,4},{3,5},{4,2},{5,3},{6,0},{7,1},{8,14},{9,15},{10,... | collective-permute-start | bytes 393224 | tf_op jit(solution)/shard_map/ppermute | solution.py:330
  10.4 0.5 collective-permute-start.3
  10.9 0.5 collective-permute-start.2
  11.4 1.6 %copy-done = bf16[2048,512]{1,0:T(8,128)(2,1)S(1)} copy-done((bf16[2048,512]{1,0:T(8,128)(2,1)S(1)}, bf16[2048,512]{1,0:T(8,128)(2,1)}, u32[]{:S(2)}) %copy-start) | copy-done | bytes 2097176
  13.0 0.9 %shard_map.42 = (bf16[256,2048]{1,0:T(8,128)(2,1)S(1)}, bf16[256,2048]{1,0:T(8,128)(2,1)S(1)}) custom-call(s32[1]{0:T(128)} %bitcast.column_ref, bf16[256,512]{1,0:T(8,128)(2,1)S(1)} %constant_dynamic-slice_fusion.rows.rows_ref, bf16[2048,512]{1,0:T(8,128)(2,1)S(1)} %copy-done), custom_call_target="tpu_custom_call" | custom-call | flops 536870912 | bytes 4456452 | tf_op jit(solution)/shard_map/pallas_call | solution.py:33
  13.9 3.9 %collective-permute-done.1.rows_ref = bf16[256,512]{1,0:T(8,128)(2,1)S(1)} collective-permute-done((bf16[256,512]{1,0:T(8,128)(2,1)S(1)}, bf16[256,512]{1,0:T(8,128)(2,1)S(1)}, u32[]{:S(2)}, u32[]{:S(2)}) %collective-permute-start.1) | collective-permute-done | bytes 262176 | tf_op jit(solution)/shard_map/ppermute | solution.py:337
  17.7 0.0 collective-permute-start
  17.7 0.9 %shard_map.43 = (bf16[256,2048]{1,0:T(8,128)(2,1)S(1)}, bf16[256,2048]{1,0:T(8,128)(2,1)S(1)}) custom-call(s32[1]{0:T(128)} %bitcast.column_ref, bf16[256,512]{1,0:T(8,128)(2,1)S(1)} %collective-permute-done.1.rows_ref, bf16[2048,512]{1,0:T(8,128)(2,1)S(1)} %copy-done, bf16[256,2048]{1,0:T(8,128)(2,1)S(1)} %get-tuple-element.40.refs_0_.refs_8_.refs_1_), custom_call_target="tpu_custom_call" | custom-call | flops 1449132032 | bytes 5505028 | tf_op jit(solution)/shard_map/pallas_call | solution.py:33
  18.6 0.1 collective-permute-start.5
  18.7 0.0 collective-permute-done.3.refs_2_
  18.7 0.5 collective-permute-start.8
  19.2 0.1 collective-permute-start.7
  19.3 4.8 %collective-permute-done.9.rows_ref.refs_3_ = bf16[256,768]{1,0:T(8,128)(2,1)S(1)} collective-permute-done((bf16[256,768]{1,0:T(8,128)(2,1)S(1)}, bf16[256,768]{1,0:T(8,128)(2,1)S(1)}, u32[]{:S(2)}, u32[]{:S(2)}) %collective-permute-start.9) | collective-permute-done | bytes 393248 | tf_op jit(solution)/shard_map/ppermute | solution.py:337
  24.1 0.9 %shard_map.44 = (bf16[256,2048]{1,0:T(8,128)(2,1)S(1)}, bf16[256,2048]{1,0:T(8,128)(2,1)S(1)}) custom-call(s32[1]{0:T(128)} %bitcast.column_ref, bf16[256,768]{1,0:T(8,128)(2,1)S(1)} %collective-permute-done.9.rows_ref.refs_3_, bf16[2048,512]{1,0:T(8,128)(2,1)S(1)} %copy-done, bf16[256,2048]{1,0:T(8,128)(2,1)S(1)} %get-tuple-element.41.refs_0_.refs_12_.refs_1_.refs_5_), custom_call_target="tpu_custom_call" | custom-call | flops 1449132032 | bytes 5636100 | tf_op jit(solution)/shard_map/pallas_call | solution.py:33
  25.0 0.4 collective-permute-done.6.refs_5_
  25.4 1.8 %shard_map.45 = (f32[256,128]{1,0:T(8,128)S(1)}, f32[304,128]{1,0:T(8,128)S(1)}, f32[304,128]{1,0:T(8,128)S(1)}) custom-call(bf16[256,256]{1,0:T(8,128)(2,1)S(1)} %get-tuple-element.43.refs_0_.own, bf16[256,256]{1,0:T(8,128)(2,1)S(1)} %collective-permute-done.2.refs_1_, bf16[256,256]{1,0:T(8,128)(2,1)S(1)} %collective-permute-done.3.refs_2_, ...), custom_call_target="tpu_custom_call" | custom-call | tf_op jit(solution)/shard_map/pallas_call | solution.py:33
  27.2 0.1 shard_map.46.refs_3_.refs_0_
  27.3 0.7 shard_map.47
  28.1 0.2 collective-permute-start.10
  28.3 0.3 collective-permute-start.11
  28.6 1.1 %collective-permute-start.12 = (f32[304,128]{1,0:T(8,128)S(1)}, f32[304,128]{1,0:T(8,128)S(1)}, u32[]{:S(2)}, u32[]{:S(2)}) collective-permute-start(f32[304,128]{1,0:T(8,128)S(1)} %get-tuple-element.50.refs_2_), channel_id=1, source_target_pairs={{24,0},{0,16},{16,8},{8,24},{25,1},{1,17},{17,9},{9,25},{26,2},{2,... | collective-permute-start | bytes 466952 | tf_op jit(solution)/shard_map/ppermute | solution.py:337
  29.7 0.4 collective-permute-done.10.received
  30.1 0.1 shard_map.48
  30.1 1.8 %collective-permute-start.13 = (f32[264,128]{1,0:T(8,128)S(1)}, f32[264,128]{1,0:T(8,128)S(1)}, u32[]{:S(2)}, u32[]{:S(2)}) collective-permute-start(f32[264,128]{1,0:T(8,128)S(1)} %get-tuple-element.54), channel_id=1, source_target_pairs={{0,2},{1,3},{2,0},{3,1},{4,6},{5,7},{6,4},{7,5},{8,10},{9,11},{10,... | collective-permute-start | bytes 405512 | tf_op jit(solution)/shard_map/ppermute | solution.py:330
  32.0 1.5 %collective-permute-start.14 = (f32[264,128]{1,0:T(8,128)S(1)}, f32[264,128]{1,0:T(8,128)S(1)}, u32[]{:S(2)}, u32[]{:S(2)}) collective-permute-start(f32[264,128]{1,0:T(8,128)S(1)} %get-tuple-element.55), channel_id=1, source_target_pairs={{0,4},{1,5},{2,6},{3,7},{4,0},{5,1},{6,2},{7,3},{8,12},{9,13},{10,... | collective-permute-start | bytes 405512 | tf_op jit(solution)/shard_map/ppermute | solution.py:330
  33.5 0.2 collective-permute-start.15
  33.7 4.2 %collective-permute-done.11.refs_2_ = f32[304,128]{1,0:T(8,128)S(1)} collective-permute-done((f32[304,128]{1,0:T(8,128)S(1)}, f32[304,128]{1,0:T(8,128)S(1)}, u32[]{:S(2)}, u32[]{:S(2)}) %collective-permute-start.11) | collective-permute-done | bytes 155680 | tf_op jit(solution)/shard_map/ppermute | solution.py:337
  37.9 2.3 %collective-permute-done.14.refs_5_ = f32[264,128]{1,0:T(8,128)S(1)} collective-permute-done((f32[264,128]{1,0:T(8,128)S(1)}, f32[264,128]{1,0:T(8,128)S(1)}, u32[]{:S(2)}, u32[]{:S(2)}) %collective-permute-start.14) | collective-permute-done | bytes 135200 | tf_op jit(solution)/shard_map/ppermute | solution.py:330
  40.2 0.1 shard_map.49
  40.3 1.4 %collective-permute-start.16 = (f32[8,128]{1,0:T(8,128)S(1)}, f32[8,128]{1,0:T(8,128)S(1)}, u32[]{:S(2)}, u32[]{:S(2)}) collective-permute-start(f32[8,128]{1,0:T(8,128)S(1)} %get-tuple-element.57.refs_0_), channel_id=1, source_target_pairs={{24,0},{0,16},{16,8},{8,24},{25,1},{1,17},{17,9},{9,25},{26,2},{2,... | collective-permute-start | bytes 12296 | tf_op jit(solution)/shard_map/ppermute | solution.py:337
  41.8 2.4 %collective-permute-start.21 = (f32[264,128]{1,0:T(8,128)S(1)}, f32[264,128]{1,0:T(8,128)S(1)}, u32[]{:S(2)}, u32[]{:S(2)}) collective-permute-start(f32[264,128]{1,0:T(8,128)S(1)} %get-tuple-element.59), channel_id=1, source_target_pairs={{16,0},{8,16},{24,8},{0,24},{17,1},{9,17},{25,9},{1,25},{18,2},{10... | collective-permute-start | bytes 405512 | tf_op jit(solution)/shard_map/ppermute | solution.py:337
  44.2 1.5 %collective-permute-start.19 = (f32[256,128]{1,0:T(8,128)S(1)}, f32[256,128]{1,0:T(8,128)S(1)}, u32[]{:S(2)}, u32[]{:S(2)}) collective-permute-start(f32[256,128]{1,0:T(8,128)S(1)} %get-tuple-element.58.refs_2_), channel_id=1, source_target_pairs={{0,6},{1,7},{2,4},{3,5},{4,2},{5,3},{6,0},{7,1},{8,14},{9,15},{10,... | collective-permute-start | bytes 393224 | tf_op jit(solution)/shard_map/ppermute | solution.py:330
  45.7 1.2 %collective-permute-start.18 = (f32[256,128]{1,0:T(8,128)S(1)}, f32[256,128]{1,0:T(8,128)S(1)}, u32[]{:S(2)}, u32[]{:S(2)}) collective-permute-start(f32[256,128]{1,0:T(8,128)S(1)} %get-tuple-element.58.refs_2_), channel_id=1, source_target_pairs={{0,4},{1,5},{2,6},{3,7},{4,0},{5,1},{6,2},{7,3},{8,12},{9,13},{10,... | collective-permute-start | bytes 393224 | tf_op jit(solution)/shard_map/ppermute | solution.py:330
  46.9 0.8 %collective-permute-start.17 = (f32[256,128]{1,0:T(8,128)S(1)}, f32[256,128]{1,0:T(8,128)S(1)}, u32[]{:S(2)}, u32[]{:S(2)}) collective-permute-start(f32[256,128]{1,0:T(8,128)S(1)} %get-tuple-element.58.refs_2_), channel_id=1, source_target_pairs={{0,2},{1,3},{2,0},{3,1},{4,6},{5,7},{6,4},{7,5},{8,10},{9,11},{10,... | collective-permute-start | bytes 393224 | tf_op jit(solution)/shard_map/ppermute | solution.py:330
  47.7 2.9 %collective-permute-done.19.refs_5_ = f32[256,128]{1,0:T(8,128)S(1)} collective-permute-done((f32[256,128]{1,0:T(8,128)S(1)}, f32[256,128]{1,0:T(8,128)S(1)}, u32[]{:S(2)}, u32[]{:S(2)}) %collective-permute-start.19) | collective-permute-done | bytes 131104 | tf_op jit(solution)/shard_map/ppermute | solution.py:330
  50.5 1.2 %collective-permute-done.18.refs_4_ = f32[256,128]{1,0:T(8,128)S(1)} collective-permute-done((f32[256,128]{1,0:T(8,128)S(1)}, f32[256,128]{1,0:T(8,128)S(1)}, u32[]{:S(2)}, u32[]{:S(2)}) %collective-permute-start.18) | collective-permute-done | bytes 131104 | tf_op jit(solution)/shard_map/ppermute | solution.py:330
  51.7 0.2 collective-permute-done.17.refs_3_
  51.9 1.1 %shard_map.50 = (bf16[1024,256]{1,0:T(8,128)(2,1)S(1)}, bf16[256,256]{1,0:T(8,128)(2,1)S(1)}, bf16[256,256]{1,0:T(8,128)(2,1)S(1)}) custom-call(f32[8,128]{1,0:T(8,128)S(1)} %get-tuple-element.57.refs_0_, f32[8,128]{1,0:T(8,128)S(1)} %collective-permute-done.16.refs_1_, f32[256,128]{1,0:T(8,128)S(1)} %get-tuple-element.58.refs_2_, ...), custom_call_target="tpu_custom_call" | custom-call | bytes 1589248 | tf_op jit(solution)/shard_map/pallas_call | solution.py:33
  53.1 0.1 collective-permute-start.23
  53.1 0.7 shard_map.51
  53.9 0.6 collective-permute-start.22
  54.4 1.0 %shard_map.52 = (f32[256,128]{1,0:T(8,128)S(1)}, f32[304,128]{1,0:T(8,128)S(1)}, f32[304,128]{1,0:T(8,128)S(1)}) custom-call(bf16[1024,256]{1,0:T(8,128)(2,1)S(1)} %get-tuple-element.63.refs_0_.refs_10_, bf16[256,2048]{1,0:T(8,128)(2,1)S(1)} %get-tuple-element.40.refs_0_.refs_8_.refs_1_, bf16[256,2048]{1,0:T(8,128)(2,1)S(1)} %get-tuple-element.44.refs_9_.refs_2_, ...), custom_call_target="tpu_custom_call" | custom-call | flops 603979776 | bytes 7258112 | tf_op jit(solution)/shard_map/pallas_call | solution.py:33
  55.5 1.0 %shard_map.53 = (f32[256,128]{1,0:T(8,128)S(1)}, f32[288,128]{1,0:T(8,128)S(1)}, f32[288,128]{1,0:T(8,128)S(1)}, f32[8,128]{1,0:T(8,128)S(1)}) custom-call(bf16[1024,256]{1,0:T(8,128)(2,1)S(1)} %collective-permute-done.23.refs_0_, bf16[256,2048]{1,0:T(8,128)(2,1)S(1)} %get-tuple-element.40.refs_0_.refs_8_.refs_1_, ...), custom_call_target="tpu_custom_call" | custom-call | flops 603979776 | bytes 8474624 | tf_op jit(solution)/shard_map/pallas_call | solution.py:33
  56.5 1.6 %collective-permute-start.26 = (f32[8,128]{1,0:T(8,128)S(1)}, f32[8,128]{1,0:T(8,128)S(1)}, u32[]{:S(2)}, u32[]{:S(2)}) collective-permute-start(f32[8,128]{1,0:T(8,128)S(1)} %get-tuple-element.68), channel_id=1, source_target_pairs={{24,0},{0,16},{16,8},{8,24},{25,1},{1,17},{17,9},{9,25},{26,2},{2,... | collective-permute-start | bytes 12296 | tf_op jit(solution)/shard_map/ppermute | solution.py:337
  58.1 0.8 %collective-permute-start.25 = (f32[8,128]{1,0:T(8,128)S(1)}, f32[8,128]{1,0:T(8,128)S(1)}, u32[]{:S(2)}, u32[]{:S(2)}) collective-permute-start(f32[8,128]{1,0:T(8,128)S(1)} %get-tuple-element.68), channel_id=1, source_target_pairs={{8,0},{24,16},{0,8},{16,24},{9,1},{25,17},{1,9},{17,25},{10,2},{26... | collective-permute-start | bytes 12296 | tf_op jit(solution)/shard_map/ppermute | solution.py:337
  59.0 2.4 %collective-permute-start.24 = (f32[8,128]{1,0:T(8,128)S(1)}, f32[8,128]{1,0:T(8,128)S(1)}, u32[]{:S(2)}, u32[]{:S(2)}) collective-permute-start(f32[8,128]{1,0:T(8,128)S(1)} %get-tuple-element.68), channel_id=1, source_target_pairs={{16,0},{8,16},{24,8},{0,24},{17,1},{9,17},{25,9},{1,25},{18,2},{10... | collective-permute-start | bytes 12296 | tf_op jit(solution)/shard_map/ppermute | solution.py:337
  61.4 0.1 collective-permute-start.28
  61.5 0.5 collective-permute-done.26
  62.0 1.1 %collective-permute-start.29 = (f32[288,128]{1,0:T(8,128)S(1)}, f32[288,128]{1,0:T(8,128)S(1)}, u32[]{:S(2)}, u32[]{:S(2)}) collective-permute-start(f32[288,128]{1,0:T(8,128)S(1)} %get-tuple-element.72), channel_id=1, source_target_pairs={{24,0},{0,16},{16,8},{8,24},{25,1},{1,17},{17,9},{9,25},{26,2},{2,... | collective-permute-start | bytes 442376 | tf_op jit(solution)/shard_map/ppermute | solution.py:337
  63.1 0.5 collective-permute-done.24
  63.6 1.2 %collective-permute-done.27.refs_1_ = f32[8,128]{1,0:T(8,128)S(1)} collective-permute-done((f32[8,128]{1,0:T(8,128)S(1)}, f32[8,128]{1,0:T(8,128)S(1)}, u32[]{:S(2)}, u32[]{:S(2)}) %collective-permute-start.27) | collective-permute-done | bytes 4128 | tf_op jit(solution)/shard_map/ppermute | solution.py:330
  64.7 0.1 shard_map.54
  64.8 0.9 %collective-permute-start.30 = (f32[264,128]{1,0:T(8,128)S(1)}, f32[264,128]{1,0:T(8,128)S(1)}, u32[]{:S(2)}, u32[]{:S(2)}) collective-permute-start(f32[264,128]{1,0:T(8,128)S(1)} %get-tuple-element.73), channel_id=1, source_target_pairs={{0,2},{1,3},{2,0},{3,1},{4,6},{5,7},{6,4},{7,5},{8,10},{9,11},{10,... | collective-permute-start | bytes 405512 | tf_op jit(solution)/shard_map/ppermute | solution.py:330
  65.7 1.5 %collective-permute-start.31 = (f32[264,128]{1,0:T(8,128)S(1)}, f32[264,128]{1,0:T(8,128)S(1)}, u32[]{:S(2)}, u32[]{:S(2)}) collective-permute-start(f32[264,128]{1,0:T(8,128)S(1)} %get-tuple-element.74), channel_id=1, source_target_pairs={{0,4},{1,5},{2,6},{3,7},{4,0},{5,1},{6,2},{7,3},{8,12},{9,13},{10,... | collective-permute-start | bytes 405512 | tf_op jit(solution)/shard_map/ppermute | solution.py:330
  67.2 1.2 %collective-permute-start.32 = (f32[264,128]{1,0:T(8,128)S(1)}, f32[264,128]{1,0:T(8,128)S(1)}, u32[]{:S(2)}, u32[]{:S(2)}) collective-permute-start(f32[264,128]{1,0:T(8,128)S(1)} %get-tuple-element.75), channel_id=1, source_target_pairs={{0,6},{1,7},{2,4},{3,5},{4,2},{5,3},{6,0},{7,1},{8,14},{9,15},{10,... | collective-permute-start | bytes 405512 | tf_op jit(solution)/shard_map/ppermute | solution.py:330
  68.4 2.9 %collective-permute-done.30.refs_4_ = f32[264,128]{1,0:T(8,128)S(1)} collective-permute-done((f32[264,128]{1,0:T(8,128)S(1)}, f32[264,128]{1,0:T(8,128)S(1)}, u32[]{:S(2)}, u32[]{:S(2)}) %collective-permute-start.30) | collective-permute-done | bytes 135200 | tf_op jit(solution)/shard_map/ppermute | solution.py:330
  71.3 1.7 %collective-permute-done.31.refs_5_ = f32[264,128]{1,0:T(8,128)S(1)} collective-permute-done((f32[264,128]{1,0:T(8,128)S(1)}, f32[264,128]{1,0:T(8,128)S(1)}, u32[]{:S(2)}, u32[]{:S(2)}) %collective-permute-start.31) | collective-permute-done | bytes 135200 | tf_op jit(solution)/shard_map/ppermute | solution.py:330
  73.0 1.0 %collective-permute-done.32.refs_6_ = f32[264,128]{1,0:T(8,128)S(1)} collective-permute-done((f32[264,128]{1,0:T(8,128)S(1)}, f32[264,128]{1,0:T(8,128)S(1)}, u32[]{:S(2)}, u32[]{:S(2)}) %collective-permute-start.32) | collective-permute-done | bytes 135200 | tf_op jit(solution)/shard_map/ppermute | solution.py:330
  74.0 1.0 %shard_map.55 = (f32[256,128]{1,0:T(8,128)}, f32[256,128]{1,0:T(8,128)}) custom-call(f32[264,128]{1,0:T(8,128)S(1)} %get-tuple-element.69.refs_0_, f32[256,128]{1,0:T(8,128)S(1)} %get-tuple-element.70.refs_1_, f32[288,128]{1,0:T(8,128)S(1)} %collective-permute-done.28.refs_2_, f32[288,128]{1,0:T(8,128)S(1)} %collective-permute-done.29.refs_3_, ...), custom_call_target="tpu_custom_call" | custom-call | bytes 1228800 | tf_op jit(solution)/shard_map/pallas_call | solution.py:33
  (23 shorter events, 0.1 us)
Async XLA Ops:
  1.6 16.1 %collective-permute-start.1 = (bf16[256,512]{1,0:T(8,128)(2,1)S(1)}, bf16[256,512]{1,0:T(8,128)(2,1)S(1)}, u32[]{:S(2)}, u32[]{:S(2)}) collective-permute-start(bf16[256,512]{1,0:T(8,128)(2,1)S(1)} %constant_dynamic-slice_fusion.rows.rows_ref), channel_id=1, source_target_pairs={{16,0},{8,16},{24,8},{0,24},{17,1},{9,17},{25,9},{1,25},{18,2},{10... | collective-permute-start | bytes 786440 | tf_op jit(solution)/shard_map/ppermute | solution.py:337
  6.7 0.9 %copy-start.1 = (f32[256,128]{1,0:T(8,128)S(1)}, f32[256,128]{1,0:T(8,128)}, u32[]{:S(2)}) copy-start(f32[256,128]{1,0:T(8,128)} %logits.1) | copy-start | bytes 393220
  7.8 16.3 %collective-permute-start.9 = (bf16[256,768]{1,0:T(8,128)(2,1)S(1)}, bf16[256,768]{1,0:T(8,128)(2,1)S(1)}, u32[]{:S(2)}, u32[]{:S(2)}) collective-permute-start(bf16[256,768]{1,0:T(8,128)(2,1)S(1)} %get-tuple-element.45), channel_id=1, source_target_pairs={{0,8},{8,0},{16,24},{24,16},{1,9},{9,1},{17,25},{25,17},{2,10},{10... | collective-permute-start | bytes 1179656 | tf_op jit(solution)/shard_map/ppermute | solution.py:337
  7.8 10.8 %collective-permute-start.4 = (bf16[256,256]{1,0:T(8,128)(2,1)S(1)}, bf16[256,256]{1,0:T(8,128)(2,1)S(1)}, u32[]{:S(2)}, u32[]{:S(2)}) collective-permute-start(bf16[256,256]{1,0:T(8,128)(2,1)S(1)} %get-tuple-element.43.refs_0_.own), channel_id=1, source_target_pairs={{0,6},{1,7},{2,4},{3,5},{4,2},{5,3},{6,0},{7,1},{8,14},{9,15},{10,... | collective-permute-start | bytes 393224 | tf_op jit(solution)/shard_map/ppermute | solution.py:330
  10.4 8.4 %collective-permute-start.3 = (bf16[256,256]{1,0:T(8,128)(2,1)S(1)}, bf16[256,256]{1,0:T(8,128)(2,1)S(1)}, u32[]{:S(2)}, u32[]{:S(2)}) collective-permute-start(bf16[256,256]{1,0:T(8,128)(2,1)S(1)} %get-tuple-element.43.refs_0_.own), channel_id=1, source_target_pairs={{0,4},{1,5},{2,6},{3,7},{4,0},{5,1},{6,2},{7,3},{8,12},{9,13},{10,... | collective-permute-start | bytes 393224 | tf_op jit(solution)/shard_map/ppermute | solution.py:330
  10.9 8.4 %collective-permute-start.2 = (bf16[256,256]{1,0:T(8,128)(2,1)S(1)}, bf16[256,256]{1,0:T(8,128)(2,1)S(1)}, u32[]{:S(2)}, u32[]{:S(2)}) collective-permute-start(bf16[256,256]{1,0:T(8,128)(2,1)S(1)} %get-tuple-element.43.refs_0_.own), channel_id=1, source_target_pairs={{0,2},{1,3},{2,0},{3,1},{4,6},{5,7},{6,4},{7,5},{8,10},{9,11},{10,... | collective-permute-start | bytes 393224 | tf_op jit(solution)/shard_map/ppermute | solution.py:330
  11.4 1.6 %copy-start = (bf16[2048,512]{1,0:T(8,128)(2,1)S(1)}, bf16[2048,512]{1,0:T(8,128)(2,1)}, u32[]{:S(2)}) copy-start(bf16[2048,512]{1,0:T(8,128)(2,1)} %plane_ref.5) | copy-start | bytes 6291460
  17.7 9.5 %collective-permute-start = (bf16[272,256]{1,0:T(8,128)(2,1)S(1)}, bf16[272,256]{1,0:T(8,128)(2,1)S(1)}, u32[]{:S(2)}, u32[]{:S(2)}) collective-permute-start(bf16[272,256]{1,0:T(8,128)(2,1)S(1)} %get-tuple-element.39), channel_id=1, source_target_pairs={{16,0},{8,16},{24,8},{0,24},{17,1},{9,17},{25,9},{1,25},{18,2},{10... | collective-permute-start | bytes 417800 | tf_op jit(solution)/shard_map/ppermute | solution.py:337
  18.6 6.3 %collective-permute-start.5 = (bf16[256,256]{1,0:T(8,128)(2,1)S(1)}, bf16[256,256]{1,0:T(8,128)(2,1)S(1)}, u32[]{:S(2)}, u32[]{:S(2)}) collective-permute-start(bf16[256,256]{1,0:T(8,128)(2,1)S(1)} %get-tuple-element.43.refs_0_.own), channel_id=1, source_target_pairs={{0,1},{1,0},{2,3},{3,2},{4,5},{5,4},{6,7},{7,6},{8,9},{9,8},{10,11... | collective-permute-start | bytes 393224 | tf_op jit(solution)/shard_map/ppermute | solution.py:330
  18.7 6.2 %collective-permute-start.8 = (bf16[256,256]{1,0:T(8,128)(2,1)S(1)}, bf16[256,256]{1,0:T(8,128)(2,1)S(1)}, u32[]{:S(2)}, u32[]{:S(2)}) collective-permute-start(bf16[256,256]{1,0:T(8,128)(2,1)S(1)} %collective-permute-done.4.refs_3_), channel_id=1, source_target_pairs={{0,1},{1,0},{2,3},{3,2},{4,5},{5,4},{6,7},{7,6},{8,9},{9,8},{10,11... | collective-permute-start | bytes 393224 | tf_op jit(solution)/shard_map/ppermute | solution.py:330
  19.2 5.7 %collective-permute-start.7 = (bf16[256,256]{1,0:T(8,128)(2,1)S(1)}, bf16[256,256]{1,0:T(8,128)(2,1)S(1)}, u32[]{:S(2)}, u32[]{:S(2)}) collective-permute-start(bf16[256,256]{1,0:T(8,128)(2,1)S(1)} %collective-permute-done.3.refs_2_), channel_id=1, source_target_pairs={{0,1},{1,0},{2,3},{3,2},{4,5},{5,4},{6,7},{7,6},{8,9},{9,8},{10,11... | collective-permute-start | bytes 393224 | tf_op jit(solution)/shard_map/ppermute | solution.py:330
  24.1 1.3 %collective-permute-start.6 = (bf16[256,256]{1,0:T(8,128)(2,1)S(1)}, bf16[256,256]{1,0:T(8,128)(2,1)S(1)}, u32[]{:S(2)}, u32[]{:S(2)}) collective-permute-start(bf16[256,256]{1,0:T(8,128)(2,1)S(1)} %collective-permute-done.2.refs_1_), channel_id=1, source_target_pairs={{0,1},{1,0},{2,3},{3,2},{4,5},{5,4},{6,7},{7,6},{8,9},{9,8},{10,11... | collective-permute-start | bytes 393224 | tf_op jit(solution)/shard_map/ppermute | solution.py:330
  28.1 2.0 %collective-permute-start.10 = (f32[1032,128]{1,0:T(8,128)S(1)}, f32[1032,128]{1,0:T(8,128)S(1)}, u32[]{:S(2)}, u32[]{:S(2)}) collective-permute-start(f32[1032,128]{1,0:T(8,128)S(1)} %get-tuple-element.52), channel_id=1, source_target_pairs={{0,1},{1,0},{2,3},{3,2},{4,5},{5,4},{6,7},{7,6},{8,9},{9,8},{10,11... | collective-permute-start | bytes 1585160 | tf_op jit(solution)/shard_map/ppermute | solution.py:330
  28.3 9.6 %collective-permute-start.11 = (f32[304,128]{1,0:T(8,128)S(1)}, f32[304,128]{1,0:T(8,128)S(1)}, u32[]{:S(2)}, u32[]{:S(2)}) collective-permute-start(f32[304,128]{1,0:T(8,128)S(1)} %get-tuple-element.49.refs_1_), channel_id=1, source_target_pairs={{0,8},{8,0},{16,24},{24,16},{1,9},{9,1},{17,25},{25,17},{2,10},{10... | collective-permute-start | bytes 466952 | tf_op jit(solution)/shard_map/ppermute | solution.py:337
  28.6 9.3 %collective-permute-start.12 = (f32[304,128]{1,0:T(8,128)S(1)}, f32[304,128]{1,0:T(8,128)S(1)}, u32[]{:S(2)}, u32[]{:S(2)}) collective-permute-start(f32[304,128]{1,0:T(8,128)S(1)} %get-tuple-element.50.refs_2_), channel_id=1, source_target_pairs={{24,0},{0,16},{16,8},{8,24},{25,1},{1,17},{17,9},{9,25},{26,2},{2,... | collective-permute-start | bytes 466952 | tf_op jit(solution)/shard_map/ppermute | solution.py:337
  30.1 7.8 %collective-permute-start.13 = (f32[264,128]{1,0:T(8,128)S(1)}, f32[264,128]{1,0:T(8,128)S(1)}, u32[]{:S(2)}, u32[]{:S(2)}) collective-permute-start(f32[264,128]{1,0:T(8,128)S(1)} %get-tuple-element.54), channel_id=1, source_target_pairs={{0,2},{1,3},{2,0},{3,1},{4,6},{5,7},{6,4},{7,5},{8,10},{9,11},{10,... | collective-permute-start | bytes 405512 | tf_op jit(solution)/shard_map/ppermute | solution.py:330
  32.0 8.3 %collective-permute-start.14 = (f32[264,128]{1,0:T(8,128)S(1)}, f32[264,128]{1,0:T(8,128)S(1)}, u32[]{:S(2)}, u32[]{:S(2)}) collective-permute-start(f32[264,128]{1,0:T(8,128)S(1)} %get-tuple-element.55), channel_id=1, source_target_pairs={{0,4},{1,5},{2,6},{3,7},{4,0},{5,1},{6,2},{7,3},{8,12},{9,13},{10,... | collective-permute-start | bytes 405512 | tf_op jit(solution)/shard_map/ppermute | solution.py:330
  33.5 6.7 %collective-permute-start.15 = (f32[264,128]{1,0:T(8,128)S(1)}, f32[264,128]{1,0:T(8,128)S(1)}, u32[]{:S(2)}, u32[]{:S(2)}) collective-permute-start(f32[264,128]{1,0:T(8,128)S(1)} %get-tuple-element.56), channel_id=1, source_target_pairs={{0,6},{1,7},{2,4},{3,5},{4,2},{5,3},{6,0},{7,1},{8,14},{9,15},{10,... | collective-permute-start | bytes 405512 | tf_op jit(solution)/shard_map/ppermute | solution.py:330
  40.3 6.6 %collective-permute-start.16 = (f32[8,128]{1,0:T(8,128)S(1)}, f32[8,128]{1,0:T(8,128)S(1)}, u32[]{:S(2)}, u32[]{:S(2)}) collective-permute-start(f32[8,128]{1,0:T(8,128)S(1)} %get-tuple-element.57.refs_0_), channel_id=1, source_target_pairs={{24,0},{0,16},{16,8},{8,24},{25,1},{1,17},{17,9},{9,25},{26,2},{2,... | collective-permute-start | bytes 12296 | tf_op jit(solution)/shard_map/ppermute | solution.py:337
  41.8 10.2 %collective-permute-start.21 = (f32[264,128]{1,0:T(8,128)S(1)}, f32[264,128]{1,0:T(8,128)S(1)}, u32[]{:S(2)}, u32[]{:S(2)}) collective-permute-start(f32[264,128]{1,0:T(8,128)S(1)} %get-tuple-element.59), channel_id=1, source_target_pairs={{16,0},{8,16},{24,8},{0,24},{17,1},{9,17},{25,9},{1,25},{18,2},{10... | collective-permute-start | bytes 405512 | tf_op jit(solution)/shard_map/ppermute | solution.py:337
  44.2 7.8 %collective-permute-start.20 = (f32[264,128]{1,0:T(8,128)S(1)}, f32[264,128]{1,0:T(8,128)S(1)}, u32[]{:S(2)}, u32[]{:S(2)}) collective-permute-start(f32[264,128]{1,0:T(8,128)S(1)} %get-tuple-element.59), channel_id=1, source_target_pairs={{0,8},{8,0},{16,24},{24,16},{1,9},{9,1},{17,25},{25,17},{2,10},{10... | collective-permute-start | bytes 405512 | tf_op jit(solution)/shard_map/ppermute | solution.py:337
  44.2 6.3 %collective-permute-start.19 = (f32[256,128]{1,0:T(8,128)S(1)}, f32[256,128]{1,0:T(8,128)S(1)}, u32[]{:S(2)}, u32[]{:S(2)}) collective-permute-start(f32[256,128]{1,0:T(8,128)S(1)} %get-tuple-element.58.refs_2_), channel_id=1, source_target_pairs={{0,6},{1,7},{2,4},{3,5},{4,2},{5,3},{6,0},{7,1},{8,14},{9,15},{10,... | collective-permute-start | bytes 393224 | tf_op jit(solution)/shard_map/ppermute | solution.py:330
  45.7 6.1 %collective-permute-start.18 = (f32[256,128]{1,0:T(8,128)S(1)}, f32[256,128]{1,0:T(8,128)S(1)}, u32[]{:S(2)}, u32[]{:S(2)}) collective-permute-start(f32[256,128]{1,0:T(8,128)S(1)} %get-tuple-element.58.refs_2_), channel_id=1, source_target_pairs={{0,4},{1,5},{2,6},{3,7},{4,0},{5,1},{6,2},{7,3},{8,12},{9,13},{10,... | collective-permute-start | bytes 393224 | tf_op jit(solution)/shard_map/ppermute | solution.py:330
  46.9 5.1 %collective-permute-start.17 = (f32[256,128]{1,0:T(8,128)S(1)}, f32[256,128]{1,0:T(8,128)S(1)}, u32[]{:S(2)}, u32[]{:S(2)}) collective-permute-start(f32[256,128]{1,0:T(8,128)S(1)} %get-tuple-element.58.refs_2_), channel_id=1, source_target_pairs={{0,2},{1,3},{2,0},{3,1},{4,6},{5,7},{6,4},{7,5},{8,10},{9,11},{10,... | collective-permute-start | bytes 393224 | tf_op jit(solution)/shard_map/ppermute | solution.py:330
  53.1 2.4 %collective-permute-start.23 = (bf16[1024,256]{1,0:T(8,128)(2,1)S(1)}, bf16[1024,256]{1,0:T(8,128)(2,1)S(1)}, u32[]{:S(2)}, u32[]{:S(2)}) collective-permute-start(bf16[1024,256]{1,0:T(8,128)(2,1)S(1)} %get-tuple-element.63.refs_0_.refs_10_), channel_id=1, source_target_pairs={{0,1},{1,0},{2,3},{3,2},{4,5},{5,4},{6,7},{7,6},{8,9},{9,8},{10,11... | collective-permute-start | bytes 1572872 | tf_op jit(solution)/shard_map/ppermute | solution.py:330
  53.9 9.7 %collective-permute-start.22 = (f32[1024,128]{1,0:T(8,128)S(1)}, f32[1024,128]{1,0:T(8,128)S(1)}, u32[]{:S(2)}, u32[]{:S(2)}) collective-permute-start(f32[1024,128]{1,0:T(8,128)S(1)} %get-tuple-element.62), channel_id=1, source_target_pairs={{0,1},{1,0},{2,3},{3,2},{4,5},{5,4},{6,7},{7,6},{8,9},{9,8},{10,11... | collective-permute-start | bytes 1572872 | tf_op jit(solution)/shard_map/ppermute | solution.py:330
  56.5 5.5 %collective-permute-start.26 = (f32[8,128]{1,0:T(8,128)S(1)}, f32[8,128]{1,0:T(8,128)S(1)}, u32[]{:S(2)}, u32[]{:S(2)}) collective-permute-start(f32[8,128]{1,0:T(8,128)S(1)} %get-tuple-element.68), channel_id=1, source_target_pairs={{24,0},{0,16},{16,8},{8,24},{25,1},{1,17},{17,9},{9,25},{26,2},{2,... | collective-permute-start | bytes 12296 | tf_op jit(solution)/shard_map/ppermute | solution.py:337
  58.1 5.0 %collective-permute-start.25 = (f32[8,128]{1,0:T(8,128)S(1)}, f32[8,128]{1,0:T(8,128)S(1)}, u32[]{:S(2)}, u32[]{:S(2)}) collective-permute-start(f32[8,128]{1,0:T(8,128)S(1)} %get-tuple-element.68), channel_id=1, source_target_pairs={{8,0},{24,16},{0,8},{16,24},{9,1},{25,17},{1,9},{17,25},{10,2},{26... | collective-permute-start | bytes 12296 | tf_op jit(solution)/shard_map/ppermute | solution.py:337
  59.0 4.6 %collective-permute-start.24 = (f32[8,128]{1,0:T(8,128)S(1)}, f32[8,128]{1,0:T(8,128)S(1)}, u32[]{:S(2)}, u32[]{:S(2)}) collective-permute-start(f32[8,128]{1,0:T(8,128)S(1)} %get-tuple-element.68), channel_id=1, source_target_pairs={{16,0},{8,16},{24,8},{0,24},{17,1},{9,17},{25,9},{1,25},{18,2},{10... | collective-permute-start | bytes 12296 | tf_op jit(solution)/shard_map/ppermute | solution.py:337
  61.4 12.6 %collective-permute-start.28 = (f32[288,128]{1,0:T(8,128)S(1)}, f32[288,128]{1,0:T(8,128)S(1)}, u32[]{:S(2)}, u32[]{:S(2)}) collective-permute-start(f32[288,128]{1,0:T(8,128)S(1)} %get-tuple-element.71), channel_id=1, source_target_pairs={{0,8},{8,0},{16,24},{24,16},{1,9},{9,1},{17,25},{25,17},{2,10},{10... | collective-permute-start | bytes 442376 | tf_op jit(solution)/shard_map/ppermute | solution.py:337
  62.0 12.1 %collective-permute-start.29 = (f32[288,128]{1,0:T(8,128)S(1)}, f32[288,128]{1,0:T(8,128)S(1)}, u32[]{:S(2)}, u32[]{:S(2)}) collective-permute-start(f32[288,128]{1,0:T(8,128)S(1)} %get-tuple-element.72), channel_id=1, source_target_pairs={{24,0},{0,16},{16,8},{8,24},{25,1},{1,17},{17,9},{9,25},{26,2},{2,... | collective-permute-start | bytes 442376 | tf_op jit(solution)/shard_map/ppermute | solution.py:337
  63.6 1.2 %collective-permute-start.27 = (f32[8,128]{1,0:T(8,128)S(1)}, f32[8,128]{1,0:T(8,128)S(1)}, u32[]{:S(2)}, u32[]{:S(2)}) collective-permute-start(f32[8,128]{1,0:T(8,128)S(1)} %add_add_fusion.refs_0_), channel_id=1, source_target_pairs={{0,1},{1,0},{2,3},{3,2},{4,5},{5,4},{6,7},{7,6},{8,9},{9,8},{10,11... | collective-permute-start | bytes 12296 | tf_op jit(solution)/shard_map/ppermute | solution.py:330
  64.8 6.5 %collective-permute-start.30 = (f32[264,128]{1,0:T(8,128)S(1)}, f32[264,128]{1,0:T(8,128)S(1)}, u32[]{:S(2)}, u32[]{:S(2)}) collective-permute-start(f32[264,128]{1,0:T(8,128)S(1)} %get-tuple-element.73), channel_id=1, source_target_pairs={{0,2},{1,3},{2,0},{3,1},{4,6},{5,7},{6,4},{7,5},{8,10},{9,11},{10,... | collective-permute-start | bytes 405512 | tf_op jit(solution)/shard_map/ppermute | solution.py:330
  65.7 7.3 %collective-permute-start.31 = (f32[264,128]{1,0:T(8,128)S(1)}, f32[264,128]{1,0:T(8,128)S(1)}, u32[]{:S(2)}, u32[]{:S(2)}) collective-permute-start(f32[264,128]{1,0:T(8,128)S(1)} %get-tuple-element.74), channel_id=1, source_target_pairs={{0,4},{1,5},{2,6},{3,7},{4,0},{5,1},{6,2},{7,3},{8,12},{9,13},{10,... | collective-permute-start | bytes 405512 | tf_op jit(solution)/shard_map/ppermute | solution.py:330
  67.2 6.8 %collective-permute-start.32 = (f32[264,128]{1,0:T(8,128)S(1)}, f32[264,128]{1,0:T(8,128)S(1)}, u32[]{:S(2)}, u32[]{:S(2)}) collective-permute-start(f32[264,128]{1,0:T(8,128)S(1)} %get-tuple-element.75), channel_id=1, source_target_pairs={{0,6},{1,7},{2,4},{3,5},{4,2},{5,3},{6,0},{7,1},{8,14},{9,15},{10,... | collective-permute-start | bytes 405512 | tf_op jit(solution)/shard_map/ppermute | solution.py:330

commit v14 on v13

--- a/solution.py
+++ b/solution.py
@@ -121,19 +121,17 @@
     own, outs = refs[:weights], refs[weights + unused :]
     n = blocks[0].shape[0]
     clusters = members[0].shape[1] // 2
+    whole_members = jnp.concatenate([piece[...] for piece in members], axis=0)
     for i, out in enumerate(outs[: kernels // 2]):
-        both, rest, start = None, None, at
-        for piece in members:
-            columns = slice(start, start + piece.shape[0])
-            start += piece.shape[0]
-            a = jnp.dot(blocks[2 * i][:, columns], piece[...], preferred_element_type=F32)
-            b = jnp.dot(
-                blocks[2 * i + 1][:, columns],
-                piece[:, :clusters],
-                preferred_element_type=F32,
-            )
-            both = a if both is None else both + a
-            rest = b if rest is None else rest + b
+        columns = slice(at, at + whole_members.shape[0])
+        both = jnp.dot(
+            blocks[2 * i][:, columns], whole_members, preferred_element_type=F32
+        )
+        rest = jnp.dot(
+            blocks[2 * i + 1][:, columns],
+            whole_members[:, :clusters],
+            preferred_element_type=F32,
+        )
         s = both[:, :clusters] + (both[:, clusters:] + rest)
         if partials:
             s += before[i][:n, :]

time: 75.2 us -> 75.2 us (level)
  no operation moved by 1% of the time
where the time goes in v14:
time: 75.2 us; the launch traced here: 75 us
  starting transfers between devices  32.2 us (43%)
  waiting for transfers between devices  28 us (37%)
  Pallas kernels  10.5 us (14%)
  local copies, waits for them, and re-layouts  3.47 us (5%)
  between operations  0.82 us (1%)
    ppermute x13, starting transfers between devices, shift(): return lax.ppermute(x, 'row', pairs)  16.5 us
    ppermute x20, starting transfers between devices, by_col(): return lax.ppermute(x, 'col', [(i, i ^ mask) for i in range(cols)])  15.6 us
    ppermute x20, waiting for transfers between devices, by_col(): return lax.ppermute(x, 'col', [(i, i ^ mask) for i in range(cols)])  14.2 us
    ppermute x13, waiting for transfers between devices, shift(): return lax.ppermute(x, 'row', pairs)  13.8 us
    pallas_call x15, Pallas kernels, call(): pl.pallas_call(body, in_specs=specs or [VMEM] * len(args), out_specs=[VME...  10.5 us
    unnamed x4, local copies, waits for them, and re-layouts  2.49 us
  transfers between devices with their start and end apart: 33, of which 15 were waited for; matrix products, arithmetic and copies ran while one was open for 0% of the time, Pallas kernels for 10%

profile of v14, /device:TPU:0, one launch (start us, length us, event | category | flops | bytes accessed | tf_op | source)
XLA Modules:
  0.0 75.0 jit_solution(13555454636142221493)
XLA Ops:
  0.6 1.0 %constant_dynamic-slice_fusion.rows.rows_ref = bf16[256,512]{1,0:T(8,128)(2,1)S(1)} fusion(bf16[2048,512]{1,0:T(8,128)(2,1)} %plane_ref.5, s32[]{:T(128)S(6)} %select_n.3), kind=kLoop, calls=%fused_computation.1 | loop fusion | bytes 524292 | tf_op jit(solution)/shard_map/dynamic_slice | solution.py:338
  1.6 5.1 %collective-permute-start.1 = (bf16[256,512]{1,0:T(8,128)(2,1)S(1)}, bf16[256,512]{1,0:T(8,128)(2,1)S(1)}, u32[]{:S(2)}, u32[]{:S(2)}) collective-permute-start(bf16[256,512]{1,0:T(8,128)(2,1)S(1)} %constant_dynamic-slice_fusion.rows.rows_ref), channel_id=1, source_target_pairs={{16,0},{8,16},{24,8},{0,24},{17,1},{9,17},{25,9},{1,25},{18,2},{10... | collective-permute-start | bytes 786440 | tf_op jit(solution)/shard_map/ppermute | solution.py:335
  6.7 0.9 %copy-done.1 = f32[256,128]{1,0:T(8,128)S(1)} copy-done((f32[256,128]{1,0:T(8,128)S(1)}, f32[256,128]{1,0:T(8,128)}, u32[]{:S(2)}) %copy-start.1) | copy-done | bytes 131096
  7.6 0.1 shard_map.41
  7.8 0.1 collective-permute-start.9
  7.8 2.5 %collective-permute-start.4 = (bf16[256,256]{1,0:T(8,128)(2,1)S(1)}, bf16[256,256]{1,0:T(8,128)(2,1)S(1)}, u32[]{:S(2)}, u32[]{:S(2)}) collective-permute-start(bf16[256,256]{1,0:T(8,128)(2,1)S(1)} %get-tuple-element.43.refs_0_.own), channel_id=1, source_target_pairs={{0,6},{1,7},{2,4},{3,5},{4,2},{5,3},{6,0},{7,1},{8,14},{9,15},{10,... | collective-permute-start | bytes 393224 | tf_op jit(solution)/shard_map/ppermute | solution.py:328
  10.4 0.5 collective-permute-start.3
  10.9 0.5 collective-permute-start.2
  11.4 1.6 %copy-done = bf16[2048,512]{1,0:T(8,128)(2,1)S(1)} copy-done((bf16[2048,512]{1,0:T(8,128)(2,1)S(1)}, bf16[2048,512]{1,0:T(8,128)(2,1)}, u32[]{:S(2)}) %copy-start) | copy-done | bytes 2097176
  13.0 0.9 %shard_map.42 = (bf16[256,2048]{1,0:T(8,128)(2,1)S(1)}, bf16[256,2048]{1,0:T(8,128)(2,1)S(1)}) custom-call(s32[1]{0:T(128)} %bitcast.column_ref, bf16[256,512]{1,0:T(8,128)(2,1)S(1)} %constant_dynamic-slice_fusion.rows.rows_ref, bf16[2048,512]{1,0:T(8,128)(2,1)S(1)} %copy-done), custom_call_target="tpu_custom_call" | custom-call | flops 536870912 | bytes 4456452 | tf_op jit(solution)/shard_map/pallas_call | solution.py:33
  13.9 3.9 %collective-permute-done.1.rows_ref = bf16[256,512]{1,0:T(8,128)(2,1)S(1)} collective-permute-done((bf16[256,512]{1,0:T(8,128)(2,1)S(1)}, bf16[256,512]{1,0:T(8,128)(2,1)S(1)}, u32[]{:S(2)}, u32[]{:S(2)}) %collective-permute-start.1) | collective-permute-done | bytes 262176 | tf_op jit(solution)/shard_map/ppermute | solution.py:335
  17.7 0.9 %shard_map.43 = (bf16[256,2048]{1,0:T(8,128)(2,1)S(1)}, bf16[256,2048]{1,0:T(8,128)(2,1)S(1)}) custom-call(s32[1]{0:T(128)} %bitcast.column_ref, bf16[256,512]{1,0:T(8,128)(2,1)S(1)} %collective-permute-done.1.rows_ref, bf16[2048,512]{1,0:T(8,128)(2,1)S(1)} %copy-done, bf16[256,2048]{1,0:T(8,128)(2,1)S(1)} %get-tuple-element.40.refs_0_.refs_8_.refs_1_), custom_call_target="tpu_custom_call" | custom-call | flops 1449132032 | bytes 5505028 | tf_op jit(solution)/shard_map/pallas_call | solution.py:33
  18.6 0.0 collective-permute-done.4.refs_3_
  18.6 0.1 collective-permute-start.5
  18.7 0.5 collective-permute-start.8
  19.2 0.0 collective-permute-done.2.refs_1_
  19.2 0.1 collective-permute-start.7
  19.3 4.8 %collective-permute-done.9.rows_ref.refs_3_ = bf16[256,768]{1,0:T(8,128)(2,1)S(1)} collective-permute-done((bf16[256,768]{1,0:T(8,128)(2,1)S(1)}, bf16[256,768]{1,0:T(8,128)(2,1)S(1)}, u32[]{:S(2)}, u32[]{:S(2)}) %collective-permute-start.9) | collective-permute-done | bytes 393248 | tf_op jit(solution)/shard_map/ppermute | solution.py:335
  24.1 0.9 %shard_map.44 = (bf16[256,2048]{1,0:T(8,128)(2,1)S(1)}, bf16[256,2048]{1,0:T(8,128)(2,1)S(1)}) custom-call(s32[1]{0:T(128)} %bitcast.column_ref, bf16[256,768]{1,0:T(8,128)(2,1)S(1)} %collective-permute-done.9.rows_ref.refs_3_, bf16[2048,512]{1,0:T(8,128)(2,1)S(1)} %copy-done, bf16[256,2048]{1,0:T(8,128)(2,1)S(1)} %get-tuple-element.41.refs_0_.refs_12_.refs_1_.refs_5_), custom_call_target="tpu_custom_call" | custom-call | flops 1449132032 | bytes 5636100 | tf_op jit(solution)/shard_map/pallas_call | solution.py:33
  25.0 0.4 collective-permute-done.6.refs_5_
  25.4 1.8 %shard_map.45 = (f32[256,128]{1,0:T(8,128)S(1)}, f32[304,128]{1,0:T(8,128)S(1)}, f32[304,128]{1,0:T(8,128)S(1)}) custom-call(bf16[256,256]{1,0:T(8,128)(2,1)S(1)} %get-tuple-element.43.refs_0_.own, bf16[256,256]{1,0:T(8,128)(2,1)S(1)} %collective-permute-done.2.refs_1_, bf16[256,256]{1,0:T(8,128)(2,1)S(1)} %collective-permute-done.3.refs_2_, ...), custom_call_target="tpu_custom_call" | custom-call | tf_op jit(solution)/shard_map/pallas_call | solution.py:33
  27.2 0.1 shard_map.46.refs_3_.refs_0_
  27.3 0.7 shard_map.47
  28.1 0.2 collective-permute-start.10
  28.3 0.3 collective-permute-start.11
  28.6 1.1 %collective-permute-start.12 = (f32[304,128]{1,0:T(8,128)S(1)}, f32[304,128]{1,0:T(8,128)S(1)}, u32[]{:S(2)}, u32[]{:S(2)}) collective-permute-start(f32[304,128]{1,0:T(8,128)S(1)} %get-tuple-element.50.refs_2_), channel_id=1, source_target_pairs={{24,0},{0,16},{16,8},{8,24},{25,1},{1,17},{17,9},{9,25},{26,2},{2,... | collective-permute-start | bytes 466952 | tf_op jit(solution)/shard_map/ppermute | solution.py:335
  29.7 0.4 collective-permute-done.10.received
  30.1 0.1 shard_map.48
  30.1 1.8 %collective-permute-start.13 = (f32[264,128]{1,0:T(8,128)S(1)}, f32[264,128]{1,0:T(8,128)S(1)}, u32[]{:S(2)}, u32[]{:S(2)}) collective-permute-start(f32[264,128]{1,0:T(8,128)S(1)} %get-tuple-element.54), channel_id=1, source_target_pairs={{0,2},{1,3},{2,0},{3,1},{4,6},{5,7},{6,4},{7,5},{8,10},{9,11},{10,... | collective-permute-start | bytes 405512 | tf_op jit(solution)/shard_map/ppermute | solution.py:328
  32.0 1.5 %collective-permute-start.14 = (f32[264,128]{1,0:T(8,128)S(1)}, f32[264,128]{1,0:T(8,128)S(1)}, u32[]{:S(2)}, u32[]{:S(2)}) collective-permute-start(f32[264,128]{1,0:T(8,128)S(1)} %get-tuple-element.55), channel_id=1, source_target_pairs={{0,4},{1,5},{2,6},{3,7},{4,0},{5,1},{6,2},{7,3},{8,12},{9,13},{10,... | collective-permute-start | bytes 405512 | tf_op jit(solution)/shard_map/ppermute | solution.py:328
  33.5 0.2 collective-permute-start.15
  33.7 4.2 %collective-permute-done.11.refs_2_ = f32[304,128]{1,0:T(8,128)S(1)} collective-permute-done((f32[304,128]{1,0:T(8,128)S(1)}, f32[304,128]{1,0:T(8,128)S(1)}, u32[]{:S(2)}, u32[]{:S(2)}) %collective-permute-start.11) | collective-permute-done | bytes 155680 | tf_op jit(solution)/shard_map/ppermute | solution.py:335
  37.9 2.3 %collective-permute-done.14.refs_5_ = f32[264,128]{1,0:T(8,128)S(1)} collective-permute-done((f32[264,128]{1,0:T(8,128)S(1)}, f32[264,128]{1,0:T(8,128)S(1)}, u32[]{:S(2)}, u32[]{:S(2)}) %collective-permute-start.14) | collective-permute-done | bytes 135200 | tf_op jit(solution)/shard_map/ppermute | solution.py:328
  40.2 0.1 shard_map.49
  40.3 1.4 %collective-permute-start.16 = (f32[8,128]{1,0:T(8,128)S(1)}, f32[8,128]{1,0:T(8,128)S(1)}, u32[]{:S(2)}, u32[]{:S(2)}) collective-permute-start(f32[8,128]{1,0:T(8,128)S(1)} %get-tuple-element.57.refs_0_), channel_id=1, source_target_pairs={{24,0},{0,16},{16,8},{8,24},{25,1},{1,17},{17,9},{9,25},{26,2},{2,... | collective-permute-start | bytes 12296 | tf_op jit(solution)/shard_map/ppermute | solution.py:335
  41.7 2.4 %collective-permute-start.21 = (f32[264,128]{1,0:T(8,128)S(1)}, f32[264,128]{1,0:T(8,128)S(1)}, u32[]{:S(2)}, u32[]{:S(2)}) collective-permute-start(f32[264,128]{1,0:T(8,128)S(1)} %get-tuple-element.59), channel_id=1, source_target_pairs={{16,0},{8,16},{24,8},{0,24},{17,1},{9,17},{25,9},{1,25},{18,2},{10... | collective-permute-start | bytes 405512 | tf_op jit(solution)/shard_map/ppermute | solution.py:335
  44.2 1.5 %collective-permute-start.19 = (f32[256,128]{1,0:T(8,128)S(1)}, f32[256,128]{1,0:T(8,128)S(1)}, u32[]{:S(2)}, u32[]{:S(2)}) collective-permute-start(f32[256,128]{1,0:T(8,128)S(1)} %get-tuple-element.58.refs_2_), channel_id=1, source_target_pairs={{0,6},{1,7},{2,4},{3,5},{4,2},{5,3},{6,0},{7,1},{8,14},{9,15},{10,... | collective-permute-start | bytes 393224 | tf_op jit(solution)/shard_map/ppermute | solution.py:328
  45.7 1.2 %collective-permute-start.18 = (f32[256,128]{1,0:T(8,128)S(1)}, f32[256,128]{1,0:T(8,128)S(1)}, u32[]{:S(2)}, u32[]{:S(2)}) collective-permute-start(f32[256,128]{1,0:T(8,128)S(1)} %get-tuple-element.58.refs_2_), channel_id=1, source_target_pairs={{0,4},{1,5},{2,6},{3,7},{4,0},{5,1},{6,2},{7,3},{8,12},{9,13},{10,... | collective-permute-start | bytes 393224 | tf_op jit(solution)/shard_map/ppermute | solution.py:328
  46.9 0.8 %collective-permute-start.17 = (f32[256,128]{1,0:T(8,128)S(1)}, f32[256,128]{1,0:T(8,128)S(1)}, u32[]{:S(2)}, u32[]{:S(2)}) collective-permute-start(f32[256,128]{1,0:T(8,128)S(1)} %get-tuple-element.58.refs_2_), channel_id=1, source_target_pairs={{0,2},{1,3},{2,0},{3,1},{4,6},{5,7},{6,4},{7,5},{8,10},{9,11},{10,... | collective-permute-start | bytes 393224 | tf_op jit(solution)/shard_map/ppermute | solution.py:328
  47.7 2.9 %collective-permute-done.19.refs_5_ = f32[256,128]{1,0:T(8,128)S(1)} collective-permute-done((f32[256,128]{1,0:T(8,128)S(1)}, f32[256,128]{1,0:T(8,128)S(1)}, u32[]{:S(2)}, u32[]{:S(2)}) %collective-permute-start.19) | collective-permute-done | bytes 131104 | tf_op jit(solution)/shard_map/ppermute | solution.py:328
  50.5 1.2 %collective-permute-done.18.refs_4_ = f32[256,128]{1,0:T(8,128)S(1)} collective-permute-done((f32[256,128]{1,0:T(8,128)S(1)}, f32[256,128]{1,0:T(8,128)S(1)}, u32[]{:S(2)}, u32[]{:S(2)}) %collective-permute-start.18) | collective-permute-done | bytes 131104 | tf_op jit(solution)/shard_map/ppermute | solution.py:328
  51.7 0.2 collective-permute-done.17.refs_3_
  51.9 1.1 %shard_map.50 = (bf16[1024,256]{1,0:T(8,128)(2,1)S(1)}, bf16[256,256]{1,0:T(8,128)(2,1)S(1)}, bf16[256,256]{1,0:T(8,128)(2,1)S(1)}) custom-call(f32[8,128]{1,0:T(8,128)S(1)} %get-tuple-element.57.refs_0_, f32[8,128]{1,0:T(8,128)S(1)} %collective-permute-done.16.refs_1_, f32[256,128]{1,0:T(8,128)S(1)} %get-tuple-element.58.refs_2_, ...), custom_call_target="tpu_custom_call" | custom-call | bytes 1589248 | tf_op jit(solution)/shard_map/pallas_call | solution.py:33
  53.1 0.1 collective-permute-start.23
  53.1 0.7 shard_map.51
  53.9 0.6 collective-permute-start.22
  54.4 1.0 %shard_map.52 = (f32[256,128]{1,0:T(8,128)S(1)}, f32[304,128]{1,0:T(8,128)S(1)}, f32[304,128]{1,0:T(8,128)S(1)}) custom-call(bf16[1024,256]{1,0:T(8,128)(2,1)S(1)} %get-tuple-element.63.refs_0_.refs_10_, bf16[256,2048]{1,0:T(8,128)(2,1)S(1)} %get-tuple-element.40.refs_0_.refs_8_.refs_1_, bf16[256,2048]{1,0:T(8,128)(2,1)S(1)} %get-tuple-element.44.refs_9_.refs_2_, ...), custom_call_target="tpu_custom_call" | custom-call | flops 603979776 | bytes 7258112 | tf_op jit(solution)/shard_map/pallas_call | solution.py:33
  55.4 1.0 %shard_map.53 = (f32[256,128]{1,0:T(8,128)S(1)}, f32[288,128]{1,0:T(8,128)S(1)}, f32[288,128]{1,0:T(8,128)S(1)}, f32[8,128]{1,0:T(8,128)S(1)}) custom-call(bf16[1024,256]{1,0:T(8,128)(2,1)S(1)} %collective-permute-done.23.refs_0_, bf16[256,2048]{1,0:T(8,128)(2,1)S(1)} %get-tuple-element.40.refs_0_.refs_8_.refs_1_, ...), custom_call_target="tpu_custom_call" | custom-call | flops 603979776 | bytes 8474624 | tf_op jit(solution)/shard_map/pallas_call | solution.py:33
  56.5 1.6 %collective-permute-start.26 = (f32[8,128]{1,0:T(8,128)S(1)}, f32[8,128]{1,0:T(8,128)S(1)}, u32[]{:S(2)}, u32[]{:S(2)}) collective-permute-start(f32[8,128]{1,0:T(8,128)S(1)} %get-tuple-element.68), channel_id=1, source_target_pairs={{24,0},{0,16},{16,8},{8,24},{25,1},{1,17},{17,9},{9,25},{26,2},{2,... | collective-permute-start | bytes 12296 | tf_op jit(solution)/shard_map/ppermute | solution.py:335
  58.1 0.8 %collective-permute-start.25 = (f32[8,128]{1,0:T(8,128)S(1)}, f32[8,128]{1,0:T(8,128)S(1)}, u32[]{:S(2)}, u32[]{:S(2)}) collective-permute-start(f32[8,128]{1,0:T(8,128)S(1)} %get-tuple-element.68), channel_id=1, source_target_pairs={{8,0},{24,16},{0,8},{16,24},{9,1},{25,17},{1,9},{17,25},{10,2},{26... | collective-permute-start | bytes 12296 | tf_op jit(solution)/shard_map/ppermute | solution.py:335
  59.0 2.4 %collective-permute-start.24 = (f32[8,128]{1,0:T(8,128)S(1)}, f32[8,128]{1,0:T(8,128)S(1)}, u32[]{:S(2)}, u32[]{:S(2)}) collective-permute-start(f32[8,128]{1,0:T(8,128)S(1)} %get-tuple-element.68), channel_id=1, source_target_pairs={{16,0},{8,16},{24,8},{0,24},{17,1},{9,17},{25,9},{1,25},{18,2},{10... | collective-permute-start | bytes 12296 | tf_op jit(solution)/shard_map/ppermute | solution.py:335
  61.4 0.1 collective-permute-start.28
  61.5 0.5 collective-permute-done.26
  61.9 1.1 %collective-permute-start.29 = (f32[288,128]{1,0:T(8,128)S(1)}, f32[288,128]{1,0:T(8,128)S(1)}, u32[]{:S(2)}, u32[]{:S(2)}) collective-permute-start(f32[288,128]{1,0:T(8,128)S(1)} %get-tuple-element.72), channel_id=1, source_target_pairs={{24,0},{0,16},{16,8},{8,24},{25,1},{1,17},{17,9},{9,25},{26,2},{2,... | collective-permute-start | bytes 442376 | tf_op jit(solution)/shard_map/ppermute | solution.py:335
  63.1 0.5 collective-permute-done.24
  63.6 1.2 %collective-permute-done.27.refs_1_ = f32[8,128]{1,0:T(8,128)S(1)} collective-permute-done((f32[8,128]{1,0:T(8,128)S(1)}, f32[8,128]{1,0:T(8,128)S(1)}, u32[]{:S(2)}, u32[]{:S(2)}) %collective-permute-start.27) | collective-permute-done | bytes 4128 | tf_op jit(solution)/shard_map/ppermute | solution.py:328
  64.7 0.1 shard_map.54
  64.8 0.9 %collective-permute-start.30 = (f32[264,128]{1,0:T(8,128)S(1)}, f32[264,128]{1,0:T(8,128)S(1)}, u32[]{:S(2)}, u32[]{:S(2)}) collective-permute-start(f32[264,128]{1,0:T(8,128)S(1)} %get-tuple-element.73), channel_id=1, source_target_pairs={{0,2},{1,3},{2,0},{3,1},{4,6},{5,7},{6,4},{7,5},{8,10},{9,11},{10,... | collective-permute-start | bytes 405512 | tf_op jit(solution)/shard_map/ppermute | solution.py:328
  65.7 1.5 %collective-permute-start.31 = (f32[264,128]{1,0:T(8,128)S(1)}, f32[264,128]{1,0:T(8,128)S(1)}, u32[]{:S(2)}, u32[]{:S(2)}) collective-permute-start(f32[264,128]{1,0:T(8,128)S(1)} %get-tuple-element.74), channel_id=1, source_target_pairs={{0,4},{1,5},{2,6},{3,7},{4,0},{5,1},{6,2},{7,3},{8,12},{9,13},{10,... | collective-permute-start | bytes 405512 | tf_op jit(solution)/shard_map/ppermute | solution.py:328
  67.2 1.2 %collective-permute-start.32 = (f32[264,128]{1,0:T(8,128)S(1)}, f32[264,128]{1,0:T(8,128)S(1)}, u32[]{:S(2)}, u32[]{:S(2)}) collective-permute-start(f32[264,128]{1,0:T(8,128)S(1)} %get-tuple-element.75), channel_id=1, source_target_pairs={{0,6},{1,7},{2,4},{3,5},{4,2},{5,3},{6,0},{7,1},{8,14},{9,15},{10,... | collective-permute-start | bytes 405512 | tf_op jit(solution)/shard_map/ppermute | solution.py:328
  68.4 2.9 %collective-permute-done.30.refs_4_ = f32[264,128]{1,0:T(8,128)S(1)} collective-permute-done((f32[264,128]{1,0:T(8,128)S(1)}, f32[264,128]{1,0:T(8,128)S(1)}, u32[]{:S(2)}, u32[]{:S(2)}) %collective-permute-start.30) | collective-permute-done | bytes 135200 | tf_op jit(solution)/shard_map/ppermute | solution.py:328
  71.3 1.7 %collective-permute-done.31.refs_5_ = f32[264,128]{1,0:T(8,128)S(1)} collective-permute-done((f32[264,128]{1,0:T(8,128)S(1)}, f32[264,128]{1,0:T(8,128)S(1)}, u32[]{:S(2)}, u32[]{:S(2)}) %collective-permute-start.31) | collective-permute-done | bytes 135200 | tf_op jit(solution)/shard_map/ppermute | solution.py:328
  73.0 1.0 %collective-permute-done.32.refs_6_ = f32[264,128]{1,0:T(8,128)S(1)} collective-permute-done((f32[264,128]{1,0:T(8,128)S(1)}, f32[264,128]{1,0:T(8,128)S(1)}, u32[]{:S(2)}, u32[]{:S(2)}) %collective-permute-start.32) | collective-permute-done | bytes 135200 | tf_op jit(solution)/shard_map/ppermute | solution.py:328
  74.0 1.0 %shard_map.55 = (f32[256,128]{1,0:T(8,128)}, f32[256,128]{1,0:T(8,128)}) custom-call(f32[264,128]{1,0:T(8,128)S(1)} %get-tuple-element.69.refs_0_, f32[256,128]{1,0:T(8,128)S(1)} %get-tuple-element.70.refs_1_, f32[288,128]{1,0:T(8,128)S(1)} %collective-permute-done.28.refs_2_, f32[288,128]{1,0:T(8,128)S(1)} %collective-permute-done.29.refs_3_, ...), custom_call_target="tpu_custom_call" | custom-call | bytes 1228800 | tf_op jit(solution)/shard_map/pallas_call | solution.py:33
  (23 shorter events, 0.1 us)
Async XLA Ops:
  1.6 16.1 %collective-permute-start.1 = (bf16[256,512]{1,0:T(8,128)(2,1)S(1)}, bf16[256,512]{1,0:T(8,128)(2,1)S(1)}, u32[]{:S(2)}, u32[]{:S(2)}) collective-permute-start(bf16[256,512]{1,0:T(8,128)(2,1)S(1)} %constant_dynamic-slice_fusion.rows.rows_ref), channel_id=1, source_target_pairs={{16,0},{8,16},{24,8},{0,24},{17,1},{9,17},{25,9},{1,25},{18,2},{10... | collective-permute-start | bytes 786440 | tf_op jit(solution)/shard_map/ppermute | solution.py:335
  6.7 0.9 %copy-start.1 = (f32[256,128]{1,0:T(8,128)S(1)}, f32[256,128]{1,0:T(8,128)}, u32[]{:S(2)}) copy-start(f32[256,128]{1,0:T(8,128)} %logits.1) | copy-start | bytes 393220
  7.8 16.3 %collective-permute-start.9 = (bf16[256,768]{1,0:T(8,128)(2,1)S(1)}, bf16[256,768]{1,0:T(8,128)(2,1)S(1)}, u32[]{:S(2)}, u32[]{:S(2)}) collective-permute-start(bf16[256,768]{1,0:T(8,128)(2,1)S(1)} %get-tuple-element.45), channel_id=1, source_target_pairs={{0,8},{8,0},{16,24},{24,16},{1,9},{9,1},{17,25},{25,17},{2,10},{10... | collective-permute-start | bytes 1179656 | tf_op jit(solution)/shard_map/ppermute | solution.py:335
  7.8 10.8 %collective-permute-start.4 = (bf16[256,256]{1,0:T(8,128)(2,1)S(1)}, bf16[256,256]{1,0:T(8,128)(2,1)S(1)}, u32[]{:S(2)}, u32[]{:S(2)}) collective-permute-start(bf16[256,256]{1,0:T(8,128)(2,1)S(1)} %get-tuple-element.43.refs_0_.own), channel_id=1, source_target_pairs={{0,6},{1,7},{2,4},{3,5},{4,2},{5,3},{6,0},{7,1},{8,14},{9,15},{10,... | collective-permute-start | bytes 393224 | tf_op jit(solution)/shard_map/ppermute | solution.py:328
  10.4 8.4 %collective-permute-start.3 = (bf16[256,256]{1,0:T(8,128)(2,1)S(1)}, bf16[256,256]{1,0:T(8,128)(2,1)S(1)}, u32[]{:S(2)}, u32[]{:S(2)}) collective-permute-start(bf16[256,256]{1,0:T(8,128)(2,1)S(1)} %get-tuple-element.43.refs_0_.own), channel_id=1, source_target_pairs={{0,4},{1,5},{2,6},{3,7},{4,0},{5,1},{6,2},{7,3},{8,12},{9,13},{10,... | collective-permute-start | bytes 393224 | tf_op jit(solution)/shard_map/ppermute | solution.py:328
  10.9 8.4 %collective-permute-start.2 = (bf16[256,256]{1,0:T(8,128)(2,1)S(1)}, bf16[256,256]{1,0:T(8,128)(2,1)S(1)}, u32[]{:S(2)}, u32[]{:S(2)}) collective-permute-start(bf16[256,256]{1,0:T(8,128)(2,1)S(1)} %get-tuple-element.43.refs_0_.own), channel_id=1, source_target_pairs={{0,2},{1,3},{2,0},{3,1},{4,6},{5,7},{6,4},{7,5},{8,10},{9,11},{10,... | collective-permute-start | bytes 393224 | tf_op jit(solution)/shard_map/ppermute | solution.py:328
  11.4 1.6 %copy-start = (bf16[2048,512]{1,0:T(8,128)(2,1)S(1)}, bf16[2048,512]{1,0:T(8,128)(2,1)}, u32[]{:S(2)}) copy-start(bf16[2048,512]{1,0:T(8,128)(2,1)} %plane_ref.5) | copy-start | bytes 6291460
  17.7 9.5 %collective-permute-start = (bf16[272,256]{1,0:T(8,128)(2,1)S(1)}, bf16[272,256]{1,0:T(8,128)(2,1)S(1)}, u32[]{:S(2)}, u32[]{:S(2)}) collective-permute-start(bf16[272,256]{1,0:T(8,128)(2,1)S(1)} %get-tuple-element.39), channel_id=1, source_target_pairs={{16,0},{8,16},{24,8},{0,24},{17,1},{9,17},{25,9},{1,25},{18,2},{10... | collective-permute-start | bytes 417800 | tf_op jit(solution)/shard_map/ppermute | solution.py:335
  18.6 6.3 %collective-permute-start.5 = (bf16[256,256]{1,0:T(8,128)(2,1)S(1)}, bf16[256,256]{1,0:T(8,128)(2,1)S(1)}, u32[]{:S(2)}, u32[]{:S(2)}) collective-permute-start(bf16[256,256]{1,0:T(8,128)(2,1)S(1)} %get-tuple-element.43.refs_0_.own), channel_id=1, source_target_pairs={{0,1},{1,0},{2,3},{3,2},{4,5},{5,4},{6,7},{7,6},{8,9},{9,8},{10,11... | collective-permute-start | bytes 393224 | tf_op jit(solution)/shard_map/ppermute | solution.py:328
  18.7 6.2 %collective-permute-start.8 = (bf16[256,256]{1,0:T(8,128)(2,1)S(1)}, bf16[256,256]{1,0:T(8,128)(2,1)S(1)}, u32[]{:S(2)}, u32[]{:S(2)}) collective-permute-start(bf16[256,256]{1,0:T(8,128)(2,1)S(1)} %collective-permute-done.4.refs_3_), channel_id=1, source_target_pairs={{0,1},{1,0},{2,3},{3,2},{4,5},{5,4},{6,7},{7,6},{8,9},{9,8},{10,11... | collective-permute-start | bytes 393224 | tf_op jit(solution)/shard_map/ppermute | solution.py:328
  19.2 5.7 %collective-permute-start.7 = (bf16[256,256]{1,0:T(8,128)(2,1)S(1)}, bf16[256,256]{1,0:T(8,128)(2,1)S(1)}, u32[]{:S(2)}, u32[]{:S(2)}) collective-permute-start(bf16[256,256]{1,0:T(8,128)(2,1)S(1)} %collective-permute-done.3.refs_2_), channel_id=1, source_target_pairs={{0,1},{1,0},{2,3},{3,2},{4,5},{5,4},{6,7},{7,6},{8,9},{9,8},{10,11... | collective-permute-start | bytes 393224 | tf_op jit(solution)/shard_map/ppermute | solution.py:328
  24.1 1.3 %collective-permute-start.6 = (bf16[256,256]{1,0:T(8,128)(2,1)S(1)}, bf16[256,256]{1,0:T(8,128)(2,1)S(1)}, u32[]{:S(2)}, u32[]{:S(2)}) collective-permute-start(bf16[256,256]{1,0:T(8,128)(2,1)S(1)} %collective-permute-done.2.refs_1_), channel_id=1, source_target_pairs={{0,1},{1,0},{2,3},{3,2},{4,5},{5,4},{6,7},{7,6},{8,9},{9,8},{10,11... | collective-permute-start | bytes 393224 | tf_op jit(solution)/shard_map/ppermute | solution.py:328
  28.1 2.0 %collective-permute-start.10 = (f32[1032,128]{1,0:T(8,128)S(1)}, f32[1032,128]{1,0:T(8,128)S(1)}, u32[]{:S(2)}, u32[]{:S(2)}) collective-permute-start(f32[1032,128]{1,0:T(8,128)S(1)} %get-tuple-element.52), channel_id=1, source_target_pairs={{0,1},{1,0},{2,3},{3,2},{4,5},{5,4},{6,7},{7,6},{8,9},{9,8},{10,11... | collective-permute-start | bytes 1585160 | tf_op jit(solution)/shard_map/ppermute | solution.py:328
  28.3 9.6 %collective-permute-start.11 = (f32[304,128]{1,0:T(8,128)S(1)}, f32[304,128]{1,0:T(8,128)S(1)}, u32[]{:S(2)}, u32[]{:S(2)}) collective-permute-start(f32[304,128]{1,0:T(8,128)S(1)} %get-tuple-element.49.refs_1_), channel_id=1, source_target_pairs={{0,8},{8,0},{16,24},{24,16},{1,9},{9,1},{17,25},{25,17},{2,10},{10... | collective-permute-start | bytes 466952 | tf_op jit(solution)/shard_map/ppermute | solution.py:335
  28.6 9.3 %collective-permute-start.12 = (f32[304,128]{1,0:T(8,128)S(1)}, f32[304,128]{1,0:T(8,128)S(1)}, u32[]{:S(2)}, u32[]{:S(2)}) collective-permute-start(f32[304,128]{1,0:T(8,128)S(1)} %get-tuple-element.50.refs_2_), channel_id=1, source_target_pairs={{24,0},{0,16},{16,8},{8,24},{25,1},{1,17},{17,9},{9,25},{26,2},{2,... | collective-permute-start | bytes 466952 | tf_op jit(solution)/shard_map/ppermute | solution.py:335
  30.1 7.8 %collective-permute-start.13 = (f32[264,128]{1,0:T(8,128)S(1)}, f32[264,128]{1,0:T(8,128)S(1)}, u32[]{:S(2)}, u32[]{:S(2)}) collective-permute-start(f32[264,128]{1,0:T(8,128)S(1)} %get-tuple-element.54), channel_id=1, source_target_pairs={{0,2},{1,3},{2,0},{3,1},{4,6},{5,7},{6,4},{7,5},{8,10},{9,11},{10,... | collective-permute-start | bytes 405512 | tf_op jit(solution)/shard_map/ppermute | solution.py:328
  32.0 8.3 %collective-permute-start.14 = (f32[264,128]{1,0:T(8,128)S(1)}, f32[264,128]{1,0:T(8,128)S(1)}, u32[]{:S(2)}, u32[]{:S(2)}) collective-permute-start(f32[264,128]{1,0:T(8,128)S(1)} %get-tuple-element.55), channel_id=1, source_target_pairs={{0,4},{1,5},{2,6},{3,7},{4,0},{5,1},{6,2},{7,3},{8,12},{9,13},{10,... | collective-permute-start | bytes 405512 | tf_op jit(solution)/shard_map/ppermute | solution.py:328
  33.5 6.7 %collective-permute-start.15 = (f32[264,128]{1,0:T(8,128)S(1)}, f32[264,128]{1,0:T(8,128)S(1)}, u32[]{:S(2)}, u32[]{:S(2)}) collective-permute-start(f32[264,128]{1,0:T(8,128)S(1)} %get-tuple-element.56), channel_id=1, source_target_pairs={{0,6},{1,7},{2,4},{3,5},{4,2},{5,3},{6,0},{7,1},{8,14},{9,15},{10,... | collective-permute-start | bytes 405512 | tf_op jit(solution)/shard_map/ppermute | solution.py:328
  40.3 6.6 %collective-permute-start.16 = (f32[8,128]{1,0:T(8,128)S(1)}, f32[8,128]{1,0:T(8,128)S(1)}, u32[]{:S(2)}, u32[]{:S(2)}) collective-permute-start(f32[8,128]{1,0:T(8,128)S(1)} %get-tuple-element.57.refs_0_), channel_id=1, source_target_pairs={{24,0},{0,16},{16,8},{8,24},{25,1},{1,17},{17,9},{9,25},{26,2},{2,... | collective-permute-start | bytes 12296 | tf_op jit(solution)/shard_map/ppermute | solution.py:335
  41.7 10.2 %collective-permute-start.21 = (f32[264,128]{1,0:T(8,128)S(1)}, f32[264,128]{1,0:T(8,128)S(1)}, u32[]{:S(2)}, u32[]{:S(2)}) collective-permute-start(f32[264,128]{1,0:T(8,128)S(1)} %get-tuple-element.59), channel_id=1, source_target_pairs={{16,0},{8,16},{24,8},{0,24},{17,1},{9,17},{25,9},{1,25},{18,2},{10... | collective-permute-start | bytes 405512 | tf_op jit(solution)/shard_map/ppermute | solution.py:335
  44.2 7.8 %collective-permute-start.20 = (f32[264,128]{1,0:T(8,128)S(1)}, f32[264,128]{1,0:T(8,128)S(1)}, u32[]{:S(2)}, u32[]{:S(2)}) collective-permute-start(f32[264,128]{1,0:T(8,128)S(1)} %get-tuple-element.59), channel_id=1, source_target_pairs={{0,8},{8,0},{16,24},{24,16},{1,9},{9,1},{17,25},{25,17},{2,10},{10... | collective-permute-start | bytes 405512 | tf_op jit(solution)/shard_map/ppermute | solution.py:335
  44.2 6.4 %collective-permute-start.19 = (f32[256,128]{1,0:T(8,128)S(1)}, f32[256,128]{1,0:T(8,128)S(1)}, u32[]{:S(2)}, u32[]{:S(2)}) collective-permute-start(f32[256,128]{1,0:T(8,128)S(1)} %get-tuple-element.58.refs_2_), channel_id=1, source_target_pairs={{0,6},{1,7},{2,4},{3,5},{4,2},{5,3},{6,0},{7,1},{8,14},{9,15},{10,... | collective-permute-start | bytes 393224 | tf_op jit(solution)/shard_map/ppermute | solution.py:328
  45.7 6.1 %collective-permute-start.18 = (f32[256,128]{1,0:T(8,128)S(1)}, f32[256,128]{1,0:T(8,128)S(1)}, u32[]{:S(2)}, u32[]{:S(2)}) collective-permute-start(f32[256,128]{1,0:T(8,128)S(1)} %get-tuple-element.58.refs_2_), channel_id=1, source_target_pairs={{0,4},{1,5},{2,6},{3,7},{4,0},{5,1},{6,2},{7,3},{8,12},{9,13},{10,... | collective-permute-start | bytes 393224 | tf_op jit(solution)/shard_map/ppermute | solution.py:328
  46.9 5.1 %collective-permute-start.17 = (f32[256,128]{1,0:T(8,128)S(1)}, f32[256,128]{1,0:T(8,128)S(1)}, u32[]{:S(2)}, u32[]{:S(2)}) collective-permute-start(f32[256,128]{1,0:T(8,128)S(1)} %get-tuple-element.58.refs_2_), channel_id=1, source_target_pairs={{0,2},{1,3},{2,0},{3,1},{4,6},{5,7},{6,4},{7,5},{8,10},{9,11},{10,... | collective-permute-start | bytes 393224 | tf_op jit(solution)/shard_map/ppermute | solution.py:328
  53.1 2.4 %collective-permute-start.23 = (bf16[1024,256]{1,0:T(8,128)(2,1)S(1)}, bf16[1024,256]{1,0:T(8,128)(2,1)S(1)}, u32[]{:S(2)}, u32[]{:S(2)}) collective-permute-start(bf16[1024,256]{1,0:T(8,128)(2,1)S(1)} %get-tuple-element.63.refs_0_.refs_10_), channel_id=1, source_target_pairs={{0,1},{1,0},{2,3},{3,2},{4,5},{5,4},{6,7},{7,6},{8,9},{9,8},{10,11... | collective-permute-start | bytes 1572872 | tf_op jit(solution)/shard_map/ppermute | solution.py:328
  53.9 9.7 %collective-permute-start.22 = (f32[1024,128]{1,0:T(8,128)S(1)}, f32[1024,128]{1,0:T(8,128)S(1)}, u32[]{:S(2)}, u32[]{:S(2)}) collective-permute-start(f32[1024,128]{1,0:T(8,128)S(1)} %get-tuple-element.62), channel_id=1, source_target_pairs={{0,1},{1,0},{2,3},{3,2},{4,5},{5,4},{6,7},{7,6},{8,9},{9,8},{10,11... | collective-permute-start | bytes 1572872 | tf_op jit(solution)/shard_map/ppermute | solution.py:328
  56.5 5.5 %collective-permute-start.26 = (f32[8,128]{1,0:T(8,128)S(1)}, f32[8,128]{1,0:T(8,128)S(1)}, u32[]{:S(2)}, u32[]{:S(2)}) collective-permute-start(f32[8,128]{1,0:T(8,128)S(1)} %get-tuple-element.68), channel_id=1, source_target_pairs={{24,0},{0,16},{16,8},{8,24},{25,1},{1,17},{17,9},{9,25},{26,2},{2,... | collective-permute-start | bytes 12296 | tf_op jit(solution)/shard_map/ppermute | solution.py:335
  58.1 5.0 %collective-permute-start.25 = (f32[8,128]{1,0:T(8,128)S(1)}, f32[8,128]{1,0:T(8,128)S(1)}, u32[]{:S(2)}, u32[]{:S(2)}) collective-permute-start(f32[8,128]{1,0:T(8,128)S(1)} %get-tuple-element.68), channel_id=1, source_target_pairs={{8,0},{24,16},{0,8},{16,24},{9,1},{25,17},{1,9},{17,25},{10,2},{26... | collective-permute-start | bytes 12296 | tf_op jit(solution)/shard_map/ppermute | solution.py:335
  59.0 4.6 %collective-permute-start.24 = (f32[8,128]{1,0:T(8,128)S(1)}, f32[8,128]{1,0:T(8,128)S(1)}, u32[]{:S(2)}, u32[]{:S(2)}) collective-permute-start(f32[8,128]{1,0:T(8,128)S(1)} %get-tuple-element.68), channel_id=1, source_target_pairs={{16,0},{8,16},{24,8},{0,24},{17,1},{9,17},{25,9},{1,25},{18,2},{10... | collective-permute-start | bytes 12296 | tf_op jit(solution)/shard_map/ppermute | solution.py:335
  61.4 12.6 %collective-permute-start.28 = (f32[288,128]{1,0:T(8,128)S(1)}, f32[288,128]{1,0:T(8,128)S(1)}, u32[]{:S(2)}, u32[]{:S(2)}) collective-permute-start(f32[288,128]{1,0:T(8,128)S(1)} %get-tuple-element.71), channel_id=1, source_target_pairs={{0,8},{8,0},{16,24},{24,16},{1,9},{9,1},{17,25},{25,17},{2,10},{10... | collective-permute-start | bytes 442376 | tf_op jit(solution)/shard_map/ppermute | solution.py:335
  61.9 12.1 %collective-permute-start.29 = (f32[288,128]{1,0:T(8,128)S(1)}, f32[288,128]{1,0:T(8,128)S(1)}, u32[]{:S(2)}, u32[]{:S(2)}) collective-permute-start(f32[288,128]{1,0:T(8,128)S(1)} %get-tuple-element.72), channel_id=1, source_target_pairs={{24,0},{0,16},{16,8},{8,24},{25,1},{1,17},{17,9},{9,25},{26,2},{2,... | collective-permute-start | bytes 442376 | tf_op jit(solution)/shard_map/ppermute | solution.py:335
  63.6 1.2 %collective-permute-start.27 = (f32[8,128]{1,0:T(8,128)S(1)}, f32[8,128]{1,0:T(8,128)S(1)}, u32[]{:S(2)}, u32[]{:S(2)}) collective-permute-start(f32[8,128]{1,0:T(8,128)S(1)} %add_add_fusion.refs_0_), channel_id=1, source_target_pairs={{0,1},{1,0},{2,3},{3,2},{4,5},{5,4},{6,7},{7,6},{8,9},{9,8},{10,11... | collective-permute-start | bytes 12296 | tf_op jit(solution)/shard_map/ppermute | solution.py:328
  64.8 6.5 %collective-permute-start.30 = (f32[264,128]{1,0:T(8,128)S(1)}, f32[264,128]{1,0:T(8,128)S(1)}, u32[]{:S(2)}, u32[]{:S(2)}) collective-permute-start(f32[264,128]{1,0:T(8,128)S(1)} %get-tuple-element.73), channel_id=1, source_target_pairs={{0,2},{1,3},{2,0},{3,1},{4,6},{5,7},{6,4},{7,5},{8,10},{9,11},{10,... | collective-permute-start | bytes 405512 | tf_op jit(solution)/shard_map/ppermute | solution.py:328
  65.7 7.3 %collective-permute-start.31 = (f32[264,128]{1,0:T(8,128)S(1)}, f32[264,128]{1,0:T(8,128)S(1)}, u32[]{:S(2)}, u32[]{:S(2)}) collective-permute-start(f32[264,128]{1,0:T(8,128)S(1)} %get-tuple-element.74), channel_id=1, source_target_pairs={{0,4},{1,5},{2,6},{3,7},{4,0},{5,1},{6,2},{7,3},{8,12},{9,13},{10,... | collective-permute-start | bytes 405512 | tf_op jit(solution)/shard_map/ppermute | solution.py:328
  67.2 6.8 %collective-permute-start.32 = (f32[264,128]{1,0:T(8,128)S(1)}, f32[264,128]{1,0:T(8,128)S(1)}, u32[]{:S(2)}, u32[]{:S(2)}) collective-permute-start(f32[264,128]{1,0:T(8,128)S(1)} %get-tuple-element.75), channel_id=1, source_target_pairs={{0,6},{1,7},{2,4},{3,5},{4,2},{5,3},{6,0},{7,1},{8,14},{9,15},{10,... | collective-permute-start | bytes 405512 | tf_op jit(solution)/shard_map/ppermute | solution.py:328
